TPU v7x, 128 devices: a whole 4x4x4 slice. The times are simulated.
128 devices in a mesh: seg: 4 (over y), node: 32 (over x, z, core).
Axes of the slice: x: 4, y: 4, z: 4, core: 2. Of those that a mesh axis runs over, the one named last changes fastest.
Arguments:
- memory_base: bfloat16 [8192, 512], P('node'), may hold values from -1 to 1
- messages: bfloat16 [4, 8192, 512], P('seg', 'node'), may hold values from -6 to 6
- touched: int32 [4, 8192], P('seg', 'node'), may hold values 0 or 1
- gru_input: bfloat16 [512, 1536], replicated, may hold values from -0.25 to 0.25
- gru_state: bfloat16 [512, 1536], replicated, may hold values from -0.25 to 0.25
- attn_weights: bfloat16 [4, 512, 512], replicated, may hold values from -0.25 to 0.25
- frequency: float32 [512], replicated, may hold values from 0.001 to 1
- request_rows: int32 [4, 32, 256], P('seg', 'node'), may hold values from 0 to 255
- event_slots: int32 [4, 8192, 9], P('seg', 'node'), may hold values from 0 to 255
- delays: int32 [4, 8192, 8], P('seg', 'node'), may hold values from 0 to 999
- upstream: bfloat16 [4, 8192, 512], P('seg', 'node'), may hold values from -6 to 6
Outputs:
- embedded: bfloat16 [4, 8192, 512], P('seg', 'node')
- memory_out: bfloat16 [4, 8192, 512], P('seg', 'node')
- memory_grad: float32 [4, 8192, 512], P('seg', 'node')
- weight_grad: float32 [4, 512, 512], replicated
Inputs may be any that keep to these rules, and one draw needn't show every extreme that they name: `request_rows`: a row within one owner. `event_slots`: a slot of the event's own block.
All inputs are finite; a program needn't handle non-finite values. No bound on the sum of `touched` on one device may be relied on, other than what follows from the above.
Results may differ from a plain program's by a relative error of at most 0.01.
Values may be sent and summed in bfloat16 or wider, within the bound.
No kernel may reach another device: no remote copies, remote signals or barrier semaphores. Data moves between devices by JAX's collectives and lax.ppermute only.
A program may use at most 128 MiB of HBM per device.

v0:
```python
import jax
import jax.numpy as jnp
from jax import lax
from jax.sharding import PartitionSpec as P

HEADS = 2


def carried_in(shard, axis, combine, identity):
    length, place = (lax.axis_size(axis), lax.axis_index(axis))
    everything = jax.tree.map(lambda part: lax.all_gather(part, axis), shard)
    start = jax.tree.map(
        lambda part, zero: jnp.broadcast_to(jnp.asarray(zero, part.dtype), part.shape),
        shard,
        identity,
    )

    def step(k, before):
        reached = k < place
        new = combine(before, jax.tree.map(lambda part: part[k], everything))
        return jax.tree.map(lambda a, b: jnp.where(reached, a, b), new, before)

    return lax.fori_loop(0, length, step, start)


def gru_update(message, state, w_input, w_state):
    width = state.shape[1]
    from_msg = jnp.dot(message, w_input, preferred_element_type=jnp.float32)
    from_state = jnp.dot(state, w_state, preferred_element_type=jnp.float32)
    update = jax.nn.sigmoid(from_msg[:, :width] + from_state[:, :width])
    reset = jax.nn.sigmoid(from_msg[:, width : 2 * width] + from_state[:, width : 2 * width])
    candidate = jnp.tanh(from_msg[:, 2 * width :] + reset * from_state[:, 2 * width :])
    return ((1.0 - update) * candidate + update * state.astype(jnp.float32)).astype(jnp.bfloat16)


def attend(source, neighbours, time_code, weights, upstream):
    count = source.shape[0]
    fanout = neighbours.shape[1]
    width = source.shape[1]
    head_size = width // HEADS
    w_query, w_key, w_value, w_out = (weights[0], weights[1], weights[2], weights[3])
    mixed = (
        (neighbours.astype(jnp.float32) + time_code)
        .astype(jnp.bfloat16)
        .reshape(count * fanout, width)
    )
    query = jnp.dot(source, w_query, preferred_element_type=jnp.float32).astype(jnp.bfloat16)
    keys = jnp.dot(mixed, w_key, preferred_element_type=jnp.float32).astype(jnp.bfloat16)
    values = jnp.dot(mixed, w_value, preferred_element_type=jnp.float32).astype(jnp.bfloat16)
    query_h = query.reshape(count, HEADS, head_size)
    keys_h = keys.reshape(count, fanout, HEADS, head_size)
    values_h = values.reshape(count, fanout, HEADS, head_size)
    scores = jnp.einsum(
        "ehd,ekhd->ehk", query_h, keys_h, preferred_element_type=jnp.float32
    ) / jnp.sqrt(jnp.float32(head_size))
    powered = jnp.exp(scores)
    probs = powered / jnp.sum(powered, axis=-1, keepdims=True)
    probs_b = probs.astype(jnp.bfloat16)
    attended = jnp.einsum("ehk,ekhd->ehd", probs_b, values_h, preferred_element_type=jnp.float32)
    attended = attended.reshape(count, width).astype(jnp.bfloat16)
    output = jnp.dot(attended, w_out, preferred_element_type=jnp.float32) + source.astype(
        jnp.float32
    )
    embedded = output.astype(jnp.bfloat16)
    grad_out = jnp.dot(attended.T, upstream, preferred_element_type=jnp.float32)
    d_att = jnp.dot(upstream, w_out.T, preferred_element_type=jnp.float32).astype(jnp.bfloat16)
    d_att_h = d_att.reshape(count, HEADS, head_size)
    d_probs = jnp.einsum("ehd,ekhd->ehk", d_att_h, values_h, preferred_element_type=jnp.float32)
    d_logits = probs * (d_probs - jnp.sum(probs * d_probs, axis=-1, keepdims=True))
    d_scores = (d_logits / jnp.sqrt(jnp.float32(head_size))).astype(jnp.bfloat16)
    d_values = (
        jnp.einsum("ehk,ehd->ekhd", probs_b, d_att_h, preferred_element_type=jnp.float32)
        .astype(jnp.bfloat16)
        .reshape(count * fanout, width)
    )
    d_query = (
        jnp.einsum("ehk,ekhd->ehd", d_scores, keys_h, preferred_element_type=jnp.float32)
        .astype(jnp.bfloat16)
        .reshape(count, width)
    )
    d_keys = (
        jnp.einsum("ehk,ehd->ekhd", d_scores, query_h, preferred_element_type=jnp.float32)
        .astype(jnp.bfloat16)
        .reshape(count * fanout, width)
    )
    grad_query = jnp.dot(source.T, d_query, preferred_element_type=jnp.float32)
    grad_key = jnp.dot(mixed.T, d_keys, preferred_element_type=jnp.float32)
    grad_value = jnp.dot(mixed.T, d_values, preferred_element_type=jnp.float32)
    d_source = upstream.astype(jnp.float32) + jnp.dot(
        d_query, w_query.T, preferred_element_type=jnp.float32
    )
    d_neighbours = jnp.dot(d_keys, w_key.T, preferred_element_type=jnp.float32) + jnp.dot(
        d_values, w_value.T, preferred_element_type=jnp.float32
    )
    weight_terms = jnp.stack([grad_query, grad_key, grad_value, grad_out])
    return (embedded, d_source, d_neighbours.reshape(count, fanout, width), weight_terms)


def latest_write(earlier, later):
    keeper = later[0] > 0
    return (jnp.maximum(earlier[0], later[0]), jnp.where(keeper[:, None], later[1], earlier[1]))


def on_device(
    memory_base,
    messages,
    touched,
    gru_input,
    gru_state,
    attn_weights,
    frequency,
    request_rows,
    event_slots,
    delays,
    upstream,
):
    nodes_here = memory_base.shape[0]
    width = memory_base.shape[1]
    owner_count = lax.axis_size("node")
    fresh = gru_update(messages[0], memory_base, gru_input, gru_state)
    own_mask = touched[0].astype(jnp.bfloat16)
    empty_rows = jnp.zeros_like(fresh)
    empty_mask = jnp.zeros_like(own_mask)
    prior_mask, prior_rows = carried_in(
        (own_mask, fresh), "seg", latest_write, (empty_mask, empty_rows)
    )
    start = jnp.where((prior_mask > 0)[:, None], prior_rows, memory_base)
    memory_now = jnp.where((touched[0] > 0)[:, None], fresh, start)
    plan_rows = request_rows[0, 0]
    slot_total = plan_rows.shape[0]
    per_owner = slot_total // owner_count
    owners = jnp.arange(slot_total, dtype=jnp.int32) // per_owner
    global_ids = owners * nodes_here + plan_rows
    piece = lax.all_gather(start, "node", axis=0, tiled=True)
    offset = global_ids
    onehot = (offset[:, None] == jnp.arange(piece.shape[0], dtype=jnp.int32)[None, :]).astype(
        jnp.bfloat16
    )
    slot_rows = jnp.dot(onehot, piece, preferred_element_type=jnp.float32).astype(jnp.bfloat16)
    chosen = event_slots[0]
    event_rows = slot_rows[chosen]
    time_code = jnp.cos(delays[0][..., None].astype(jnp.float32) * frequency)
    embedded, d_source, d_neighbours, weight_terms = attend(
        event_rows[:, 0], event_rows[:, 1:], time_code, attn_weights, upstream[0]
    )
    event_grads = jnp.concatenate([d_source[:, None], d_neighbours], axis=1).reshape(-1, width)
    slot_grads = jnp.zeros((slot_total, width), jnp.float32).at[chosen.reshape(-1)].add(event_grads)
    offset = global_ids
    inside = (offset >= 0) & (offset < nodes_here * lax.axis_size("node"))
    offset = jnp.where(inside, offset, nodes_here * lax.axis_size("node"))
    memory_grad = lax.psum_scatter(
        jnp.zeros((nodes_here * lax.axis_size("node"), width), jnp.float32)
        .at[offset]
        .add(slot_grads, mode="drop")
        .astype(jnp.bfloat16),
        "node",
        scatter_dimension=0,
        tiled=True,
    ).astype(jnp.float32)
    weight_grad = lax.psum(weight_terms, ("seg", "node"))
    return (embedded[None], memory_now[None], memory_grad[None], weight_grad)


def solution(mesh):
    in_specs = (
        P("node", None),
        P("seg", "node", None),
        P("seg", "node"),
        P(),
        P(),
        P(),
        P(),
        P("seg", "node", None),
        P("seg", "node", None),
        P("seg", "node", None),
        P("seg", "node", None),
    )
    out_specs = (P("seg", "node", None), P("seg", "node", None), P("seg", "node", None), P())
    return jax.shard_map(
        on_device, mesh=mesh, in_specs=in_specs, out_specs=out_specs, check_vma=False
    )
```

profile of v0, /device:TPU:1, one launch (start us, length us, event | category | flops | bytes accessed | tf_op | source)
XLA Modules:
  0.0 505.4 jit_solution(13062977628557586307)
XLA Ops:
  7.3 1.8 copy-done
  9.1 1.5 fusion.55
  10.6 1.5 fusion.70
  12.1 1.1 fusion.26
  13.4 8.9 %all-gather.1 = bf16[4,1,256]{2,1,0:T(2,128)(2,1)S(1)} all-gather(bf16[1,1,256]{2,1,0:T(2,128)(2,1)S(1)} %convert_bitcast_fusion.2), channel_id=1, replica_groups=mesh['seg'=4,'node'=32] {'seg'}, dimensions={0}, use_global_device_ids=true | all-gather | bytes 2560 | tf_op jit(solution)/shard_map/all_gather | solution.py:11
  22.4 17.4 %all-gather.7.cloned.1.call-done = bf16[1024,512]{1,0:T(8,128)(2,1)} async-done(((bf16[256,512]{1,0:T(8,128)(2,1)}), bf16[1024,512]{1,0:T(8,128)(2,1)}) %all-gather.7.cloned.1.call-update) | async-done | bytes 1048592 | tf_op jit(solution)/shard_map/all_gather | solution.py:11
  39.8 4.6 while.16
  39.8 1.1 select_select_fusion.2
  41.0 1.1 select_select_fusion.2
  42.1 1.1 select_select_fusion.2
  43.3 1.1 select_select_fusion.2
  45.4 1.4 convolution_convert_fusion.2
  48.1 52.0 %all-gather.5.cloned.1.call-done = bf16[8192,512]{1,0:T(8,128)(2,1)} async-done(((bf16[256,512]{1,0:T(8,128)(2,1)}), bf16[8192,512]{1,0:T(8,128)(2,1)}) %all-gather.5.cloned.1.call-update) | async-done | bytes 8388624 | tf_op jit(solution)/shard_map/all_gather | solution.py:134
  100.1 5.7 %fusion.15 = bf16[256,512]{1,0:T(8,128)(2,1)S(1)} fusion(bf16[8192,512]{1,0:T(8,128)(2,1)} %all-gather.5.cloned.1.call-done, s32[256]{0:T(256)S(1)} %fusion.61), kind=kOutput, calls=%fused_computation.38 | convolution fusion | flops 2149711872 | bytes 8651776 | tf_op jit(solution)/shard_map/dot_general | solution.py:139
  105.9 7.5 %gather_fusion = bf16[2304,512]{1,0:T(8,128)(2,1)} fusion(bf16[256,512]{1,0:T(8,128)(2,1)S(1)} %fusion.15, s32[3072]{0:T(1024)S(1)} %pad_clamp_fusion), kind=kCustom, calls=%fused_computation | custom fusion | bytes 4727808 | tf_op jit(solution)/shard_map/gather | solution.py:141
  113.4 5.3 %reshape.208 = bf16[256,9,512]{2,1,0:T(8,128)(2,1)} reshape(bf16[2304,512]{1,0:T(8,128)(2,1)} %gather_fusion) | data formatting | bytes 4718592 | tf_op jit(solution)/shard_map/gather | solution.py:141
  118.7 1.9 slice.56
  120.6 1.5 convolution_convert_fusion.3
  123.1 16.6 %convolution_convert_fusion = bf16[2048,512]{1,0:T(8,128)(2,1)S(1)} fusion(bf16[4,512,512]{2,1,0:T(8,128)(2,1)} %param.18, bf16[256,9,512]{2,1,0:T(8,128)(2,1)} %reshape.208, f32[512]{0:T(512)S(1)} %copy-done.22, f32[256,8]{1,0:T(8,128)S(1)} %copy.28), kind=kOutput, calls=%fused_computation.21 | convolution fusion | flops 1078984704 | bytes 4728832 | tf_op jit(solution)/shard_map/dot_general | solution.py:49
  139.7 17.6 %convolution_convert_fusion.1 = bf16[2048,512]{1,0:T(8,128)(2,1)} fusion(bf16[4,512,512]{2,1,0:T(8,128)(2,1)} %param.18, bf16[256,9,512]{2,1,0:T(8,128)(2,1)S(1)} %copy-done.5, f32[512]{0:T(512)S(1)} %copy-done.22, f32[256,8]{1,0:T(8,128)S(1)} %copy.28), kind=kOutput, calls=%fused_computation.22 | convolution fusion | flops 1078984704 | bytes 4851712 | tf_op jit(solution)/shard_map/dot_general | solution.py:48
  157.3 1.0 convert.13
  159.0 1.6 copy.36
  160.6 2.3 fusion.71
  162.9 1.6 copy.32
  164.4 6.6 %fusion.9 = f32[256,2,8]{1,2,0:T(8,128)S(1)} fusion(f32[256,2,1,8]{1,3,0,2:T(8,128)S(1)} %copy.32), kind=kOutput, calls=%fused_computation.26 | output fusion | flops 8711 | bytes 32768 | tf_op jit(solution)/shard_map/div | solution.py:57
  171.0 1.2 convert_convert_fusion
  172.2 5.4 %fusion.69 = (f32[256,2,8]{1,2,0:T(8,128)S(1)}, bf16[256,2,8]{1,2,0:T(8,128)(2,1)S(1)}) fusion(f32[256,2,8]{1,2,0:T(8,128)S(1)} %fusion.9, f32[256,2,1,8]{1,3,0,2:T(8,128)S(1)} %copy.36), kind=kOutput, calls=%fused_computation.120 | output fusion | flops 25095 | bytes 57344 | tf_op jit(solution)/shard_map/sub | solution.py:69
  177.7 3.8 copy.37
  181.5 2.5 fusion.74
  185.2 3.4 fusion.7
  189.2 3.8 fusion.8
  193.5 1.3 fusion.39
  194.9 1.3 add_bitcast_fusion
  196.2 4.5 pad_maximum_fusion
  200.7 7.3 %reshape.219 = f32[2304,512]{1,0:T(8,128)} reshape(f32[256,9,512]{2,1,0:T(8,128)} %pad_maximum_fusion) | data formatting | bytes 9437184 | tf_op jit(solution)/shard_map/reshape | solution.py:146
  207.9 16.4 %scatter_custom_fusion = f32[256,512]{1,0:T(8,128)S(1)} fusion(s32[2304]{0:T(1024)S(1)} %fusion.59, f32[2304,512]{1,0:T(8,128)} %reshape.219, f32[]{:T(128)} %constant.76.clone.1), kind=kCustom, calls=%fused_computation.90 | custom fusion | flops 1179648 | bytes 524800 | tf_op jit(solution)/shard_map/scatter-add | solution.py:147
  224.3 8.9 %scatter_custom_fusion.1 = f32[8192,512]{1,0:T(8,128)} fusion(s32[256]{0:T(256)S(1)} %bitcast.154, f32[256,512]{1,0:T(8,128)S(1)} %scatter_custom_fusion, f32[]{:T(128)} %constant.76.clone.1), kind=kCustom, calls=%fused_computation.11 | custom fusion | flops 131072 | bytes 16777220 | tf_op jit(solution)/shard_map/scatter-add | solution.py:154
  233.2 9.0 %convert_element_type.108 = bf16[8192,512]{1,0:T(8,128)(2,1)} convert(f32[8192,512]{1,0:T(8,128)} %scatter_custom_fusion.1) | non-fusion elementwise | flops 4194304 | bytes 25165824 | tf_op jit(solution)/shard_map/convert_element_type | solution.py:155
  243.2 3.1 copy.33
  246.2 2.4 fusion.72
  249.7 16.8 %convolution_bitcast_fusion.2 = f32[1,512,512]{2,1,0:T(8,128)S(1)} fusion(bf16[2048,512]{1,0:T(8,128)(2,1)} %bitcast.141, bf16[256,9,512]{2,1,0:T(8,128)(2,1)S(1)} %copy-done.6, f32[512]{0:T(512)S(1)} %copy-done.23, f32[256,8]{1,0:T(8,128)S(1)} %copy.28), kind=kOutput, calls=%fused_computation.32 | convolution fusion | flops 1077936128 | bytes 5376000 | tf_op jit(solution)/shard_map/dot_general | solution.py:88
  266.5 15.1 %convolution_bitcast_fusion.3 = f32[1,512,512]{2,1,0:T(8,128)S(1)} fusion(bf16[2048,512]{1,0:T(8,128)(2,1)S(1)} %bitcast.143, bf16[256,9,512]{2,1,0:T(8,128)(2,1)S(1)} %copy-done.6, f32[512]{0:T(512)S(1)} %copy-done.23, f32[256,8]{1,0:T(8,128)S(1)} %copy.28), kind=kOutput, calls=%fused_computation.33 | convolution fusion | flops 1077936128 | bytes 5376000 | tf_op jit(solution)/shard_map/dot_general | solution.py:87
  281.6 2.5 pad_maximum_fusion.1
  284.1 2.1 fusion.17
  286.2 46.3 %reduce-scatter.2.cloned.1.call-done = bf16[256,512]{1,0:T(8,128)(2,1)} async-done(((bf16[8192,512]{1,0:T(8,128)(2,1)}), bf16[256,512]{1,0:T(8,128)(2,1)}) %reduce-scatter.2.cloned.1.call-update) | async-done | bytes 262160 | tf_op jit(solution)/shard_map/reduce_scatter | solution.py:151
  332.5 1.8 bitcast_convert_fusion.2
  334.3 159.4 %all-reduce.2.cloned.1.call-done = f32[4,512,512]{2,1,0:T(8,128)} async-done(((f32[4,512,512]{2,1,0:T(8,128)}), f32[4,512,512]{2,1,0:T(8,128)}) %all-reduce.2.cloned.1.call-update) | async-done | bytes 4194320 | tf_op jit(solution)/shard_map/psum | solution.py:160
  493.7 4.8 copy.66
  (103 shorter events, 8.5 us)
Async XLA Ops:
  7.2 1.9 copy-start
  7.2 4.9 copy-start.9
  7.2 3.4 copy-start.12
  7.2 32.6 %all-gather.7.cloned.1.call-start = ((), (), s32[]{:S(2)}) async-start(), calls=%async_computation.4 | async-start | bytes 1310720 | tf_op jit(solution)/shard_map/all_gather | solution.py:11
  10.6 2.8 copy-start.21
  12.1 33.2 %copy-start.16 = (bf16[1,256,512]{2,1,0:T(8,128)(2,1)S(1)}, bf16[1,256,512]{2,1,0:T(8,128)(2,1)}, u32[]{:S(2)}) copy-start(bf16[1,256,512]{2,1,0:T(8,128)(2,1)} %param.23) | copy-start | bytes 786436
  13.3 31.1 %copy-start.8 = (bf16[256,512]{1,0:T(8,128)(2,1)S(1)}, bf16[256,512]{1,0:T(8,128)(2,1)}, u32[]{:S(2)}) copy-start(bf16[256,512]{1,0:T(8,128)(2,1)} %fusion.26) | copy-start | bytes 786436
  13.3 33.7 %copy-start.18 = (s32[1,256,9]{1,0,2:T(1,128)S(1)}, s32[1,256,9]{1,0,2:T(1,128)}, u32[]{:S(2)}) copy-start(s32[1,256,9]{1,0,2:T(1,128)} %param.21) | copy-start | bytes 27652
  13.3 86.8 %all-gather.5.cloned.1.call-start = ((), (), s32[]{:S(2)}) async-start(), calls=%async_computation.1 | async-start | bytes 8650752 | tf_op jit(solution)/shard_map/all_gather | solution.py:134
  39.8 7.7 %copy-start.19 = (s32[1,256,8]{1,2,0:T(8,128)S(1)}, s32[1,256,8]{1,2,0:T(8,128)}, u32[]{:S(2)}) copy-start(s32[1,256,8]{1,2,0:T(8,128)} %param.22) | copy-start | bytes 24580
  39.8 8.3 %copy-start.20 = (s32[1,1,256]{2,1,0:T(1,128)S(1)}, s32[1,1,256]{2,1,0:T(1,128)}, u32[]{:S(2)}) copy-start(s32[1,1,256]{2,1,0:T(1,128)} %param.20) | copy-start | bytes 3076
  45.3 287.2 %reduce-scatter.2.cloned.1.call-start = ((), (), s32[]{:S(2)}) async-start(), calls=%async_computation.2 | async-start | bytes 8650752 | tf_op jit(solution)/shard_map/reduce_scatter | solution.py:151
  113.4 9.7 %copy-start.22 = (f32[512]{0:T(512)S(1)}, f32[512]{0:T(512)}, u32[]{:S(2)}) copy-start(f32[512]{0:T(512)} %param.19) | copy-start | bytes 6148
  120.6 19.1 %copy-start.14 = (bf16[256,1,512]{2,1,0:T(2,128)(2,1)}, bf16[256,1,512]{2,1,0:T(2,128)(2,1)S(1)}, u32[]{:S(2)}) copy-start(bf16[256,1,512]{2,1,0:T(2,128)(2,1)S(1)} %slice.56) | copy-start | bytes 786436
  123.1 16.6 %copy-start.5 = (bf16[256,9,512]{2,1,0:T(8,128)(2,1)S(1)}, bf16[256,9,512]{2,1,0:T(8,128)(2,1)}, u32[]{:S(2)}) copy-start(bf16[256,9,512]{2,1,0:T(8,128)(2,1)} %reshape.208) | copy-start | bytes 7077892
  139.7 18.6 %copy-start.24 = (bf16[2048,512]{1,0:T(8,128)(2,1)}, bf16[2048,512]{1,0:T(8,128)(2,1)S(1)}, u32[]{:S(2)}) copy-start(bf16[2048,512]{1,0:T(8,128)(2,1)S(1)} %convolution_convert_fusion) | copy-start | bytes 6291460
  157.3 3.2 copy-start.17
  177.7 7.5 %copy-start.11 = (f32[256,2,256]{2,1,0:T(2,128)S(1)}, f32[256,2,256]{2,1,0:T(2,128)}, u32[]{:S(2)}) copy-start(f32[256,2,256]{2,1,0:T(2,128)} %convert.13) | copy-start | bytes 1572868
  181.5 2.8 copy-start.13
  185.2 4.0 copy-start.7
  189.2 5.7 %copy-start.3 = (bf16[256,8,2,256]{3,1,2,0:T(8,128)(2,1)}, bf16[256,8,2,256]{3,1,2,0:T(8,128)(2,1)S(1)}, u32[]{:S(2)}) copy-start(bf16[256,8,2,256]{3,1,2,0:T(8,128)(2,1)S(1)} %copy.43) | copy-start | bytes 6291460
  193.5 1.3 copy-start.2
  242.1 1.0 copy-start.10
  242.2 7.2 %copy-start.15 = (bf16[256,1,512]{2,1,0:T(2,128)(2,1)S(1)}, bf16[256,1,512]{2,1,0:T(2,128)(2,1)}, u32[]{:S(2)}) copy-start(bf16[256,1,512]{2,1,0:T(2,128)(2,1)} %copy-done.14) | copy-start | bytes 786436
  242.2 7.5 %copy-start.23 = (f32[512]{0:T(512)S(1)}, f32[512]{0:T(512)}, u32[]{:S(2)}) copy-start(f32[512]{0:T(512)} %param.19) | copy-start | bytes 6148
  242.2 251.5 %all-reduce.2.cloned.1.call-start = ((), (), s32[]{:S(2)}) async-start(), calls=%async_computation.3 | async-start | bytes 8388608 | tf_op jit(solution)/shard_map/psum | solution.py:160
  246.2 3.5 copy-start.6
  249.7 16.8 %copy-start.4 = (bf16[256,8,2,256]{3,1,2,0:T(8,128)(2,1)S(1)}, bf16[256,8,2,256]{3,1,2,0:T(8,128)(2,1)}, u32[]{:S(2)}) copy-start(bf16[256,8,2,256]{3,1,2,0:T(8,128)(2,1)} %copy-done.3) | copy-start | bytes 6291460
  493.7 4.8 copy-start.1
Sparse Core Ops, SparseCore 0:
  13.4 26.2 all-gather.6
  45.4 54.6 all-gather.4
  242.3 90.1 reduce-scatter.1
  338.7 154.9 all-reduce.1
where the time goes:
time: 514 us; the launch traced here: 505 us
  waiting for transfers between devices  275 us (54%)
  matrix products  91.3 us (18%)
  other arithmetic  71.1 us (14%)
  local copies, waits for them, and re-layouts  43.7 us (9%)
  between operations  14.8 us (3%)
  blocking collectives  8.92 us (2%)
    psum x1, waiting for transfers between devices, on_device(): weight_grad = lax.psum(weight_terms, ('seg', 'node'))  159 us
    all_gather x1, waiting for transfers between devices, on_device(): piece = lax.all_gather(start, 'node', axis=0, tiled=True)  52 us
    reduce_scatter x1, waiting for transfers between devices, on_device(): lax.psum_scatter(jnp.zeros((nodes_here * lax.axis_size('node'), width), j...  46.3 us
    dot_general x1, matrix products, attend(): jnp.dot(mixed, w_key, preferred_element_type=jnp.float32)  17.6 us
    all_gather x1, waiting for transfers between devices, carried_in(): everything = jax.tree.map(lambda part: lax.all_gather(part, axis), shard)  17.4 us
    dot_general x1, matrix products, attend(): grad_value = jnp.dot(mixed.T, d_values, preferred_element_type=jnp.float32)  16.8 us
    dot_general x1, matrix products, attend(): jnp.dot(mixed, w_value, preferred_element_type=jnp.float32)  16.6 us
    scatter-add x1, other arithmetic, on_device(): jnp.zeros((slot_total, width), jnp.float32).at[chosen.reshape(-1)]  16.4 us
  transfers between devices with their start and end apart: 4, of which 4 were waited for; matrix products, arithmetic and copies ran while one was open for 9% of the time, Pallas kernels for 0%

commit v1 on v0

v1 whole, which is shorter than its diff:
```python
import functools
import math

import jax
import jax.numpy as jnp
from jax import lax
from jax.experimental import pallas as pl
from jax.experimental.pallas import tpu as pltpu
from jax.sharding import Mesh
from jax.sharding import PartitionSpec as P

SEG, X, Z, CORES = 4, 4, 4, 2
OWNERS = X * Z * CORES
PLANE = X * Z
DM = 512
HEADS = 2
HEAD = DM // HEADS
K = 8
E = 256
N = 256
CAP = 8
SLOTS = 256
PIECE = 64
HALF = PIECE // 2
CUT = DM // SEG
TILE = 128
TILES = E // TILE
ROWS = K * TILE
STEP = 32
ABSENT = 2.0
NODE = ("x", "z", "core")
FLAT = ("x", "z")
BF = jnp.bfloat16
F32 = jnp.float32

COS = (
    0.9999999698385398,
    -19.739198571306687,
    64.93882672218028,
    -85.44499716023202,
    60.126952745697146,
    -25.820504473745327,
    6.330480832160802,
)


def dot(a, b):
    return jnp.dot(a, b, preferred_element_type=F32)


def dot_tn(a, b):
    return lax.dot_general(a, b, (((0,), (0,)), ((), ())), preferred_element_type=F32)


def dot_nt(a, b):
    return lax.dot_general(a, b, (((1,), (1,)), ((), ())), preferred_element_type=F32)


def iota(shape, axis):
    return lax.broadcasted_iota(jnp.int32, shape, axis)


def column(row):
    n = row.shape[1]
    square = jnp.where(iota((n, n), 0) == iota((n, n), 1), row.astype(F32), 0.0)
    return jnp.sum(square, axis=1, keepdims=True)


def gru_kernel(touched, state, message, w_input, w_state, out, wi, ws, sem):
    copies = [
        pltpu.make_async_copy(w_state, ws, sem.at[0]),
        pltpu.make_async_copy(w_input, wi, sem.at[1]),
    ]
    for copy in copies:
        copy.start()
    keep = column(touched[...]) > 0.5
    m, s = message[...], state[...]
    copies[0].wait()
    from_state = [dot(s, ws[:, i * DM : (i + 1) * DM]) for i in range(3)]
    copies[1].wait()
    update = jax.nn.sigmoid(dot(m, wi[:, :DM]) + from_state[0])
    reset = jax.nn.sigmoid(dot(m, wi[:, DM : 2 * DM]) + from_state[1])
    candidate = jnp.tanh(dot(m, wi[:, 2 * DM :]) + reset * from_state[2])
    fresh = (1.0 - update) * candidate + update * s.astype(F32)
    out[...] = jnp.where(keep, fresh, ABSENT).astype(BF)


def gru(touched, state, message, w_input, w_state):
    whole = pl.BlockSpec(memory_space=pltpu.VMEM)
    far = pl.BlockSpec(memory_space=pl.ANY)
    return pl.pallas_call(
        gru_kernel,
        in_specs=[whole] * 3 + [far] * 2,
        out_specs=whole,
        out_shape=jax.ShapeDtypeStruct((N, DM), BF),
        scratch_shapes=[
            pltpu.VMEM((DM, 3 * DM), BF),
            pltpu.VMEM((DM, 3 * DM), BF),
            pltpu.SemaphoreType.DMA((2,)),
        ],
        compiler_params=pltpu.CompilerParams(vmem_limit_bytes=56 << 20),
        cost_estimate=pl.CostEstimate(
            flops=4 * N * DM * 3 * DM, bytes_accessed=4 << 20, transcendentals=3 * N * DM
        ),
        name="gru",
    )(touched, state, message, w_input, w_state)


def code_kernel(delays, frequency, code, code_t):
    k = pl.program_id(0)
    turns = frequency[...] * (1.0 / (2.0 * math.pi))
    high = jnp.round(turns * 16384.0) * (1.0 / 16384.0)
    low = turns - high
    lane = iota((E, K), 1)
    delay = jnp.sum(jnp.where(lane == k, delays[...].astype(F32), 0.0), axis=1, keepdims=True)
    coarse = delay * high
    part = (coarse - jnp.round(coarse)) + delay * low
    u = part * part
    wave = jnp.full_like(u, COS[-1])
    for c in COS[-2::-1]:
        wave = wave * u + c
    wave_b = wave.astype(BF)
    for i in range(TILES):
        code[i, 0] = wave_b[i * TILE : (i + 1) * TILE]
        code_t[i] = wave[i * TILE : (i + 1) * TILE].T.astype(BF)


def time_code(delays, frequency):
    return pl.pallas_call(
        code_kernel,
        grid=(K,),
        in_specs=[
            pl.BlockSpec((E, K), lambda k: (0, 0)),
            pl.BlockSpec((1, DM), lambda k: (0, 0)),
        ],
        out_specs=[
            pl.BlockSpec((TILES, 1, TILE, DM), lambda k: (0, k, 0, 0)),
            pl.BlockSpec((TILES, DM, TILE), lambda k: (0, 0, k)),
        ],
        out_shape=[
            jax.ShapeDtypeStruct((TILES, K, TILE, DM), BF),
            jax.ShapeDtypeStruct((TILES, DM, ROWS), BF),
        ],
        compiler_params=pltpu.CompilerParams(vmem_limit_bytes=16 << 20),
        cost_estimate=pl.CostEstimate(
            flops=20 * K * E * DM, bytes_accessed=4 << 20, transcendentals=K * E * DM
        ),
        name="time_code",
    )(delays, frequency)


def project_kernel(code, w, up, time_k, time_v, d_att):
    rows = code[0].reshape(K // 2 * TILE, DM)
    time_k[0] = dot(rows, w[1]).astype(BF).reshape(K // 2, TILE, DM)
    time_v[0] = dot(rows, w[2]).astype(BF).reshape(K // 2, TILE, DM)

    @pl.when((pl.program_id(0) == 0) & (pl.program_id(1) == 0))
    def _():
        d_att[...] = dot_nt(up[...], w[3]).astype(BF)


def project(code, weights, up):
    block = pl.BlockSpec((1, K // 2, TILE, DM), lambda i, j: (i, j, 0, 0))
    time = jax.ShapeDtypeStruct((TILES, K, TILE, DM), BF)
    whole = pl.BlockSpec((E, DM), lambda i, j: (0, 0))
    return pl.pallas_call(
        project_kernel,
        grid=(TILES, 2),
        in_specs=[block, pl.BlockSpec((4, DM, DM), lambda i, j: (0, 0, 0)), whole],
        out_specs=[block, block, whole],
        out_shape=[time, time, jax.ShapeDtypeStruct((E, DM), BF)],
        compiler_params=pltpu.CompilerParams(vmem_limit_bytes=16 << 20),
        cost_estimate=pl.CostEstimate(
            flops=4 * K * E * DM * DM, bytes_accessed=8 << 20, transcendentals=0
        ),
        name="time_projections",
    )(code, weights, up)


def owner_pick(asked):
    ids = jnp.concatenate([asked] * (N // 128), axis=1)
    return (ids == iota(ids.shape, 1)).astype(F32).astype(BF)


def start_kernel(seg, state, written, r1, r2, r3, asked, memory, rows):
    start = state[...]
    for back, r in ((3, r3), (2, r2), (1, r1)):
        row = r[...]
        start = jnp.where((row.astype(F32) < 1.5) & (seg[0] >= back), row, start)
    own = written[...]
    memory[...] = jnp.where(own.astype(F32) < 1.5, own, start)
    rows[...] = dot(owner_pick(asked[...]), start).astype(BF)


def start_rows(seg, state, written, r1, r2, r3, asked):
    whole = pl.BlockSpec(memory_space=pltpu.VMEM)
    return pl.pallas_call(
        start_kernel,
        in_specs=[pl.BlockSpec(memory_space=pltpu.SMEM)] + [whole] * 6,
        out_specs=[whole] * 2,
        out_shape=[
            jax.ShapeDtypeStruct((N, DM), BF),
            jax.ShapeDtypeStruct((SLOTS, DM), BF),
        ],
        compiler_params=pltpu.CompilerParams(vmem_limit_bytes=16 << 20),
        cost_estimate=pl.CostEstimate(
            flops=2 * N * DM * SLOTS, bytes_accessed=2 << 20, transcendentals=0
        ),
        name="start_rows",
    )(seg, state, written, r1, r2, r3, asked)


def attend_kernel(
    core, slots, chosen, chosen_t, tk, tv, tt, d_att, up, wq,
    embedded, d_slots, mine, other,
    skv, qf, src, both, dkv, att, dq, sums,
):
    rows = slots[...]
    pick = (chosen[:, 0:1] == iota((E, SLOTS), 1)).astype(F32).astype(BF)
    src[...] = dot(pick, rows)
    skv[:, :DM] = dot(rows, wq[1]).astype(BF)
    skv[:, DM:] = dot(rows, wq[2]).astype(BF)
    qf[...] = dot(pick, dot(rows, wq[0]).astype(BF))

    lane = iota((STEP, 128), 1)
    first = lane < K
    second = (lane >= K) & (lane < 2 * K)
    scale = 1.0 / math.sqrt(HEAD)

    def per_head(x):
        a = jnp.sum(jnp.where(first, x, 0.0), axis=1, keepdims=True)
        b = jnp.sum(jnp.where(second, x, 0.0), axis=1, keepdims=True)
        return jnp.where(first, a, b)

    def gather(i):
        ids = chosen[i * TILE : (i + 1) * TILE, :]
        slot = iota((TILE, SLOTS), 1)
        pick = jnp.concatenate(
            [(ids[:, 1 + k : 2 + k] == slot).astype(F32) for k in range(K)], axis=0
        ).astype(BF)
        both[i] = dot(pick, skv[...])

    def step(i, j):
        at = slice(i * TILE + j * STEP, i * TILE + (j + 1) * STEP)
        scores = jnp.zeros((STEP, 128), F32)
        d_probs = jnp.zeros((STEP, 128), F32)
        for h in range(HEADS):
            part = slice(h * HEAD, (h + 1) * HEAD)
            part_v = slice(DM + h * HEAD, DM + (h + 1) * HEAD)
            query = qf[at, part]
            d_out = d_att[at, part].astype(F32)
            for k in range(K):
                row = slice(k * TILE + j * STEP, k * TILE + (j + 1) * STEP)
                local = slice(j * STEP, (j + 1) * STEP)
                key = both[i, row, part] + tk[i, k, local, part].astype(F32)
                value = both[i, row, part_v] + tv[i, k, local, part].astype(F32)
                both[i, row, part] = key
                both[i, row, part_v] = value
                here = lane == h * K + k
                scores = jnp.where(here, jnp.sum(query * key, axis=1, keepdims=True), scores)
                d_probs = jnp.where(here, jnp.sum(d_out * value, axis=1, keepdims=True), d_probs)
        powered = jnp.exp(scores * scale)
        probs = powered / per_head(powered)
        d_scores = probs * (d_probs - per_head(probs * d_probs)) * scale
        for h in range(HEADS):
            part = slice(h * HEAD, (h + 1) * HEAD)
            part_v = slice(DM + h * HEAD, DM + (h + 1) * HEAD)
            query = qf[at, part]
            d_out = d_att[at, part].astype(F32)
            attended = jnp.zeros((STEP, HEAD), F32)
            d_query = jnp.zeros((STEP, HEAD), F32)
            for k in range(K):
                row = slice(k * TILE + j * STEP, k * TILE + (j + 1) * STEP)
                c = h * K + k
                p = jnp.broadcast_to(probs[:, c : c + 1], (STEP, HEAD))
                d = jnp.broadcast_to(d_scores[:, c : c + 1], (STEP, HEAD))
                attended += p * both[i, row, part_v]
                d_query += d * both[i, row, part]
                dkv[i, row, part] = (d * query).astype(BF)
                dkv[i, row, part_v] = (p * d_out).astype(BF)
            att[at, part] = attended.astype(BF)
            dq[at, part] = d_query.astype(BF)

    for i in range(TILES):
        gather(i)
    sub = iota((SLOTS, TILE), 0)
    s_kv = g_kv = None
    for i in range(TILES):
        for j in range(TILE // STEP):
            step(i, j)
        spread = jnp.concatenate(
            [
                (sub == chosen_t[1 + k : 2 + k, i * TILE : (i + 1) * TILE]).astype(F32)
                for k in range(K)
            ],
            axis=1,
        ).astype(BF)
        one, two = dot(spread, dkv[i]), dot(tt[i], dkv[i])
        s_kv = one if i == 0 else s_kv + one
        g_kv = two if i == 0 else g_kv + two
    s_kv = s_kv.astype(BF)
    pick_t = (iota((SLOTS, E), 0) == chosen_t[0:1, :]).astype(F32).astype(BF)
    s_q = dot(pick_t, dq[...]).astype(BF)

    def store(i, value):
        sums[i * 4 : (i + 1) * 4] = value.astype(BF).reshape(4, CORES, PIECE, DM)

    store(0, dot_tn(rows, s_q))
    g_kv += dot_tn(rows, s_kv)
    store(1, g_kv[:, :DM])
    store(2, g_kv[:, DM:])
    store(3, dot_tn(att[...], up[...]))
    mine[...] = sums[:, core[0]]
    other[...] = sums[:, 1 - core[0]]
    embedded[...] = (dot(att[...], wq[3]) + src[...]).astype(BF)
    grads = dot(pick_t, up[...]) + dot_nt(s_q, wq[0])
    grads += dot_nt(s_kv[:, :DM], wq[1]) + dot_nt(s_kv[:, DM:], wq[2])
    d_slots[...] = grads.astype(BF)


def attend(core, slots, chosen, chosen_t, time_k, time_v, time_t, d_att, up, weights):
    whole = pl.BlockSpec(memory_space=pltpu.VMEM)
    return pl.pallas_call(
        attend_kernel,
        in_specs=[pl.BlockSpec(memory_space=pltpu.SMEM)] + [whole] * 9,
        out_specs=[whole] * 4,
        out_shape=[
            jax.ShapeDtypeStruct((E, DM), BF),
            jax.ShapeDtypeStruct((SLOTS, DM), BF),
            jax.ShapeDtypeStruct((PLANE, PIECE, DM), BF),
            jax.ShapeDtypeStruct((PLANE, PIECE, DM), BF),
        ],
        scratch_shapes=[
            pltpu.VMEM((SLOTS, 2 * DM), BF),
            pltpu.VMEM((E, DM), F32),
            pltpu.VMEM((E, DM), F32),
            pltpu.VMEM((TILES, ROWS, 2 * DM), F32),
            pltpu.VMEM((TILES, ROWS, 2 * DM), BF),
            pltpu.VMEM((E, DM), BF),
            pltpu.VMEM((E, DM), BF),
            pltpu.VMEM((PLANE, CORES, PIECE, DM), BF),
        ],
        compiler_params=pltpu.CompilerParams(vmem_limit_bytes=40 << 20),
        cost_estimate=pl.CostEstimate(
            flops=6 << 30, bytes_accessed=14 << 20, transcendentals=E * 128
        ),
        name="attend",
    )(core, slots, chosen, chosen_t, time_k, time_v, time_t, d_att, up, weights)


def small(kernel, name, out_shape, in_specs, out_specs, scratch=(), moved=1 << 20):
    return pl.pallas_call(
        kernel,
        in_specs=in_specs,
        out_specs=out_specs,
        out_shape=out_shape,
        scratch_shapes=scratch,
        compiler_params=pltpu.CompilerParams(vmem_limit_bytes=16 << 20),
        cost_estimate=pl.CostEstimate(flops=1 << 19, bytes_accessed=moved, transcendentals=0),
        name=name,
    )


WHOLE = pl.BlockSpec(memory_space=pltpu.VMEM)
SCALAR = pl.BlockSpec(memory_space=pltpu.SMEM)
A_SHAPE = jax.ShapeDtypeStruct((PLANE, HALF, DM), BF)
B_SHAPE = jax.ShapeDtypeStruct((PLANE, HALF, CUT), BF)


def columns_of(seg, back):
    place = lax.rem(seg[0] + back + SEG, SEG)
    return pl.ds(pl.multiple_of(place * CUT, CUT), CUT)


def pair_kernel(seg, mine, partner, a, *bs):
    a[...] = (mine[:, :HALF].astype(F32) + partner[:, :HALF].astype(F32)).astype(BF)
    for ahead, b in enumerate(bs):
        at = columns_of(seg, ahead)
        b[...] = (mine[:, HALF:, at].astype(F32) + partner[:, HALF:, at].astype(F32)).astype(BF)


def pair_sum(seg, mine, partner):
    shapes = [A_SHAPE] + [B_SHAPE] * SEG
    return small(pair_kernel, "pair_sum", shapes, [SCALAR, WHOLE, WHOLE], [WHOLE] * 5)(
        seg, mine, partner
    )


def first_kernel(a, b0, b1, b2, b3, d_slots, part, pack):
    total = a[0].astype(F32)
    for i in range(1, PLANE):
        total += a[i].astype(F32)
    part[...] = total.astype(BF)
    b = (b0[...].astype(F32) + b1[...].astype(F32)) + (b2[...].astype(F32) + b3[...].astype(F32))
    pack[:, :HALF] = b.astype(BF)
    for i in range(SEG):
        at = slice(HALF + i * 2 * CAP, HALF + (i + 1) * 2 * CAP)
        pack[:, at] = d_slots[:, :, i * CUT : (i + 1) * CUT]


def first_sum(a, bs, d_slots):
    shapes = [
        jax.ShapeDtypeStruct((HALF, DM), BF),
        jax.ShapeDtypeStruct((PLANE, HALF + SEG * 2 * CAP, CUT), BF),
    ]
    return small(first_kernel, "first_sum", shapes, [WHOLE] * 6, [WHOLE] * 2)(
        a, *bs, d_slots.reshape(PLANE, 2 * CAP, DM)
    )


def second_kernel(seg, core, pack, own, p1, p2, p3, a, b, keep, give, parts):
    for back, r in enumerate((own, p1, p2, p3)):
        parts[lax.rem(seg[0] + SEG - back, SEG)] = r[...].astype(F32)
    a_total = ((parts[0] + parts[1]) + (parts[2] + parts[3])).astype(BF)
    total = pack[0, :HALF].astype(F32)
    for i in range(1, PLANE):
        total += pack[i, :HALF].astype(F32)
    b_total = total.astype(BF)
    for i in range(PLANE):
        a[i] = a_total
        b[i] = b_total
    first = core[0] == 0
    for i in range(SEG):
        grads = pack[:, HALF + i * 2 * CAP : HALF + (i + 1) * 2 * CAP].astype(F32)
        low = grads[:, :CAP].reshape(SLOTS // 2, CUT)
        high = grads[:, CAP:].reshape(SLOTS // 2, CUT)
        at = slice(i * CUT, (i + 1) * CUT)
        keep[:, at] = jnp.where(first, low, high).astype(BF)
        give[:, at] = jnp.where(first, high, low).astype(BF)


def second_sum(seg, core, pack, own, turned):
    grads = jax.ShapeDtypeStruct((SLOTS // 2, DM), BF)
    shapes = [A_SHAPE, B_SHAPE, grads, grads]
    scratch = [pltpu.VMEM((SEG, HALF, DM), F32)]
    return small(
        second_kernel, "second_sum", shapes, [SCALAR] * 2 + [WHOLE] * 5, [WHOLE] * 4, scratch
    )(seg, core, pack, own, *turned)


def join_kernel(seg, b0, b1, b2, b3, out):
    for back, b in enumerate((b0, b1, b2, b3)):
        out[:, :, columns_of(seg, -back)] = b[...]


def join(seg, bs):
    return small(join_kernel, "join", A_SHAPE, [SCALAR] + [WHOLE] * 4, WHOLE)(seg, *bs)


def whole_kernel(core, a, b, a_far, b_far, out):
    out[:, core[0], :HALF] = a[...].astype(F32)
    out[:, core[0], HALF:] = b[...].astype(F32)
    out[:, 1 - core[0], :HALF] = a_far[...].astype(F32)
    out[:, 1 - core[0], HALF:] = b_far[...].astype(F32)


def whole_grad(core, a, b, a_far, b_far):
    spec = pl.BlockSpec((4, HALF, DM), lambda i: (i, 0, 0))
    return pl.pallas_call(
        whole_kernel,
        grid=(PLANE // 4,),
        in_specs=[SCALAR] + [spec] * 4,
        out_specs=pl.BlockSpec((4, CORES, PIECE, DM), lambda i: (i, 0, 0, 0)),
        out_shape=jax.ShapeDtypeStruct((PLANE, CORES, PIECE, DM), F32),
        compiler_params=pltpu.CompilerParams(vmem_limit_bytes=16 << 20),
        cost_estimate=pl.CostEstimate(flops=1 << 19, bytes_accessed=6 << 20, transcendentals=0),
        name="whole_grad",
    )(core, a, b, a_far, b_far)


def spread_kernel(ids, out):
    out[...] = jnp.broadcast_to(column(ids[...]), (SLOTS, 128)).astype(jnp.int32)


def spread(ids):
    whole = pl.BlockSpec(memory_space=pltpu.VMEM)
    return pl.pallas_call(
        spread_kernel,
        in_specs=[whole],
        out_specs=whole,
        out_shape=jax.ShapeDtypeStruct((SLOTS, 128), jnp.int32),
        compiler_params=pltpu.CompilerParams(vmem_limit_bytes=16 << 20),
        cost_estimate=pl.CostEstimate(flops=1 << 17, bytes_accessed=1 << 17, transcendentals=0),
        name="spread",
    )(ids)


def owner_kernel(core, asked, keep, got, out):
    near = asked[:, core[0]].reshape(SLOTS // 2, 128)
    far = asked[:, 1 - core[0]].reshape(SLOTS // 2, 128)
    out[...] = dot_tn(owner_pick(near), keep[...]) + dot_tn(owner_pick(far), got[...])


def owner_sum(core, asked, keep, got):
    whole = pl.BlockSpec(memory_space=pltpu.VMEM)
    return pl.pallas_call(
        owner_kernel,
        in_specs=[pl.BlockSpec(memory_space=pltpu.SMEM)] + [whole] * 3,
        out_specs=whole,
        out_shape=jax.ShapeDtypeStruct((N, DM), F32),
        compiler_params=pltpu.CompilerParams(vmem_limit_bytes=16 << 20),
        cost_estimate=pl.CostEstimate(
            flops=2 * N * DM * SLOTS, bytes_accessed=1 << 20, transcendentals=0
        ),
        name="owner_sum",
    )(core, asked.reshape(PLANE, CORES, CAP, 128), keep, got)


def exchange(rows, axes, count):
    blocks = rows.reshape(count, -1, rows.shape[-1])
    return lax.all_to_all(blocks, axes, split_axis=0, concat_axis=0, tiled=True).reshape(rows.shape)


def on_device(
    memory_base,
    messages,
    touched,
    gru_input,
    gru_state,
    attn_weights,
    frequency,
    request_rows,
    event_slots,
    delays,
    upstream,
):
    seg = lax.axis_index("y").reshape(1)
    core = lax.axis_index("core").reshape(1)
    asked = exchange(spread(request_rows.reshape(1, SLOTS)), NODE, OWNERS)
    written = gru(touched, memory_base, messages[0], gru_input, gru_state)
    r1 = lax.ppermute(written, "y", [(0, 1), (1, 2), (2, 3)])
    r3 = lax.ppermute(written, "y", [(0, 3)])
    r2 = lax.ppermute(r1, "y", [(1, 2), (2, 3)])
    up = upstream[0]
    written, late, chosen, chosen_t = lax.optimization_barrier(
        (written, delays[0], event_slots[0], event_slots[0].T)
    )
    code, code_t = time_code(late, frequency.reshape(1, DM))
    written, code, code_t = lax.optimization_barrier((written, code, code_t))
    memory, rows = start_rows(seg, memory_base, written, r1, r2, r3, asked)
    rows, code = lax.optimization_barrier((rows, code))
    slots = exchange(rows, NODE, OWNERS)
    time_k, time_v, d_att = project(code, attn_weights, up)
    embedded, d_slots, mine, other = attend(
        core, slots, chosen, chosen_t, time_k, time_v, code_t, d_att, up, attn_weights
    )
    swap = [(0, 1), (1, 0)]

    def turn(x):
        return [
            lax.ppermute(x, "y", [(i, (i + s) % SEG) for i in range(SEG)]) for s in range(1, SEG)
        ]

    def plane(x):
        return lax.all_to_all(x, FLAT, split_axis=0, concat_axis=0, tiled=True)

    a, b0, *bs = pair_sum(seg, mine, lax.ppermute(other, "core", swap))
    bs = [
        lax.ppermute(b, "y", [(i, (i + s) % SEG) for i in range(SEG)])
        for s, b in enumerate(bs, start=1)
    ]
    part, pack = first_sum(plane(a), [b0] + bs, d_slots)
    a, b, keep, give = second_sum(seg, core, plane(pack), part, turn(part))
    b = plane(b)
    a, b = lax.optimization_barrier((a, b))
    turned = turn(b)
    a = plane(a)
    a, b, *turned = lax.optimization_barrier((a, b, *turned))
    a_far = lax.ppermute(a, "core", swap)
    b = join(seg, [b] + turned)
    b_far = lax.ppermute(b, "core", swap)
    memory_grad = owner_sum(core, asked, keep, lax.ppermute(give, "core", swap))
    weight_grad = whole_grad(core, a, b, a_far, b_far)
    return embedded[None], memory[None], memory_grad[None], weight_grad.reshape(4, DM, DM)


def solution(mesh):
    fine = Mesh(mesh.devices.reshape(SEG, X, Z, CORES), ("y", "x", "z", "core"))
    both = P("y", NODE, None)
    in_specs = (P(NODE, None), both, P("y", NODE), P(), P(), P(), P(), both, both, both, both)
    out_specs = (both, both, both, P())
    return jax.shard_map(
        on_device, mesh=fine, in_specs=in_specs, out_specs=out_specs, check_vma=False
    )
```

time: 514 us -> 142 us (0.28); the launches traced: 505 us -> 142 us
  waiting for transfers between devices: 275 us -> 22.4 us
  matrix products: 91.3 us -> 0 us
  other arithmetic: 71.1 us -> 0 us
  starting transfers between devices: 0.34 us -> 62.4 us
  Pallas kernels: 0 us -> 28.8 us
  local copies, waits for them, and re-layouts: 43.7 us -> 15.1 us
  between operations: 14.8 us -> 0.91 us
    psum x1 -> x0, waiting for transfers between devices: 159 us -> none  [on_device(): weight_grad = lax.psum(weight_terms, ('seg', 'node'))]
    dot_general x19 -> x0, matrix products: 91.3 us -> none  [the longest x1 17.6 us: attend(): jnp.dot(mixed, w_key, preferred_element_type=jnp.float32)]
    all_gather x2 -> x0, waiting for transfers between devices: 69.4 us -> none  [the longest x1 52 us: on_device(): piece = lax.all_gather(start, 'node', axis=0, tiled=True)]
    reduce_scatter x1 -> x0, waiting for transfers between devices: 46.3 us -> none  [on_device(): lax.psum_scatter(jnp.zeros((nodes_here * lax.axis_size('node'), width), j...]
    all_to_all x0 -> x5, starting transfers between devices: none -> 33.1 us  [the longest x3 16.5 us: plane(): return lax.all_to_all(x, FLAT, split_axis=0, concat_axis=0, tiled=True)]
    ppermute x0 -> x16, starting transfers between devices: none -> 29.3 us  [the longest x3 8.37 us: on_device(): lax.ppermute(b, 'y', [(i, (i + s) % SEG) for i in range(SEG)])]
    pallas_call x0 -> x12, Pallas kernels: none -> 28.8 us  [the longest x1 8.31 us: attend(): pl.pallas_call(attend_kernel, in_specs=[pl.BlockSpec(memory_space=pltpu.S...]
    scatter-add x2 -> x0, other arithmetic: 25.2 us -> none  [the longest x1 16.4 us: on_device(): jnp.zeros((slot_total, width), jnp.float32).at[chosen.reshape(-1)]]
  transfers between devices with their start and end apart: 4 -> 21, of which waited for: 4 -> 12; matrix products, arithmetic and copies ran while one was open for 9% -> 0% of each run, Pallas kernels for 0% -> 7%
where the time goes in v1:
time: 142 us
  starting transfers between devices  62.4 us (44%)
  Pallas kernels  28.8 us (20%)
  waiting for transfers between devices  22.4 us (16%)
  local copies, waits for them, and re-layouts  15.1 us (11%)
  blocking collectives  11.9 us (8%)
    all_to_all x3, starting transfers between devices, plane(): return lax.all_to_all(x, FLAT, split_axis=0, concat_axis=0, tiled=True)  16.5 us
    all_to_all x2, starting transfers between devices, exchange(): lax.all_to_all(blocks, axes, split_axis=0, concat_axis=0, tiled=True)  16.5 us
    unnamed x36, local copies, waits for them, and re-layouts  15 us
    all_to_all x1, blocking collectives, plane(): return lax.all_to_all(x, FLAT, split_axis=0, concat_axis=0, tiled=True)  11.9 us
    ppermute x6, waiting for transfers between devices, turn(): lax.ppermute(x, 'y', [(i, (i + s) % SEG) for i in range(SEG)])  8.83 us
    ppermute x3, starting transfers between devices, on_device(): lax.ppermute(b, 'y', [(i, (i + s) % SEG) for i in range(SEG)])  8.37 us
    pallas_call x1, Pallas kernels, attend(): pl.pallas_call(attend_kernel, in_specs=[pl.BlockSpec(memory_space=pltpu.S...  8.31 us
    ppermute x1, starting transfers between devices, on_device(): b_far = lax.ppermute(b, 'core', swap)  6.8 us
  transfers between devices with their start and end apart: 21, of which 12 were waited for; matrix products, arithmetic and copies ran while one was open for 0% of the time, Pallas kernels for 7%

profile of v1, /device:TPU:1, one launch (start us, length us, event | category | flops | bytes accessed | tf_op | source)
XLA Modules:
  0.0 141.6 jit_solution(12119033646313920494)
XLA Ops:
  0.7 4.4 %gru.1.written = bf16[256,512]{1,0:T(8,128)(2,1)} custom-call(s32[1,256]{1,0:T(1,128)} %touched.1, bf16[256,512]{1,0:T(8,128)(2,1)} %state.3, bf16[256,512]{1,0:T(8,128)(2,1)} %bitcast.36, bf16[512,1536]{1,0:T(8,128)(2,1)} %w_input.1, bf16[512,1536]{1,0:T(8,128)(2,1)} %w_state.1), custom_call_target="tpu_custom_call" | custom-call | flops 805306368 | bytes 4194304 | tf_op jit(solution)/shard_map/gru/pallas_call | solution.py:91
  5.1 4.2 %collective-permute-start = (bf16[256,512]{1,0:T(8,128)(2,1)}, bf16[256,512]{1,0:T(8,128)(2,1)S(1)}, u32[]{:S(2)}, u32[]{:S(2)}) collective-permute-start(bf16[256,512]{1,0:T(8,128)(2,1)} %gru.1.written), channel_id=1, source_target_pairs={{0,32},{32,64},{64,96},{1,33},{33,65},{65,97},{2,34},{34,66},{66,9... | collective-permute-start | bytes 786440 | tf_op jit(solution)/shard_map/ppermute | solution.py:531
  9.3 2.7 %collective-permute-start.2 = (bf16[256,512]{1,0:T(8,128)(2,1)}, bf16[256,512]{1,0:T(8,128)(2,1)S(1)}, u32[]{:S(2)}, u32[]{:S(2)}) collective-permute-start(bf16[256,512]{1,0:T(8,128)(2,1)} %gru.1.written), channel_id=1, source_target_pairs={{0,96},{1,97},{2,98},{3,99},{4,100},{5,101},{6,102},{7,103},{8,104... | collective-permute-start | bytes 786440 | tf_op jit(solution)/shard_map/ppermute | solution.py:532
  12.0 2.5 %collective-permute-done.r1 = bf16[256,512]{1,0:T(8,128)(2,1)S(1)} collective-permute-done((bf16[256,512]{1,0:T(8,128)(2,1)}, bf16[256,512]{1,0:T(8,128)(2,1)S(1)}, u32[]{:S(2)}, u32[]{:S(2)}) %collective-permute-start) | collective-permute-done | bytes 262176 | tf_op jit(solution)/shard_map/ppermute | solution.py:531
  15.2 0.8 spread.1
  16.0 9.5 %all-to-all-start = ((s32[32,8,128]{2,1,0:T(8,128)}), s32[32,8,128]{2,1,0:T(8,128)S(1)}, u32[]{:S(2)}, u32[]{:S(2)}) async-start(s32[32,8,128]{2,1,0:T(8,128)} %bitcast.7), calls=%async_computation | async-start | bytes 262144 | tf_op jit(solution)/shard_map/all_to_all | solution.py:511
  25.7 4.5 %time_code.1 = (bf16[2,8,128,512]{3,2,1,0:T(8,128)(2,1)S(1)}, bf16[2,512,1024]{2,1,0:T(8,128)(2,1)S(1)}) custom-call(s32[256,8]{1,0:T(8,128)S(1)} %bitcast.27, f32[1,512]{1,0:T(1,128)S(1)} %bitcast.33), custom_call_target="tpu_custom_call" | custom-call | flops 20971520 | bytes 4194304 | tf_op jit(solution)/shard_map/time_code/pallas_call | solution.py:129
  30.2 1.3 copy-done.7
  31.5 1.3 copy-done.9
  33.2 1.2 start_rows.1
  34.5 7.1 %all-to-all-start.1 = ((bf16[32,8,512]{2,1,0:T(8,128)(2,1)}), bf16[32,8,512]{2,1,0:T(8,128)(2,1)S(1)}, u32[]{:S(2)}, u32[]{:S(2)}) async-start(bf16[32,8,512]{2,1,0:T(8,128)(2,1)} %bitcast.9), calls=%async_computation.1 | async-start | bytes 524288 | tf_op jit(solution)/shard_map/all_to_all | solution.py:511
  41.7 1.6 %copy-done.3 = bf16[4,512,512]{2,1,0:T(8,128)(2,1)S(1)} copy-done((bf16[4,512,512]{2,1,0:T(8,128)(2,1)S(1)}, bf16[4,512,512]{2,1,0:T(8,128)(2,1)}, u32[]{:S(2)}) %copy-start.3) | copy-done | bytes 2097176
  43.2 1.6 %copy-done.10 = bf16[2,8,128,512]{3,2,1,0:T(8,128)(2,1)S(1)} copy-done((bf16[2,8,128,512]{3,2,1,0:T(8,128)(2,1)S(1)}, bf16[2,8,128,512]{3,2,1,0:T(8,128)(2,1)}, u32[]{:S(2)}) %copy-start.10) | copy-done | bytes 2097176
  44.8 3.2 %time_projections.1 = (bf16[2,8,128,512]{3,2,1,0:T(8,128)(2,1)S(1)}, bf16[2,8,128,512]{3,2,1,0:T(8,128)(2,1)S(1)}, bf16[256,512]{1,0:T(8,128)(2,1)S(1)}) custom-call(bf16[2,8,128,512]{3,2,1,0:T(8,128)(2,1)S(1)} %copy-done.10, bf16[4,512,512]{2,1,0:T(8,128)(2,1)S(1)} %copy-done.3, bf16[256,512]{1,0:T(8,128)(2,1)S(1)} %bitcast.31), custom_call_target="tpu_custom_call" | custom-call | flops 2147483648 | bytes 8388608 | tf_op jit(solution)/shard_map/time_projections/pallas_call | solution.py:166
  48.0 1.3 copy-done.11
  49.3 1.3 copy-done.13
  50.7 1.6 %copy-done.4 = bf16[4,512,512]{2,1,0:T(8,128)(2,1)S(1)} copy-done((bf16[4,512,512]{2,1,0:T(8,128)(2,1)S(1)}, bf16[4,512,512]{2,1,0:T(8,128)(2,1)}, u32[]{:S(2)}) %copy-start.4) | copy-done | bytes 2097176
  52.3 1.6 %copy-done.8 = bf16[2,512,1024]{2,1,0:T(8,128)(2,1)S(1)} copy-done((bf16[2,512,1024]{2,1,0:T(8,128)(2,1)S(1)}, bf16[2,512,1024]{2,1,0:T(8,128)(2,1)}, u32[]{:S(2)}) %copy-start.8) | copy-done | bytes 2097176
  53.9 1.6 %copy-done.12 = bf16[2,8,128,512]{3,2,1,0:T(8,128)(2,1)S(1)} copy-done((bf16[2,8,128,512]{3,2,1,0:T(8,128)(2,1)S(1)}, bf16[2,8,128,512]{3,2,1,0:T(8,128)(2,1)}, u32[]{:S(2)}) %copy-start.12) | copy-done | bytes 2097176
  55.5 1.6 %copy-done.14 = bf16[2,8,128,512]{3,2,1,0:T(8,128)(2,1)S(1)} copy-done((bf16[2,8,128,512]{3,2,1,0:T(8,128)(2,1)S(1)}, bf16[2,8,128,512]{3,2,1,0:T(8,128)(2,1)}, u32[]{:S(2)}) %copy-start.14) | copy-done | bytes 2097176
  57.0 8.3 %attend.1 = (bf16[256,512]{1,0:T(8,128)(2,1)}, bf16[256,512]{1,0:T(8,128)(2,1)S(1)}, bf16[16,64,512]{2,1,0:T(8,128)(2,1)S(1)}, bf16[16,64,512]{2,1,0:T(8,128)(2,1)S(1)}) custom-call(s32[1]{0:T(128)} %bitcast.core, bf16[256,512]{1,0:T(8,128)(2,1)S(1)} %bitcast.26, s32[256,9]{1,0:T(8,128)S(1)} %copy.16.chosen, s32[9,256]{1,0:T(8,128)S(1)} %bitcast.29, ...), custom_call_target="tpu_custom_call" | custom-call | flops 6442450944 | bytes 14680064 | tf_op jit(solution)/shard_map/attend/pallas_call | solution.py:323
  65.7 2.4 %collective-permute-done.3.partner = bf16[16,64,512]{2,1,0:T(8,128)(2,1)S(1)} collective-permute-done((bf16[16,64,512]{2,1,0:T(8,128)(2,1)S(1)}, bf16[16,64,512]{2,1,0:T(8,128)(2,1)S(1)}, u32[]{:S(2)}, u32[]{:S(2)}) %collective-permute-start.3) | collective-permute-done | bytes 1048608 | tf_op jit(solution)/shard_map/ppermute | solution.py:557
  68.1 1.0 pair_sum.1
  69.1 6.7 %all-to-all-start.2 = ((bf16[16,32,512]{2,1,0:T(8,128)(2,1)}), bf16[16,32,512]{2,1,0:T(8,128)(2,1)S(1)}, u32[]{:S(2)}, u32[]{:S(2)}) async-start(bf16[16,32,512]{2,1,0:T(8,128)(2,1)} %get-tuple-element.61), calls=%async_computation.2 | async-start | bytes 1048576 | tf_op jit(solution)/shard_map/all_to_all | solution.py:555
  75.8 5.0 %collective-permute-start.4 = (bf16[16,32,128]{2,1,0:T(8,128)(2,1)S(1)}, bf16[16,32,128]{2,1,0:T(8,128)(2,1)S(1)}, u32[]{:S(2)}, u32[]{:S(2)}) collective-permute-start(bf16[16,32,128]{2,1,0:T(8,128)(2,1)S(1)} %get-tuple-element.63), channel_id=1, source_target_pairs={{0,32},{32,64},{64,96},{96,0},{1,33},{33,65},{65,97},{97,1},{2,34}... | collective-permute-start | bytes 393224 | tf_op jit(solution)/shard_map/ppermute | solution.py:559
  80.8 1.4 %collective-permute-start.5 = (bf16[16,32,128]{2,1,0:T(8,128)(2,1)S(1)}, bf16[16,32,128]{2,1,0:T(8,128)(2,1)S(1)}, u32[]{:S(2)}, u32[]{:S(2)}) collective-permute-start(bf16[16,32,128]{2,1,0:T(8,128)(2,1)S(1)} %get-tuple-element.64), channel_id=1, source_target_pairs={{0,64},{32,96},{64,0},{96,32},{1,65},{33,97},{65,1},{97,33},{2,66}... | collective-permute-start | bytes 393224 | tf_op jit(solution)/shard_map/ppermute | solution.py:559
  82.2 2.0 %collective-permute-start.6 = (bf16[16,32,128]{2,1,0:T(8,128)(2,1)S(1)}, bf16[16,32,128]{2,1,0:T(8,128)(2,1)S(1)}, u32[]{:S(2)}, u32[]{:S(2)}) collective-permute-start(bf16[16,32,128]{2,1,0:T(8,128)(2,1)S(1)} %get-tuple-element.65), channel_id=1, source_target_pairs={{0,96},{32,0},{64,32},{96,64},{1,97},{33,1},{65,33},{97,65},{2,98}... | collective-permute-start | bytes 393224 | tf_op jit(solution)/shard_map/ppermute | solution.py:559
  84.2 4.0 %collective-permute-done.5.b2 = bf16[16,32,128]{2,1,0:T(8,128)(2,1)S(1)} collective-permute-done((bf16[16,32,128]{2,1,0:T(8,128)(2,1)S(1)}, bf16[16,32,128]{2,1,0:T(8,128)(2,1)S(1)}, u32[]{:S(2)}, u32[]{:S(2)}) %collective-permute-start.5) | collective-permute-done | bytes 131104 | tf_op jit(solution)/shard_map/ppermute | solution.py:559
  88.2 0.8 first_sum.1
  89.0 6.3 %all-to-all-start.3 = ((bf16[16,96,128]{2,1,0:T(8,128)(2,1)}), bf16[16,96,128]{2,1,0:T(8,128)(2,1)S(1)}, u32[]{:S(2)}, u32[]{:S(2)}) async-start(bf16[16,96,128]{2,1,0:T(8,128)(2,1)} %get-tuple-element.67), calls=%async_computation.3 | async-start | bytes 786432 | tf_op jit(solution)/shard_map/all_to_all | solution.py:555
  95.3 2.0 %collective-permute-start.9 = (bf16[32,512]{1,0:T(8,128)(2,1)S(1)}, bf16[32,512]{1,0:T(8,128)(2,1)S(1)}, u32[]{:S(2)}, u32[]{:S(2)}) collective-permute-start(bf16[32,512]{1,0:T(8,128)(2,1)S(1)} %get-tuple-element.68.own), channel_id=1, source_target_pairs={{0,96},{32,0},{64,32},{96,64},{1,97},{33,1},{65,33},{97,65},{2,98}... | collective-permute-start | bytes 98312 | tf_op jit(solution)/shard_map/ppermute | solution.py:551
  97.3 0.9 collective-permute-start.8
  98.2 0.8 collective-permute-start.7
  99.0 2.6 %collective-permute-done.8.p2 = bf16[32,512]{1,0:T(8,128)(2,1)S(1)} collective-permute-done((bf16[32,512]{1,0:T(8,128)(2,1)S(1)}, bf16[32,512]{1,0:T(8,128)(2,1)S(1)}, u32[]{:S(2)}, u32[]{:S(2)}) %collective-permute-start.8) | collective-permute-done | bytes 32800 | tf_op jit(solution)/shard_map/ppermute | solution.py:551
  101.6 0.9 collective-permute-done.7.p1
  102.5 0.8 all-to-all-done.3.pack
  103.3 0.9 second_sum.1
  104.2 11.9 %all_to_all.30.b0 = bf16[16,32,128]{2,1,0:T(8,128)(2,1)S(1)} all-to-all(bf16[16,32,128]{2,1,0:T(8,128)(2,1)S(1)} %get-tuple-element.72), channel_id=1, replica_groups=mesh['y'=4,'x'=4,'z'=4,'core'=2] {'x','z'}, dimensions={0} | all-to-all | bytes 262144 | tf_op jit(solution)/shard_map/all_to_all | solution.py:555
  116.1 3.6 %all-to-all-start.5 = ((bf16[16,32,512]{2,1,0:T(8,128)(2,1)}), bf16[16,32,512]{2,1,0:T(8,128)(2,1)S(1)}, u32[]{:S(2)}, u32[]{:S(2)}) async-start(bf16[16,32,512]{2,1,0:T(8,128)(2,1)} %get-tuple-element.73), calls=%async_computation.5 | async-start | bytes 1048576 | tf_op jit(solution)/shard_map/all_to_all | solution.py:555
  120.4 1.0 collective-permute-start.12
  121.8 1.8 %collective-permute-done.13.b3 = bf16[16,32,128]{2,1,0:T(8,128)(2,1)S(1)} collective-permute-done((bf16[16,32,128]{2,1,0:T(8,128)(2,1)S(1)}, bf16[16,32,128]{2,1,0:T(8,128)(2,1)S(1)}, u32[]{:S(2)}, u32[]{:S(2)}) %collective-permute-start.13) | collective-permute-done | bytes 131104 | tf_op jit(solution)/shard_map/ppermute | solution.py:551
  123.6 2.2 %collective-permute-done.12.b2 = bf16[16,32,128]{2,1,0:T(8,128)(2,1)S(1)} collective-permute-done((bf16[16,32,128]{2,1,0:T(8,128)(2,1)S(1)}, bf16[16,32,128]{2,1,0:T(8,128)(2,1)S(1)}, u32[]{:S(2)}, u32[]{:S(2)}) %collective-permute-start.12) | collective-permute-done | bytes 131104 | tf_op jit(solution)/shard_map/ppermute | solution.py:551
  125.8 1.3 collective-permute-done.11.b1
  127.1 1.5 %all-to-all-done.5.a = bf16[16,32,512]{2,1,0:T(8,128)(2,1)S(1)} async-done(((bf16[16,32,512]{2,1,0:T(8,128)(2,1)}), bf16[16,32,512]{2,1,0:T(8,128)(2,1)S(1)}, u32[]{:S(2)}, u32[]{:S(2)}) %all-to-all-start.5) | async-done | bytes 524320 | tf_op jit(solution)/shard_map/all_to_all | solution.py:555
  128.7 6.8 %collective-permute-start.15 = (bf16[16,32,512]{2,1,0:T(8,128)(2,1)S(1)}, bf16[16,32,512]{2,1,0:T(8,128)(2,1)S(1)}, u32[]{:S(2)}, u32[]{:S(2)}) collective-permute-start(bf16[16,32,512]{2,1,0:T(8,128)(2,1)S(1)} %join.1.b), channel_id=1, source_target_pairs={{0,1},{1,0},{2,3},{3,2},{4,5},{5,4},{6,7},{7,6},{8,9},{9,8},{10,11... | collective-permute-start | bytes 1572872 | tf_op jit(solution)/shard_map/ppermute | solution.py:571
  136.1 2.0 %collective-permute-done.10.got = bf16[128,512]{1,0:T(8,128)(2,1)S(1)} collective-permute-done((bf16[128,512]{1,0:T(8,128)(2,1)S(1)}, bf16[128,512]{1,0:T(8,128)(2,1)S(1)}, u32[]{:S(2)}, u32[]{:S(2)}) %collective-permute-start.10) | collective-permute-done | bytes 131104 | tf_op jit(solution)/shard_map/ppermute | solution.py:572
  138.0 1.1 owner_sum.1
  139.1 2.4 %whole_grad.1 = f32[16,2,64,512]{3,2,1,0:T(8,128)} custom-call(s32[1]{0:T(128)} %bitcast.core, bf16[16,32,512]{2,1,0:T(8,128)(2,1)S(1)} %all-to-all-done.5.a, bf16[16,32,512]{2,1,0:T(8,128)(2,1)S(1)} %join.1.b, bf16[16,32,512]{2,1,0:T(8,128)(2,1)S(1)} %collective-permute-done.14.a_far, bf16[16,32,512]{2,1,0:T(8,128)(2,1)S(1)} %collective-permute-done.15.b_far), custom_call_target="tpu_custom_call" | custom-call | flops 524288 | bytes 6291456 | tf_op jit(solution)/shard_map/whole_grad/pallas_call | solution.py:459
  (44 shorter events, 3.4 us)
Async XLA Ops:
  0.6 14.6 %copy-start.2 = (s32[1,1,256]{2,1,0:T(1,128)S(1)}, s32[1,1,256]{2,1,0:T(1,128)}, u32[]{:S(2)}) copy-start(s32[1,1,256]{2,1,0:T(1,128)} %param.18) | copy-start | bytes 3076
  0.6 24.9 %copy-start.15 = (s32[1,256,9]{1,0,2:T(1,128)S(1)}, s32[1,256,9]{1,0,2:T(1,128)}, u32[]{:S(2)}) copy-start(s32[1,256,9]{1,0,2:T(1,128)} %param.19) | copy-start | bytes 27652
  0.7 24.9 %copy-start.16 = (s32[1,256,8]{1,2,0:T(8,128)S(1)}, s32[1,256,8]{1,2,0:T(8,128)}, u32[]{:S(2)}) copy-start(s32[1,256,8]{1,2,0:T(8,128)} %param.20) | copy-start | bytes 24580
  0.7 25.0 %copy-start.6 = (f32[512]{0:T(512)S(1)}, f32[512]{0:T(512)}, u32[]{:S(2)}) copy-start(f32[512]{0:T(512)} %param.17) | copy-start | bytes 6148
  5.1 28.1 %copy-start = (bf16[256,512]{1,0:T(8,128)(2,1)S(1)}, bf16[256,512]{1,0:T(8,128)(2,1)}, u32[]{:S(2)}) copy-start(bf16[256,512]{1,0:T(8,128)(2,1)} %state.3) | copy-start | bytes 786436
  5.1 28.1 %copy-start.1 = (bf16[256,512]{1,0:T(8,128)(2,1)S(1)}, bf16[256,512]{1,0:T(8,128)(2,1)}, u32[]{:S(2)}) copy-start(bf16[256,512]{1,0:T(8,128)(2,1)} %gru.1.written) | copy-start | bytes 786436
  5.1 9.4 %collective-permute-start = (bf16[256,512]{1,0:T(8,128)(2,1)}, bf16[256,512]{1,0:T(8,128)(2,1)S(1)}, u32[]{:S(2)}, u32[]{:S(2)}) collective-permute-start(bf16[256,512]{1,0:T(8,128)(2,1)} %gru.1.written), channel_id=1, source_target_pairs={{0,32},{32,64},{64,96},{1,33},{33,65},{65,97},{2,34},{34,66},{66,9... | collective-permute-start | bytes 786440 | tf_op jit(solution)/shard_map/ppermute | solution.py:531
  9.3 23.9 %collective-permute-start.2 = (bf16[256,512]{1,0:T(8,128)(2,1)}, bf16[256,512]{1,0:T(8,128)(2,1)S(1)}, u32[]{:S(2)}, u32[]{:S(2)}) collective-permute-start(bf16[256,512]{1,0:T(8,128)(2,1)} %gru.1.written), channel_id=1, source_target_pairs={{0,96},{1,97},{2,98},{3,99},{4,100},{5,101},{6,102},{7,103},{8,104... | collective-permute-start | bytes 786440 | tf_op jit(solution)/shard_map/ppermute | solution.py:532
  14.6 18.6 %collective-permute-start.1 = (bf16[256,512]{1,0:T(8,128)(2,1)S(1)}, bf16[256,512]{1,0:T(8,128)(2,1)S(1)}, u32[]{:S(2)}, u32[]{:S(2)}) collective-permute-start(bf16[256,512]{1,0:T(8,128)(2,1)S(1)} %collective-permute-done.r1), channel_id=1, source_target_pairs={{32,64},{64,96},{33,65},{65,97},{34,66},{66,98},{35,67},{67,99},{3... | collective-permute-start | bytes 786440 | tf_op jit(solution)/shard_map/ppermute | solution.py:533
  16.0 17.2 %all-to-all-start = ((s32[32,8,128]{2,1,0:T(8,128)}), s32[32,8,128]{2,1,0:T(8,128)S(1)}, u32[]{:S(2)}, u32[]{:S(2)}) async-start(s32[32,8,128]{2,1,0:T(8,128)} %bitcast.7), calls=%async_computation | async-start | bytes 262144 | tf_op jit(solution)/shard_map/all_to_all | solution.py:511
  25.7 16.0 %copy-start.5 = (bf16[1,256,512]{2,1,0:T(8,128)(2,1)S(1)}, bf16[1,256,512]{2,1,0:T(8,128)(2,1)}, u32[]{:S(2)}) copy-start(bf16[1,256,512]{2,1,0:T(8,128)(2,1)} %param.21) | copy-start | bytes 786436
  30.2 1.3 copy-start.7
  31.5 1.3 copy-start.9
  34.5 16.2 %all-to-all-start.1 = ((bf16[32,8,512]{2,1,0:T(8,128)(2,1)}), bf16[32,8,512]{2,1,0:T(8,128)(2,1)S(1)}, u32[]{:S(2)}, u32[]{:S(2)}) async-start(bf16[32,8,512]{2,1,0:T(8,128)(2,1)} %bitcast.9), calls=%async_computation.1 | async-start | bytes 524288 | tf_op jit(solution)/shard_map/all_to_all | solution.py:511
  41.7 1.6 %copy-start.3 = (bf16[4,512,512]{2,1,0:T(8,128)(2,1)S(1)}, bf16[4,512,512]{2,1,0:T(8,128)(2,1)}, u32[]{:S(2)}) copy-start(bf16[4,512,512]{2,1,0:T(8,128)(2,1)} %wq.1) | copy-start | bytes 6291460
  43.2 1.6 %copy-start.10 = (bf16[2,8,128,512]{3,2,1,0:T(8,128)(2,1)S(1)}, bf16[2,8,128,512]{3,2,1,0:T(8,128)(2,1)}, u32[]{:S(2)}) copy-start(bf16[2,8,128,512]{3,2,1,0:T(8,128)(2,1)} %copy-done.9) | copy-start | bytes 6291460
  48.0 1.3 copy-start.11
  49.3 1.3 copy-start.13
  50.7 1.6 %copy-start.4 = (bf16[4,512,512]{2,1,0:T(8,128)(2,1)S(1)}, bf16[4,512,512]{2,1,0:T(8,128)(2,1)}, u32[]{:S(2)}) copy-start(bf16[4,512,512]{2,1,0:T(8,128)(2,1)} %wq.1) | copy-start | bytes 6291460
  52.3 1.6 %copy-start.8 = (bf16[2,512,1024]{2,1,0:T(8,128)(2,1)S(1)}, bf16[2,512,1024]{2,1,0:T(8,128)(2,1)}, u32[]{:S(2)}) copy-start(bf16[2,512,1024]{2,1,0:T(8,128)(2,1)} %copy-done.7) | copy-start | bytes 6291460
  53.9 1.6 %copy-start.12 = (bf16[2,8,128,512]{3,2,1,0:T(8,128)(2,1)S(1)}, bf16[2,8,128,512]{3,2,1,0:T(8,128)(2,1)}, u32[]{:S(2)}) copy-start(bf16[2,8,128,512]{3,2,1,0:T(8,128)(2,1)} %copy-done.11) | copy-start | bytes 6291460
  55.5 1.6 %copy-start.14 = (bf16[2,8,128,512]{3,2,1,0:T(8,128)(2,1)S(1)}, bf16[2,8,128,512]{3,2,1,0:T(8,128)(2,1)}, u32[]{:S(2)}) copy-start(bf16[2,8,128,512]{3,2,1,0:T(8,128)(2,1)} %copy-done.13) | copy-start | bytes 6291460
  65.4 2.8 %collective-permute-start.3 = (bf16[16,64,512]{2,1,0:T(8,128)(2,1)S(1)}, bf16[16,64,512]{2,1,0:T(8,128)(2,1)S(1)}, u32[]{:S(2)}, u32[]{:S(2)}) collective-permute-start(bf16[16,64,512]{2,1,0:T(8,128)(2,1)S(1)} %get-tuple-element.60), channel_id=1, source_target_pairs={{0,1},{1,0},{2,3},{3,2},{4,5},{5,4},{6,7},{7,6},{8,9},{9,8},{10,11... | collective-permute-start | bytes 3145736 | tf_op jit(solution)/shard_map/ppermute | solution.py:557
  69.1 19.1 %all-to-all-start.2 = ((bf16[16,32,512]{2,1,0:T(8,128)(2,1)}), bf16[16,32,512]{2,1,0:T(8,128)(2,1)S(1)}, u32[]{:S(2)}, u32[]{:S(2)}) async-start(bf16[16,32,512]{2,1,0:T(8,128)(2,1)} %get-tuple-element.61), calls=%async_computation.2 | async-start | bytes 1048576 | tf_op jit(solution)/shard_map/all_to_all | solution.py:555
  75.8 8.4 %collective-permute-start.4 = (bf16[16,32,128]{2,1,0:T(8,128)(2,1)S(1)}, bf16[16,32,128]{2,1,0:T(8,128)(2,1)S(1)}, u32[]{:S(2)}, u32[]{:S(2)}) collective-permute-start(bf16[16,32,128]{2,1,0:T(8,128)(2,1)S(1)} %get-tuple-element.63), channel_id=1, source_target_pairs={{0,32},{32,64},{64,96},{96,0},{1,33},{33,65},{65,97},{97,1},{2,34}... | collective-permute-start | bytes 393224 | tf_op jit(solution)/shard_map/ppermute | solution.py:559
  80.8 7.4 %collective-permute-start.5 = (bf16[16,32,128]{2,1,0:T(8,128)(2,1)S(1)}, bf16[16,32,128]{2,1,0:T(8,128)(2,1)S(1)}, u32[]{:S(2)}, u32[]{:S(2)}) collective-permute-start(bf16[16,32,128]{2,1,0:T(8,128)(2,1)S(1)} %get-tuple-element.64), channel_id=1, source_target_pairs={{0,64},{32,96},{64,0},{96,32},{1,65},{33,97},{65,1},{97,33},{2,66}... | collective-permute-start | bytes 393224 | tf_op jit(solution)/shard_map/ppermute | solution.py:559
  82.2 6.0 %collective-permute-start.6 = (bf16[16,32,128]{2,1,0:T(8,128)(2,1)S(1)}, bf16[16,32,128]{2,1,0:T(8,128)(2,1)S(1)}, u32[]{:S(2)}, u32[]{:S(2)}) collective-permute-start(bf16[16,32,128]{2,1,0:T(8,128)(2,1)S(1)} %get-tuple-element.65), channel_id=1, source_target_pairs={{0,96},{32,0},{64,32},{96,64},{1,97},{33,1},{65,33},{97,65},{2,98}... | collective-permute-start | bytes 393224 | tf_op jit(solution)/shard_map/ppermute | solution.py:559
  89.0 14.3 %all-to-all-start.3 = ((bf16[16,96,128]{2,1,0:T(8,128)(2,1)}), bf16[16,96,128]{2,1,0:T(8,128)(2,1)S(1)}, u32[]{:S(2)}, u32[]{:S(2)}) async-start(bf16[16,96,128]{2,1,0:T(8,128)(2,1)} %get-tuple-element.67), calls=%async_computation.3 | async-start | bytes 786432 | tf_op jit(solution)/shard_map/all_to_all | solution.py:555
  95.3 3.7 %collective-permute-start.9 = (bf16[32,512]{1,0:T(8,128)(2,1)S(1)}, bf16[32,512]{1,0:T(8,128)(2,1)S(1)}, u32[]{:S(2)}, u32[]{:S(2)}) collective-permute-start(bf16[32,512]{1,0:T(8,128)(2,1)S(1)} %get-tuple-element.68.own), channel_id=1, source_target_pairs={{0,96},{32,0},{64,32},{96,64},{1,97},{33,1},{65,33},{97,65},{2,98}... | collective-permute-start | bytes 98312 | tf_op jit(solution)/shard_map/ppermute | solution.py:551
  97.3 4.3 %collective-permute-start.8 = (bf16[32,512]{1,0:T(8,128)(2,1)S(1)}, bf16[32,512]{1,0:T(8,128)(2,1)S(1)}, u32[]{:S(2)}, u32[]{:S(2)}) collective-permute-start(bf16[32,512]{1,0:T(8,128)(2,1)S(1)} %get-tuple-element.68.own), channel_id=1, source_target_pairs={{0,64},{32,96},{64,0},{96,32},{1,65},{33,97},{65,1},{97,33},{2,66}... | collective-permute-start | bytes 98312 | tf_op jit(solution)/shard_map/ppermute | solution.py:551
  98.2 4.3 %collective-permute-start.7 = (bf16[32,512]{1,0:T(8,128)(2,1)S(1)}, bf16[32,512]{1,0:T(8,128)(2,1)S(1)}, u32[]{:S(2)}, u32[]{:S(2)}) collective-permute-start(bf16[32,512]{1,0:T(8,128)(2,1)S(1)} %get-tuple-element.68.own), channel_id=1, source_target_pairs={{0,32},{32,64},{64,96},{96,0},{1,33},{33,65},{65,97},{97,1},{2,34}... | collective-permute-start | bytes 98312 | tf_op jit(solution)/shard_map/ppermute | solution.py:551
  116.1 12.5 %all-to-all-start.5 = ((bf16[16,32,512]{2,1,0:T(8,128)(2,1)}), bf16[16,32,512]{2,1,0:T(8,128)(2,1)S(1)}, u32[]{:S(2)}, u32[]{:S(2)}) async-start(bf16[16,32,512]{2,1,0:T(8,128)(2,1)} %get-tuple-element.73), calls=%async_computation.5 | async-start | bytes 1048576 | tf_op jit(solution)/shard_map/all_to_all | solution.py:555
  119.7 3.9 %collective-permute-start.13 = (bf16[16,32,128]{2,1,0:T(8,128)(2,1)S(1)}, bf16[16,32,128]{2,1,0:T(8,128)(2,1)S(1)}, u32[]{:S(2)}, u32[]{:S(2)}) collective-permute-start(bf16[16,32,128]{2,1,0:T(8,128)(2,1)S(1)} %all_to_all.30.b0), channel_id=1, source_target_pairs={{0,96},{32,0},{64,32},{96,64},{1,97},{33,1},{65,33},{97,65},{2,98}... | collective-permute-start | bytes 393224 | tf_op jit(solution)/shard_map/ppermute | solution.py:551
  120.4 5.4 %collective-permute-start.12 = (bf16[16,32,128]{2,1,0:T(8,128)(2,1)S(1)}, bf16[16,32,128]{2,1,0:T(8,128)(2,1)S(1)}, u32[]{:S(2)}, u32[]{:S(2)}) collective-permute-start(bf16[16,32,128]{2,1,0:T(8,128)(2,1)S(1)} %all_to_all.30.b0), channel_id=1, source_target_pairs={{0,64},{32,96},{64,0},{96,32},{1,65},{33,97},{65,1},{97,33},{2,66}... | collective-permute-start | bytes 393224 | tf_op jit(solution)/shard_map/ppermute | solution.py:551
  121.4 5.7 %collective-permute-start.11 = (bf16[16,32,128]{2,1,0:T(8,128)(2,1)S(1)}, bf16[16,32,128]{2,1,0:T(8,128)(2,1)S(1)}, u32[]{:S(2)}, u32[]{:S(2)}) collective-permute-start(bf16[16,32,128]{2,1,0:T(8,128)(2,1)S(1)} %all_to_all.30.b0), channel_id=1, source_target_pairs={{0,32},{32,64},{64,96},{96,0},{1,33},{33,65},{65,97},{97,1},{2,34}... | collective-permute-start | bytes 393224 | tf_op jit(solution)/shard_map/ppermute | solution.py:551
  128.7 10.4 %collective-permute-start.15 = (bf16[16,32,512]{2,1,0:T(8,128)(2,1)S(1)}, bf16[16,32,512]{2,1,0:T(8,128)(2,1)S(1)}, u32[]{:S(2)}, u32[]{:S(2)}) collective-permute-start(bf16[16,32,512]{2,1,0:T(8,128)(2,1)S(1)} %join.1.b), channel_id=1, source_target_pairs={{0,1},{1,0},{2,3},{3,2},{4,5},{5,4},{6,7},{7,6},{8,9},{9,8},{10,11... | collective-permute-start | bytes 1572872 | tf_op jit(solution)/shard_map/ppermute | solution.py:571
  135.5 3.6 %collective-permute-start.14 = (bf16[16,32,512]{2,1,0:T(8,128)(2,1)S(1)}, bf16[16,32,512]{2,1,0:T(8,128)(2,1)S(1)}, u32[]{:S(2)}, u32[]{:S(2)}) collective-permute-start(bf16[16,32,512]{2,1,0:T(8,128)(2,1)S(1)} %all-to-all-done.5.a), channel_id=1, source_target_pairs={{0,1},{1,0},{2,3},{3,2},{4,5},{5,4},{6,7},{7,6},{8,9},{9,8},{10,11... | collective-permute-start | bytes 1572872 | tf_op jit(solution)/shard_map/ppermute | solution.py:569
  135.6 2.4 %collective-permute-start.10 = (bf16[128,512]{1,0:T(8,128)(2,1)S(1)}, bf16[128,512]{1,0:T(8,128)(2,1)S(1)}, u32[]{:S(2)}, u32[]{:S(2)}) collective-permute-start(bf16[128,512]{1,0:T(8,128)(2,1)S(1)} %get-tuple-element.70), channel_id=1, source_target_pairs={{0,1},{1,0},{2,3},{3,2},{4,5},{5,4},{6,7},{7,6},{8,9},{9,8},{10,11... | collective-permute-start | bytes 393224 | tf_op jit(solution)/shard_map/ppermute | solution.py:572

commit v2 on v1

--- a/solution.py
+++ b/solution.py
@@ -21,8 +21,6 @@
 CAP = 8
 SLOTS = 256
 PIECE = 64
-HALF = PIECE // 2
-CUT = DM // SEG
 TILE = 128
 TILES = E // TILE
 ROWS = K * TILE
@@ -141,7 +139,7 @@
             jax.ShapeDtypeStruct((TILES, K, TILE, DM), BF),
             jax.ShapeDtypeStruct((TILES, DM, ROWS), BF),
         ],
-        compiler_params=pltpu.CompilerParams(vmem_limit_bytes=16 << 20),
+        compiler_params=pltpu.CompilerParams(vmem_limit_bytes=56 << 20),
         cost_estimate=pl.CostEstimate(
             flops=20 * K * E * DM, bytes_accessed=4 << 20, transcendentals=K * E * DM
         ),
@@ -149,32 +147,29 @@
     )(delays, frequency)
 
 
-def project_kernel(code, w, up, time_k, time_v, d_att):
+def project_kernel(code, w, time_kv):
     rows = code[0].reshape(K // 2 * TILE, DM)
-    time_k[0] = dot(rows, w[1]).astype(BF).reshape(K // 2, TILE, DM)
-    time_v[0] = dot(rows, w[2]).astype(BF).reshape(K // 2, TILE, DM)
-
-    @pl.when((pl.program_id(0) == 0) & (pl.program_id(1) == 0))
-    def _():
-        d_att[...] = dot_nt(up[...], w[3]).astype(BF)
-
-
-def project(code, weights, up):
-    block = pl.BlockSpec((1, K // 2, TILE, DM), lambda i, j: (i, j, 0, 0))
-    time = jax.ShapeDtypeStruct((TILES, K, TILE, DM), BF)
-    whole = pl.BlockSpec((E, DM), lambda i, j: (0, 0))
+    for i in range(2):
+        part = dot(rows, w[1 + i]).astype(BF).reshape(K // 2, TILE, DM)
+        time_kv[0, :, :, i * DM : (i + 1) * DM] = part
+
+
+def project(code, weights):
     return pl.pallas_call(
         project_kernel,
         grid=(TILES, 2),
-        in_specs=[block, pl.BlockSpec((4, DM, DM), lambda i, j: (0, 0, 0)), whole],
-        out_specs=[block, block, whole],
-        out_shape=[time, time, jax.ShapeDtypeStruct((E, DM), BF)],
-        compiler_params=pltpu.CompilerParams(vmem_limit_bytes=16 << 20),
+        in_specs=[
+            pl.BlockSpec((1, K // 2, TILE, DM), lambda i, j: (i, j, 0, 0)),
+            pl.BlockSpec((4, DM, DM), lambda i, j: (0, 0, 0)),
+        ],
+        out_specs=pl.BlockSpec((1, K // 2, TILE, 2 * DM), lambda i, j: (i, j, 0, 0)),
+        out_shape=jax.ShapeDtypeStruct((TILES, K, TILE, 2 * DM), BF),
+        compiler_params=pltpu.CompilerParams(vmem_limit_bytes=56 << 20),
         cost_estimate=pl.CostEstimate(
             flops=4 * K * E * DM * DM, bytes_accessed=8 << 20, transcendentals=0
         ),
         name="time_projections",
-    )(code, weights, up)
+    )(code, weights)
 
 
 def owner_pick(asked):
@@ -211,16 +206,23 @@
 
 
 def attend_kernel(
-    core, slots, chosen, chosen_t, tk, tv, tt, d_att, up, wq,
+    core, slots, chosen, chosen_t, time_kv, time_t, up, w,
     embedded, d_slots, mine, other,
-    skv, qf, src, both, dkv, att, dq, sums,
+    tkv, tt, wq, sem, skv, d_att, qf, src, both, dkv, att, dq, sums,
 ):
+    moves = ((w, wq), (time_kv, tkv), (time_t, tt))
+    copies = [pltpu.make_async_copy(a, b, sem.at[i]) for i, (a, b) in enumerate(moves)]
+    for copy in copies:
+        copy.start()
     rows = slots[...]
     pick = (chosen[:, 0:1] == iota((E, SLOTS), 1)).astype(F32).astype(BF)
     src[...] = dot(pick, rows)
+    copies[0].wait()
     skv[:, :DM] = dot(rows, wq[1]).astype(BF)
     skv[:, DM:] = dot(rows, wq[2]).astype(BF)
     qf[...] = dot(pick, dot(rows, wq[0]).astype(BF))
+    d_att[...] = dot_nt(up[...], wq[3])
+    copies[1].wait()
 
     lane = iota((STEP, 128), 1)
     first = lane < K
@@ -248,12 +250,12 @@
             part = slice(h * HEAD, (h + 1) * HEAD)
             part_v = slice(DM + h * HEAD, DM + (h + 1) * HEAD)
             query = qf[at, part]
-            d_out = d_att[at, part].astype(F32)
+            d_out = d_att[at, part]
             for k in range(K):
                 row = slice(k * TILE + j * STEP, k * TILE + (j + 1) * STEP)
                 local = slice(j * STEP, (j + 1) * STEP)
-                key = both[i, row, part] + tk[i, k, local, part].astype(F32)
-                value = both[i, row, part_v] + tv[i, k, local, part].astype(F32)
+                key = both[i, row, part] + tkv[i, k, local, part].astype(F32)
+                value = both[i, row, part_v] + tkv[i, k, local, part_v].astype(F32)
                 both[i, row, part] = key
                 both[i, row, part_v] = value
                 here = lane == h * K + k
@@ -266,7 +268,7 @@
             part = slice(h * HEAD, (h + 1) * HEAD)
             part_v = slice(DM + h * HEAD, DM + (h + 1) * HEAD)
             query = qf[at, part]
-            d_out = d_att[at, part].astype(F32)
+            d_out = d_att[at, part]
             attended = jnp.zeros((STEP, HEAD), F32)
             d_query = jnp.zeros((STEP, HEAD), F32)
             for k in range(K):
@@ -284,10 +286,12 @@
     for i in range(TILES):
         gather(i)
     sub = iota((SLOTS, TILE), 0)
-    s_kv = g_kv = None
+    s_kv = dot_t = None
     for i in range(TILES):
         for j in range(TILE // STEP):
             step(i, j)
+        if i == 0:
+            copies[2].wait()
         spread = jnp.concatenate(
             [
                 (sub == chosen_t[1 + k : 2 + k, i * TILE : (i + 1) * TILE]).astype(F32)
@@ -297,7 +301,7 @@
         ).astype(BF)
         one, two = dot(spread, dkv[i]), dot(tt[i], dkv[i])
         s_kv = one if i == 0 else s_kv + one
-        g_kv = two if i == 0 else g_kv + two
+        dot_t = two if i == 0 else dot_t + two
     s_kv = s_kv.astype(BF)
     pick_t = (iota((SLOTS, E), 0) == chosen_t[0:1, :]).astype(F32).astype(BF)
     s_q = dot(pick_t, dq[...]).astype(BF)
@@ -306,7 +310,7 @@
         sums[i * 4 : (i + 1) * 4] = value.astype(BF).reshape(4, CORES, PIECE, DM)
 
     store(0, dot_tn(rows, s_q))
-    g_kv += dot_tn(rows, s_kv)
+    g_kv = dot_t + dot_tn(rows, s_kv)
     store(1, g_kv[:, :DM])
     store(2, g_kv[:, DM:])
     store(3, dot_tn(att[...], up[...]))
@@ -318,11 +322,16 @@
     d_slots[...] = grads.astype(BF)
 
 
-def attend(core, slots, chosen, chosen_t, time_k, time_v, time_t, d_att, up, weights):
-    whole = pl.BlockSpec(memory_space=pltpu.VMEM)
+def attend(core, slots, chosen, chosen_t, time_kv, time_t, up, weights):
+    whole = pl.BlockSpec(memory_space=pltpu.VMEM)
+    far = pl.BlockSpec(memory_space=pl.ANY)
     return pl.pallas_call(
         attend_kernel,
-        in_specs=[pl.BlockSpec(memory_space=pltpu.SMEM)] + [whole] * 9,
+        in_specs=[pl.BlockSpec(memory_space=pltpu.SMEM)]
+        + [whole] * 3
+        + [far] * 2
+        + [whole]
+        + [far],
         out_specs=[whole] * 4,
         out_shape=[
             jax.ShapeDtypeStruct((E, DM), BF),
@@ -331,7 +340,12 @@
             jax.ShapeDtypeStruct((PLANE, PIECE, DM), BF),
         ],
         scratch_shapes=[
+            pltpu.VMEM((TILES, K, TILE, 2 * DM), BF),
+            pltpu.VMEM((TILES, DM, ROWS), BF),
+            pltpu.VMEM((4, DM, DM), BF),
+            pltpu.SemaphoreType.DMA((3,)),
             pltpu.VMEM((SLOTS, 2 * DM), BF),
+            pltpu.VMEM((E, DM), F32),
             pltpu.VMEM((E, DM), F32),
             pltpu.VMEM((E, DM), F32),
             pltpu.VMEM((TILES, ROWS, 2 * DM), F32),
@@ -340,132 +354,125 @@
             pltpu.VMEM((E, DM), BF),
             pltpu.VMEM((PLANE, CORES, PIECE, DM), BF),
         ],
-        compiler_params=pltpu.CompilerParams(vmem_limit_bytes=40 << 20),
+        compiler_params=pltpu.CompilerParams(vmem_limit_bytes=50 << 20),
         cost_estimate=pl.CostEstimate(
             flops=6 << 30, bytes_accessed=14 << 20, transcendentals=E * 128
         ),
         name="attend",
-    )(core, slots, chosen, chosen_t, time_k, time_v, time_t, d_att, up, weights)
-
-
-def small(kernel, name, out_shape, in_specs, out_specs, scratch=(), moved=1 << 20):
-    return pl.pallas_call(
-        kernel,
-        in_specs=in_specs,
-        out_specs=out_specs,
-        out_shape=out_shape,
-        scratch_shapes=scratch,
-        compiler_params=pltpu.CompilerParams(vmem_limit_bytes=16 << 20),
-        cost_estimate=pl.CostEstimate(flops=1 << 19, bytes_accessed=moved, transcendentals=0),
-        name=name,
-    )
-
-
-WHOLE = pl.BlockSpec(memory_space=pltpu.VMEM)
-SCALAR = pl.BlockSpec(memory_space=pltpu.SMEM)
-A_SHAPE = jax.ShapeDtypeStruct((PLANE, HALF, DM), BF)
-B_SHAPE = jax.ShapeDtypeStruct((PLANE, HALF, CUT), BF)
-
-
-def columns_of(seg, back):
-    place = lax.rem(seg[0] + back + SEG, SEG)
-    return pl.ds(pl.multiple_of(place * CUT, CUT), CUT)
-
-
-def pair_kernel(seg, mine, partner, a, *bs):
-    a[...] = (mine[:, :HALF].astype(F32) + partner[:, :HALF].astype(F32)).astype(BF)
-    for ahead, b in enumerate(bs):
-        at = columns_of(seg, ahead)
-        b[...] = (mine[:, HALF:, at].astype(F32) + partner[:, HALF:, at].astype(F32)).astype(BF)
-
-
-def pair_sum(seg, mine, partner):
-    shapes = [A_SHAPE] + [B_SHAPE] * SEG
-    return small(pair_kernel, "pair_sum", shapes, [SCALAR, WHOLE, WHOLE], [WHOLE] * 5)(
-        seg, mine, partner
-    )
-
-
-def first_kernel(a, b0, b1, b2, b3, d_slots, part, pack):
-    total = a[0].astype(F32)
+    )(core, slots, chosen, chosen_t, time_kv, time_t, up, weights)
+
+
+def pair_kernel(a, b, d_slots, out):
+    out[:, :PIECE] = (a[...].astype(F32) + b[...].astype(F32)).astype(BF)
+    out[:, PIECE:] = d_slots[...]
+
+
+def pair_sum(a, b, d_slots):
+    spec = pl.BlockSpec((4, PIECE, DM), lambda i: (i, 0, 0))
+    return pl.pallas_call(
+        pair_kernel,
+        grid=(PLANE // 4,),
+        in_specs=[spec, spec, pl.BlockSpec((4, 2 * CAP, DM), lambda i: (i, 0, 0))],
+        out_specs=pl.BlockSpec((4, PIECE + 2 * CAP, DM), lambda i: (i, 0, 0)),
+        out_shape=jax.ShapeDtypeStruct((PLANE, PIECE + 2 * CAP, DM), BF),
+        compiler_params=pltpu.CompilerParams(vmem_limit_bytes=16 << 20),
+        cost_estimate=pl.CostEstimate(flops=1 << 19, bytes_accessed=3 << 20, transcendentals=0),
+        name="pair_sum",
+    )(a, b, d_slots.reshape(PLANE, 2 * CAP, DM))
+
+
+def plane_kernel(core, a, part, keep, give):
+    total = a[0, :PIECE].astype(F32)
     for i in range(1, PLANE):
-        total += a[i].astype(F32)
+        total += a[i, :PIECE].astype(F32)
     part[...] = total.astype(BF)
-    b = (b0[...].astype(F32) + b1[...].astype(F32)) + (b2[...].astype(F32) + b3[...].astype(F32))
-    pack[:, :HALF] = b.astype(BF)
-    for i in range(SEG):
-        at = slice(HALF + i * 2 * CAP, HALF + (i + 1) * 2 * CAP)
-        pack[:, at] = d_slots[:, :, i * CUT : (i + 1) * CUT]
-
-
-def first_sum(a, bs, d_slots):
-    shapes = [
-        jax.ShapeDtypeStruct((HALF, DM), BF),
-        jax.ShapeDtypeStruct((PLANE, HALF + SEG * 2 * CAP, CUT), BF),
-    ]
-    return small(first_kernel, "first_sum", shapes, [WHOLE] * 6, [WHOLE] * 2)(
-        a, *bs, d_slots.reshape(PLANE, 2 * CAP, DM)
-    )
-
-
-def second_kernel(seg, core, pack, own, p1, p2, p3, a, b, keep, give, parts):
-    for back, r in enumerate((own, p1, p2, p3)):
-        parts[lax.rem(seg[0] + SEG - back, SEG)] = r[...].astype(F32)
-    a_total = ((parts[0] + parts[1]) + (parts[2] + parts[3])).astype(BF)
-    total = pack[0, :HALF].astype(F32)
-    for i in range(1, PLANE):
-        total += pack[i, :HALF].astype(F32)
-    b_total = total.astype(BF)
+    grads = a[:, PIECE:].astype(F32)
+    low, high = grads[:, :CAP].reshape(SLOTS // 2, DM), grads[:, CAP:].reshape(SLOTS // 2, DM)
+    first = core[0] == 0
+    keep[...] = jnp.where(first, low, high).astype(BF)
+    give[...] = jnp.where(first, high, low).astype(BF)
+
+
+def plane_sum(core, a):
+    whole = pl.BlockSpec(memory_space=pltpu.VMEM)
+    half = jax.ShapeDtypeStruct((SLOTS // 2, DM), BF)
+    return pl.pallas_call(
+        plane_kernel,
+        in_specs=[pl.BlockSpec(memory_space=pltpu.SMEM), whole],
+        out_specs=[whole] * 3,
+        out_shape=[jax.ShapeDtypeStruct((PIECE, DM), BF), half, half],
+        compiler_params=pltpu.CompilerParams(vmem_limit_bytes=16 << 20),
+        cost_estimate=pl.CostEstimate(flops=1 << 19, bytes_accessed=2 << 20, transcendentals=0),
+        name="plane_sum",
+    )(core, a)
+
+
+def swap_kernel(a, b, out):
+    out[...] = (a[...].astype(F32) + b[...].astype(F32)).astype(BF)
+
+
+def swap_sum(a, b):
+    whole = pl.BlockSpec(memory_space=pltpu.VMEM)
+    return pl.pallas_call(
+        swap_kernel,
+        in_specs=[whole] * 2,
+        out_specs=whole,
+        out_shape=jax.ShapeDtypeStruct((PIECE, DM), BF),
+        compiler_params=pltpu.CompilerParams(vmem_limit_bytes=16 << 20),
+        cost_estimate=pl.CostEstimate(flops=1 << 15, bytes_accessed=1 << 17, transcendentals=0),
+        name="swap_sum",
+    )(a, b)
+
+
+def seg_kernel(a, b, out):
+    total = (a[...].astype(F32) + b[...].astype(F32)).astype(BF)
     for i in range(PLANE):
-        a[i] = a_total
-        b[i] = b_total
-    first = core[0] == 0
-    for i in range(SEG):
-        grads = pack[:, HALF + i * 2 * CAP : HALF + (i + 1) * 2 * CAP].astype(F32)
-        low = grads[:, :CAP].reshape(SLOTS // 2, CUT)
-        high = grads[:, CAP:].reshape(SLOTS // 2, CUT)
-        at = slice(i * CUT, (i + 1) * CUT)
-        keep[:, at] = jnp.where(first, low, high).astype(BF)
-        give[:, at] = jnp.where(first, high, low).astype(BF)
-
-
-def second_sum(seg, core, pack, own, turned):
-    grads = jax.ShapeDtypeStruct((SLOTS // 2, DM), BF)
-    shapes = [A_SHAPE, B_SHAPE, grads, grads]
-    scratch = [pltpu.VMEM((SEG, HALF, DM), F32)]
-    return small(
-        second_kernel, "second_sum", shapes, [SCALAR] * 2 + [WHOLE] * 5, [WHOLE] * 4, scratch
-    )(seg, core, pack, own, *turned)
-
-
-def join_kernel(seg, b0, b1, b2, b3, out):
-    for back, b in enumerate((b0, b1, b2, b3)):
-        out[:, :, columns_of(seg, -back)] = b[...]
-
-
-def join(seg, bs):
-    return small(join_kernel, "join", A_SHAPE, [SCALAR] + [WHOLE] * 4, WHOLE)(seg, *bs)
-
-
-def whole_kernel(core, a, b, a_far, b_far, out):
-    out[:, core[0], :HALF] = a[...].astype(F32)
-    out[:, core[0], HALF:] = b[...].astype(F32)
-    out[:, 1 - core[0], :HALF] = a_far[...].astype(F32)
-    out[:, 1 - core[0], HALF:] = b_far[...].astype(F32)
-
-
-def whole_grad(core, a, b, a_far, b_far):
-    spec = pl.BlockSpec((4, HALF, DM), lambda i: (i, 0, 0))
-    return pl.pallas_call(
-        whole_kernel,
-        grid=(PLANE // 4,),
-        in_specs=[SCALAR] + [spec] * 4,
-        out_specs=pl.BlockSpec((4, CORES, PIECE, DM), lambda i: (i, 0, 0, 0)),
+        out[i] = total
+
+
+def seg_sum(a, b):
+    whole = pl.BlockSpec(memory_space=pltpu.VMEM)
+    return pl.pallas_call(
+        seg_kernel,
+        in_specs=[whole] * 2,
+        out_specs=whole,
+        out_shape=jax.ShapeDtypeStruct((PLANE, PIECE, DM), BF),
+        compiler_params=pltpu.CompilerParams(vmem_limit_bytes=16 << 20),
+        cost_estimate=pl.CostEstimate(flops=1 << 15, bytes_accessed=1 << 20, transcendentals=0),
+        name="seg_sum",
+    )(a, b)
+
+
+def own_kernel(core, half, out):
+    out[:, 0] = half[...].astype(F32)
+
+
+def far_kernel(core, half, before, out):
+    out[:, 0] = half[...].astype(F32)
+
+
+def whole_grad(core, half, before=None):
+    own = before is None
+
+    def place(i, core):
+        return (i, core[0] if own else 1 - core[0], 0, 0)
+
+    spec = pl.BlockSpec((4, PIECE, DM), lambda i, core: (i, 0, 0))
+    far = pl.BlockSpec(memory_space=pl.ANY)
+    return pl.pallas_call(
+        own_kernel if own else far_kernel,
+        grid_spec=pltpu.PrefetchScalarGridSpec(
+            num_scalar_prefetch=1,
+            grid=(PLANE // 4,),
+            in_specs=[spec] if own else [spec, far],
+            out_specs=pl.BlockSpec((4, 1, PIECE, DM), place),
+        ),
         out_shape=jax.ShapeDtypeStruct((PLANE, CORES, PIECE, DM), F32),
-        compiler_params=pltpu.CompilerParams(vmem_limit_bytes=16 << 20),
-        cost_estimate=pl.CostEstimate(flops=1 << 19, bytes_accessed=6 << 20, transcendentals=0),
-        name="whole_grad",
-    )(core, a, b, a_far, b_far)
+        input_output_aliases={} if own else {2: 0},
+        compiler_params=pltpu.CompilerParams(vmem_limit_bytes=16 << 20),
+        cost_estimate=pl.CostEstimate(flops=1 << 18, bytes_accessed=3 << 20, transcendentals=0),
+        name="own_half" if own else "far_half",
+    )(core, half, *([] if own else [before]))
 
 
 def spread_kernel(ids, out):
@@ -509,6 +516,10 @@
 def exchange(rows, axes, count):
     blocks = rows.reshape(count, -1, rows.shape[-1])
     return lax.all_to_all(blocks, axes, split_axis=0, concat_axis=0, tiled=True).reshape(rows.shape)
+
+
+def plane(x):
+    return lax.all_to_all(x, FLAT, split_axis=0, concat_axis=0, tiled=True)
 
 
 def on_device(
@@ -529,8 +540,8 @@
     asked = exchange(spread(request_rows.reshape(1, SLOTS)), NODE, OWNERS)
     written = gru(touched, memory_base, messages[0], gru_input, gru_state)
     r1 = lax.ppermute(written, "y", [(0, 1), (1, 2), (2, 3)])
+    r2 = lax.ppermute(written, "y", [(0, 2), (1, 3)])
     r3 = lax.ppermute(written, "y", [(0, 3)])
-    r2 = lax.ppermute(r1, "y", [(1, 2), (2, 3)])
     up = upstream[0]
     written, late, chosen, chosen_t = lax.optimization_barrier(
         (written, delays[0], event_slots[0], event_slots[0].T)
@@ -540,37 +551,22 @@
     memory, rows = start_rows(seg, memory_base, written, r1, r2, r3, asked)
     rows, code = lax.optimization_barrier((rows, code))
     slots = exchange(rows, NODE, OWNERS)
-    time_k, time_v, d_att = project(code, attn_weights, up)
+    time_kv = project(code, attn_weights)
     embedded, d_slots, mine, other = attend(
-        core, slots, chosen, chosen_t, time_k, time_v, code_t, d_att, up, attn_weights
+        core, slots, chosen, chosen_t, time_kv, code_t, up, attn_weights
     )
     swap = [(0, 1), (1, 0)]
-
-    def turn(x):
-        return [
-            lax.ppermute(x, "y", [(i, (i + s) % SEG) for i in range(SEG)]) for s in range(1, SEG)
-        ]
-
-    def plane(x):
-        return lax.all_to_all(x, FLAT, split_axis=0, concat_axis=0, tiled=True)
-
-    a, b0, *bs = pair_sum(seg, mine, lax.ppermute(other, "core", swap))
-    bs = [
-        lax.ppermute(b, "y", [(i, (i + s) % SEG) for i in range(SEG)])
-        for s, b in enumerate(bs, start=1)
-    ]
-    part, pack = first_sum(plane(a), [b0] + bs, d_slots)
-    a, b, keep, give = second_sum(seg, core, plane(pack), part, turn(part))
-    b = plane(b)
-    a, b = lax.optimization_barrier((a, b))
-    turned = turn(b)
-    a = plane(a)
-    a, b, *turned = lax.optimization_barrier((a, b, *turned))
-    a_far = lax.ppermute(a, "core", swap)
-    b = join(seg, [b] + turned)
-    b_far = lax.ppermute(b, "core", swap)
-    memory_grad = owner_sum(core, asked, keep, lax.ppermute(give, "core", swap))
-    weight_grad = whole_grad(core, a, b, a_far, b_far)
+    partner = lax.ppermute(other, "core", swap)
+    parts = plane(pair_sum(mine, partner, d_slots))
+    part, keep, give = plane_sum(core, parts)
+    got = lax.ppermute(give, "core", swap)
+    part = swap_sum(part, lax.ppermute(part, "y", [(0, 1), (1, 0), (2, 3), (3, 2)]))
+    turned = lax.ppermute(part, "y", [(0, 3), (3, 0), (1, 2), (2, 1)])
+    memory_grad = owner_sum(core, asked, keep, got)
+    part, turned, memory_grad = lax.optimization_barrier((part, turned, memory_grad))
+    half = plane(seg_sum(part, turned))
+    far = lax.ppermute(half, "core", swap)
+    weight_grad = whole_grad(core, far, whole_grad(core, half))
     return embedded[None], memory[None], memory_grad[None], weight_grad.reshape(4, DM, DM)
 
 

time: 142 us -> 124 us (0.87)
  starting transfers between devices: 62.4 us -> 31 us
  blocking collectives: 11.9 us -> 41.1 us
  local copies, waits for them, and re-layouts: 15.1 us -> 0.94 us
  waiting for transfers between devices: 22.4 us -> 12.4 us
  Pallas kernels: 28.8 us -> 37.2 us
    all_to_all x1 -> x2, blocking collectives: 11.9 us -> 41.1 us  [plane(): return lax.all_to_all(x, FLAT, split_axis=0, concat_axis=0, tiled=True)]
    all_to_all x3 -> x0, starting transfers between devices: 16.5 us -> none  [plane(): return lax.all_to_all(x, FLAT, split_axis=0, concat_axis=0, tiled=True)]
    ppermute x14 -> x6, starting transfers between devices: 22.4 us -> 6.58 us  [the longest x1 3.08 us: on_device(): far = lax.ppermute(half, 'core', swap)]
    unnamed x36 -> x14, local copies, waits for them, and re-layouts: 15 us -> 0.82 us
    ppermute x14 -> x6, waiting for transfers between devices: 17.2 us -> 9.76 us  [the longest x1 3.65 us: on_device(): lax.ppermute(part, 'y', [(0, 1), (1, 0), (2, 3), (3, 2)])]
    pallas_call x1, Pallas kernels: 8.31 us -> 12.3 us  [attend(): pl.pallas_call(attend_kernel, in_specs=[pl.BlockSpec(memory_space=pltpu.S...]
    ppermute x1, starting transfers between devices: 2.73 us -> 5.61 us  [on_device(): r3 = lax.ppermute(written, 'y', [(0, 3)])]
    ppermute x1, waiting for transfers between devices: 2.52 us -> 0.01 us  [on_device(): r1 = lax.ppermute(written, 'y', [(0, 1), (1, 2), (2, 3)])]
  transfers between devices with their start and end apart: 21 -> 10, of which waited for: 12 -> 6; matrix products, arithmetic and copies ran while one was open for 0% -> 1% of each run, Pallas kernels for 7% -> 14%
where the time goes in v2:
time: 124 us
  blocking collectives  41.1 us (33%)
  Pallas kernels  37.2 us (30%)
  starting transfers between devices  31 us (25%)
  waiting for transfers between devices  12.4 us (10%)
    all_to_all x2, blocking collectives, plane(): return lax.all_to_all(x, FLAT, split_axis=0, concat_axis=0, tiled=True)  41.1 us
    all_to_all x2, starting transfers between devices, exchange(): lax.all_to_all(blocks, axes, split_axis=0, concat_axis=0, tiled=True)  16.3 us
    pallas_call x1, Pallas kernels, attend(): pl.pallas_call(attend_kernel, in_specs=[pl.BlockSpec(memory_space=pltpu.S...  12.3 us
    pallas_call x1, Pallas kernels, time_code(): pl.pallas_call(code_kernel, grid=(K,), in_specs=[pl.BlockSpec((E, K), lam...  6.65 us
    pallas_call x1, Pallas kernels, project(): pl.pallas_call(project_kernel, grid=(TILES, 2), in_specs=[pl.BlockSpec((1...  6.41 us
    ppermute x1, starting transfers between devices, on_device(): r3 = lax.ppermute(written, 'y', [(0, 3)])  5.61 us
    pallas_call x1, Pallas kernels, gru(): pl.pallas_call(gru_kernel, in_specs=[whole] * 3 + [far] * 2, out_specs=wh...  4.41 us
    pallas_call x2, Pallas kernels, whole_grad(): pl.pallas_call(own_kernel if own else far_kernel, grid_spec=pltpu.Prefetc...  3.66 us
  transfers between devices with their start and end apart: 10, of which 6 were waited for; matrix products, arithmetic and copies ran while one was open for 1% of the time, Pallas kernels for 14%

profile of v2, /device:TPU:1, one launch (start us, length us, event | category | flops | bytes accessed | tf_op | source)
XLA Modules:
  0.0 123.5 jit_solution(4945383581081688482)
XLA Ops:
  0.6 0.0 copy-start.2
  0.6 0.0 copy-start.4
  0.7 0.0 copy-start.5
  0.7 4.4 %gru.1.written = bf16[256,512]{1,0:T(8,128)(2,1)} custom-call(s32[1,256]{1,0:T(1,128)} %touched.1, bf16[256,512]{1,0:T(8,128)(2,1)} %state.3, bf16[256,512]{1,0:T(8,128)(2,1)} %bitcast.33, bf16[512,1536]{1,0:T(8,128)(2,1)} %w_input.1, bf16[512,1536]{1,0:T(8,128)(2,1)} %w_state.1), custom_call_target="tpu_custom_call" | custom-call | flops 805306368 | bytes 4194304 | tf_op jit(solution)/shard_map/gru/pallas_call | solution.py:89
  5.1 0.0 copy-start
  5.1 0.0 copy-start.1
  5.1 5.6 %collective-permute-start.2 = (bf16[256,512]{1,0:T(8,128)(2,1)}, bf16[256,512]{1,0:T(8,128)(2,1)S(1)}, u32[]{:S(2)}, u32[]{:S(2)}) collective-permute-start(bf16[256,512]{1,0:T(8,128)(2,1)} %gru.1.written), channel_id=1, source_target_pairs={{0,96},{1,97},{2,98},{3,99},{4,100},{5,101},{6,102},{7,103},{8,104... | collective-permute-start | bytes 786440 | tf_op jit(solution)/shard_map/ppermute | solution.py:544
  10.7 1.3 %collective-permute-start.1 = (bf16[256,512]{1,0:T(8,128)(2,1)}, bf16[256,512]{1,0:T(8,128)(2,1)S(1)}, u32[]{:S(2)}, u32[]{:S(2)}) collective-permute-start(bf16[256,512]{1,0:T(8,128)(2,1)} %gru.1.written), channel_id=1, source_target_pairs={{0,64},{32,96},{1,65},{33,97},{2,66},{34,98},{3,67},{35,99},{4,68}... | collective-permute-start | bytes 786440 | tf_op jit(solution)/shard_map/ppermute | solution.py:543
  12.0 2.5 %collective-permute-start = (bf16[256,512]{1,0:T(8,128)(2,1)}, bf16[256,512]{1,0:T(8,128)(2,1)S(1)}, u32[]{:S(2)}, u32[]{:S(2)}) collective-permute-start(bf16[256,512]{1,0:T(8,128)(2,1)} %gru.1.written), channel_id=1, source_target_pairs={{0,32},{32,64},{64,96},{1,33},{33,65},{65,97},{2,34},{34,66},{66,9... | collective-permute-start | bytes 786440 | tf_op jit(solution)/shard_map/ppermute | solution.py:542
  14.5 0.0 copy-done.2
  14.5 0.8 spread.1
  15.3 9.2 %all-to-all-start = ((s32[32,8,128]{2,1,0:T(8,128)}), s32[32,8,128]{2,1,0:T(8,128)S(1)}, u32[]{:S(2)}, u32[]{:S(2)}) async-start(s32[32,8,128]{2,1,0:T(8,128)} %bitcast.7), calls=%async_computation | async-start | bytes 262144 | tf_op jit(solution)/shard_map/all_to_all | solution.py:518
  24.5 0.0 copy-done.4
  24.5 0.0 copy-done.5
  24.5 0.8 copy.16
  25.3 6.6 %time_code.1 = (bf16[2,8,128,512]{3,2,1,0:T(8,128)(2,1)}, bf16[2,512,1024]{2,1,0:T(8,128)(2,1)}) custom-call(s32[256,8]{1,0:T(8,128)} %bitcast.34, f32[1,512]{1,0:T(1,128)} %bitcast.36), custom_call_target="tpu_custom_call" | custom-call | flops 20971520 | bytes 4194304 | tf_op jit(solution)/shard_map/time_code/pallas_call | solution.py:127
  32.0 0.2 all-to-all-done
  32.2 0.0 collective-permute-done.2.r3
  32.2 0.0 collective-permute-done.1.r2
  32.2 0.0 collective-permute-done.r1
  32.2 0.0 copy-done
  32.2 0.0 copy-done.1
  32.2 1.2 %start_rows.1 = (bf16[256,512]{1,0:T(8,128)(2,1)}, bf16[256,512]{1,0:T(8,128)(2,1)}) custom-call(s32[1]{0:T(128)} %bitcast.1.seg, bf16[256,512]{1,0:T(8,128)(2,1)S(1)} %copy-done, bf16[256,512]{1,0:T(8,128)(2,1)S(1)} %copy-done.1, bf16[256,512]{1,0:T(8,128)(2,1)S(1)} %collective-permute-done.r1, bf16[256,512]{1,0:T(8,128)(2,1)S(1)} %collective-permute-done.1.r2, ...), custom_call_target="tpu_custom_call" | custom-call | flops 67108864 | bytes 2097152 | tf_op jit(solution)/shard_map/start_rows/pallas_call | solution.py:192
  33.5 7.2 %all-to-all-start.1 = ((bf16[32,8,512]{2,1,0:T(8,128)(2,1)}), bf16[32,8,512]{2,1,0:T(8,128)(2,1)S(1)}, u32[]{:S(2)}, u32[]{:S(2)}) async-start(bf16[32,8,512]{2,1,0:T(8,128)(2,1)} %bitcast.9), calls=%async_computation.1 | async-start | bytes 524288 | tf_op jit(solution)/shard_map/all_to_all | solution.py:518
  40.7 0.1 copy.17.chosen
  40.8 0.0 copy-start.3
  40.8 6.4 %time_projections.1.time_kv = bf16[2,8,128,1024]{3,2,1,0:T(8,128)(2,1)} custom-call(bf16[2,8,128,512]{3,2,1,0:T(8,128)(2,1)} %get-tuple-element.37.code, bf16[4,512,512]{2,1,0:T(8,128)(2,1)} %w.3), custom_call_target="tpu_custom_call" | custom-call | flops 2147483648 | bytes 8388608 | tf_op jit(solution)/shard_map/time_projections/pallas_call | solution.py:158
  47.2 2.4 %all-to-all-done.1 = bf16[32,8,512]{2,1,0:T(8,128)(2,1)S(1)} async-done(((bf16[32,8,512]{2,1,0:T(8,128)(2,1)}), bf16[32,8,512]{2,1,0:T(8,128)(2,1)S(1)}, u32[]{:S(2)}, u32[]{:S(2)}) %all-to-all-start.1) | async-done | bytes 262176 | tf_op jit(solution)/shard_map/all_to_all | solution.py:518
  49.6 0.0 copy-done.3
  49.6 12.3 %attend.1 = (bf16[256,512]{1,0:T(8,128)(2,1)}, bf16[256,512]{1,0:T(8,128)(2,1)S(1)}, bf16[16,64,512]{2,1,0:T(8,128)(2,1)S(1)}, bf16[16,64,512]{2,1,0:T(8,128)(2,1)S(1)}) custom-call(s32[1]{0:T(128)} %bitcast.core, bf16[256,512]{1,0:T(8,128)(2,1)S(1)} %bitcast.26, s32[256,9]{1,0:T(8,128)S(1)} %copy.17.chosen, s32[9,256]{1,0:T(8,128)S(1)} %bitcast.28, ...), custom_call_target="tpu_custom_call" | custom-call | flops 6442450944 | bytes 14680064 | tf_op jit(solution)/shard_map/attend/pallas_call | solution.py:328
  61.9 0.3 collective-permute-start.3
  62.2 2.5 %collective-permute-done.3.b = bf16[16,64,512]{2,1,0:T(8,128)(2,1)S(1)} collective-permute-done((bf16[16,64,512]{2,1,0:T(8,128)(2,1)S(1)}, bf16[16,64,512]{2,1,0:T(8,128)(2,1)S(1)}, u32[]{:S(2)}, u32[]{:S(2)}) %collective-permute-start.3) | collective-permute-done | bytes 1048608 | tf_op jit(solution)/shard_map/ppermute | solution.py:559
  64.7 0.3 pair_sum.1
  65.0 23.0 %all_to_all.20.a = bf16[16,80,512]{2,1,0:T(8,128)(2,1)S(1)} all-to-all(bf16[16,80,512]{2,1,0:T(8,128)(2,1)S(1)} %pair_sum.1), channel_id=1, replica_groups=mesh['y'=4,'x'=4,'z'=4,'core'=2] {'x','z'}, dimensions={0} | all-to-all | bytes 2621440 | tf_op jit(solution)/shard_map/all_to_all | solution.py:522
  88.0 0.2 plane_sum.1
  88.2 1.9 %collective-permute-start.6 = (bf16[128,512]{1,0:T(8,128)(2,1)S(1)}, bf16[128,512]{1,0:T(8,128)(2,1)S(1)}, u32[]{:S(2)}, u32[]{:S(2)}) collective-permute-start(bf16[128,512]{1,0:T(8,128)(2,1)S(1)} %get-tuple-element.46), channel_id=1, source_target_pairs={{0,1},{1,0},{2,3},{3,2},{4,5},{5,4},{6,7},{7,6},{8,9},{9,8},{10,11... | collective-permute-start | bytes 393224 | tf_op jit(solution)/shard_map/ppermute | solution.py:562
  90.0 0.0 collective-permute-start.4
  90.0 3.6 %collective-permute-done.4.b = bf16[64,512]{1,0:T(8,128)(2,1)S(1)} collective-permute-done((bf16[64,512]{1,0:T(8,128)(2,1)S(1)}, bf16[64,512]{1,0:T(8,128)(2,1)S(1)}, u32[]{:S(2)}, u32[]{:S(2)}) %collective-permute-start.4) | collective-permute-done | bytes 65568 | tf_op jit(solution)/shard_map/ppermute | solution.py:563
  93.7 0.1 collective-permute-start.5
  93.8 0.0 collective-permute-done.6.got
  93.8 1.1 owner_sum.1
  94.9 3.2 %collective-permute-done.5.b = bf16[64,512]{1,0:T(8,128)(2,1)S(1)} collective-permute-done((bf16[64,512]{1,0:T(8,128)(2,1)S(1)}, bf16[64,512]{1,0:T(8,128)(2,1)S(1)}, u32[]{:S(2)}, u32[]{:S(2)}) %collective-permute-start.5) | collective-permute-done | bytes 65568 | tf_op jit(solution)/shard_map/ppermute | solution.py:564
  98.1 0.1 seg_sum.1
  98.2 18.1 %all_to_all.21.half = bf16[16,64,512]{2,1,0:T(8,128)(2,1)S(1)} all-to-all(bf16[16,64,512]{2,1,0:T(8,128)(2,1)S(1)} %seg_sum.1), channel_id=1, replica_groups=mesh['y'=4,'x'=4,'z'=4,'core'=2] {'x','z'}, dimensions={0} | all-to-all | bytes 2097152 | tf_op jit(solution)/shard_map/all_to_all | solution.py:522
  116.3 3.1 %collective-permute-start.7 = (bf16[16,64,512]{2,1,0:T(8,128)(2,1)S(1)}, bf16[16,64,512]{2,1,0:T(8,128)(2,1)S(1)}, u32[]{:S(2)}, u32[]{:S(2)}) collective-permute-start(bf16[16,64,512]{2,1,0:T(8,128)(2,1)S(1)} %all_to_all.21.half), channel_id=1, source_target_pairs={{0,1},{1,0},{2,3},{3,2},{4,5},{5,4},{6,7},{7,6},{8,9},{9,8},{10,11... | collective-permute-start | bytes 3145736 | tf_op jit(solution)/shard_map/ppermute | solution.py:568
  119.4 1.8 %own_half.1.before = f32[16,2,64,512]{3,2,1,0:T(8,128)} custom-call(s32[1]{0:T(128)} %bitcast.core, bf16[16,64,512]{2,1,0:T(8,128)(2,1)S(1)} %all_to_all.21.half), custom_call_target="tpu_custom_call" | custom-call | flops 262144 | bytes 3145728 | tf_op jit(solution)/shard_map/own_half/pallas_call | solution.py:462
  121.2 0.5 collective-permute-done.7.half
  121.7 1.8 %far_half.1 = f32[16,2,64,512]{3,2,1,0:T(8,128)} custom-call(s32[1]{0:T(128)} %bitcast.core, bf16[16,64,512]{2,1,0:T(8,128)(2,1)S(1)} %collective-permute-done.7.half, f32[16,2,64,512]{3,2,1,0:T(8,128)} %own_half.1.before), custom_call_target="tpu_custom_call", output_to_operand_aliasing={{}: (2, {})} | custom-call | flops 262144 | bytes 3145728 | tf_op jit(solution)/shard_map/far_half/pallas_call | solution.py:462
  (2 shorter events, 0.0 us)
Async XLA Ops:
  0.6 13.9 %copy-start.2 = (s32[1,1,256]{2,1,0:T(1,128)S(1)}, s32[1,1,256]{2,1,0:T(1,128)}, u32[]{:S(2)}) copy-start(s32[1,1,256]{2,1,0:T(1,128)} %param.18) | copy-start | bytes 3076
  0.6 23.8 %copy-start.4 = (s32[1,256,9]{1,0,2:T(1,128)S(1)}, s32[1,256,9]{1,0,2:T(1,128)}, u32[]{:S(2)}) copy-start(s32[1,256,9]{1,0,2:T(1,128)} %param.19) | copy-start | bytes 27652
  0.7 23.9 %copy-start.5 = (s32[1,256,8]{1,2,0:T(8,128)S(1)}, s32[1,256,8]{1,2,0:T(8,128)}, u32[]{:S(2)}) copy-start(s32[1,256,8]{1,2,0:T(8,128)} %param.20) | copy-start | bytes 24580
  5.1 27.1 %copy-start = (bf16[256,512]{1,0:T(8,128)(2,1)S(1)}, bf16[256,512]{1,0:T(8,128)(2,1)}, u32[]{:S(2)}) copy-start(bf16[256,512]{1,0:T(8,128)(2,1)} %state.3) | copy-start | bytes 786436
  5.1 27.1 %copy-start.1 = (bf16[256,512]{1,0:T(8,128)(2,1)S(1)}, bf16[256,512]{1,0:T(8,128)(2,1)}, u32[]{:S(2)}) copy-start(bf16[256,512]{1,0:T(8,128)(2,1)} %gru.1.written) | copy-start | bytes 786436
  5.1 27.1 %collective-permute-start.2 = (bf16[256,512]{1,0:T(8,128)(2,1)}, bf16[256,512]{1,0:T(8,128)(2,1)S(1)}, u32[]{:S(2)}, u32[]{:S(2)}) collective-permute-start(bf16[256,512]{1,0:T(8,128)(2,1)} %gru.1.written), channel_id=1, source_target_pairs={{0,96},{1,97},{2,98},{3,99},{4,100},{5,101},{6,102},{7,103},{8,104... | collective-permute-start | bytes 786440 | tf_op jit(solution)/shard_map/ppermute | solution.py:544
  10.7 21.5 %collective-permute-start.1 = (bf16[256,512]{1,0:T(8,128)(2,1)}, bf16[256,512]{1,0:T(8,128)(2,1)S(1)}, u32[]{:S(2)}, u32[]{:S(2)}) collective-permute-start(bf16[256,512]{1,0:T(8,128)(2,1)} %gru.1.written), channel_id=1, source_target_pairs={{0,64},{32,96},{1,65},{33,97},{2,66},{34,98},{3,67},{35,99},{4,68}... | collective-permute-start | bytes 786440 | tf_op jit(solution)/shard_map/ppermute | solution.py:543
  12.0 20.2 %collective-permute-start = (bf16[256,512]{1,0:T(8,128)(2,1)}, bf16[256,512]{1,0:T(8,128)(2,1)S(1)}, u32[]{:S(2)}, u32[]{:S(2)}) collective-permute-start(bf16[256,512]{1,0:T(8,128)(2,1)} %gru.1.written), channel_id=1, source_target_pairs={{0,32},{32,64},{64,96},{1,33},{33,65},{65,97},{2,34},{34,66},{66,9... | collective-permute-start | bytes 786440 | tf_op jit(solution)/shard_map/ppermute | solution.py:542
  15.3 16.9 %all-to-all-start = ((s32[32,8,128]{2,1,0:T(8,128)}), s32[32,8,128]{2,1,0:T(8,128)S(1)}, u32[]{:S(2)}, u32[]{:S(2)}) async-start(s32[32,8,128]{2,1,0:T(8,128)} %bitcast.7), calls=%async_computation | async-start | bytes 262144 | tf_op jit(solution)/shard_map/all_to_all | solution.py:518
  33.5 16.2 %all-to-all-start.1 = ((bf16[32,8,512]{2,1,0:T(8,128)(2,1)}), bf16[32,8,512]{2,1,0:T(8,128)(2,1)S(1)}, u32[]{:S(2)}, u32[]{:S(2)}) async-start(bf16[32,8,512]{2,1,0:T(8,128)(2,1)} %bitcast.9), calls=%async_computation.1 | async-start | bytes 524288 | tf_op jit(solution)/shard_map/all_to_all | solution.py:518
  40.8 8.9 %copy-start.3 = (bf16[1,256,512]{2,1,0:T(8,128)(2,1)S(1)}, bf16[1,256,512]{2,1,0:T(8,128)(2,1)}, u32[]{:S(2)}) copy-start(bf16[1,256,512]{2,1,0:T(8,128)(2,1)} %param.21) | copy-start | bytes 786436
  61.9 2.7 %collective-permute-start.3 = (bf16[16,64,512]{2,1,0:T(8,128)(2,1)S(1)}, bf16[16,64,512]{2,1,0:T(8,128)(2,1)S(1)}, u32[]{:S(2)}, u32[]{:S(2)}) collective-permute-start(bf16[16,64,512]{2,1,0:T(8,128)(2,1)S(1)} %get-tuple-element.42), channel_id=1, source_target_pairs={{0,1},{1,0},{2,3},{3,2},{4,5},{5,4},{6,7},{7,6},{8,9},{9,8},{10,11... | collective-permute-start | bytes 3145736 | tf_op jit(solution)/shard_map/ppermute | solution.py:559
  88.2 5.6 %collective-permute-start.6 = (bf16[128,512]{1,0:T(8,128)(2,1)S(1)}, bf16[128,512]{1,0:T(8,128)(2,1)S(1)}, u32[]{:S(2)}, u32[]{:S(2)}) collective-permute-start(bf16[128,512]{1,0:T(8,128)(2,1)S(1)} %get-tuple-element.46), channel_id=1, source_target_pairs={{0,1},{1,0},{2,3},{3,2},{4,5},{5,4},{6,7},{7,6},{8,9},{9,8},{10,11... | collective-permute-start | bytes 393224 | tf_op jit(solution)/shard_map/ppermute | solution.py:562
  90.0 3.6 %collective-permute-start.4 = (bf16[64,512]{1,0:T(8,128)(2,1)S(1)}, bf16[64,512]{1,0:T(8,128)(2,1)S(1)}, u32[]{:S(2)}, u32[]{:S(2)}) collective-permute-start(bf16[64,512]{1,0:T(8,128)(2,1)S(1)} %get-tuple-element.44.a), channel_id=1, source_target_pairs={{0,32},{32,0},{64,96},{96,64},{1,33},{33,1},{65,97},{97,65},{2,34}... | collective-permute-start | bytes 196616 | tf_op jit(solution)/shard_map/ppermute | solution.py:563
  93.7 4.4 %collective-permute-start.5 = (bf16[64,512]{1,0:T(8,128)(2,1)S(1)}, bf16[64,512]{1,0:T(8,128)(2,1)S(1)}, u32[]{:S(2)}, u32[]{:S(2)}) collective-permute-start(bf16[64,512]{1,0:T(8,128)(2,1)S(1)} %swap_sum.1.a), channel_id=1, source_target_pairs={{0,96},{96,0},{32,64},{64,32},{1,97},{97,1},{33,65},{65,33},{2,98}... | collective-permute-start | bytes 196616 | tf_op jit(solution)/shard_map/ppermute | solution.py:564
  116.3 5.4 %collective-permute-start.7 = (bf16[16,64,512]{2,1,0:T(8,128)(2,1)S(1)}, bf16[16,64,512]{2,1,0:T(8,128)(2,1)S(1)}, u32[]{:S(2)}, u32[]{:S(2)}) collective-permute-start(bf16[16,64,512]{2,1,0:T(8,128)(2,1)S(1)} %all_to_all.21.half), channel_id=1, source_target_pairs={{0,1},{1,0},{2,3},{3,2},{4,5},{5,4},{6,7},{7,6},{8,9},{9,8},{10,11... | collective-permute-start | bytes 3145736 | tf_op jit(solution)/shard_map/ppermute | solution.py:568

commit v3 on v2

--- a/solution.py
+++ b/solution.py
@@ -64,18 +64,22 @@
     return jnp.sum(square, axis=1, keepdims=True)
 
 
-def gru_kernel(touched, state, message, w_input, w_state, out, wi, ws, sem):
-    copies = [
-        pltpu.make_async_copy(w_state, ws, sem.at[0]),
-        pltpu.make_async_copy(w_input, wi, sem.at[1]),
-    ]
+def gru_kernel(
+    touched, ids, state, message, w_input, w_state, out, spread, st, ms, wi, ws, sem
+):
+    moves = ((state, st), (w_state, ws), (message, ms), (w_input, wi))
+    copies = [pltpu.make_async_copy(a, b, sem.at[i]) for i, (a, b) in enumerate(moves)]
     for copy in copies:
         copy.start()
     keep = column(touched[...]) > 0.5
-    m, s = message[...], state[...]
+    spread[...] = jnp.broadcast_to(column(ids[...]), (SLOTS, 128)).astype(jnp.int32)
     copies[0].wait()
+    copies[1].wait()
+    s = st[...]
     from_state = [dot(s, ws[:, i * DM : (i + 1) * DM]) for i in range(3)]
-    copies[1].wait()
+    copies[2].wait()
+    copies[3].wait()
+    m = ms[...]
     update = jax.nn.sigmoid(dot(m, wi[:, :DM]) + from_state[0])
     reset = jax.nn.sigmoid(dot(m, wi[:, DM : 2 * DM]) + from_state[1])
     candidate = jnp.tanh(dot(m, wi[:, 2 * DM :]) + reset * from_state[2])
@@ -83,93 +87,80 @@
     out[...] = jnp.where(keep, fresh, ABSENT).astype(BF)
 
 
-def gru(touched, state, message, w_input, w_state):
+def gru(touched, ids, state, message, w_input, w_state):
     whole = pl.BlockSpec(memory_space=pltpu.VMEM)
     far = pl.BlockSpec(memory_space=pl.ANY)
     return pl.pallas_call(
         gru_kernel,
-        in_specs=[whole] * 3 + [far] * 2,
-        out_specs=whole,
-        out_shape=jax.ShapeDtypeStruct((N, DM), BF),
+        in_specs=[whole] * 2 + [far] * 4,
+        out_specs=[whole] * 2,
+        out_shape=[
+            jax.ShapeDtypeStruct((N, DM), BF),
+            jax.ShapeDtypeStruct((SLOTS, 128), jnp.int32),
+        ],
         scratch_shapes=[
+            pltpu.VMEM((N, DM), BF),
+            pltpu.VMEM((N, DM), BF),
             pltpu.VMEM((DM, 3 * DM), BF),
             pltpu.VMEM((DM, 3 * DM), BF),
-            pltpu.SemaphoreType.DMA((2,)),
+            pltpu.SemaphoreType.DMA((4,)),
         ],
         compiler_params=pltpu.CompilerParams(vmem_limit_bytes=56 << 20),
         cost_estimate=pl.CostEstimate(
             flops=4 * N * DM * 3 * DM, bytes_accessed=4 << 20, transcendentals=3 * N * DM
         ),
         name="gru",
-    )(touched, state, message, w_input, w_state)
-
-
-def code_kernel(delays, frequency, code, code_t):
-    k = pl.program_id(0)
+    )(touched, ids, state, message, w_input, w_state)
+
+
+def time_kernel(tile, delays, frequency, w_key, w_value, code_t, time_kv):
+    g = pl.program_id(0)
     turns = frequency[...] * (1.0 / (2.0 * math.pi))
     high = jnp.round(turns * 16384.0) * (1.0 / 16384.0)
     low = turns - high
-    lane = iota((E, K), 1)
-    delay = jnp.sum(jnp.where(lane == k, delays[...].astype(F32), 0.0), axis=1, keepdims=True)
-    coarse = delay * high
-    part = (coarse - jnp.round(coarse)) + delay * low
-    u = part * part
-    wave = jnp.full_like(u, COS[-1])
-    for c in COS[-2::-1]:
-        wave = wave * u + c
-    wave_b = wave.astype(BF)
-    for i in range(TILES):
-        code[i, 0] = wave_b[i * TILE : (i + 1) * TILE]
-        code_t[i] = wave[i * TILE : (i + 1) * TILE].T.astype(BF)
-
-
-def time_code(delays, frequency):
-    return pl.pallas_call(
-        code_kernel,
-        grid=(K,),
+    waves = []
+    for i in range(2):
+        block = delays[:, tile * TILE : (tile + 1) * TILE].astype(F32)
+        here = iota((K, TILE), 0) == 2 * g + i
+        delay = column(jnp.sum(jnp.where(here, block, 0.0), axis=0, keepdims=True))
+        coarse = delay * high
+        part = (coarse - jnp.round(coarse)) + delay * low
+        u = part * part
+        wave = jnp.full_like(u, COS[-1])
+        for c in COS[-2::-1]:
+            wave = wave * u + c
+        waves.append(wave)
+    wave = jnp.concatenate(waves, axis=0)
+    code_t[0] = wave.T.astype(BF)
+    wave = wave.astype(BF)
+    time_kv[:, :DM] = dot(wave, w_key[0]).astype(BF)
+    time_kv[:, DM:] = dot(wave, w_value[0]).astype(BF)
+
+
+def time_tile(tile, delays, frequency, weights):
+    return pl.pallas_call(
+        functools.partial(time_kernel, tile),
+        grid=(K // 2,),
         in_specs=[
-            pl.BlockSpec((E, K), lambda k: (0, 0)),
-            pl.BlockSpec((1, DM), lambda k: (0, 0)),
+            pl.BlockSpec((K, E), lambda g: (0, 0)),
+            pl.BlockSpec((1, DM), lambda g: (0, 0)),
+            pl.BlockSpec((1, DM, DM), lambda g: (1, 0, 0)),
+            pl.BlockSpec((1, DM, DM), lambda g: (2, 0, 0)),
         ],
         out_specs=[
-            pl.BlockSpec((TILES, 1, TILE, DM), lambda k: (0, k, 0, 0)),
-            pl.BlockSpec((TILES, DM, TILE), lambda k: (0, 0, k)),
+            pl.BlockSpec((1, DM, 2 * TILE), lambda g: (g, 0, 0)),
+            pl.BlockSpec((2 * TILE, 2 * DM), lambda g: (g, 0)),
         ],
         out_shape=[
-            jax.ShapeDtypeStruct((TILES, K, TILE, DM), BF),
-            jax.ShapeDtypeStruct((TILES, DM, ROWS), BF),
+            jax.ShapeDtypeStruct((K // 2, DM, 2 * TILE), BF),
+            jax.ShapeDtypeStruct((ROWS, 2 * DM), BF),
         ],
         compiler_params=pltpu.CompilerParams(vmem_limit_bytes=56 << 20),
         cost_estimate=pl.CostEstimate(
-            flops=20 * K * E * DM, bytes_accessed=4 << 20, transcendentals=K * E * DM
+            flops=4 * ROWS * DM * DM, bytes_accessed=5 << 20, transcendentals=ROWS * DM
         ),
-        name="time_code",
-    )(delays, frequency)
-
-
-def project_kernel(code, w, time_kv):
-    rows = code[0].reshape(K // 2 * TILE, DM)
-    for i in range(2):
-        part = dot(rows, w[1 + i]).astype(BF).reshape(K // 2, TILE, DM)
-        time_kv[0, :, :, i * DM : (i + 1) * DM] = part
-
-
-def project(code, weights):
-    return pl.pallas_call(
-        project_kernel,
-        grid=(TILES, 2),
-        in_specs=[
-            pl.BlockSpec((1, K // 2, TILE, DM), lambda i, j: (i, j, 0, 0)),
-            pl.BlockSpec((4, DM, DM), lambda i, j: (0, 0, 0)),
-        ],
-        out_specs=pl.BlockSpec((1, K // 2, TILE, 2 * DM), lambda i, j: (i, j, 0, 0)),
-        out_shape=jax.ShapeDtypeStruct((TILES, K, TILE, 2 * DM), BF),
-        compiler_params=pltpu.CompilerParams(vmem_limit_bytes=56 << 20),
-        cost_estimate=pl.CostEstimate(
-            flops=4 * K * E * DM * DM, bytes_accessed=8 << 20, transcendentals=0
-        ),
-        name="time_projections",
-    )(code, weights)
+        name="time_tile",
+    )(delays, frequency, weights, weights)
 
 
 def owner_pick(asked):
@@ -206,13 +197,21 @@
 
 
 def attend_kernel(
-    core, slots, chosen, chosen_t, time_kv, time_t, up, w,
+    core, slots, chosen, chosen_t, kv0, t0, kv1, t1, up, w,
     embedded, d_slots, mine, other,
     tkv, tt, wq, sem, skv, d_att, qf, src, both, dkv, att, dq, sums,
 ):
-    moves = ((w, wq), (time_kv, tkv), (time_t, tt))
+    moves = (
+        (w.at[pl.ds(1, 2)], wq.at[pl.ds(1, 2)]),
+        (w.at[0], wq.at[0]),
+        (w.at[3], wq.at[3]),
+        (kv0, tkv.at[0]),
+        (kv1, tkv.at[1]),
+        (t0, tt.at[0]),
+        (t1, tt.at[1]),
+    )
     copies = [pltpu.make_async_copy(a, b, sem.at[i]) for i, (a, b) in enumerate(moves)]
-    for copy in copies:
+    for copy in copies[:4]:
         copy.start()
     rows = slots[...]
     pick = (chosen[:, 0:1] == iota((E, SLOTS), 1)).astype(F32).astype(BF)
@@ -220,9 +219,13 @@
     copies[0].wait()
     skv[:, :DM] = dot(rows, wq[1]).astype(BF)
     skv[:, DM:] = dot(rows, wq[2]).astype(BF)
+    for copy in copies[4:]:
+        copy.start()
+    copies[1].wait()
     qf[...] = dot(pick, dot(rows, wq[0]).astype(BF))
+    copies[2].wait()
     d_att[...] = dot_nt(up[...], wq[3])
-    copies[1].wait()
+    copies[3].wait()
 
     lane = iota((STEP, 128), 1)
     first = lane < K
@@ -253,9 +256,8 @@
             d_out = d_att[at, part]
             for k in range(K):
                 row = slice(k * TILE + j * STEP, k * TILE + (j + 1) * STEP)
-                local = slice(j * STEP, (j + 1) * STEP)
-                key = both[i, row, part] + tkv[i, k, local, part].astype(F32)
-                value = both[i, row, part_v] + tkv[i, k, local, part_v].astype(F32)
+                key = both[i, row, part] + tkv[i, row, part].astype(F32)
+                value = both[i, row, part_v] + tkv[i, row, part_v].astype(F32)
                 both[i, row, part] = key
                 both[i, row, part_v] = value
                 here = lane == h * K + k
@@ -288,10 +290,12 @@
     sub = iota((SLOTS, TILE), 0)
     s_kv = dot_t = None
     for i in range(TILES):
+        if i == 1:
+            copies[4].wait()
         for j in range(TILE // STEP):
             step(i, j)
-        if i == 0:
-            copies[2].wait()
+        copies[5 + i].wait()
+        code = jnp.concatenate([tt[i, g] for g in range(K // 2)], axis=1)
         spread = jnp.concatenate(
             [
                 (sub == chosen_t[1 + k : 2 + k, i * TILE : (i + 1) * TILE]).astype(F32)
@@ -299,7 +303,7 @@
             ],
             axis=1,
         ).astype(BF)
-        one, two = dot(spread, dkv[i]), dot(tt[i], dkv[i])
+        one, two = dot(spread, dkv[i]), dot(code, dkv[i])
         s_kv = one if i == 0 else s_kv + one
         dot_t = two if i == 0 else dot_t + two
     s_kv = s_kv.astype(BF)
@@ -322,14 +326,14 @@
     d_slots[...] = grads.astype(BF)
 
 
-def attend(core, slots, chosen, chosen_t, time_kv, time_t, up, weights):
+def attend(core, slots, chosen, chosen_t, times, up, weights):
     whole = pl.BlockSpec(memory_space=pltpu.VMEM)
     far = pl.BlockSpec(memory_space=pl.ANY)
     return pl.pallas_call(
         attend_kernel,
         in_specs=[pl.BlockSpec(memory_space=pltpu.SMEM)]
         + [whole] * 3
-        + [far] * 2
+        + [far] * 4
         + [whole]
         + [far],
         out_specs=[whole] * 4,
@@ -340,10 +344,10 @@
             jax.ShapeDtypeStruct((PLANE, PIECE, DM), BF),
         ],
         scratch_shapes=[
-            pltpu.VMEM((TILES, K, TILE, 2 * DM), BF),
-            pltpu.VMEM((TILES, DM, ROWS), BF),
+            pltpu.VMEM((TILES, ROWS, 2 * DM), BF),
+            pltpu.VMEM((TILES, K // 2, DM, 2 * TILE), BF),
             pltpu.VMEM((4, DM, DM), BF),
-            pltpu.SemaphoreType.DMA((3,)),
+            pltpu.SemaphoreType.DMA((7,)),
             pltpu.VMEM((SLOTS, 2 * DM), BF),
             pltpu.VMEM((E, DM), F32),
             pltpu.VMEM((E, DM), F32),
@@ -359,7 +363,7 @@
             flops=6 << 30, bytes_accessed=14 << 20, transcendentals=E * 128
         ),
         name="attend",
-    )(core, slots, chosen, chosen_t, time_kv, time_t, up, weights)
+    )(core, slots, chosen, chosen_t, *times, up, weights)
 
 
 def pair_kernel(a, b, d_slots, out):
@@ -385,7 +389,9 @@
     total = a[0, :PIECE].astype(F32)
     for i in range(1, PLANE):
         total += a[i, :PIECE].astype(F32)
-    part[...] = total.astype(BF)
+    total = total.astype(BF)
+    for i in range(SEG):
+        part[i] = total
     grads = a[:, PIECE:].astype(F32)
     low, high = grads[:, :CAP].reshape(SLOTS // 2, DM), grads[:, CAP:].reshape(SLOTS // 2, DM)
     first = core[0] == 0
@@ -400,96 +406,63 @@
         plane_kernel,
         in_specs=[pl.BlockSpec(memory_space=pltpu.SMEM), whole],
         out_specs=[whole] * 3,
-        out_shape=[jax.ShapeDtypeStruct((PIECE, DM), BF), half, half],
+        out_shape=[jax.ShapeDtypeStruct((SEG, PIECE, DM), BF), half, half],
         compiler_params=pltpu.CompilerParams(vmem_limit_bytes=16 << 20),
         cost_estimate=pl.CostEstimate(flops=1 << 19, bytes_accessed=2 << 20, transcendentals=0),
         name="plane_sum",
     )(core, a)
 
 
-def swap_kernel(a, b, out):
-    out[...] = (a[...].astype(F32) + b[...].astype(F32)).astype(BF)
-
-
-def swap_sum(a, b):
-    whole = pl.BlockSpec(memory_space=pltpu.VMEM)
-    return pl.pallas_call(
-        swap_kernel,
-        in_specs=[whole] * 2,
-        out_specs=whole,
-        out_shape=jax.ShapeDtypeStruct((PIECE, DM), BF),
-        compiler_params=pltpu.CompilerParams(vmem_limit_bytes=16 << 20),
-        cost_estimate=pl.CostEstimate(flops=1 << 15, bytes_accessed=1 << 17, transcendentals=0),
-        name="swap_sum",
-    )(a, b)
-
-
-def seg_kernel(a, b, out):
-    total = (a[...].astype(F32) + b[...].astype(F32)).astype(BF)
+def seg_kernel(parts, out):
+    total = (parts[0].astype(F32) + parts[1].astype(F32)) + (
+        parts[2].astype(F32) + parts[3].astype(F32)
+    )
+    total = total.astype(BF)
     for i in range(PLANE):
         out[i] = total
 
 
-def seg_sum(a, b):
+def seg_sum(parts):
     whole = pl.BlockSpec(memory_space=pltpu.VMEM)
     return pl.pallas_call(
         seg_kernel,
-        in_specs=[whole] * 2,
+        in_specs=[whole],
         out_specs=whole,
         out_shape=jax.ShapeDtypeStruct((PLANE, PIECE, DM), BF),
         compiler_params=pltpu.CompilerParams(vmem_limit_bytes=16 << 20),
-        cost_estimate=pl.CostEstimate(flops=1 << 15, bytes_accessed=1 << 20, transcendentals=0),
+        cost_estimate=pl.CostEstimate(flops=1 << 17, bytes_accessed=1 << 20, transcendentals=0),
         name="seg_sum",
-    )(a, b)
-
-
-def own_kernel(core, half, out):
-    out[:, 0] = half[...].astype(F32)
-
-
-def far_kernel(core, half, before, out):
-    out[:, 0] = half[...].astype(F32)
+    )(parts)
+
+
+def half_kernel(own, core, half, *rest):
+    out, wide, sem = rest[-3:]
+    place = core[0] if own else 1 - core[0]
+    copies = []
+    for i in range(4):
+        at = pl.ds(i * PLANE // 4, PLANE // 4)
+        wide[at] = half[at].astype(F32)
+        copies.append(pltpu.make_async_copy(wide.at[at], out.at[at, place], sem.at[i]))
+        copies[-1].start()
+    for copy in copies:
+        copy.wait()
 
 
 def whole_grad(core, half, before=None):
     own = before is None
-
-    def place(i, core):
-        return (i, core[0] if own else 1 - core[0], 0, 0)
-
-    spec = pl.BlockSpec((4, PIECE, DM), lambda i, core: (i, 0, 0))
     far = pl.BlockSpec(memory_space=pl.ANY)
     return pl.pallas_call(
-        own_kernel if own else far_kernel,
-        grid_spec=pltpu.PrefetchScalarGridSpec(
-            num_scalar_prefetch=1,
-            grid=(PLANE // 4,),
-            in_specs=[spec] if own else [spec, far],
-            out_specs=pl.BlockSpec((4, 1, PIECE, DM), place),
-        ),
+        functools.partial(half_kernel, own),
+        in_specs=[pl.BlockSpec(memory_space=pltpu.SMEM), pl.BlockSpec(memory_space=pltpu.VMEM)]
+        + ([] if own else [far]),
+        out_specs=far,
         out_shape=jax.ShapeDtypeStruct((PLANE, CORES, PIECE, DM), F32),
+        scratch_shapes=[pltpu.VMEM((PLANE, PIECE, DM), F32), pltpu.SemaphoreType.DMA((4,))],
         input_output_aliases={} if own else {2: 0},
         compiler_params=pltpu.CompilerParams(vmem_limit_bytes=16 << 20),
         cost_estimate=pl.CostEstimate(flops=1 << 18, bytes_accessed=3 << 20, transcendentals=0),
         name="own_half" if own else "far_half",
     )(core, half, *([] if own else [before]))
-
-
-def spread_kernel(ids, out):
-    out[...] = jnp.broadcast_to(column(ids[...]), (SLOTS, 128)).astype(jnp.int32)
-
-
-def spread(ids):
-    whole = pl.BlockSpec(memory_space=pltpu.VMEM)
-    return pl.pallas_call(
-        spread_kernel,
-        in_specs=[whole],
-        out_specs=whole,
-        out_shape=jax.ShapeDtypeStruct((SLOTS, 128), jnp.int32),
-        compiler_params=pltpu.CompilerParams(vmem_limit_bytes=16 << 20),
-        cost_estimate=pl.CostEstimate(flops=1 << 17, bytes_accessed=1 << 17, transcendentals=0),
-        name="spread",
-    )(ids)
 
 
 def owner_kernel(core, asked, keep, got, out):
@@ -537,34 +510,36 @@
 ):
     seg = lax.axis_index("y").reshape(1)
     core = lax.axis_index("core").reshape(1)
-    asked = exchange(spread(request_rows.reshape(1, SLOTS)), NODE, OWNERS)
-    written = gru(touched, memory_base, messages[0], gru_input, gru_state)
+    written, ids = gru(
+        touched, request_rows.reshape(1, SLOTS), memory_base, messages[0], gru_input, gru_state
+    )
     r1 = lax.ppermute(written, "y", [(0, 1), (1, 2), (2, 3)])
     r2 = lax.ppermute(written, "y", [(0, 2), (1, 3)])
     r3 = lax.ppermute(written, "y", [(0, 3)])
+    asked = exchange(ids, NODE, OWNERS)
     up = upstream[0]
     written, late, chosen, chosen_t = lax.optimization_barrier(
-        (written, delays[0], event_slots[0], event_slots[0].T)
+        (written, delays[0].T, event_slots[0], event_slots[0].T)
     )
-    code, code_t = time_code(late, frequency.reshape(1, DM))
-    written, code, code_t = lax.optimization_barrier((written, code, code_t))
+    waves = frequency.reshape(1, DM)
+    t0, kv0 = time_tile(0, late, waves, attn_weights)
+    written, late, t0, kv0 = lax.optimization_barrier((written, late, t0, kv0))
     memory, rows = start_rows(seg, memory_base, written, r1, r2, r3, asked)
-    rows, code = lax.optimization_barrier((rows, code))
+    rows, late = lax.optimization_barrier((rows, late))
     slots = exchange(rows, NODE, OWNERS)
-    time_kv = project(code, attn_weights)
+    t1, kv1 = time_tile(1, late, waves, attn_weights)
     embedded, d_slots, mine, other = attend(
-        core, slots, chosen, chosen_t, time_kv, code_t, up, attn_weights
+        core, slots, chosen, chosen_t, (kv0, t0, kv1, t1), up, attn_weights
     )
     swap = [(0, 1), (1, 0)]
     partner = lax.ppermute(other, "core", swap)
     parts = plane(pair_sum(mine, partner, d_slots))
     part, keep, give = plane_sum(core, parts)
     got = lax.ppermute(give, "core", swap)
-    part = swap_sum(part, lax.ppermute(part, "y", [(0, 1), (1, 0), (2, 3), (3, 2)]))
-    turned = lax.ppermute(part, "y", [(0, 3), (3, 0), (1, 2), (2, 1)])
+    parts = lax.all_to_all(part, "y", split_axis=0, concat_axis=0, tiled=True)
+    parts, got = lax.optimization_barrier((parts, got))
+    half = plane(seg_sum(parts))
     memory_grad = owner_sum(core, asked, keep, got)
-    part, turned, memory_grad = lax.optimization_barrier((part, turned, memory_grad))
-    half = plane(seg_sum(part, turned))
     far = lax.ppermute(half, "core", swap)
     weight_grad = whole_grad(core, far, whole_grad(core, half))
     return embedded[None], memory[None], memory_grad[None], weight_grad.reshape(4, DM, DM)

time: 124 us -> 121 us (0.976)
  starting transfers between devices: 31 us -> 34.4 us
  blocking collectives: 41.1 us -> 38.4 us
  Pallas kernels: 37.2 us -> 34.6 us
    ppermute x2 -> x0, waiting for transfers between devices: 6.83 us -> none  [the longest x1 3.65 us: on_device(): lax.ppermute(part, 'y', [(0, 1), (1, 0), (2, 3), (3, 2)])]
    pallas_call x8 -> x6, Pallas kernels: 22 us -> 17.5 us  [the longest x2 10.4 us: time_tile(): pl.pallas_call(functools.partial(time_kernel, tile), grid=(K // 2,), in_s...]
    ppermute x1, starting transfers between devices: 5.61 us -> 1.31 us  [on_device(): r3 = lax.ppermute(written, 'y', [(0, 3)])]
    all_to_all x0 -> x1, starting transfers between devices: none -> 3.41 us  [on_device(): parts = lax.all_to_all(part, 'y', split_axis=0, concat_axis=0, tiled=True)]
    all_to_all x2, waiting for transfers between devices: 2.67 us -> 6.05 us  [exchange(): lax.all_to_all(blocks, axes, split_axis=0, concat_axis=0, tiled=True)]
    ppermute x1, starting transfers between devices: 1.31 us -> 4.53 us  [on_device(): r2 = lax.ppermute(written, 'y', [(0, 2), (1, 3)])]
    all_to_all x2, blocking collectives: 41.1 us -> 38.4 us  [plane(): return lax.all_to_all(x, FLAT, split_axis=0, concat_axis=0, tiled=True)]
    all_to_all x0 -> x1, waiting for transfers between devices: none -> 2.66 us  [on_device(): parts = lax.all_to_all(part, 'y', split_axis=0, concat_axis=0, tiled=True)]
  transfers between devices with their start and end apart: 10 -> 9, of which waited for: 6 -> 5; matrix products, arithmetic and copies ran while one was open for 1% -> 0% of each run, Pallas kernels for 14% -> 11%
where the time goes in v3:
time: 121 us
  blocking collectives  38.4 us (32%)
  Pallas kernels  34.6 us (29%)
  starting transfers between devices  34.4 us (28%)
  waiting for transfers between devices  12.2 us (10%)
    all_to_all x2, blocking collectives, plane(): return lax.all_to_all(x, FLAT, split_axis=0, concat_axis=0, tiled=True)  38.4 us
    all_to_all x2, starting transfers between devices, exchange(): lax.all_to_all(blocks, axes, split_axis=0, concat_axis=0, tiled=True)  14.1 us
    pallas_call x1, Pallas kernels, attend(): pl.pallas_call(attend_kernel, in_specs=[pl.BlockSpec(memory_space=pltpu.S...  13.6 us
    pallas_call x2, Pallas kernels, time_tile(): pl.pallas_call(functools.partial(time_kernel, tile), grid=(K // 2,), in_s...  10.4 us
    all_to_all x2, waiting for transfers between devices, exchange(): lax.all_to_all(blocks, axes, split_axis=0, concat_axis=0, tiled=True)  6.05 us
    ppermute x1, starting transfers between devices, on_device(): far = lax.ppermute(half, 'core', swap)  4.91 us
    ppermute x1, starting transfers between devices, on_device(): r2 = lax.ppermute(written, 'y', [(0, 2), (1, 3)])  4.53 us
    pallas_call x1, Pallas kernels, gru(): pl.pallas_call(gru_kernel, in_specs=[whole] * 2 + [far] * 4, out_specs=[w...  4.16 us
  transfers between devices with their start and end apart: 9, of which 5 were waited for; matrix products, arithmetic and copies ran while one was open for 0% of the time, Pallas kernels for 11%

profile of v3, /device:TPU:1, one launch (start us, length us, event | category | flops | bytes accessed | tf_op | source)
XLA Modules:
  0.0 120.7 jit_solution(6770886654703366618)
XLA Ops:
  0.6 0.0 copy-start.4
  0.6 4.2 %gru.1 = (bf16[256,512]{1,0:T(8,128)(2,1)}, s32[256,128]{1,0:T(8,128)}) custom-call(s32[1,256]{1,0:T(1,128)} %touched.1, s32[1,256]{1,0:T(1,128)} %bitcast.40, bf16[256,512]{1,0:T(8,128)(2,1)} %state.3, bf16[256,512]{1,0:T(8,128)(2,1)} %bitcast.34, bf16[512,1536]{1,0:T(8,128)(2,1)} %w_input.1, bf16[512,1536]{1,0:T(8,128)(2,1)} %w_state.1), custom_call_target="tpu_custom_call" | custom-call | flops 805306368 | bytes 4194304 | tf_op jit(solution)/shard_map/gru/pallas_call | solution.py:93
  4.8 4.0 %collective-permute-start = (bf16[256,512]{1,0:T(8,128)(2,1)}, bf16[256,512]{1,0:T(8,128)(2,1)S(1)}, u32[]{:S(2)}, u32[]{:S(2)}) collective-permute-start(bf16[256,512]{1,0:T(8,128)(2,1)} %get-tuple-element.36.written), channel_id=1, source_target_pairs={{0,32},{32,64},{64,96},{1,33},{33,65},{65,97},{2,34},{34,66},{66,9... | collective-permute-start | bytes 786440 | tf_op jit(solution)/shard_map/ppermute | solution.py:516
  8.9 4.5 %collective-permute-start.1 = (bf16[256,512]{1,0:T(8,128)(2,1)}, bf16[256,512]{1,0:T(8,128)(2,1)S(1)}, u32[]{:S(2)}, u32[]{:S(2)}) collective-permute-start(bf16[256,512]{1,0:T(8,128)(2,1)} %get-tuple-element.36.written), channel_id=1, source_target_pairs={{0,64},{32,96},{1,65},{33,97},{2,66},{34,98},{3,67},{35,99},{4,68}... | collective-permute-start | bytes 786440 | tf_op jit(solution)/shard_map/ppermute | solution.py:517
  13.4 1.3 %collective-permute-start.2 = (bf16[256,512]{1,0:T(8,128)(2,1)}, bf16[256,512]{1,0:T(8,128)(2,1)S(1)}, u32[]{:S(2)}, u32[]{:S(2)}) collective-permute-start(bf16[256,512]{1,0:T(8,128)(2,1)} %get-tuple-element.36.written), channel_id=1, source_target_pairs={{0,96},{1,97},{2,98},{3,99},{4,100},{5,101},{6,102},{7,103},{8,104... | collective-permute-start | bytes 786440 | tf_op jit(solution)/shard_map/ppermute | solution.py:518
  14.7 9.2 %all-to-all-start = ((s32[32,8,128]{2,1,0:T(8,128)}), s32[32,8,128]{2,1,0:T(8,128)S(1)}, u32[]{:S(2)}, u32[]{:S(2)}) async-start(s32[32,8,128]{2,1,0:T(8,128)} %bitcast.35), calls=%async_computation | async-start | bytes 262144 | tf_op jit(solution)/shard_map/all_to_all | solution.py:491
  23.9 0.0 copy-done.4
  23.9 0.0 copy-start
  23.9 0.0 copy-start.1
  23.9 5.2 %time_tile.2 = (bf16[4,512,256]{2,1,0:T(8,128)(2,1)}, bf16[1024,1024]{1,0:T(8,128)(2,1)}) custom-call(s32[8,256]{1,0:T(8,128)} %bitcast.36, f32[1,512]{1,0:T(1,128)} %bitcast.38, bf16[4,512,512]{2,1,0:T(8,128)(2,1)} %w.1, bf16[4,512,512]{2,1,0:T(8,128)(2,1)} %w.1), custom_call_target="tpu_custom_call" | custom-call | flops 1073741824 | bytes 5242880 | tf_op jit(solution)/shard_map/time_tile/pallas_call | solution.py:141
  29.1 2.5 %all-to-all-done = s32[32,8,128]{2,1,0:T(8,128)S(1)} async-done(((s32[32,8,128]{2,1,0:T(8,128)}), s32[32,8,128]{2,1,0:T(8,128)S(1)}, u32[]{:S(2)}, u32[]{:S(2)}) %all-to-all-start) | async-done | bytes 131104 | tf_op jit(solution)/shard_map/all_to_all | solution.py:491
  31.6 0.0 collective-permute-done.r1
  31.6 0.0 collective-permute-done.1.r2
  31.6 0.0 collective-permute-done.2.r3
  31.6 0.0 copy-done
  31.6 0.0 copy-done.1
  31.6 1.2 %start_rows.1 = (bf16[256,512]{1,0:T(8,128)(2,1)}, bf16[256,512]{1,0:T(8,128)(2,1)}) custom-call(s32[1]{0:T(128)} %bitcast.1.seg, bf16[256,512]{1,0:T(8,128)(2,1)S(1)} %copy-done, bf16[256,512]{1,0:T(8,128)(2,1)S(1)} %copy-done.1, bf16[256,512]{1,0:T(8,128)(2,1)S(1)} %collective-permute-done.r1, bf16[256,512]{1,0:T(8,128)(2,1)S(1)} %collective-permute-done.1.r2, ...), custom_call_target="tpu_custom_call" | custom-call | flops 67108864 | bytes 2097152 | tf_op jit(solution)/shard_map/start_rows/pallas_call | solution.py:183
  32.9 4.9 %all-to-all-start.1 = ((bf16[32,8,512]{2,1,0:T(8,128)(2,1)}), bf16[32,8,512]{2,1,0:T(8,128)(2,1)S(1)}, u32[]{:S(2)}, u32[]{:S(2)}) async-start(bf16[32,8,512]{2,1,0:T(8,128)(2,1)} %bitcast.10), calls=%async_computation.1 | async-start | bytes 524288 | tf_op jit(solution)/shard_map/all_to_all | solution.py:491
  37.8 0.1 copy.16.chosen
  37.9 0.0 copy-start.2
  38.0 0.0 copy-start.3
  38.0 5.3 %time_tile.3 = (bf16[4,512,256]{2,1,0:T(8,128)(2,1)}, bf16[1024,1024]{1,0:T(8,128)(2,1)}) custom-call(s32[8,256]{1,0:T(8,128)} %bitcast.37, f32[1,512]{1,0:T(1,128)} %bitcast.39, bf16[4,512,512]{2,1,0:T(8,128)(2,1)} %w.1, bf16[4,512,512]{2,1,0:T(8,128)(2,1)} %w.1), custom_call_target="tpu_custom_call" | custom-call | flops 1073741824 | bytes 5242880 | tf_op jit(solution)/shard_map/time_tile/pallas_call | solution.py:141
  43.2 3.6 %all-to-all-done.1 = bf16[32,8,512]{2,1,0:T(8,128)(2,1)S(1)} async-done(((bf16[32,8,512]{2,1,0:T(8,128)(2,1)}), bf16[32,8,512]{2,1,0:T(8,128)(2,1)S(1)}, u32[]{:S(2)}, u32[]{:S(2)}) %all-to-all-start.1) | async-done | bytes 262176 | tf_op jit(solution)/shard_map/all_to_all | solution.py:491
  46.8 0.0 copy-done.2
  46.8 0.0 copy-done.3
  46.8 13.6 %attend.1 = (bf16[256,512]{1,0:T(8,128)(2,1)}, bf16[256,512]{1,0:T(8,128)(2,1)S(1)}, bf16[16,64,512]{2,1,0:T(8,128)(2,1)S(1)}, bf16[16,64,512]{2,1,0:T(8,128)(2,1)S(1)}) custom-call(s32[1]{0:T(128)} %bitcast.core, bf16[256,512]{1,0:T(8,128)(2,1)S(1)} %bitcast.28, s32[256,9]{1,0:T(8,128)S(1)} %copy.16.chosen, s32[9,256]{1,0:T(8,128)S(1)} %bitcast.30, ...), custom_call_target="tpu_custom_call" | custom-call | flops 6442450944 | bytes 14680064 | tf_op jit(solution)/shard_map/attend/pallas_call | solution.py:332
  60.4 0.3 collective-permute-start.3
  60.7 2.5 %collective-permute-done.3.b = bf16[16,64,512]{2,1,0:T(8,128)(2,1)S(1)} collective-permute-done((bf16[16,64,512]{2,1,0:T(8,128)(2,1)S(1)}, bf16[16,64,512]{2,1,0:T(8,128)(2,1)S(1)}, u32[]{:S(2)}, u32[]{:S(2)}) %collective-permute-start.3) | collective-permute-done | bytes 1048608 | tf_op jit(solution)/shard_map/ppermute | solution.py:535
  63.1 0.3 pair_sum.1
  63.4 21.9 %all_to_all.25.a = bf16[16,80,512]{2,1,0:T(8,128)(2,1)S(1)} all-to-all(bf16[16,80,512]{2,1,0:T(8,128)(2,1)S(1)} %pair_sum.1), channel_id=1, replica_groups=mesh['y'=4,'x'=4,'z'=4,'core'=2] {'x','z'}, dimensions={0} | all-to-all | bytes 2621440 | tf_op jit(solution)/shard_map/all_to_all | solution.py:495
  85.3 0.8 plane_sum.1
  86.1 3.4 %all-to-all-start.3 = ((bf16[4,64,512]{2,1,0:T(8,128)(2,1)}), bf16[4,64,512]{2,1,0:T(8,128)(2,1)S(1)}, u32[]{:S(2)}, u32[]{:S(2)}) async-start(bf16[4,64,512]{2,1,0:T(8,128)(2,1)} %get-tuple-element.54), calls=%async_computation.3 | async-start | bytes 524288 | tf_op jit(solution)/shard_map/all_to_all | solution.py:539
  89.6 1.9 %collective-permute-start.4 = (bf16[128,512]{1,0:T(8,128)(2,1)S(1)}, bf16[128,512]{1,0:T(8,128)(2,1)S(1)}, u32[]{:S(2)}, u32[]{:S(2)}) collective-permute-start(bf16[128,512]{1,0:T(8,128)(2,1)S(1)} %get-tuple-element.55), channel_id=1, source_target_pairs={{0,1},{1,0},{2,3},{3,2},{4,5},{5,4},{6,7},{7,6},{8,9},{9,8},{10,11... | collective-permute-start | bytes 393224 | tf_op jit(solution)/shard_map/ppermute | solution.py:538
  91.4 1.0 collective-permute-done.4.got
  92.4 2.7 %all-to-all-done.3.parts = bf16[4,64,512]{2,1,0:T(8,128)(2,1)S(1)} async-done(((bf16[4,64,512]{2,1,0:T(8,128)(2,1)}), bf16[4,64,512]{2,1,0:T(8,128)(2,1)S(1)}, u32[]{:S(2)}, u32[]{:S(2)}) %all-to-all-start.3) | async-done | bytes 262176 | tf_op jit(solution)/shard_map/all_to_all | solution.py:539
  95.0 0.1 seg_sum.1
  95.2 16.6 %all_to_all.26.half = bf16[16,64,512]{2,1,0:T(8,128)(2,1)S(1)} all-to-all(bf16[16,64,512]{2,1,0:T(8,128)(2,1)S(1)} %seg_sum.1), channel_id=1, replica_groups=mesh['y'=4,'x'=4,'z'=4,'core'=2] {'x','z'}, dimensions={0} | all-to-all | bytes 2097152 | tf_op jit(solution)/shard_map/all_to_all | solution.py:495
  111.7 4.9 %collective-permute-start.5 = (bf16[16,64,512]{2,1,0:T(8,128)(2,1)S(1)}, bf16[16,64,512]{2,1,0:T(8,128)(2,1)S(1)}, u32[]{:S(2)}, u32[]{:S(2)}) collective-permute-start(bf16[16,64,512]{2,1,0:T(8,128)(2,1)S(1)} %all_to_all.26.half), channel_id=1, source_target_pairs={{0,1},{1,0},{2,3},{3,2},{4,5},{5,4},{6,7},{7,6},{8,9},{9,8},{10,11... | collective-permute-start | bytes 3145736 | tf_op jit(solution)/shard_map/ppermute | solution.py:543
  116.6 1.1 owner_sum.1
  117.8 1.4 %own_half.1.rest_0_ = f32[16,2,64,512]{3,2,1,0:T(8,128)} custom-call(s32[1]{0:T(128)} %bitcast.core, bf16[16,64,512]{2,1,0:T(8,128)(2,1)S(1)} %all_to_all.26.half), custom_call_target="tpu_custom_call" | custom-call | flops 262144 | bytes 3145728 | tf_op jit(solution)/shard_map/own_half/pallas_call | solution.py:454
  119.1 0.0 collective-permute-done.5.half
  119.1 1.4 %far_half.1 = f32[16,2,64,512]{3,2,1,0:T(8,128)} custom-call(s32[1]{0:T(128)} %bitcast.core, bf16[16,64,512]{2,1,0:T(8,128)(2,1)S(1)} %collective-permute-done.5.half, f32[16,2,64,512]{3,2,1,0:T(8,128)} %own_half.1.rest_0_), custom_call_target="tpu_custom_call", output_to_operand_aliasing={{}: (2, {})} | custom-call | flops 262144 | bytes 3145728 | tf_op jit(solution)/shard_map/far_half/pallas_call | solution.py:454
  (1 shorter events, 0.0 us)
Async XLA Ops:
  0.6 23.3 %copy-start.4 = (s32[1,256,9]{1,0,2:T(1,128)S(1)}, s32[1,256,9]{1,0,2:T(1,128)}, u32[]{:S(2)}) copy-start(s32[1,256,9]{1,0,2:T(1,128)} %param.19) | copy-start | bytes 27652
  4.8 26.8 %collective-permute-start = (bf16[256,512]{1,0:T(8,128)(2,1)}, bf16[256,512]{1,0:T(8,128)(2,1)S(1)}, u32[]{:S(2)}, u32[]{:S(2)}) collective-permute-start(bf16[256,512]{1,0:T(8,128)(2,1)} %get-tuple-element.36.written), channel_id=1, source_target_pairs={{0,32},{32,64},{64,96},{1,33},{33,65},{65,97},{2,34},{34,66},{66,9... | collective-permute-start | bytes 786440 | tf_op jit(solution)/shard_map/ppermute | solution.py:516
  8.9 22.7 %collective-permute-start.1 = (bf16[256,512]{1,0:T(8,128)(2,1)}, bf16[256,512]{1,0:T(8,128)(2,1)S(1)}, u32[]{:S(2)}, u32[]{:S(2)}) collective-permute-start(bf16[256,512]{1,0:T(8,128)(2,1)} %get-tuple-element.36.written), channel_id=1, source_target_pairs={{0,64},{32,96},{1,65},{33,97},{2,66},{34,98},{3,67},{35,99},{4,68}... | collective-permute-start | bytes 786440 | tf_op jit(solution)/shard_map/ppermute | solution.py:517
  13.4 18.2 %collective-permute-start.2 = (bf16[256,512]{1,0:T(8,128)(2,1)}, bf16[256,512]{1,0:T(8,128)(2,1)S(1)}, u32[]{:S(2)}, u32[]{:S(2)}) collective-permute-start(bf16[256,512]{1,0:T(8,128)(2,1)} %get-tuple-element.36.written), channel_id=1, source_target_pairs={{0,96},{1,97},{2,98},{3,99},{4,100},{5,101},{6,102},{7,103},{8,104... | collective-permute-start | bytes 786440 | tf_op jit(solution)/shard_map/ppermute | solution.py:518
  14.7 16.9 %all-to-all-start = ((s32[32,8,128]{2,1,0:T(8,128)}), s32[32,8,128]{2,1,0:T(8,128)S(1)}, u32[]{:S(2)}, u32[]{:S(2)}) async-start(s32[32,8,128]{2,1,0:T(8,128)} %bitcast.35), calls=%async_computation | async-start | bytes 262144 | tf_op jit(solution)/shard_map/all_to_all | solution.py:491
  23.9 7.7 %copy-start = (bf16[256,512]{1,0:T(8,128)(2,1)S(1)}, bf16[256,512]{1,0:T(8,128)(2,1)}, u32[]{:S(2)}) copy-start(bf16[256,512]{1,0:T(8,128)(2,1)} %state.3) | copy-start | bytes 786436
  23.9 7.7 %copy-start.1 = (bf16[256,512]{1,0:T(8,128)(2,1)S(1)}, bf16[256,512]{1,0:T(8,128)(2,1)}, u32[]{:S(2)}) copy-start(bf16[256,512]{1,0:T(8,128)(2,1)} %get-tuple-element.36.written) | copy-start | bytes 786436
  32.9 13.9 %all-to-all-start.1 = ((bf16[32,8,512]{2,1,0:T(8,128)(2,1)}), bf16[32,8,512]{2,1,0:T(8,128)(2,1)S(1)}, u32[]{:S(2)}, u32[]{:S(2)}) async-start(bf16[32,8,512]{2,1,0:T(8,128)(2,1)} %bitcast.10), calls=%async_computation.1 | async-start | bytes 524288 | tf_op jit(solution)/shard_map/all_to_all | solution.py:491
  37.9 8.9 %copy-start.2 = (bf16[4,512,256]{2,1,0:T(8,128)(2,1)S(1)}, bf16[4,512,256]{2,1,0:T(8,128)(2,1)}, u32[]{:S(2)}) copy-start(bf16[4,512,256]{2,1,0:T(8,128)(2,1)} %get-tuple-element.44.t0) | copy-start | bytes 3145732
  38.0 8.9 %copy-start.3 = (bf16[1,256,512]{2,1,0:T(8,128)(2,1)S(1)}, bf16[1,256,512]{2,1,0:T(8,128)(2,1)}, u32[]{:S(2)}) copy-start(bf16[1,256,512]{2,1,0:T(8,128)(2,1)} %param.21) | copy-start | bytes 786436
  60.4 2.7 %collective-permute-start.3 = (bf16[16,64,512]{2,1,0:T(8,128)(2,1)S(1)}, bf16[16,64,512]{2,1,0:T(8,128)(2,1)S(1)}, u32[]{:S(2)}, u32[]{:S(2)}) collective-permute-start(bf16[16,64,512]{2,1,0:T(8,128)(2,1)S(1)} %get-tuple-element.51), channel_id=1, source_target_pairs={{0,1},{1,0},{2,3},{3,2},{4,5},{5,4},{6,7},{7,6},{8,9},{9,8},{10,11... | collective-permute-start | bytes 3145736 | tf_op jit(solution)/shard_map/ppermute | solution.py:535
  86.1 8.9 %all-to-all-start.3 = ((bf16[4,64,512]{2,1,0:T(8,128)(2,1)}), bf16[4,64,512]{2,1,0:T(8,128)(2,1)S(1)}, u32[]{:S(2)}, u32[]{:S(2)}) async-start(bf16[4,64,512]{2,1,0:T(8,128)(2,1)} %get-tuple-element.54), calls=%async_computation.3 | async-start | bytes 524288 | tf_op jit(solution)/shard_map/all_to_all | solution.py:539
  89.6 2.8 %collective-permute-start.4 = (bf16[128,512]{1,0:T(8,128)(2,1)S(1)}, bf16[128,512]{1,0:T(8,128)(2,1)S(1)}, u32[]{:S(2)}, u32[]{:S(2)}) collective-permute-start(bf16[128,512]{1,0:T(8,128)(2,1)S(1)} %get-tuple-element.55), channel_id=1, source_target_pairs={{0,1},{1,0},{2,3},{3,2},{4,5},{5,4},{6,7},{7,6},{8,9},{9,8},{10,11... | collective-permute-start | bytes 393224 | tf_op jit(solution)/shard_map/ppermute | solution.py:538
  111.7 7.4 %collective-permute-start.5 = (bf16[16,64,512]{2,1,0:T(8,128)(2,1)S(1)}, bf16[16,64,512]{2,1,0:T(8,128)(2,1)S(1)}, u32[]{:S(2)}, u32[]{:S(2)}) collective-permute-start(bf16[16,64,512]{2,1,0:T(8,128)(2,1)S(1)} %all_to_all.26.half), channel_id=1, source_target_pairs={{0,1},{1,0},{2,3},{3,2},{4,5},{5,4},{6,7},{7,6},{8,9},{9,8},{10,11... | collective-permute-start | bytes 3145736 | tf_op jit(solution)/shard_map/ppermute | solution.py:543

commit v4 on v3

--- a/solution.py
+++ b/solution.py
@@ -113,54 +113,42 @@
     )(touched, ids, state, message, w_input, w_state)
 
 
-def time_kernel(tile, delays, frequency, w_key, w_value, code_t, time_kv):
-    g = pl.program_id(0)
+def time_kernel(delays, frequency, w, code_t, time_kv):
     turns = frequency[...] * (1.0 / (2.0 * math.pi))
     high = jnp.round(turns * 16384.0) * (1.0 / 16384.0)
     low = turns - high
-    waves = []
-    for i in range(2):
-        block = delays[:, tile * TILE : (tile + 1) * TILE].astype(F32)
-        here = iota((K, TILE), 0) == 2 * g + i
-        delay = column(jnp.sum(jnp.where(here, block, 0.0), axis=0, keepdims=True))
-        coarse = delay * high
-        part = (coarse - jnp.round(coarse)) + delay * low
-        u = part * part
-        wave = jnp.full_like(u, COS[-1])
-        for c in COS[-2::-1]:
-            wave = wave * u + c
-        waves.append(wave)
-    wave = jnp.concatenate(waves, axis=0)
-    code_t[0] = wave.T.astype(BF)
-    wave = wave.astype(BF)
-    time_kv[:, :DM] = dot(wave, w_key[0]).astype(BF)
-    time_kv[:, DM:] = dot(wave, w_value[0]).astype(BF)
-
-
-def time_tile(tile, delays, frequency, weights):
-    return pl.pallas_call(
-        functools.partial(time_kernel, tile),
-        grid=(K // 2,),
-        in_specs=[
-            pl.BlockSpec((K, E), lambda g: (0, 0)),
-            pl.BlockSpec((1, DM), lambda g: (0, 0)),
-            pl.BlockSpec((1, DM, DM), lambda g: (1, 0, 0)),
-            pl.BlockSpec((1, DM, DM), lambda g: (2, 0, 0)),
+    for tile in range(TILES):
+        for k in range(K):
+            delay = column(delays[k : k + 1, tile * TILE : (tile + 1) * TILE])
+            coarse = delay * high
+            part = (coarse - jnp.round(coarse)) + delay * low
+            u = part * part
+            wave = jnp.full_like(u, COS[-1])
+            for c in COS[-2::-1]:
+                wave = wave * u + c
+            at = slice(k * TILE, (k + 1) * TILE)
+            code_t[tile, :, at] = wave.T.astype(BF)
+            wave = wave.astype(BF)
+            time_kv[tile, at, :DM] = dot(wave, w[1]).astype(BF)
+            time_kv[tile, at, DM:] = dot(wave, w[2]).astype(BF)
+
+
+def time_parts(delays, frequency, weights):
+    whole = pl.BlockSpec(memory_space=pltpu.VMEM)
+    return pl.pallas_call(
+        time_kernel,
+        in_specs=[whole] * 3,
+        out_specs=[whole] * 2,
+        out_shape=[
+            jax.ShapeDtypeStruct((TILES, DM, ROWS), BF),
+            jax.ShapeDtypeStruct((TILES, ROWS, 2 * DM), BF),
         ],
-        out_specs=[
-            pl.BlockSpec((1, DM, 2 * TILE), lambda g: (g, 0, 0)),
-            pl.BlockSpec((2 * TILE, 2 * DM), lambda g: (g, 0)),
-        ],
-        out_shape=[
-            jax.ShapeDtypeStruct((K // 2, DM, 2 * TILE), BF),
-            jax.ShapeDtypeStruct((ROWS, 2 * DM), BF),
-        ],
-        compiler_params=pltpu.CompilerParams(vmem_limit_bytes=56 << 20),
+        compiler_params=pltpu.CompilerParams(vmem_limit_bytes=24 << 20),
         cost_estimate=pl.CostEstimate(
-            flops=4 * ROWS * DM * DM, bytes_accessed=5 << 20, transcendentals=ROWS * DM
+            flops=4 * K * E * DM * DM, bytes_accessed=8 << 20, transcendentals=K * E * DM
         ),
-        name="time_tile",
-    )(delays, frequency, weights, weights)
+        name="time_parts",
+    )(delays, frequency, weights)
 
 
 def owner_pick(asked):
@@ -197,35 +185,17 @@
 
 
 def attend_kernel(
-    core, slots, chosen, chosen_t, kv0, t0, kv1, t1, up, w,
+    core, slots, chosen, chosen_t, tkv, tt, up, wq,
     embedded, d_slots, mine, other,
-    tkv, tt, wq, sem, skv, d_att, qf, src, both, dkv, att, dq, sums,
+    skv, d_att, qf, src, both, dkv, att, dq, sums,
 ):
-    moves = (
-        (w.at[pl.ds(1, 2)], wq.at[pl.ds(1, 2)]),
-        (w.at[0], wq.at[0]),
-        (w.at[3], wq.at[3]),
-        (kv0, tkv.at[0]),
-        (kv1, tkv.at[1]),
-        (t0, tt.at[0]),
-        (t1, tt.at[1]),
-    )
-    copies = [pltpu.make_async_copy(a, b, sem.at[i]) for i, (a, b) in enumerate(moves)]
-    for copy in copies[:4]:
-        copy.start()
     rows = slots[...]
     pick = (chosen[:, 0:1] == iota((E, SLOTS), 1)).astype(F32).astype(BF)
     src[...] = dot(pick, rows)
-    copies[0].wait()
     skv[:, :DM] = dot(rows, wq[1]).astype(BF)
     skv[:, DM:] = dot(rows, wq[2]).astype(BF)
-    for copy in copies[4:]:
-        copy.start()
-    copies[1].wait()
     qf[...] = dot(pick, dot(rows, wq[0]).astype(BF))
-    copies[2].wait()
     d_att[...] = dot_nt(up[...], wq[3])
-    copies[3].wait()
 
     lane = iota((STEP, 128), 1)
     first = lane < K
@@ -290,12 +260,8 @@
     sub = iota((SLOTS, TILE), 0)
     s_kv = dot_t = None
     for i in range(TILES):
-        if i == 1:
-            copies[4].wait()
         for j in range(TILE // STEP):
             step(i, j)
-        copies[5 + i].wait()
-        code = jnp.concatenate([tt[i, g] for g in range(K // 2)], axis=1)
         spread = jnp.concatenate(
             [
                 (sub == chosen_t[1 + k : 2 + k, i * TILE : (i + 1) * TILE]).astype(F32)
@@ -303,7 +269,7 @@
             ],
             axis=1,
         ).astype(BF)
-        one, two = dot(spread, dkv[i]), dot(code, dkv[i])
+        one, two = dot(spread, dkv[i]), dot(tt[i], dkv[i])
         s_kv = one if i == 0 else s_kv + one
         dot_t = two if i == 0 else dot_t + two
     s_kv = s_kv.astype(BF)
@@ -326,16 +292,11 @@
     d_slots[...] = grads.astype(BF)
 
 
-def attend(core, slots, chosen, chosen_t, times, up, weights):
-    whole = pl.BlockSpec(memory_space=pltpu.VMEM)
-    far = pl.BlockSpec(memory_space=pl.ANY)
+def attend(core, slots, chosen, chosen_t, time_kv, code_t, up, weights):
+    whole = pl.BlockSpec(memory_space=pltpu.VMEM)
     return pl.pallas_call(
         attend_kernel,
-        in_specs=[pl.BlockSpec(memory_space=pltpu.SMEM)]
-        + [whole] * 3
-        + [far] * 4
-        + [whole]
-        + [far],
+        in_specs=[pl.BlockSpec(memory_space=pltpu.SMEM)] + [whole] * 7,
         out_specs=[whole] * 4,
         out_shape=[
             jax.ShapeDtypeStruct((E, DM), BF),
@@ -344,10 +305,6 @@
             jax.ShapeDtypeStruct((PLANE, PIECE, DM), BF),
         ],
         scratch_shapes=[
-            pltpu.VMEM((TILES, ROWS, 2 * DM), BF),
-            pltpu.VMEM((TILES, K // 2, DM, 2 * TILE), BF),
-            pltpu.VMEM((4, DM, DM), BF),
-            pltpu.SemaphoreType.DMA((7,)),
             pltpu.VMEM((SLOTS, 2 * DM), BF),
             pltpu.VMEM((E, DM), F32),
             pltpu.VMEM((E, DM), F32),
@@ -358,12 +315,12 @@
             pltpu.VMEM((E, DM), BF),
             pltpu.VMEM((PLANE, CORES, PIECE, DM), BF),
         ],
-        compiler_params=pltpu.CompilerParams(vmem_limit_bytes=50 << 20),
+        compiler_params=pltpu.CompilerParams(vmem_limit_bytes=40 << 20),
         cost_estimate=pl.CostEstimate(
             flops=6 << 30, bytes_accessed=14 << 20, transcendentals=E * 128
         ),
         name="attend",
-    )(core, slots, chosen, chosen_t, *times, up, weights)
+    )(core, slots, chosen, chosen_t, time_kv, code_t, up, weights)
 
 
 def pair_kernel(a, b, d_slots, out):
@@ -389,9 +346,7 @@
     total = a[0, :PIECE].astype(F32)
     for i in range(1, PLANE):
         total += a[i, :PIECE].astype(F32)
-    total = total.astype(BF)
-    for i in range(SEG):
-        part[i] = total
+    part[...] = total.astype(BF)
     grads = a[:, PIECE:].astype(F32)
     low, high = grads[:, :CAP].reshape(SLOTS // 2, DM), grads[:, CAP:].reshape(SLOTS // 2, DM)
     first = core[0] == 0
@@ -406,33 +361,33 @@
         plane_kernel,
         in_specs=[pl.BlockSpec(memory_space=pltpu.SMEM), whole],
         out_specs=[whole] * 3,
-        out_shape=[jax.ShapeDtypeStruct((SEG, PIECE, DM), BF), half, half],
+        out_shape=[jax.ShapeDtypeStruct((PIECE, DM), BF), half, half],
         compiler_params=pltpu.CompilerParams(vmem_limit_bytes=16 << 20),
         cost_estimate=pl.CostEstimate(flops=1 << 19, bytes_accessed=2 << 20, transcendentals=0),
         name="plane_sum",
     )(core, a)
 
 
-def seg_kernel(parts, out):
-    total = (parts[0].astype(F32) + parts[1].astype(F32)) + (
-        parts[2].astype(F32) + parts[3].astype(F32)
-    )
-    total = total.astype(BF)
+def seg_kernel(seg, own, r1, r2, r3, out, parts):
+    for back, r in enumerate((own, r1, r2, r3)):
+        parts[lax.rem(seg[0] + SEG - back, SEG)] = r[...].astype(F32)
+    total = ((parts[0] + parts[1]) + (parts[2] + parts[3])).astype(BF)
     for i in range(PLANE):
         out[i] = total
 
 
-def seg_sum(parts):
+def seg_sum(seg, own, r1, r2, r3):
     whole = pl.BlockSpec(memory_space=pltpu.VMEM)
     return pl.pallas_call(
         seg_kernel,
-        in_specs=[whole],
+        in_specs=[pl.BlockSpec(memory_space=pltpu.SMEM)] + [whole] * 4,
         out_specs=whole,
         out_shape=jax.ShapeDtypeStruct((PLANE, PIECE, DM), BF),
+        scratch_shapes=[pltpu.VMEM((SEG, PIECE, DM), F32)],
         compiler_params=pltpu.CompilerParams(vmem_limit_bytes=16 << 20),
         cost_estimate=pl.CostEstimate(flops=1 << 17, bytes_accessed=1 << 20, transcendentals=0),
         name="seg_sum",
-    )(parts)
+    )(seg, own, r1, r2, r3)
 
 
 def half_kernel(own, core, half, *rest):
@@ -513,33 +468,33 @@
     written, ids = gru(
         touched, request_rows.reshape(1, SLOTS), memory_base, messages[0], gru_input, gru_state
     )
+    written, ids, seg, core, late, chosen, chosen_t = lax.optimization_barrier(
+        (written, ids, seg, core, delays[0].T, event_slots[0], event_slots[0].T)
+    )
     r1 = lax.ppermute(written, "y", [(0, 1), (1, 2), (2, 3)])
     r2 = lax.ppermute(written, "y", [(0, 2), (1, 3)])
     r3 = lax.ppermute(written, "y", [(0, 3)])
     asked = exchange(ids, NODE, OWNERS)
+    asked, late = lax.optimization_barrier((asked, late))
+    code_t, time_kv = time_parts(late, frequency.reshape(1, DM), attn_weights)
+    written, code_t, time_kv = lax.optimization_barrier((written, code_t, time_kv))
+    memory, rows = start_rows(seg, memory_base, written, r1, r2, r3, asked)
+    slots = exchange(rows, NODE, OWNERS)
     up = upstream[0]
-    written, late, chosen, chosen_t = lax.optimization_barrier(
-        (written, delays[0].T, event_slots[0], event_slots[0].T)
-    )
-    waves = frequency.reshape(1, DM)
-    t0, kv0 = time_tile(0, late, waves, attn_weights)
-    written, late, t0, kv0 = lax.optimization_barrier((written, late, t0, kv0))
-    memory, rows = start_rows(seg, memory_base, written, r1, r2, r3, asked)
-    rows, late = lax.optimization_barrier((rows, late))
-    slots = exchange(rows, NODE, OWNERS)
-    t1, kv1 = time_tile(1, late, waves, attn_weights)
     embedded, d_slots, mine, other = attend(
-        core, slots, chosen, chosen_t, (kv0, t0, kv1, t1), up, attn_weights
+        core, slots, chosen, chosen_t, time_kv, code_t, up, attn_weights
     )
     swap = [(0, 1), (1, 0)]
     partner = lax.ppermute(other, "core", swap)
     parts = plane(pair_sum(mine, partner, d_slots))
     part, keep, give = plane_sum(core, parts)
     got = lax.ppermute(give, "core", swap)
-    parts = lax.all_to_all(part, "y", split_axis=0, concat_axis=0, tiled=True)
-    parts, got = lax.optimization_barrier((parts, got))
-    half = plane(seg_sum(parts))
+    r2, r1, r3 = (
+        lax.ppermute(part, "y", [(i, (i + s) % SEG) for i in range(SEG)]) for s in (2, 1, 3)
+    )
     memory_grad = owner_sum(core, asked, keep, got)
+    r2, memory_grad = lax.optimization_barrier((r2, memory_grad))
+    half = plane(seg_sum(seg, part, r1, r2, r3))
     far = lax.ppermute(half, "core", swap)
     weight_grad = whole_grad(core, far, whole_grad(core, half))
     return embedded[None], memory[None], memory_grad[None], weight_grad.reshape(4, DM, DM)

time: 121 us -> 124 us (1.025)
  Pallas kernels: 34.6 us -> 22.6 us
  local copies, waits for them, and re-layouts: 0.15 us -> 8.11 us
  waiting for transfers between devices: 12.2 us -> 16.2 us
  starting transfers between devices: 34.4 us -> 36.1 us
  blocking collectives: 38.4 us -> 39.8 us
    unnamed x11 -> x21, local copies, waits for them, and re-layouts: 0.03 us -> 7.99 us
    pallas_call x3 -> x2, Pallas kernels: 10.5 us -> 4.4 us  [the longest x1 4.26 us: time_parts(): pl.pallas_call(time_kernel, in_specs=[whole] * 3, out_specs=[whole] * 2,...]
    pallas_call x1, Pallas kernels: 13.6 us -> 8.46 us  [attend(): pl.pallas_call(attend_kernel, in_specs=[pl.BlockSpec(memory_space=pltpu.S...]
    ppermute x0 -> x3, starting transfers between devices: none -> 5.03 us  [on_device(): lax.ppermute(part, 'y', [(i, (i + s) % SEG) for i in range(SEG)])]
    all_to_all x1 -> x0, starting transfers between devices: 3.41 us -> none  [on_device(): parts = lax.all_to_all(part, 'y', split_axis=0, concat_axis=0, tiled=True)]
    all_to_all x2, starting transfers between devices: 14.1 us -> 17.5 us  [exchange(): lax.all_to_all(blocks, axes, split_axis=0, concat_axis=0, tiled=True)]
    ppermute x1, starting transfers between devices: 1.31 us -> 4.65 us  [on_device(): r3 = lax.ppermute(written, 'y', [(0, 3)])]
    ppermute x1, starting transfers between devices: 4.53 us -> 1.31 us  [on_device(): r2 = lax.ppermute(written, 'y', [(0, 2), (1, 3)])]
  transfers between devices with their start and end apart: 9 -> 11, of which waited for: 5 -> 6; matrix products, arithmetic and copies ran while one was open for 0% -> 0% of each run, Pallas kernels for 11% -> 5%
where the time goes in v4:
time: 124 us
  blocking collectives  39.8 us (32%)
  starting transfers between devices  36.1 us (29%)
  Pallas kernels  22.6 us (18%)
  waiting for transfers between devices  16.2 us (13%)
  local copies, waits for them, and re-layouts  8.11 us (7%)
    all_to_all x2, blocking collectives, plane(): return lax.all_to_all(x, FLAT, split_axis=0, concat_axis=0, tiled=True)  39.8 us
    all_to_all x2, starting transfers between devices, exchange(): lax.all_to_all(blocks, axes, split_axis=0, concat_axis=0, tiled=True)  17.5 us
    all_to_all x2, waiting for transfers between devices, exchange(): lax.all_to_all(blocks, axes, split_axis=0, concat_axis=0, tiled=True)  8.87 us
    pallas_call x1, Pallas kernels, attend(): pl.pallas_call(attend_kernel, in_specs=[pl.BlockSpec(memory_space=pltpu.S...  8.46 us
    unnamed x21, local copies, waits for them, and re-layouts  7.99 us
    ppermute x3, starting transfers between devices, on_device(): lax.ppermute(part, 'y', [(i, (i + s) % SEG) for i in range(SEG)])  5.03 us
    ppermute x1, starting transfers between devices, on_device(): r3 = lax.ppermute(written, 'y', [(0, 3)])  4.65 us
    pallas_call x1, Pallas kernels, time_parts(): pl.pallas_call(time_kernel, in_specs=[whole] * 3, out_specs=[whole] * 2,...  4.26 us
  transfers between devices with their start and end apart: 11, of which 6 were waited for; matrix products, arithmetic and copies ran while one was open for 0% of the time, Pallas kernels for 5%

profile of v4, /device:TPU:1, one launch (start us, length us, event | category | flops | bytes accessed | tf_op | source)
XLA Modules:
  0.0 123.8 jit_solution(3244523403095357643)
XLA Ops:
  0.6 0.0 copy-start.4
  0.6 0.0 copy-start.2
  0.7 0.0 copy-start.5
  0.7 0.8 copy.20
  1.5 4.2 %gru.1 = (bf16[256,512]{1,0:T(8,128)(2,1)}, s32[256,128]{1,0:T(8,128)}) custom-call(s32[1,256]{1,0:T(1,128)} %touched.1, s32[1,256]{1,0:T(1,128)} %bitcast.38, bf16[256,512]{1,0:T(8,128)(2,1)} %state.3, bf16[256,512]{1,0:T(8,128)(2,1)} %bitcast.36, bf16[512,1536]{1,0:T(8,128)(2,1)} %w_input.1, bf16[512,1536]{1,0:T(8,128)(2,1)} %w_state.1), custom_call_target="tpu_custom_call" | custom-call | flops 805306368 | bytes 4194304 | tf_op jit(solution)/shard_map/gru/pallas_call | solution.py:93
  5.7 9.4 %all-to-all-start = ((s32[32,8,128]{2,1,0:T(8,128)}), s32[32,8,128]{2,1,0:T(8,128)S(1)}, u32[]{:S(2)}, u32[]{:S(2)}) async-start(s32[32,8,128]{2,1,0:T(8,128)} %bitcast.37), calls=%async_computation | async-start | bytes 262144 | tf_op jit(solution)/shard_map/all_to_all | solution.py:446
  15.1 4.7 %collective-permute-start.2 = (bf16[256,512]{1,0:T(8,128)(2,1)}, bf16[256,512]{1,0:T(8,128)(2,1)S(1)}, u32[]{:S(2)}, u32[]{:S(2)}) collective-permute-start(bf16[256,512]{1,0:T(8,128)(2,1)} %get-tuple-element.41.written), channel_id=1, source_target_pairs={{0,96},{1,97},{2,98},{3,99},{4,100},{5,101},{6,102},{7,103},{8,104... | collective-permute-start | bytes 786440 | tf_op jit(solution)/shard_map/ppermute | solution.py:476
  19.8 1.3 %collective-permute-start.1 = (bf16[256,512]{1,0:T(8,128)(2,1)}, bf16[256,512]{1,0:T(8,128)(2,1)S(1)}, u32[]{:S(2)}, u32[]{:S(2)}) collective-permute-start(bf16[256,512]{1,0:T(8,128)(2,1)} %get-tuple-element.41.written), channel_id=1, source_target_pairs={{0,64},{32,96},{1,65},{33,97},{2,66},{34,98},{3,67},{35,99},{4,68}... | collective-permute-start | bytes 786440 | tf_op jit(solution)/shard_map/ppermute | solution.py:475
  21.1 2.5 %collective-permute-start = (bf16[256,512]{1,0:T(8,128)(2,1)}, bf16[256,512]{1,0:T(8,128)(2,1)S(1)}, u32[]{:S(2)}, u32[]{:S(2)}) collective-permute-start(bf16[256,512]{1,0:T(8,128)(2,1)} %get-tuple-element.41.written), channel_id=1, source_target_pairs={{0,32},{32,64},{64,96},{1,33},{33,65},{65,97},{2,34},{34,66},{66,9... | collective-permute-start | bytes 786440 | tf_op jit(solution)/shard_map/ppermute | solution.py:474
  23.6 0.0 all-to-all-done
  23.6 0.0 copy-start
  23.7 0.0 copy-start.1
  23.7 4.3 %time_parts.1 = (bf16[2,512,1024]{2,1,0:T(8,128)(2,1)S(1)}, bf16[2,1024,1024]{2,1,0:T(8,128)(2,1)S(1)}) custom-call(s32[8,256]{1,0:T(8,128)S(1)} %bitcast.32, f32[1,512]{1,0:T(1,128)S(1)} %bitcast.33, bf16[4,512,512]{2,1,0:T(8,128)(2,1)S(1)} %copy-done.2), custom_call_target="tpu_custom_call" | custom-call | flops 2147483648 | bytes 8388608 | tf_op jit(solution)/shard_map/time_parts/pallas_call | solution.py:138
  27.9 0.0 copy-start.6
  27.9 2.0 %copy-done.6 = bf16[2,1024,1024]{2,1,0:T(8,128)(2,1)} copy-done((bf16[2,1024,1024]{2,1,0:T(8,128)(2,1)}, bf16[2,1024,1024]{2,1,0:T(8,128)(2,1)S(1)}, u32[]{:S(2)}) %copy-start.6) | copy-done | bytes 4194328
  30.0 1.3 %copy-done.8 = bf16[2,512,1024]{2,1,0:T(8,128)(2,1)} copy-done((bf16[2,512,1024]{2,1,0:T(8,128)(2,1)}, bf16[2,512,1024]{2,1,0:T(8,128)(2,1)S(1)}, u32[]{:S(2)}) %copy-start.8) | copy-done | bytes 2097176
  31.3 0.0 collective-permute-done.2.r3
  31.3 0.0 collective-permute-done.1.r2
  31.3 1.2 collective-permute-done.r1
  32.5 0.0 copy-done
  32.5 1.2 %start_rows.1 = (bf16[256,512]{1,0:T(8,128)(2,1)}, bf16[256,512]{1,0:T(8,128)(2,1)}) custom-call(s32[1]{0:T(128)} %bitcast.2.seg, bf16[256,512]{1,0:T(8,128)(2,1)S(1)} %copy-done, bf16[256,512]{1,0:T(8,128)(2,1)S(1)} %copy-done.1, bf16[256,512]{1,0:T(8,128)(2,1)S(1)} %collective-permute-done.r1, bf16[256,512]{1,0:T(8,128)(2,1)S(1)} %collective-permute-done.1.r2, ...), custom_call_target="tpu_custom_call" | custom-call | flops 67108864 | bytes 2097152 | tf_op jit(solution)/shard_map/start_rows/pallas_call | solution.py:171
  33.8 8.1 %all-to-all-start.1 = ((bf16[32,8,512]{2,1,0:T(8,128)(2,1)}), bf16[32,8,512]{2,1,0:T(8,128)(2,1)S(1)}, u32[]{:S(2)}, u32[]{:S(2)}) async-start(bf16[32,8,512]{2,1,0:T(8,128)(2,1)} %bitcast.10), calls=%async_computation.1 | async-start | bytes 524288 | tf_op jit(solution)/shard_map/all_to_all | solution.py:446
  41.9 0.1 copy.16.chosen
  42.0 8.9 %all-to-all-done.1 = bf16[32,8,512]{2,1,0:T(8,128)(2,1)S(1)} async-done(((bf16[32,8,512]{2,1,0:T(8,128)(2,1)}), bf16[32,8,512]{2,1,0:T(8,128)(2,1)S(1)}, u32[]{:S(2)}, u32[]{:S(2)}) %all-to-all-start.1) | async-done | bytes 262176 | tf_op jit(solution)/shard_map/all_to_all | solution.py:446
  50.8 0.0 copy-done.3
  50.8 2.2 %copy-done.7 = bf16[2,1024,1024]{2,1,0:T(8,128)(2,1)S(1)} copy-done((bf16[2,1024,1024]{2,1,0:T(8,128)(2,1)S(1)}, bf16[2,1024,1024]{2,1,0:T(8,128)(2,1)}, u32[]{:S(2)}) %copy-start.7) | copy-done | bytes 4194328
  53.0 1.6 %copy-done.9 = bf16[2,512,1024]{2,1,0:T(8,128)(2,1)S(1)} copy-done((bf16[2,512,1024]{2,1,0:T(8,128)(2,1)S(1)}, bf16[2,512,1024]{2,1,0:T(8,128)(2,1)}, u32[]{:S(2)}) %copy-start.9) | copy-done | bytes 2097176
  54.6 8.5 %attend.1 = (bf16[256,512]{1,0:T(8,128)(2,1)}, bf16[256,512]{1,0:T(8,128)(2,1)S(1)}, bf16[16,64,512]{2,1,0:T(8,128)(2,1)S(1)}, bf16[16,64,512]{2,1,0:T(8,128)(2,1)S(1)}) custom-call(s32[1]{0:T(128)} %bitcast.3.core, bf16[256,512]{1,0:T(8,128)(2,1)S(1)} %bitcast.28, s32[256,9]{1,0:T(8,128)S(1)} %copy.16.chosen, s32[9,256]{1,0:T(8,128)S(1)} %bitcast.30, ...), custom_call_target="tpu_custom_call" | custom-call | flops 6442450944 | bytes 14680064 | tf_op jit(solution)/shard_map/attend/pallas_call | solution.py:297
  63.1 0.2 collective-permute-start.3
  63.3 2.5 %collective-permute-done.3.b = bf16[16,64,512]{2,1,0:T(8,128)(2,1)S(1)} collective-permute-done((bf16[16,64,512]{2,1,0:T(8,128)(2,1)S(1)}, bf16[16,64,512]{2,1,0:T(8,128)(2,1)S(1)}, u32[]{:S(2)}, u32[]{:S(2)}) %collective-permute-start.3) | collective-permute-done | bytes 1048608 | tf_op jit(solution)/shard_map/ppermute | solution.py:488
  65.7 0.3 pair_sum.1
  66.0 21.7 %all_to_all.20.a = bf16[16,80,512]{2,1,0:T(8,128)(2,1)S(1)} all-to-all(bf16[16,80,512]{2,1,0:T(8,128)(2,1)S(1)} %pair_sum.1), channel_id=1, replica_groups=mesh['y'=4,'x'=4,'z'=4,'core'=2] {'x','z'}, dimensions={0} | all-to-all | bytes 2621440 | tf_op jit(solution)/shard_map/all_to_all | solution.py:450
  87.7 0.2 plane_sum.1
  87.9 1.9 %collective-permute-start.5 = (bf16[128,512]{1,0:T(8,128)(2,1)S(1)}, bf16[128,512]{1,0:T(8,128)(2,1)S(1)}, u32[]{:S(2)}, u32[]{:S(2)}) collective-permute-start(bf16[128,512]{1,0:T(8,128)(2,1)S(1)} %get-tuple-element.55), channel_id=1, source_target_pairs={{0,1},{1,0},{2,3},{3,2},{4,5},{5,4},{6,7},{7,6},{8,9},{9,8},{10,11... | collective-permute-start | bytes 393224 | tf_op jit(solution)/shard_map/ppermute | solution.py:491
  89.8 3.6 %collective-permute-start.4 = (bf16[64,512]{1,0:T(8,128)(2,1)S(1)}, bf16[64,512]{1,0:T(8,128)(2,1)S(1)}, u32[]{:S(2)}, u32[]{:S(2)}) collective-permute-start(bf16[64,512]{1,0:T(8,128)(2,1)S(1)} %get-tuple-element.53.own), channel_id=1, source_target_pairs={{0,64},{32,96},{64,0},{96,32},{1,65},{33,97},{65,1},{97,33},{2,66}... | collective-permute-start | bytes 196616 | tf_op jit(solution)/shard_map/ppermute | solution.py:493
  93.3 0.9 collective-permute-start.7
  94.3 0.5 collective-permute-start.6
  94.8 0.0 collective-permute-done.5.got
  94.8 1.1 owner_sum.1
  95.9 0.0 collective-permute-done.4.r2
  95.9 0.5 collective-permute-done.7.r3
  96.5 2.1 %collective-permute-done.6.r1 = bf16[64,512]{1,0:T(8,128)(2,1)S(1)} collective-permute-done((bf16[64,512]{1,0:T(8,128)(2,1)S(1)}, bf16[64,512]{1,0:T(8,128)(2,1)S(1)}, u32[]{:S(2)}, u32[]{:S(2)}) %collective-permute-start.6) | collective-permute-done | bytes 65568 | tf_op jit(solution)/shard_map/ppermute | solution.py:493
  98.6 0.1 seg_sum.1
  98.7 18.1 %all_to_all.21.half = bf16[16,64,512]{2,1,0:T(8,128)(2,1)S(1)} all-to-all(bf16[16,64,512]{2,1,0:T(8,128)(2,1)S(1)} %seg_sum.1), channel_id=1, replica_groups=mesh['y'=4,'x'=4,'z'=4,'core'=2] {'x','z'}, dimensions={0} | all-to-all | bytes 2097152 | tf_op jit(solution)/shard_map/all_to_all | solution.py:450
  116.9 3.1 %collective-permute-start.8 = (bf16[16,64,512]{2,1,0:T(8,128)(2,1)S(1)}, bf16[16,64,512]{2,1,0:T(8,128)(2,1)S(1)}, u32[]{:S(2)}, u32[]{:S(2)}) collective-permute-start(bf16[16,64,512]{2,1,0:T(8,128)(2,1)S(1)} %all_to_all.21.half), channel_id=1, source_target_pairs={{0,1},{1,0},{2,3},{3,2},{4,5},{5,4},{6,7},{7,6},{8,9},{9,8},{10,11... | collective-permute-start | bytes 3145736 | tf_op jit(solution)/shard_map/ppermute | solution.py:498
  120.0 1.4 %own_half.1.rest_0_ = f32[16,2,64,512]{3,2,1,0:T(8,128)} custom-call(s32[1]{0:T(128)} %bitcast.3.core, bf16[16,64,512]{2,1,0:T(8,128)(2,1)S(1)} %all_to_all.21.half), custom_call_target="tpu_custom_call" | custom-call | flops 262144 | bytes 3145728 | tf_op jit(solution)/shard_map/own_half/pallas_call | solution.py:409
  121.3 0.9 collective-permute-done.8.half
  122.2 1.4 %far_half.1 = f32[16,2,64,512]{3,2,1,0:T(8,128)} custom-call(s32[1]{0:T(128)} %bitcast.3.core, bf16[16,64,512]{2,1,0:T(8,128)(2,1)S(1)} %collective-permute-done.8.half, f32[16,2,64,512]{3,2,1,0:T(8,128)} %own_half.1.rest_0_), custom_call_target="tpu_custom_call", output_to_operand_aliasing={{}: (2, {})} | custom-call | flops 262144 | bytes 3145728 | tf_op jit(solution)/shard_map/far_half/pallas_call | solution.py:409
  (8 shorter events, 0.0 us)
Async XLA Ops:
  0.6 23.0 %copy-start.4 = (s32[1,256,8]{1,2,0:T(8,128)S(1)}, s32[1,256,8]{1,2,0:T(8,128)}, u32[]{:S(2)}) copy-start(s32[1,256,8]{1,2,0:T(8,128)} %param.20) | copy-start | bytes 24580
  0.6 23.0 %copy-start.2 = (bf16[4,512,512]{2,1,0:T(8,128)(2,1)S(1)}, bf16[4,512,512]{2,1,0:T(8,128)(2,1)}, u32[]{:S(2)}) copy-start(bf16[4,512,512]{2,1,0:T(8,128)(2,1)} %wq.1) | copy-start | bytes 6291460
  0.7 23.0 %copy-start.5 = (f32[512]{0:T(512)S(1)}, f32[512]{0:T(512)}, u32[]{:S(2)}) copy-start(f32[512]{0:T(512)} %param.17) | copy-start | bytes 6148
  5.7 17.9 %all-to-all-start = ((s32[32,8,128]{2,1,0:T(8,128)}), s32[32,8,128]{2,1,0:T(8,128)S(1)}, u32[]{:S(2)}, u32[]{:S(2)}) async-start(s32[32,8,128]{2,1,0:T(8,128)} %bitcast.37), calls=%async_computation | async-start | bytes 262144 | tf_op jit(solution)/shard_map/all_to_all | solution.py:446
  15.1 16.2 %collective-permute-start.2 = (bf16[256,512]{1,0:T(8,128)(2,1)}, bf16[256,512]{1,0:T(8,128)(2,1)S(1)}, u32[]{:S(2)}, u32[]{:S(2)}) collective-permute-start(bf16[256,512]{1,0:T(8,128)(2,1)} %get-tuple-element.41.written), channel_id=1, source_target_pairs={{0,96},{1,97},{2,98},{3,99},{4,100},{5,101},{6,102},{7,103},{8,104... | collective-permute-start | bytes 786440 | tf_op jit(solution)/shard_map/ppermute | solution.py:476
  19.8 11.5 %collective-permute-start.1 = (bf16[256,512]{1,0:T(8,128)(2,1)}, bf16[256,512]{1,0:T(8,128)(2,1)S(1)}, u32[]{:S(2)}, u32[]{:S(2)}) collective-permute-start(bf16[256,512]{1,0:T(8,128)(2,1)} %get-tuple-element.41.written), channel_id=1, source_target_pairs={{0,64},{32,96},{1,65},{33,97},{2,66},{34,98},{3,67},{35,99},{4,68}... | collective-permute-start | bytes 786440 | tf_op jit(solution)/shard_map/ppermute | solution.py:475
  21.1 11.4 %collective-permute-start = (bf16[256,512]{1,0:T(8,128)(2,1)}, bf16[256,512]{1,0:T(8,128)(2,1)S(1)}, u32[]{:S(2)}, u32[]{:S(2)}) collective-permute-start(bf16[256,512]{1,0:T(8,128)(2,1)} %get-tuple-element.41.written), channel_id=1, source_target_pairs={{0,32},{32,64},{64,96},{1,33},{33,65},{65,97},{2,34},{34,66},{66,9... | collective-permute-start | bytes 786440 | tf_op jit(solution)/shard_map/ppermute | solution.py:474
  23.6 8.9 %copy-start = (bf16[256,512]{1,0:T(8,128)(2,1)S(1)}, bf16[256,512]{1,0:T(8,128)(2,1)}, u32[]{:S(2)}) copy-start(bf16[256,512]{1,0:T(8,128)(2,1)} %state.3) | copy-start | bytes 786436
  23.7 8.9 %copy-start.1 = (bf16[256,512]{1,0:T(8,128)(2,1)S(1)}, bf16[256,512]{1,0:T(8,128)(2,1)}, u32[]{:S(2)}) copy-start(bf16[256,512]{1,0:T(8,128)(2,1)} %get-tuple-element.41.written) | copy-start | bytes 786436
  27.9 2.0 %copy-start.6 = (bf16[2,1024,1024]{2,1,0:T(8,128)(2,1)}, bf16[2,1024,1024]{2,1,0:T(8,128)(2,1)S(1)}, u32[]{:S(2)}) copy-start(bf16[2,1024,1024]{2,1,0:T(8,128)(2,1)S(1)} %get-tuple-element.46.tkv) | copy-start | bytes 12582916
  29.9 1.3 %copy-start.8 = (bf16[2,512,1024]{2,1,0:T(8,128)(2,1)}, bf16[2,512,1024]{2,1,0:T(8,128)(2,1)S(1)}, u32[]{:S(2)}) copy-start(bf16[2,512,1024]{2,1,0:T(8,128)(2,1)S(1)} %get-tuple-element.47.tt) | copy-start | bytes 6291460
  31.3 19.6 %copy-start.3 = (bf16[1,256,512]{2,1,0:T(8,128)(2,1)S(1)}, bf16[1,256,512]{2,1,0:T(8,128)(2,1)}, u32[]{:S(2)}) copy-start(bf16[1,256,512]{2,1,0:T(8,128)(2,1)} %param.21) | copy-start | bytes 786436
  33.8 17.1 %all-to-all-start.1 = ((bf16[32,8,512]{2,1,0:T(8,128)(2,1)}), bf16[32,8,512]{2,1,0:T(8,128)(2,1)S(1)}, u32[]{:S(2)}, u32[]{:S(2)}) async-start(bf16[32,8,512]{2,1,0:T(8,128)(2,1)} %bitcast.10), calls=%async_computation.1 | async-start | bytes 524288 | tf_op jit(solution)/shard_map/all_to_all | solution.py:446
  50.8 2.2 %copy-start.7 = (bf16[2,1024,1024]{2,1,0:T(8,128)(2,1)S(1)}, bf16[2,1024,1024]{2,1,0:T(8,128)(2,1)}, u32[]{:S(2)}) copy-start(bf16[2,1024,1024]{2,1,0:T(8,128)(2,1)} %copy-done.6) | copy-start | bytes 12582916
  53.0 1.6 %copy-start.9 = (bf16[2,512,1024]{2,1,0:T(8,128)(2,1)S(1)}, bf16[2,512,1024]{2,1,0:T(8,128)(2,1)}, u32[]{:S(2)}) copy-start(bf16[2,512,1024]{2,1,0:T(8,128)(2,1)} %copy-done.8) | copy-start | bytes 6291460
  63.1 2.7 %collective-permute-start.3 = (bf16[16,64,512]{2,1,0:T(8,128)(2,1)S(1)}, bf16[16,64,512]{2,1,0:T(8,128)(2,1)S(1)}, u32[]{:S(2)}, u32[]{:S(2)}) collective-permute-start(bf16[16,64,512]{2,1,0:T(8,128)(2,1)S(1)} %get-tuple-element.51), channel_id=1, source_target_pairs={{0,1},{1,0},{2,3},{3,2},{4,5},{5,4},{6,7},{7,6},{8,9},{9,8},{10,11... | collective-permute-start | bytes 3145736 | tf_op jit(solution)/shard_map/ppermute | solution.py:488
  87.9 6.9 %collective-permute-start.5 = (bf16[128,512]{1,0:T(8,128)(2,1)S(1)}, bf16[128,512]{1,0:T(8,128)(2,1)S(1)}, u32[]{:S(2)}, u32[]{:S(2)}) collective-permute-start(bf16[128,512]{1,0:T(8,128)(2,1)S(1)} %get-tuple-element.55), channel_id=1, source_target_pairs={{0,1},{1,0},{2,3},{3,2},{4,5},{5,4},{6,7},{7,6},{8,9},{9,8},{10,11... | collective-permute-start | bytes 393224 | tf_op jit(solution)/shard_map/ppermute | solution.py:491
  89.8 6.2 %collective-permute-start.4 = (bf16[64,512]{1,0:T(8,128)(2,1)S(1)}, bf16[64,512]{1,0:T(8,128)(2,1)S(1)}, u32[]{:S(2)}, u32[]{:S(2)}) collective-permute-start(bf16[64,512]{1,0:T(8,128)(2,1)S(1)} %get-tuple-element.53.own), channel_id=1, source_target_pairs={{0,64},{32,96},{64,0},{96,32},{1,65},{33,97},{65,1},{97,33},{2,66}... | collective-permute-start | bytes 196616 | tf_op jit(solution)/shard_map/ppermute | solution.py:493
  93.3 3.1 %collective-permute-start.7 = (bf16[64,512]{1,0:T(8,128)(2,1)S(1)}, bf16[64,512]{1,0:T(8,128)(2,1)S(1)}, u32[]{:S(2)}, u32[]{:S(2)}) collective-permute-start(bf16[64,512]{1,0:T(8,128)(2,1)S(1)} %get-tuple-element.53.own), channel_id=1, source_target_pairs={{0,96},{32,0},{64,32},{96,64},{1,97},{33,1},{65,33},{97,65},{2,98}... | collective-permute-start | bytes 196616 | tf_op jit(solution)/shard_map/ppermute | solution.py:493
  94.3 4.3 %collective-permute-start.6 = (bf16[64,512]{1,0:T(8,128)(2,1)S(1)}, bf16[64,512]{1,0:T(8,128)(2,1)S(1)}, u32[]{:S(2)}, u32[]{:S(2)}) collective-permute-start(bf16[64,512]{1,0:T(8,128)(2,1)S(1)} %get-tuple-element.53.own), channel_id=1, source_target_pairs={{0,32},{32,64},{64,96},{96,0},{1,33},{33,65},{65,97},{97,1},{2,34}... | collective-permute-start | bytes 196616 | tf_op jit(solution)/shard_map/ppermute | solution.py:493
  116.9 5.4 %collective-permute-start.8 = (bf16[16,64,512]{2,1,0:T(8,128)(2,1)S(1)}, bf16[16,64,512]{2,1,0:T(8,128)(2,1)S(1)}, u32[]{:S(2)}, u32[]{:S(2)}) collective-permute-start(bf16[16,64,512]{2,1,0:T(8,128)(2,1)S(1)} %all_to_all.21.half), channel_id=1, source_target_pairs={{0,1},{1,0},{2,3},{3,2},{4,5},{5,4},{6,7},{7,6},{8,9},{9,8},{10,11... | collective-permute-start | bytes 3145736 | tf_op jit(solution)/shard_map/ppermute | solution.py:498

commit v5 on v4

--- a/solution.py
+++ b/solution.py
@@ -113,7 +113,12 @@
     )(touched, ids, state, message, w_input, w_state)
 
 
-def time_kernel(delays, frequency, w, code_t, time_kv):
+def time_kernel(delays, frequency, w, chosen, code_t, time_kv, picked):
+    lane = iota((E, 128), 1)
+    columns = jnp.zeros((E, 128), F32)
+    for j in range(K + 1):
+        columns = jnp.where(lane == j, column(chosen[j]), columns)
+    picked[...] = columns.astype(jnp.int32)
     turns = frequency[...] * (1.0 / (2.0 * math.pi))
     high = jnp.round(turns * 16384.0) * (1.0 / 16384.0)
     low = turns - high
@@ -133,22 +138,23 @@
             time_kv[tile, at, DM:] = dot(wave, w[2]).astype(BF)
 
 
-def time_parts(delays, frequency, weights):
+def time_parts(delays, frequency, weights, chosen):
     whole = pl.BlockSpec(memory_space=pltpu.VMEM)
     return pl.pallas_call(
         time_kernel,
-        in_specs=[whole] * 3,
-        out_specs=[whole] * 2,
+        in_specs=[whole] * 4,
+        out_specs=[whole] * 3,
         out_shape=[
             jax.ShapeDtypeStruct((TILES, DM, ROWS), BF),
             jax.ShapeDtypeStruct((TILES, ROWS, 2 * DM), BF),
+            jax.ShapeDtypeStruct((E, 128), jnp.int32),
         ],
         compiler_params=pltpu.CompilerParams(vmem_limit_bytes=24 << 20),
         cost_estimate=pl.CostEstimate(
             flops=4 * K * E * DM * DM, bytes_accessed=8 << 20, transcendentals=K * E * DM
         ),
         name="time_parts",
-    )(delays, frequency, weights)
+    )(delays, frequency, weights, chosen)
 
 
 def owner_pick(asked):
@@ -264,7 +270,7 @@
             step(i, j)
         spread = jnp.concatenate(
             [
-                (sub == chosen_t[1 + k : 2 + k, i * TILE : (i + 1) * TILE]).astype(F32)
+                (sub == chosen_t[1 + k, :, i * TILE : (i + 1) * TILE]).astype(F32)
                 for k in range(K)
             ],
             axis=1,
@@ -273,7 +279,7 @@
         s_kv = one if i == 0 else s_kv + one
         dot_t = two if i == 0 else dot_t + two
     s_kv = s_kv.astype(BF)
-    pick_t = (iota((SLOTS, E), 0) == chosen_t[0:1, :]).astype(F32).astype(BF)
+    pick_t = (iota((SLOTS, E), 0) == chosen_t[0]).astype(F32).astype(BF)
     s_q = dot(pick_t, dq[...]).astype(BF)
 
     def store(i, value):
@@ -468,16 +474,16 @@
     written, ids = gru(
         touched, request_rows.reshape(1, SLOTS), memory_base, messages[0], gru_input, gru_state
     )
-    written, ids, seg, core, late, chosen, chosen_t = lax.optimization_barrier(
-        (written, ids, seg, core, delays[0].T, event_slots[0], event_slots[0].T)
-    )
     r1 = lax.ppermute(written, "y", [(0, 1), (1, 2), (2, 3)])
     r2 = lax.ppermute(written, "y", [(0, 2), (1, 3)])
     r3 = lax.ppermute(written, "y", [(0, 3)])
+    written, late, seg, core = lax.optimization_barrier((written, delays[0].T, seg, core))
+    chosen_t = event_slots.transpose(2, 0, 1)
+    code_t, time_kv, chosen = time_parts(late, frequency.reshape(1, DM), attn_weights, chosen_t)
+    written, ids, code_t, time_kv, chosen = lax.optimization_barrier(
+        (written, ids, code_t, time_kv, chosen)
+    )
     asked = exchange(ids, NODE, OWNERS)
-    asked, late = lax.optimization_barrier((asked, late))
-    code_t, time_kv = time_parts(late, frequency.reshape(1, DM), attn_weights)
-    written, code_t, time_kv = lax.optimization_barrier((written, code_t, time_kv))
     memory, rows = start_rows(seg, memory_base, written, r1, r2, r3, asked)
     slots = exchange(rows, NODE, OWNERS)
     up = upstream[0]

time: 124 us -> 116 us (0.935)
  blocking collectives: 39.8 us -> 69.2 us
  starting transfers between devices: 36.1 us -> 16.5 us
  waiting for transfers between devices: 16.2 us -> 6.57 us
  local copies, waits for them, and re-layouts: 8.11 us -> 0.04 us
    all_to_all x0 -> x2, blocking collectives: none -> 29.3 us  [exchange(): lax.all_to_all(blocks, axes, split_axis=0, concat_axis=0, tiled=True)]
    all_to_all x2 -> x0, starting transfers between devices: 17.5 us -> none  [exchange(): lax.all_to_all(blocks, axes, split_axis=0, concat_axis=0, tiled=True)]
    all_to_all x2 -> x0, waiting for transfers between devices: 8.87 us -> none  [exchange(): lax.all_to_all(blocks, axes, split_axis=0, concat_axis=0, tiled=True)]
    unnamed x21 -> x16, local copies, waits for them, and re-layouts: 7.99 us -> 0.04 us
    ppermute x3, starting transfers between devices: 5.03 us -> 2.13 us  [on_device(): lax.ppermute(part, 'y', [(i, (i + s) % SEG) for i in range(SEG)])]
  transfers between devices with their start and end apart: 11 -> 9, of which waited for: 6 -> 4; matrix products, arithmetic and copies ran while one was open for 0% -> 0% of each run, Pallas kernels for 5% -> 6%
where the time goes in v5:
time: 116 us
  blocking collectives  69.2 us (60%)
  Pallas kernels  22.7 us (20%)
  starting transfers between devices  16.5 us (14%)
  waiting for transfers between devices  6.57 us (6%)
    all_to_all x2, blocking collectives, plane(): return lax.all_to_all(x, FLAT, split_axis=0, concat_axis=0, tiled=True)  39.8 us
    all_to_all x2, blocking collectives, exchange(): lax.all_to_all(blocks, axes, split_axis=0, concat_axis=0, tiled=True)  29.3 us
    pallas_call x1, Pallas kernels, attend(): pl.pallas_call(attend_kernel, in_specs=[pl.BlockSpec(memory_space=pltpu.S...  8.54 us
    ppermute x1, starting transfers between devices, on_device(): r3 = lax.ppermute(written, 'y', [(0, 3)])  5.48 us
    pallas_call x1, Pallas kernels, time_parts(): pl.pallas_call(time_kernel, in_specs=[whole] * 4, out_specs=[whole] * 3,...  4.32 us
    pallas_call x1, Pallas kernels, gru(): pl.pallas_call(gru_kernel, in_specs=[whole] * 2 + [far] * 4, out_specs=[w...  4.3 us
    ppermute x3, waiting for transfers between devices, on_device(): lax.ppermute(part, 'y', [(i, (i + s) % SEG) for i in range(SEG)])  3.2 us
    ppermute x1, starting transfers between devices, on_device(): far = lax.ppermute(half, 'core', swap)  3.07 us
  transfers between devices with their start and end apart: 9, of which 4 were waited for; matrix products, arithmetic and copies ran while one was open for 0% of the time, Pallas kernels for 6%

profile of v5, /device:TPU:1, one launch (start us, length us, event | category | flops | bytes accessed | tf_op | source)
XLA Modules:
  0.0 116.1 jit_solution(1731017681291887230)
XLA Ops:
  0.6 0.0 copy-start.5
  0.6 0.0 copy-start.2
  0.7 0.0 copy-start.4
  0.7 0.0 copy-start.6
  0.7 4.3 %gru.1 = (bf16[256,512]{1,0:T(8,128)(2,1)}, s32[256,128]{1,0:T(8,128)}) custom-call(s32[1,256]{1,0:T(1,128)} %touched.1, s32[1,256]{1,0:T(1,128)} %bitcast.34, bf16[256,512]{1,0:T(8,128)(2,1)} %state.3, bf16[256,512]{1,0:T(8,128)(2,1)} %bitcast.32, bf16[512,1536]{1,0:T(8,128)(2,1)} %w_input.1, bf16[512,1536]{1,0:T(8,128)(2,1)} %w_state.1), custom_call_target="tpu_custom_call" | custom-call | flops 805306368 | bytes 4194304 | tf_op jit(solution)/shard_map/gru/pallas_call | solution.py:93
  5.0 5.5 %collective-permute-start.2 = (bf16[256,512]{1,0:T(8,128)(2,1)}, bf16[256,512]{1,0:T(8,128)(2,1)S(1)}, u32[]{:S(2)}, u32[]{:S(2)}) collective-permute-start(bf16[256,512]{1,0:T(8,128)(2,1)} %get-tuple-element.38.written), channel_id=1, source_target_pairs={{0,96},{1,97},{2,98},{3,99},{4,100},{5,101},{6,102},{7,103},{8,104... | collective-permute-start | bytes 786440 | tf_op jit(solution)/shard_map/ppermute | solution.py:479
  10.5 1.3 %collective-permute-start.1 = (bf16[256,512]{1,0:T(8,128)(2,1)}, bf16[256,512]{1,0:T(8,128)(2,1)S(1)}, u32[]{:S(2)}, u32[]{:S(2)}) collective-permute-start(bf16[256,512]{1,0:T(8,128)(2,1)} %get-tuple-element.38.written), channel_id=1, source_target_pairs={{0,64},{32,96},{1,65},{33,97},{2,66},{34,98},{3,67},{35,99},{4,68}... | collective-permute-start | bytes 786440 | tf_op jit(solution)/shard_map/ppermute | solution.py:478
  11.8 2.5 %collective-permute-start = (bf16[256,512]{1,0:T(8,128)(2,1)}, bf16[256,512]{1,0:T(8,128)(2,1)S(1)}, u32[]{:S(2)}, u32[]{:S(2)}) collective-permute-start(bf16[256,512]{1,0:T(8,128)(2,1)} %get-tuple-element.38.written), channel_id=1, source_target_pairs={{0,32},{32,64},{64,96},{1,33},{33,65},{65,97},{2,34},{34,66},{66,9... | collective-permute-start | bytes 786440 | tf_op jit(solution)/shard_map/ppermute | solution.py:477
  14.3 0.0 copy-done.5
  14.3 0.0 copy-done.2
  14.3 0.0 copy-done.4
  14.3 0.0 copy-done.6
  14.3 0.0 copy-start.7
  14.3 0.0 copy-start
  14.4 0.0 copy-start.1
  14.4 4.3 %time_parts.1 = (bf16[2,512,1024]{2,1,0:T(8,128)(2,1)S(1)}, bf16[2,1024,1024]{2,1,0:T(8,128)(2,1)S(1)}, s32[256,128]{1,0:T(8,128)S(1)}) custom-call(s32[8,256]{1,0:T(8,128)S(1)} %bitcast.28, f32[1,512]{1,0:T(1,128)S(1)} %bitcast.29, bf16[4,512,512]{2,1,0:T(8,128)(2,1)S(1)} %copy-done.2, s32[9,1,256]{2,1,0:T(1,128)S(1)} %bitcast.26), custom_call_target="tpu_custom_call" | custom-call | flops 2147483648 | bytes 8388608 | tf_op jit(solution)/shard_map/time_parts/pallas_call | solution.py:143
  18.7 0.0 copy-start.3
  18.7 0.0 copy-done.7
  18.7 16.8 %all_to_all.20 = s32[32,8,128]{2,1,0:T(8,128)S(1)} all-to-all(s32[32,8,128]{2,1,0:T(8,128)S(1)} %bitcast.33), channel_id=1, replica_groups=mesh['y'=4,'x'=4,'z'=4,'core'=2] {'x','z','core'}, dimensions={0} | all-to-all | bytes 262144 | tf_op jit(solution)/shard_map/all_to_all | solution.py:452
  35.5 0.0 collective-permute-done.2.r3
  35.5 0.0 collective-permute-done.1.r2
  35.5 0.0 collective-permute-done.r1
  35.5 0.0 copy-done
  35.5 0.0 copy-done.1
  35.5 1.1 start_rows.1
  36.6 12.5 %all_to_all.21 = bf16[32,8,512]{2,1,0:T(8,128)(2,1)S(1)} all-to-all(bf16[32,8,512]{2,1,0:T(8,128)(2,1)S(1)} %bitcast.24), channel_id=1, replica_groups=mesh['y'=4,'x'=4,'z'=4,'core'=2] {'x','z','core'}, dimensions={0} | all-to-all | bytes 524288 | tf_op jit(solution)/shard_map/all_to_all | solution.py:452
  49.2 0.0 copy-done.3
  49.2 8.5 %attend.1 = (bf16[256,512]{1,0:T(8,128)(2,1)}, bf16[256,512]{1,0:T(8,128)(2,1)S(1)}, bf16[16,64,512]{2,1,0:T(8,128)(2,1)S(1)}, bf16[16,64,512]{2,1,0:T(8,128)(2,1)S(1)}) custom-call(s32[1]{0:T(128)} %bitcast.5.core, bf16[256,512]{1,0:T(8,128)(2,1)S(1)} %bitcast.23, s32[256,128]{1,0:T(8,128)S(1)} %get-tuple-element.41.chosen, s32[9,1,256]{2,1,0:T(1,128)S(1)} %bitcast.27, ...), custom_call_target="tpu_custom_call" | custom-call | flops 6442450944 | bytes 14680064 | tf_op jit(solution)/shard_map/attend/pallas_call | solution.py:303
  57.7 0.2 collective-permute-start.3
  57.9 2.5 %collective-permute-done.3.b = bf16[16,64,512]{2,1,0:T(8,128)(2,1)S(1)} collective-permute-done((bf16[16,64,512]{2,1,0:T(8,128)(2,1)S(1)}, bf16[16,64,512]{2,1,0:T(8,128)(2,1)S(1)}, u32[]{:S(2)}, u32[]{:S(2)}) %collective-permute-start.3) | collective-permute-done | bytes 1048608 | tf_op jit(solution)/shard_map/ppermute | solution.py:494
  60.4 0.3 pair_sum.1
  60.7 21.7 %all_to_all.22.a = bf16[16,80,512]{2,1,0:T(8,128)(2,1)S(1)} all-to-all(bf16[16,80,512]{2,1,0:T(8,128)(2,1)S(1)} %pair_sum.1), channel_id=1, replica_groups=mesh['y'=4,'x'=4,'z'=4,'core'=2] {'x','z'}, dimensions={0} | all-to-all | bytes 2621440 | tf_op jit(solution)/shard_map/all_to_all | solution.py:456
  82.4 0.2 plane_sum.1
  82.6 1.9 %collective-permute-start.5 = (bf16[128,512]{1,0:T(8,128)(2,1)S(1)}, bf16[128,512]{1,0:T(8,128)(2,1)S(1)}, u32[]{:S(2)}, u32[]{:S(2)}) collective-permute-start(bf16[128,512]{1,0:T(8,128)(2,1)S(1)} %get-tuple-element.51), channel_id=1, source_target_pairs={{0,1},{1,0},{2,3},{3,2},{4,5},{5,4},{6,7},{7,6},{8,9},{9,8},{10,11... | collective-permute-start | bytes 393224 | tf_op jit(solution)/shard_map/ppermute | solution.py:497
  84.4 0.0 collective-permute-start.4
  84.4 2.1 %collective-permute-start.7 = (bf16[64,512]{1,0:T(8,128)(2,1)S(1)}, bf16[64,512]{1,0:T(8,128)(2,1)S(1)}, u32[]{:S(2)}, u32[]{:S(2)}) collective-permute-start(bf16[64,512]{1,0:T(8,128)(2,1)S(1)} %get-tuple-element.49.own), channel_id=1, source_target_pairs={{0,96},{32,0},{64,32},{96,64},{1,97},{33,1},{65,33},{97,65},{2,98}... | collective-permute-start | bytes 196616 | tf_op jit(solution)/shard_map/ppermute | solution.py:499
  86.6 0.0 collective-permute-start.6
  86.6 0.0 collective-permute-done.5.got
  86.6 1.1 owner_sum.1
  87.7 1.9 %collective-permute-done.4.r2 = bf16[64,512]{1,0:T(8,128)(2,1)S(1)} collective-permute-done((bf16[64,512]{1,0:T(8,128)(2,1)S(1)}, bf16[64,512]{1,0:T(8,128)(2,1)S(1)}, u32[]{:S(2)}, u32[]{:S(2)}) %collective-permute-start.4) | collective-permute-done | bytes 65568 | tf_op jit(solution)/shard_map/ppermute | solution.py:499
  89.6 0.0 collective-permute-done.7.r3
  89.6 1.3 %collective-permute-done.6.r1 = bf16[64,512]{1,0:T(8,128)(2,1)S(1)} collective-permute-done((bf16[64,512]{1,0:T(8,128)(2,1)S(1)}, bf16[64,512]{1,0:T(8,128)(2,1)S(1)}, u32[]{:S(2)}, u32[]{:S(2)}) %collective-permute-start.6) | collective-permute-done | bytes 65568 | tf_op jit(solution)/shard_map/ppermute | solution.py:499
  90.9 0.1 seg_sum.1
  91.0 18.1 %all_to_all.23.half = bf16[16,64,512]{2,1,0:T(8,128)(2,1)S(1)} all-to-all(bf16[16,64,512]{2,1,0:T(8,128)(2,1)S(1)} %seg_sum.1), channel_id=1, replica_groups=mesh['y'=4,'x'=4,'z'=4,'core'=2] {'x','z'}, dimensions={0} | all-to-all | bytes 2097152 | tf_op jit(solution)/shard_map/all_to_all | solution.py:456
  109.2 3.1 %collective-permute-start.8 = (bf16[16,64,512]{2,1,0:T(8,128)(2,1)S(1)}, bf16[16,64,512]{2,1,0:T(8,128)(2,1)S(1)}, u32[]{:S(2)}, u32[]{:S(2)}) collective-permute-start(bf16[16,64,512]{2,1,0:T(8,128)(2,1)S(1)} %all_to_all.23.half), channel_id=1, source_target_pairs={{0,1},{1,0},{2,3},{3,2},{4,5},{5,4},{6,7},{7,6},{8,9},{9,8},{10,11... | collective-permute-start | bytes 3145736 | tf_op jit(solution)/shard_map/ppermute | solution.py:504
  112.2 1.4 %own_half.1.rest_0_ = f32[16,2,64,512]{3,2,1,0:T(8,128)} custom-call(s32[1]{0:T(128)} %bitcast.5.core, bf16[16,64,512]{2,1,0:T(8,128)(2,1)S(1)} %all_to_all.23.half), custom_call_target="tpu_custom_call" | custom-call | flops 262144 | bytes 3145728 | tf_op jit(solution)/shard_map/own_half/pallas_call | solution.py:415
  113.6 0.9 collective-permute-done.8.half
  114.5 1.4 %far_half.1 = f32[16,2,64,512]{3,2,1,0:T(8,128)} custom-call(s32[1]{0:T(128)} %bitcast.5.core, bf16[16,64,512]{2,1,0:T(8,128)(2,1)S(1)} %collective-permute-done.8.half, f32[16,2,64,512]{3,2,1,0:T(8,128)} %own_half.1.rest_0_), custom_call_target="tpu_custom_call", output_to_operand_aliasing={{}: (2, {})} | custom-call | flops 262144 | bytes 3145728 | tf_op jit(solution)/shard_map/far_half/pallas_call | solution.py:415
Async XLA Ops:
  0.6 13.7 %copy-start.5 = (s32[1,256,8]{1,2,0:T(8,128)S(1)}, s32[1,256,8]{1,2,0:T(8,128)}, u32[]{:S(2)}) copy-start(s32[1,256,8]{1,2,0:T(8,128)} %param.20) | copy-start | bytes 24580
  0.6 13.7 %copy-start.2 = (bf16[4,512,512]{2,1,0:T(8,128)(2,1)S(1)}, bf16[4,512,512]{2,1,0:T(8,128)(2,1)}, u32[]{:S(2)}) copy-start(bf16[4,512,512]{2,1,0:T(8,128)(2,1)} %wq.1) | copy-start | bytes 6291460
  0.7 13.7 %copy-start.4 = (s32[1,256,9]{1,0,2:T(1,128)S(1)}, s32[1,256,9]{1,0,2:T(1,128)}, u32[]{:S(2)}) copy-start(s32[1,256,9]{1,0,2:T(1,128)} %param.19) | copy-start | bytes 27652
  0.7 13.7 %copy-start.6 = (f32[512]{0:T(512)S(1)}, f32[512]{0:T(512)}, u32[]{:S(2)}) copy-start(f32[512]{0:T(512)} %param.17) | copy-start | bytes 6148
  5.0 30.5 %collective-permute-start.2 = (bf16[256,512]{1,0:T(8,128)(2,1)}, bf16[256,512]{1,0:T(8,128)(2,1)S(1)}, u32[]{:S(2)}, u32[]{:S(2)}) collective-permute-start(bf16[256,512]{1,0:T(8,128)(2,1)} %get-tuple-element.38.written), channel_id=1, source_target_pairs={{0,96},{1,97},{2,98},{3,99},{4,100},{5,101},{6,102},{7,103},{8,104... | collective-permute-start | bytes 786440 | tf_op jit(solution)/shard_map/ppermute | solution.py:479
  10.5 25.0 %collective-permute-start.1 = (bf16[256,512]{1,0:T(8,128)(2,1)}, bf16[256,512]{1,0:T(8,128)(2,1)S(1)}, u32[]{:S(2)}, u32[]{:S(2)}) collective-permute-start(bf16[256,512]{1,0:T(8,128)(2,1)} %get-tuple-element.38.written), channel_id=1, source_target_pairs={{0,64},{32,96},{1,65},{33,97},{2,66},{34,98},{3,67},{35,99},{4,68}... | collective-permute-start | bytes 786440 | tf_op jit(solution)/shard_map/ppermute | solution.py:478
  11.8 23.7 %collective-permute-start = (bf16[256,512]{1,0:T(8,128)(2,1)}, bf16[256,512]{1,0:T(8,128)(2,1)S(1)}, u32[]{:S(2)}, u32[]{:S(2)}) collective-permute-start(bf16[256,512]{1,0:T(8,128)(2,1)} %get-tuple-element.38.written), channel_id=1, source_target_pairs={{0,32},{32,64},{64,96},{1,33},{33,65},{65,97},{2,34},{34,66},{66,9... | collective-permute-start | bytes 786440 | tf_op jit(solution)/shard_map/ppermute | solution.py:477
  14.3 4.4 %copy-start.7 = (s32[256,128]{1,0:T(8,128)S(1)}, s32[256,128]{1,0:T(8,128)}, u32[]{:S(2)}) copy-start(s32[256,128]{1,0:T(8,128)} %get-tuple-element.39) | copy-start | bytes 393220
  14.3 21.2 %copy-start = (bf16[256,512]{1,0:T(8,128)(2,1)S(1)}, bf16[256,512]{1,0:T(8,128)(2,1)}, u32[]{:S(2)}) copy-start(bf16[256,512]{1,0:T(8,128)(2,1)} %state.3) | copy-start | bytes 786436
  14.4 21.2 %copy-start.1 = (bf16[256,512]{1,0:T(8,128)(2,1)S(1)}, bf16[256,512]{1,0:T(8,128)(2,1)}, u32[]{:S(2)}) copy-start(bf16[256,512]{1,0:T(8,128)(2,1)} %get-tuple-element.38.written) | copy-start | bytes 786436
  18.7 30.5 %copy-start.3 = (bf16[1,256,512]{2,1,0:T(8,128)(2,1)S(1)}, bf16[1,256,512]{2,1,0:T(8,128)(2,1)}, u32[]{:S(2)}) copy-start(bf16[1,256,512]{2,1,0:T(8,128)(2,1)} %param.21) | copy-start | bytes 786436
  57.7 2.7 %collective-permute-start.3 = (bf16[16,64,512]{2,1,0:T(8,128)(2,1)S(1)}, bf16[16,64,512]{2,1,0:T(8,128)(2,1)S(1)}, u32[]{:S(2)}, u32[]{:S(2)}) collective-permute-start(bf16[16,64,512]{2,1,0:T(8,128)(2,1)S(1)} %get-tuple-element.47), channel_id=1, source_target_pairs={{0,1},{1,0},{2,3},{3,2},{4,5},{5,4},{6,7},{7,6},{8,9},{9,8},{10,11... | collective-permute-start | bytes 3145736 | tf_op jit(solution)/shard_map/ppermute | solution.py:494
  82.6 4.0 %collective-permute-start.5 = (bf16[128,512]{1,0:T(8,128)(2,1)S(1)}, bf16[128,512]{1,0:T(8,128)(2,1)S(1)}, u32[]{:S(2)}, u32[]{:S(2)}) collective-permute-start(bf16[128,512]{1,0:T(8,128)(2,1)S(1)} %get-tuple-element.51), channel_id=1, source_target_pairs={{0,1},{1,0},{2,3},{3,2},{4,5},{5,4},{6,7},{7,6},{8,9},{9,8},{10,11... | collective-permute-start | bytes 393224 | tf_op jit(solution)/shard_map/ppermute | solution.py:497
  84.4 5.2 %collective-permute-start.4 = (bf16[64,512]{1,0:T(8,128)(2,1)S(1)}, bf16[64,512]{1,0:T(8,128)(2,1)S(1)}, u32[]{:S(2)}, u32[]{:S(2)}) collective-permute-start(bf16[64,512]{1,0:T(8,128)(2,1)S(1)} %get-tuple-element.49.own), channel_id=1, source_target_pairs={{0,64},{32,96},{64,0},{96,32},{1,65},{33,97},{65,1},{97,33},{2,66}... | collective-permute-start | bytes 196616 | tf_op jit(solution)/shard_map/ppermute | solution.py:499
  84.4 5.2 %collective-permute-start.7 = (bf16[64,512]{1,0:T(8,128)(2,1)S(1)}, bf16[64,512]{1,0:T(8,128)(2,1)S(1)}, u32[]{:S(2)}, u32[]{:S(2)}) collective-permute-start(bf16[64,512]{1,0:T(8,128)(2,1)S(1)} %get-tuple-element.49.own), channel_id=1, source_target_pairs={{0,96},{32,0},{64,32},{96,64},{1,97},{33,1},{65,33},{97,65},{2,98}... | collective-permute-start | bytes 196616 | tf_op jit(solution)/shard_map/ppermute | solution.py:499
  86.6 4.3 %collective-permute-start.6 = (bf16[64,512]{1,0:T(8,128)(2,1)S(1)}, bf16[64,512]{1,0:T(8,128)(2,1)S(1)}, u32[]{:S(2)}, u32[]{:S(2)}) collective-permute-start(bf16[64,512]{1,0:T(8,128)(2,1)S(1)} %get-tuple-element.49.own), channel_id=1, source_target_pairs={{0,32},{32,64},{64,96},{96,0},{1,33},{33,65},{65,97},{97,1},{2,34}... | collective-permute-start | bytes 196616 | tf_op jit(solution)/shard_map/ppermute | solution.py:499
  109.2 5.4 %collective-permute-start.8 = (bf16[16,64,512]{2,1,0:T(8,128)(2,1)S(1)}, bf16[16,64,512]{2,1,0:T(8,128)(2,1)S(1)}, u32[]{:S(2)}, u32[]{:S(2)}) collective-permute-start(bf16[16,64,512]{2,1,0:T(8,128)(2,1)S(1)} %all_to_all.23.half), channel_id=1, source_target_pairs={{0,1},{1,0},{2,3},{3,2},{4,5},{5,4},{6,7},{7,6},{8,9},{9,8},{10,11... | collective-permute-start | bytes 3145736 | tf_op jit(solution)/shard_map/ppermute | solution.py:504

commit v6 on v5

--- a/solution.py
+++ b/solution.py
@@ -67,22 +67,36 @@
 def gru_kernel(
     touched, ids, state, message, w_input, w_state, out, spread, st, ms, wi, ws, sem
 ):
-    moves = ((state, st), (w_state, ws), (message, ms), (w_input, wi))
+    near, rest = pl.ds(0, DM // 2), pl.ds(DM // 2, DM // 2)
+    moves = (
+        (state, st),
+        (w_state.at[near], ws.at[near]),
+        (w_state.at[rest], ws.at[rest]),
+        (message, ms),
+        (w_input.at[near], wi.at[near]),
+        (w_input.at[rest], wi.at[rest]),
+    )
     copies = [pltpu.make_async_copy(a, b, sem.at[i]) for i, (a, b) in enumerate(moves)]
     for copy in copies:
         copy.start()
     keep = column(touched[...]) > 0.5
     spread[...] = jnp.broadcast_to(column(ids[...]), (SLOTS, 128)).astype(jnp.int32)
-    copies[0].wait()
-    copies[1].wait()
+
+    def product(rows, w, waits):
+        waits[0].wait()
+        waits[1].wait()
+        low = [dot(rows[:, : DM // 2], w[: DM // 2, i * DM : (i + 1) * DM]) for i in range(3)]
+        waits[2].wait()
+        return [
+            low[i] + dot(rows[:, DM // 2 :], w[DM // 2 :, i * DM : (i + 1) * DM]) for i in range(3)
+        ]
+
+    from_state = product(st, ws, copies[:3])
+    from_msg = product(ms, wi, copies[3:])
     s = st[...]
-    from_state = [dot(s, ws[:, i * DM : (i + 1) * DM]) for i in range(3)]
-    copies[2].wait()
-    copies[3].wait()
-    m = ms[...]
-    update = jax.nn.sigmoid(dot(m, wi[:, :DM]) + from_state[0])
-    reset = jax.nn.sigmoid(dot(m, wi[:, DM : 2 * DM]) + from_state[1])
-    candidate = jnp.tanh(dot(m, wi[:, 2 * DM :]) + reset * from_state[2])
+    update = jax.nn.sigmoid(from_msg[0] + from_state[0])
+    reset = jax.nn.sigmoid(from_msg[1] + from_state[1])
+    candidate = jnp.tanh(from_msg[2] + reset * from_state[2])
     fresh = (1.0 - update) * candidate + update * s.astype(F32)
     out[...] = jnp.where(keep, fresh, ABSENT).astype(BF)
 
@@ -103,7 +117,7 @@
             pltpu.VMEM((N, DM), BF),
             pltpu.VMEM((DM, 3 * DM), BF),
             pltpu.VMEM((DM, 3 * DM), BF),
-            pltpu.SemaphoreType.DMA((4,)),
+            pltpu.SemaphoreType.DMA((6,)),
         ],
         compiler_params=pltpu.CompilerParams(vmem_limit_bytes=56 << 20),
         cost_estimate=pl.CostEstimate(
@@ -113,7 +127,7 @@
     )(touched, ids, state, message, w_input, w_state)
 
 
-def time_kernel(delays, frequency, w, chosen, code_t, time_kv, picked):
+def time_kernel(delays, frequency, w, chosen, times, picked, held, sem):
     lane = iota((E, 128), 1)
     columns = jnp.zeros((E, 128), F32)
     for j in range(K + 1):
@@ -122,6 +136,7 @@
     turns = frequency[...] * (1.0 / (2.0 * math.pi))
     high = jnp.round(turns * 16384.0) * (1.0 / 16384.0)
     low = turns - high
+    copies = []
     for tile in range(TILES):
         for k in range(K):
             delay = column(delays[k : k + 1, tile * TILE : (tile + 1) * TILE])
@@ -132,24 +147,40 @@
             for c in COS[-2::-1]:
                 wave = wave * u + c
             at = slice(k * TILE, (k + 1) * TILE)
-            code_t[tile, :, at] = wave.T.astype(BF)
+            held[tile, ROWS:, at] = wave.T.astype(BF)
             wave = wave.astype(BF)
-            time_kv[tile, at, :DM] = dot(wave, w[1]).astype(BF)
-            time_kv[tile, at, DM:] = dot(wave, w[2]).astype(BF)
+            held[tile, at, :DM] = dot(wave, w[1]).astype(BF)
+            held[tile, at, DM:] = dot(wave, w[2]).astype(BF)
+            moves = []
+            if k % 2 == 1:
+                moves.append(pl.ds((k - 1) * TILE, 2 * TILE))
+            if k == K - 1:
+                moves.append(pl.ds(ROWS, DM))
+            for rows in moves:
+                n = len(copies)
+                copy = pltpu.make_async_copy(held.at[tile, rows], times.at[tile, rows], sem.at[n])
+                copy.start()
+                copies.append(copy)
+    for copy in copies:
+        copy.wait()
 
 
 def time_parts(delays, frequency, weights, chosen):
     whole = pl.BlockSpec(memory_space=pltpu.VMEM)
+    far = pl.BlockSpec(memory_space=pl.ANY)
     return pl.pallas_call(
         time_kernel,
         in_specs=[whole] * 4,
-        out_specs=[whole] * 3,
+        out_specs=[far, whole],
         out_shape=[
-            jax.ShapeDtypeStruct((TILES, DM, ROWS), BF),
-            jax.ShapeDtypeStruct((TILES, ROWS, 2 * DM), BF),
+            jax.ShapeDtypeStruct((TILES, ROWS + DM, ROWS), BF),
             jax.ShapeDtypeStruct((E, 128), jnp.int32),
         ],
-        compiler_params=pltpu.CompilerParams(vmem_limit_bytes=24 << 20),
+        scratch_shapes=[
+            pltpu.VMEM((TILES, ROWS + DM, ROWS), BF),
+            pltpu.SemaphoreType.DMA((TILES * (K // 2 + 1),)),
+        ],
+        compiler_params=pltpu.CompilerParams(vmem_limit_bytes=56 << 20),
         cost_estimate=pl.CostEstimate(
             flops=4 * K * E * DM * DM, bytes_accessed=8 << 20, transcendentals=K * E * DM
         ),
@@ -191,10 +222,15 @@
 
 
 def attend_kernel(
-    core, slots, chosen, chosen_t, tkv, tt, up, wq,
+    core, slots, chosen, chosen_t, times, up, wq,
     embedded, d_slots, mine, other,
-    skv, d_att, qf, src, both, dkv, att, dq, sums,
+    tkv, tt, sem, skv, d_att, qf, src, both, dkv, att, dq, sums,
 ):
+    moves = [(times.at[i, pl.ds(0, ROWS)], tkv.at[i]) for i in range(TILES)]
+    moves += [(times.at[i, pl.ds(ROWS, DM)], tt.at[i]) for i in range(TILES)]
+    copies = [pltpu.make_async_copy(a, b, sem.at[i]) for i, (a, b) in enumerate(moves)]
+    for i in (0, 2, 1, 3):
+        copies[i].start()
     rows = slots[...]
     pick = (chosen[:, 0:1] == iota((E, SLOTS), 1)).astype(F32).astype(BF)
     src[...] = dot(pick, rows)
@@ -266,8 +302,10 @@
     sub = iota((SLOTS, TILE), 0)
     s_kv = dot_t = None
     for i in range(TILES):
+        copies[i].wait()
         for j in range(TILE // STEP):
             step(i, j)
+        copies[TILES + i].wait()
         spread = jnp.concatenate(
             [
                 (sub == chosen_t[1 + k, :, i * TILE : (i + 1) * TILE]).astype(F32)
@@ -298,11 +336,12 @@
     d_slots[...] = grads.astype(BF)
 
 
-def attend(core, slots, chosen, chosen_t, time_kv, code_t, up, weights):
-    whole = pl.BlockSpec(memory_space=pltpu.VMEM)
+def attend(core, slots, chosen, chosen_t, times, up, weights):
+    whole = pl.BlockSpec(memory_space=pltpu.VMEM)
+    far = pl.BlockSpec(memory_space=pl.ANY)
     return pl.pallas_call(
         attend_kernel,
-        in_specs=[pl.BlockSpec(memory_space=pltpu.SMEM)] + [whole] * 7,
+        in_specs=[pl.BlockSpec(memory_space=pltpu.SMEM)] + [whole] * 3 + [far] + [whole] * 2,
         out_specs=[whole] * 4,
         out_shape=[
             jax.ShapeDtypeStruct((E, DM), BF),
@@ -311,6 +350,9 @@
             jax.ShapeDtypeStruct((PLANE, PIECE, DM), BF),
         ],
         scratch_shapes=[
+            pltpu.VMEM((TILES, ROWS, 2 * DM), BF),
+            pltpu.VMEM((TILES, DM, ROWS), BF),
+            pltpu.SemaphoreType.DMA((2 * TILES,)),
             pltpu.VMEM((SLOTS, 2 * DM), BF),
             pltpu.VMEM((E, DM), F32),
             pltpu.VMEM((E, DM), F32),
@@ -321,12 +363,12 @@
             pltpu.VMEM((E, DM), BF),
             pltpu.VMEM((PLANE, CORES, PIECE, DM), BF),
         ],
-        compiler_params=pltpu.CompilerParams(vmem_limit_bytes=40 << 20),
+        compiler_params=pltpu.CompilerParams(vmem_limit_bytes=49 << 20),
         cost_estimate=pl.CostEstimate(
             flops=6 << 30, bytes_accessed=14 << 20, transcendentals=E * 128
         ),
         name="attend",
-    )(core, slots, chosen, chosen_t, time_kv, code_t, up, weights)
+    )(core, slots, chosen, chosen_t, times, up, weights)
 
 
 def pair_kernel(a, b, d_slots, out):
@@ -477,18 +519,16 @@
     r1 = lax.ppermute(written, "y", [(0, 1), (1, 2), (2, 3)])
     r2 = lax.ppermute(written, "y", [(0, 2), (1, 3)])
     r3 = lax.ppermute(written, "y", [(0, 3)])
+    asked = exchange(ids, NODE, OWNERS)
     written, late, seg, core = lax.optimization_barrier((written, delays[0].T, seg, core))
     chosen_t = event_slots.transpose(2, 0, 1)
-    code_t, time_kv, chosen = time_parts(late, frequency.reshape(1, DM), attn_weights, chosen_t)
-    written, ids, code_t, time_kv, chosen = lax.optimization_barrier(
-        (written, ids, code_t, time_kv, chosen)
-    )
-    asked = exchange(ids, NODE, OWNERS)
+    times, chosen = time_parts(late, frequency.reshape(1, DM), attn_weights, chosen_t)
+    written, times, chosen = lax.optimization_barrier((written, times, chosen))
     memory, rows = start_rows(seg, memory_base, written, r1, r2, r3, asked)
     slots = exchange(rows, NODE, OWNERS)
     up = upstream[0]
     embedded, d_slots, mine, other = attend(
-        core, slots, chosen, chosen_t, time_kv, code_t, up, attn_weights
+        core, slots, chosen, chosen_t, times, up, attn_weights
     )
     swap = [(0, 1), (1, 0)]
     partner = lax.ppermute(other, "core", swap)

time: 116 us -> 123 us (1.060)
  blocking collectives: 69.2 us -> 56 us
  starting transfers between devices: 16.5 us -> 25.8 us
  Pallas kernels: 22.7 us -> 31.9 us
  local copies, waits for them, and re-layouts: 0.04 us -> 1.88 us
    all_to_all x2 -> x1, blocking collectives: 29.3 us -> 16.2 us  [exchange(): lax.all_to_all(blocks, axes, split_axis=0, concat_axis=0, tiled=True)]
    all_to_all x0 -> x1, starting transfers between devices: none -> 9.17 us  [exchange(): lax.all_to_all(blocks, axes, split_axis=0, concat_axis=0, tiled=True)]
    pallas_call x1, Pallas kernels: 8.54 us -> 13.8 us  [attend(): pl.pallas_call(attend_kernel, in_specs=[pl.BlockSpec(memory_space=pltpu.S...]
    pallas_call x1, Pallas kernels: 4.32 us -> 8.24 us  [time_parts(): pl.pallas_call(time_kernel, in_specs=[whole] * 4, out_specs=[far, whole],...]
    unnamed x16 -> x12, local copies, waits for them, and re-layouts: 0.04 us -> 1.88 us
  transfers between devices with their start and end apart: 9 -> 10, of which waited for: 4 -> 4; matrix products, arithmetic and copies ran while one was open for 0% -> 0% of each run, Pallas kernels for 6% -> 9%
where the time goes in v6:
time: 123 us
  blocking collectives  56 us (46%)
  Pallas kernels  31.9 us (26%)
  starting transfers between devices  25.8 us (21%)
  waiting for transfers between devices  6.58 us (5%)
  local copies, waits for them, and re-layouts  1.88 us (2%)
    all_to_all x2, blocking collectives, plane(): return lax.all_to_all(x, FLAT, split_axis=0, concat_axis=0, tiled=True)  39.8 us
    all_to_all x1, blocking collectives, exchange(): lax.all_to_all(blocks, axes, split_axis=0, concat_axis=0, tiled=True)  16.2 us
    pallas_call x1, Pallas kernels, attend(): pl.pallas_call(attend_kernel, in_specs=[pl.BlockSpec(memory_space=pltpu.S...  13.8 us
    all_to_all x1, starting transfers between devices, exchange(): lax.all_to_all(blocks, axes, split_axis=0, concat_axis=0, tiled=True)  9.17 us
    pallas_call x1, Pallas kernels, time_parts(): pl.pallas_call(time_kernel, in_specs=[whole] * 4, out_specs=[far, whole],...  8.24 us
    ppermute x1, starting transfers between devices, on_device(): r3 = lax.ppermute(written, 'y', [(0, 3)])  5.49 us
    pallas_call x1, Pallas kernels, gru(): pl.pallas_call(gru_kernel, in_specs=[whole] * 2 + [far] * 4, out_specs=[w...  4.21 us
    ppermute x3, waiting for transfers between devices, on_device(): lax.ppermute(part, 'y', [(i, (i + s) % SEG) for i in range(SEG)])  3.2 us
  transfers between devices with their start and end apart: 10, of which 4 were waited for; matrix products, arithmetic and copies ran while one was open for 0% of the time, Pallas kernels for 9%

profile of v6, /device:TPU:1, one launch (start us, length us, event | category | flops | bytes accessed | tf_op | source)
XLA Modules:
  0.0 123.1 jit_solution(10628170702110349706)
XLA Ops:
  0.6 4.2 %gru.1 = (bf16[256,512]{1,0:T(8,128)(2,1)}, s32[256,128]{1,0:T(8,128)}) custom-call(s32[1,256]{1,0:T(1,128)} %touched.1, s32[1,256]{1,0:T(1,128)} %bitcast.32, bf16[256,512]{1,0:T(8,128)(2,1)} %state.3, bf16[256,512]{1,0:T(8,128)(2,1)} %bitcast.30, bf16[512,1536]{1,0:T(8,128)(2,1)} %w_input.1, bf16[512,1536]{1,0:T(8,128)(2,1)} %w_state.1), custom_call_target="tpu_custom_call" | custom-call | flops 805306368 | bytes 4194304 | tf_op jit(solution)/shard_map/gru/pallas_call | solution.py:107
  4.8 5.5 %collective-permute-start.2 = (bf16[256,512]{1,0:T(8,128)(2,1)}, bf16[256,512]{1,0:T(8,128)(2,1)S(1)}, u32[]{:S(2)}, u32[]{:S(2)}) collective-permute-start(bf16[256,512]{1,0:T(8,128)(2,1)} %get-tuple-element.33.written), channel_id=1, source_target_pairs={{0,96},{1,97},{2,98},{3,99},{4,100},{5,101},{6,102},{7,103},{8,104... | collective-permute-start | bytes 786440 | tf_op jit(solution)/shard_map/ppermute | solution.py:521
  10.3 1.3 %collective-permute-start.1 = (bf16[256,512]{1,0:T(8,128)(2,1)}, bf16[256,512]{1,0:T(8,128)(2,1)S(1)}, u32[]{:S(2)}, u32[]{:S(2)}) collective-permute-start(bf16[256,512]{1,0:T(8,128)(2,1)} %get-tuple-element.33.written), channel_id=1, source_target_pairs={{0,64},{32,96},{1,65},{33,97},{2,66},{34,98},{3,67},{35,99},{4,68}... | collective-permute-start | bytes 786440 | tf_op jit(solution)/shard_map/ppermute | solution.py:520
  11.7 2.5 %collective-permute-start = (bf16[256,512]{1,0:T(8,128)(2,1)}, bf16[256,512]{1,0:T(8,128)(2,1)S(1)}, u32[]{:S(2)}, u32[]{:S(2)}) collective-permute-start(bf16[256,512]{1,0:T(8,128)(2,1)} %get-tuple-element.33.written), channel_id=1, source_target_pairs={{0,32},{32,64},{64,96},{1,33},{33,65},{65,97},{2,34},{34,66},{66,9... | collective-permute-start | bytes 786440 | tf_op jit(solution)/shard_map/ppermute | solution.py:519
  14.1 9.2 %all-to-all-start = ((s32[32,8,128]{2,1,0:T(8,128)}), s32[32,8,128]{2,1,0:T(8,128)S(1)}, u32[]{:S(2)}, u32[]{:S(2)}) async-start(s32[32,8,128]{2,1,0:T(8,128)} %bitcast.31), calls=%async_computation | async-start | bytes 262144 | tf_op jit(solution)/shard_map/all_to_all | solution.py:494
  23.3 0.0 copy-start
  23.3 0.0 copy-start.1
  23.4 0.0 copy-start.2
  23.4 0.0 copy-start.4
  23.4 8.2 %time_parts.1 = (bf16[2,1536,1024]{2,1,0:T(8,128)(2,1)}, s32[256,128]{1,0:T(8,128)}) custom-call(s32[8,256]{1,0:T(8,128)} %bitcast.34, f32[1,512]{1,0:T(1,128)} %bitcast.35, bf16[4,512,512]{2,1,0:T(8,128)(2,1)} %wq.1, s32[9,1,256]{2,1,0:T(1,128)} %bitcast.26), custom_call_target="tpu_custom_call" | custom-call | flops 2147483648 | bytes 8388608 | tf_op jit(solution)/shard_map/time_parts/pallas_call | solution.py:171
  31.6 0.0 all-to-all-done
  31.6 0.0 collective-permute-done.2.r3
  31.7 0.0 collective-permute-done.1.r2
  31.7 0.0 collective-permute-done.r1
  31.7 0.0 copy-done
  31.7 0.0 copy-done.1
  31.7 1.1 start_rows.1
  32.8 16.2 %all_to_all.20 = bf16[32,8,512]{2,1,0:T(8,128)(2,1)S(1)} all-to-all(bf16[32,8,512]{2,1,0:T(8,128)(2,1)S(1)} %bitcast.24), channel_id=1, replica_groups=mesh['y'=4,'x'=4,'z'=4,'core'=2] {'x','z','core'}, dimensions={0} | all-to-all | bytes 524288 | tf_op jit(solution)/shard_map/all_to_all | solution.py:494
  48.9 0.0 copy-done.2
  48.9 0.0 copy-done.4
  48.9 0.0 copy-start.3
  48.9 0.9 copy-done.3
  49.9 0.0 copy-start.5
  49.9 0.9 copy-done.5
  50.8 13.8 %attend.1 = (bf16[256,512]{1,0:T(8,128)(2,1)}, bf16[256,512]{1,0:T(8,128)(2,1)S(1)}, bf16[16,64,512]{2,1,0:T(8,128)(2,1)S(1)}, bf16[16,64,512]{2,1,0:T(8,128)(2,1)S(1)}) custom-call(s32[1]{0:T(128)} %bitcast.5.core, bf16[256,512]{1,0:T(8,128)(2,1)S(1)} %bitcast.23, s32[256,128]{1,0:T(8,128)S(1)} %copy-done.5, s32[9,1,256]{2,1,0:T(1,128)S(1)} %bitcast.27, ...), custom_call_target="tpu_custom_call" | custom-call | flops 6442450944 | bytes 14680064 | tf_op jit(solution)/shard_map/attend/pallas_call | solution.py:342
  64.6 0.3 collective-permute-start.3
  64.9 2.5 %collective-permute-done.3.b = bf16[16,64,512]{2,1,0:T(8,128)(2,1)S(1)} collective-permute-done((bf16[16,64,512]{2,1,0:T(8,128)(2,1)S(1)}, bf16[16,64,512]{2,1,0:T(8,128)(2,1)S(1)}, u32[]{:S(2)}, u32[]{:S(2)}) %collective-permute-start.3) | collective-permute-done | bytes 1048608 | tf_op jit(solution)/shard_map/ppermute | solution.py:534
  67.4 0.3 pair_sum.1
  67.7 21.7 %all_to_all.21.a = bf16[16,80,512]{2,1,0:T(8,128)(2,1)S(1)} all-to-all(bf16[16,80,512]{2,1,0:T(8,128)(2,1)S(1)} %pair_sum.1), channel_id=1, replica_groups=mesh['y'=4,'x'=4,'z'=4,'core'=2] {'x','z'}, dimensions={0} | all-to-all | bytes 2621440 | tf_op jit(solution)/shard_map/all_to_all | solution.py:498
  89.4 0.2 plane_sum.1
  89.6 1.9 %collective-permute-start.5 = (bf16[128,512]{1,0:T(8,128)(2,1)S(1)}, bf16[128,512]{1,0:T(8,128)(2,1)S(1)}, u32[]{:S(2)}, u32[]{:S(2)}) collective-permute-start(bf16[128,512]{1,0:T(8,128)(2,1)S(1)} %get-tuple-element.45), channel_id=1, source_target_pairs={{0,1},{1,0},{2,3},{3,2},{4,5},{5,4},{6,7},{7,6},{8,9},{9,8},{10,11... | collective-permute-start | bytes 393224 | tf_op jit(solution)/shard_map/ppermute | solution.py:537
  91.4 0.0 collective-permute-start.4
  91.4 2.1 %collective-permute-start.7 = (bf16[64,512]{1,0:T(8,128)(2,1)S(1)}, bf16[64,512]{1,0:T(8,128)(2,1)S(1)}, u32[]{:S(2)}, u32[]{:S(2)}) collective-permute-start(bf16[64,512]{1,0:T(8,128)(2,1)S(1)} %get-tuple-element.43.own), channel_id=1, source_target_pairs={{0,96},{32,0},{64,32},{96,64},{1,97},{33,1},{65,33},{97,65},{2,98}... | collective-permute-start | bytes 196616 | tf_op jit(solution)/shard_map/ppermute | solution.py:539
  93.6 0.0 collective-permute-start.6
  93.6 0.0 collective-permute-done.5.got
  93.6 1.1 owner_sum.1
  94.7 1.9 %collective-permute-done.4.r2 = bf16[64,512]{1,0:T(8,128)(2,1)S(1)} collective-permute-done((bf16[64,512]{1,0:T(8,128)(2,1)S(1)}, bf16[64,512]{1,0:T(8,128)(2,1)S(1)}, u32[]{:S(2)}, u32[]{:S(2)}) %collective-permute-start.4) | collective-permute-done | bytes 65568 | tf_op jit(solution)/shard_map/ppermute | solution.py:539
  96.6 0.0 collective-permute-done.7.r3
  96.6 1.3 %collective-permute-done.6.r1 = bf16[64,512]{1,0:T(8,128)(2,1)S(1)} collective-permute-done((bf16[64,512]{1,0:T(8,128)(2,1)S(1)}, bf16[64,512]{1,0:T(8,128)(2,1)S(1)}, u32[]{:S(2)}, u32[]{:S(2)}) %collective-permute-start.6) | collective-permute-done | bytes 65568 | tf_op jit(solution)/shard_map/ppermute | solution.py:539
  97.9 0.1 seg_sum.1
  98.0 18.1 %all_to_all.22.half = bf16[16,64,512]{2,1,0:T(8,128)(2,1)S(1)} all-to-all(bf16[16,64,512]{2,1,0:T(8,128)(2,1)S(1)} %seg_sum.1), channel_id=1, replica_groups=mesh['y'=4,'x'=4,'z'=4,'core'=2] {'x','z'}, dimensions={0} | all-to-all | bytes 2097152 | tf_op jit(solution)/shard_map/all_to_all | solution.py:498
  116.2 3.1 %collective-permute-start.8 = (bf16[16,64,512]{2,1,0:T(8,128)(2,1)S(1)}, bf16[16,64,512]{2,1,0:T(8,128)(2,1)S(1)}, u32[]{:S(2)}, u32[]{:S(2)}) collective-permute-start(bf16[16,64,512]{2,1,0:T(8,128)(2,1)S(1)} %all_to_all.22.half), channel_id=1, source_target_pairs={{0,1},{1,0},{2,3},{3,2},{4,5},{5,4},{6,7},{7,6},{8,9},{9,8},{10,11... | collective-permute-start | bytes 3145736 | tf_op jit(solution)/shard_map/ppermute | solution.py:544
  119.2 1.4 %own_half.1.rest_0_ = f32[16,2,64,512]{3,2,1,0:T(8,128)} custom-call(s32[1]{0:T(128)} %bitcast.5.core, bf16[16,64,512]{2,1,0:T(8,128)(2,1)S(1)} %all_to_all.22.half), custom_call_target="tpu_custom_call" | custom-call | flops 262144 | bytes 3145728 | tf_op jit(solution)/shard_map/own_half/pallas_call | solution.py:457
  120.6 0.9 collective-permute-done.8.half
  121.5 1.4 %far_half.1 = f32[16,2,64,512]{3,2,1,0:T(8,128)} custom-call(s32[1]{0:T(128)} %bitcast.5.core, bf16[16,64,512]{2,1,0:T(8,128)(2,1)S(1)} %collective-permute-done.8.half, f32[16,2,64,512]{3,2,1,0:T(8,128)} %own_half.1.rest_0_), custom_call_target="tpu_custom_call", output_to_operand_aliasing={{}: (2, {})} | custom-call | flops 262144 | bytes 3145728 | tf_op jit(solution)/shard_map/far_half/pallas_call | solution.py:457
Async XLA Ops:
  4.8 26.8 %collective-permute-start.2 = (bf16[256,512]{1,0:T(8,128)(2,1)}, bf16[256,512]{1,0:T(8,128)(2,1)S(1)}, u32[]{:S(2)}, u32[]{:S(2)}) collective-permute-start(bf16[256,512]{1,0:T(8,128)(2,1)} %get-tuple-element.33.written), channel_id=1, source_target_pairs={{0,96},{1,97},{2,98},{3,99},{4,100},{5,101},{6,102},{7,103},{8,104... | collective-permute-start | bytes 786440 | tf_op jit(solution)/shard_map/ppermute | solution.py:521
  10.3 21.3 %collective-permute-start.1 = (bf16[256,512]{1,0:T(8,128)(2,1)}, bf16[256,512]{1,0:T(8,128)(2,1)S(1)}, u32[]{:S(2)}, u32[]{:S(2)}) collective-permute-start(bf16[256,512]{1,0:T(8,128)(2,1)} %get-tuple-element.33.written), channel_id=1, source_target_pairs={{0,64},{32,96},{1,65},{33,97},{2,66},{34,98},{3,67},{35,99},{4,68}... | collective-permute-start | bytes 786440 | tf_op jit(solution)/shard_map/ppermute | solution.py:520
  11.7 20.0 %collective-permute-start = (bf16[256,512]{1,0:T(8,128)(2,1)}, bf16[256,512]{1,0:T(8,128)(2,1)S(1)}, u32[]{:S(2)}, u32[]{:S(2)}) collective-permute-start(bf16[256,512]{1,0:T(8,128)(2,1)} %get-tuple-element.33.written), channel_id=1, source_target_pairs={{0,32},{32,64},{64,96},{1,33},{33,65},{65,97},{2,34},{34,66},{66,9... | collective-permute-start | bytes 786440 | tf_op jit(solution)/shard_map/ppermute | solution.py:519
  14.1 17.5 %all-to-all-start = ((s32[32,8,128]{2,1,0:T(8,128)}), s32[32,8,128]{2,1,0:T(8,128)S(1)}, u32[]{:S(2)}, u32[]{:S(2)}) async-start(s32[32,8,128]{2,1,0:T(8,128)} %bitcast.31), calls=%async_computation | async-start | bytes 262144 | tf_op jit(solution)/shard_map/all_to_all | solution.py:494
  23.3 8.3 %copy-start = (bf16[256,512]{1,0:T(8,128)(2,1)S(1)}, bf16[256,512]{1,0:T(8,128)(2,1)}, u32[]{:S(2)}) copy-start(bf16[256,512]{1,0:T(8,128)(2,1)} %state.3) | copy-start | bytes 786436
  23.3 8.3 %copy-start.1 = (bf16[256,512]{1,0:T(8,128)(2,1)S(1)}, bf16[256,512]{1,0:T(8,128)(2,1)}, u32[]{:S(2)}) copy-start(bf16[256,512]{1,0:T(8,128)(2,1)} %get-tuple-element.33.written) | copy-start | bytes 786436
  23.4 25.6 %copy-start.2 = (bf16[4,512,512]{2,1,0:T(8,128)(2,1)S(1)}, bf16[4,512,512]{2,1,0:T(8,128)(2,1)}, u32[]{:S(2)}) copy-start(bf16[4,512,512]{2,1,0:T(8,128)(2,1)} %wq.1) | copy-start | bytes 6291460
  23.4 25.6 %copy-start.4 = (s32[1,256,9]{1,0,2:T(1,128)S(1)}, s32[1,256,9]{1,0,2:T(1,128)}, u32[]{:S(2)}) copy-start(s32[1,256,9]{1,0,2:T(1,128)} %param.19) | copy-start | bytes 27652
  48.9 1.0 copy-start.3
  49.9 0.9 copy-start.5
  64.6 2.7 %collective-permute-start.3 = (bf16[16,64,512]{2,1,0:T(8,128)(2,1)S(1)}, bf16[16,64,512]{2,1,0:T(8,128)(2,1)S(1)}, u32[]{:S(2)}, u32[]{:S(2)}) collective-permute-start(bf16[16,64,512]{2,1,0:T(8,128)(2,1)S(1)} %get-tuple-element.41), channel_id=1, source_target_pairs={{0,1},{1,0},{2,3},{3,2},{4,5},{5,4},{6,7},{7,6},{8,9},{9,8},{10,11... | collective-permute-start | bytes 3145736 | tf_op jit(solution)/shard_map/ppermute | solution.py:534
  89.6 4.0 %collective-permute-start.5 = (bf16[128,512]{1,0:T(8,128)(2,1)S(1)}, bf16[128,512]{1,0:T(8,128)(2,1)S(1)}, u32[]{:S(2)}, u32[]{:S(2)}) collective-permute-start(bf16[128,512]{1,0:T(8,128)(2,1)S(1)} %get-tuple-element.45), channel_id=1, source_target_pairs={{0,1},{1,0},{2,3},{3,2},{4,5},{5,4},{6,7},{7,6},{8,9},{9,8},{10,11... | collective-permute-start | bytes 393224 | tf_op jit(solution)/shard_map/ppermute | solution.py:537
  91.4 5.2 %collective-permute-start.4 = (bf16[64,512]{1,0:T(8,128)(2,1)S(1)}, bf16[64,512]{1,0:T(8,128)(2,1)S(1)}, u32[]{:S(2)}, u32[]{:S(2)}) collective-permute-start(bf16[64,512]{1,0:T(8,128)(2,1)S(1)} %get-tuple-element.43.own), channel_id=1, source_target_pairs={{0,64},{32,96},{64,0},{96,32},{1,65},{33,97},{65,1},{97,33},{2,66}... | collective-permute-start | bytes 196616 | tf_op jit(solution)/shard_map/ppermute | solution.py:539
  91.4 5.2 %collective-permute-start.7 = (bf16[64,512]{1,0:T(8,128)(2,1)S(1)}, bf16[64,512]{1,0:T(8,128)(2,1)S(1)}, u32[]{:S(2)}, u32[]{:S(2)}) collective-permute-start(bf16[64,512]{1,0:T(8,128)(2,1)S(1)} %get-tuple-element.43.own), channel_id=1, source_target_pairs={{0,96},{32,0},{64,32},{96,64},{1,97},{33,1},{65,33},{97,65},{2,98}... | collective-permute-start | bytes 196616 | tf_op jit(solution)/shard_map/ppermute | solution.py:539
  93.6 4.3 %collective-permute-start.6 = (bf16[64,512]{1,0:T(8,128)(2,1)S(1)}, bf16[64,512]{1,0:T(8,128)(2,1)S(1)}, u32[]{:S(2)}, u32[]{:S(2)}) collective-permute-start(bf16[64,512]{1,0:T(8,128)(2,1)S(1)} %get-tuple-element.43.own), channel_id=1, source_target_pairs={{0,32},{32,64},{64,96},{96,0},{1,33},{33,65},{65,97},{97,1},{2,34}... | collective-permute-start | bytes 196616 | tf_op jit(solution)/shard_map/ppermute | solution.py:539
  116.2 5.4 %collective-permute-start.8 = (bf16[16,64,512]{2,1,0:T(8,128)(2,1)S(1)}, bf16[16,64,512]{2,1,0:T(8,128)(2,1)S(1)}, u32[]{:S(2)}, u32[]{:S(2)}) collective-permute-start(bf16[16,64,512]{2,1,0:T(8,128)(2,1)S(1)} %all_to_all.22.half), channel_id=1, source_target_pairs={{0,1},{1,0},{2,3},{3,2},{4,5},{5,4},{6,7},{7,6},{8,9},{9,8},{10,11... | collective-permute-start | bytes 3145736 | tf_op jit(solution)/shard_map/ppermute | solution.py:544

commit v7 on v5

--- a/solution.py
+++ b/solution.py
@@ -64,15 +64,12 @@
     return jnp.sum(square, axis=1, keepdims=True)
 
 
-def gru_kernel(
-    touched, ids, state, message, w_input, w_state, out, spread, st, ms, wi, ws, sem
-):
+def gru_kernel(touched, state, message, w_input, w_state, out, st, ms, wi, ws, sem):
     moves = ((state, st), (w_state, ws), (message, ms), (w_input, wi))
     copies = [pltpu.make_async_copy(a, b, sem.at[i]) for i, (a, b) in enumerate(moves)]
     for copy in copies:
         copy.start()
     keep = column(touched[...]) > 0.5
-    spread[...] = jnp.broadcast_to(column(ids[...]), (SLOTS, 128)).astype(jnp.int32)
     copies[0].wait()
     copies[1].wait()
     s = st[...]
@@ -87,17 +84,14 @@
     out[...] = jnp.where(keep, fresh, ABSENT).astype(BF)
 
 
-def gru(touched, ids, state, message, w_input, w_state):
+def gru(touched, state, message, w_input, w_state):
     whole = pl.BlockSpec(memory_space=pltpu.VMEM)
     far = pl.BlockSpec(memory_space=pl.ANY)
     return pl.pallas_call(
         gru_kernel,
-        in_specs=[whole] * 2 + [far] * 4,
-        out_specs=[whole] * 2,
-        out_shape=[
-            jax.ShapeDtypeStruct((N, DM), BF),
-            jax.ShapeDtypeStruct((SLOTS, 128), jnp.int32),
-        ],
+        in_specs=[whole] + [far] * 4,
+        out_specs=whole,
+        out_shape=jax.ShapeDtypeStruct((N, DM), BF),
         scratch_shapes=[
             pltpu.VMEM((N, DM), BF),
             pltpu.VMEM((N, DM), BF),
@@ -110,10 +104,15 @@
             flops=4 * N * DM * 3 * DM, bytes_accessed=4 << 20, transcendentals=3 * N * DM
         ),
         name="gru",
-    )(touched, ids, state, message, w_input, w_state)
-
-
-def time_kernel(delays, frequency, w, chosen, code_t, time_kv, picked):
+    )(touched, state, message, w_input, w_state)
+
+
+def time_kernel(core, ids, ids_far, delays, frequency, w, chosen, code_t, time_kv, picked, wanted):
+    first = core[0] == 0
+    for side, row in ((0, ids), (1, ids_far)):
+        blocks = jnp.broadcast_to(column(row[...]), (SLOTS, 128)).reshape(PLANE, CORES, CAP, 128)
+        mine = jnp.where(first, blocks[:, 0], blocks[:, 1]).astype(jnp.int32)
+        wanted[:, core[0] if side == 0 else 1 - core[0]] = mine
     lane = iota((E, 128), 1)
     columns = jnp.zeros((E, 128), F32)
     for j in range(K + 1):
@@ -138,23 +137,24 @@
             time_kv[tile, at, DM:] = dot(wave, w[2]).astype(BF)
 
 
-def time_parts(delays, frequency, weights, chosen):
+def time_parts(core, ids, ids_far, delays, frequency, weights, chosen):
     whole = pl.BlockSpec(memory_space=pltpu.VMEM)
     return pl.pallas_call(
         time_kernel,
-        in_specs=[whole] * 4,
-        out_specs=[whole] * 3,
+        in_specs=[pl.BlockSpec(memory_space=pltpu.SMEM)] + [whole] * 6,
+        out_specs=[whole] * 4,
         out_shape=[
             jax.ShapeDtypeStruct((TILES, DM, ROWS), BF),
             jax.ShapeDtypeStruct((TILES, ROWS, 2 * DM), BF),
             jax.ShapeDtypeStruct((E, 128), jnp.int32),
+            jax.ShapeDtypeStruct((PLANE, CORES, CAP, 128), jnp.int32),
         ],
         compiler_params=pltpu.CompilerParams(vmem_limit_bytes=24 << 20),
         cost_estimate=pl.CostEstimate(
             flops=4 * K * E * DM * DM, bytes_accessed=8 << 20, transcendentals=K * E * DM
         ),
         name="time_parts",
-    )(delays, frequency, weights, chosen)
+    )(core, ids, ids_far, delays, frequency, weights, chosen)
 
 
 def owner_pick(asked):
@@ -192,26 +192,26 @@
 
 def attend_kernel(
     core, slots, chosen, chosen_t, tkv, tt, up, wq,
-    embedded, d_slots, mine, other,
-    skv, d_att, qf, src, both, dkv, att, dq, sums,
+    mine, other, att, src, pick_t, s_qkv,
+    skv, d_att, qf, both, dkv, dq,
 ):
     rows = slots[...]
     pick = (chosen[:, 0:1] == iota((E, SLOTS), 1)).astype(F32).astype(BF)
-    src[...] = dot(pick, rows)
+    src[...] = dot(pick, rows).astype(BF)
     skv[:, :DM] = dot(rows, wq[1]).astype(BF)
     skv[:, DM:] = dot(rows, wq[2]).astype(BF)
     qf[...] = dot(pick, dot(rows, wq[0]).astype(BF))
     d_att[...] = dot_nt(up[...], wq[3])
 
     lane = iota((STEP, 128), 1)
-    first = lane < K
-    second = (lane >= K) & (lane < 2 * K)
+    lane_a = lane < K
+    lane_b = (lane >= K) & (lane < 2 * K)
     scale = 1.0 / math.sqrt(HEAD)
 
     def per_head(x):
-        a = jnp.sum(jnp.where(first, x, 0.0), axis=1, keepdims=True)
-        b = jnp.sum(jnp.where(second, x, 0.0), axis=1, keepdims=True)
-        return jnp.where(first, a, b)
+        a = jnp.sum(jnp.where(lane_a, x, 0.0), axis=1, keepdims=True)
+        b = jnp.sum(jnp.where(lane_b, x, 0.0), axis=1, keepdims=True)
+        return jnp.where(lane_a, a, b)
 
     def gather(i):
         ids = chosen[i * TILE : (i + 1) * TILE, :]
@@ -279,23 +279,44 @@
         s_kv = one if i == 0 else s_kv + one
         dot_t = two if i == 0 else dot_t + two
     s_kv = s_kv.astype(BF)
-    pick_t = (iota((SLOTS, E), 0) == chosen_t[0]).astype(F32).astype(BF)
-    s_q = dot(pick_t, dq[...]).astype(BF)
+    pick_t[...] = (iota((SLOTS, E), 0) == chosen_t[0]).astype(F32).astype(BF)
+    s_q = dot(pick_t[...], dq[...]).astype(BF)
+    s_qkv[:, :DM] = s_q
+    s_qkv[:, DM:] = s_kv
+    first = core[0] == 0
 
     def store(i, value):
-        sums[i * 4 : (i + 1) * 4] = value.astype(BF).reshape(4, CORES, PIECE, DM)
+        blocks = value.reshape(4, CORES, PIECE, DM)
+        at = slice(i * 4, (i + 1) * 4)
+        mine[at] = jnp.where(first, blocks[:, 0], blocks[:, 1]).astype(BF)
+        other[at] = jnp.where(first, blocks[:, 1], blocks[:, 0]).astype(BF)
 
     store(0, dot_tn(rows, s_q))
     g_kv = dot_t + dot_tn(rows, s_kv)
     store(1, g_kv[:, :DM])
     store(2, g_kv[:, DM:])
     store(3, dot_tn(att[...], up[...]))
-    mine[...] = sums[:, core[0]]
-    other[...] = sums[:, 1 - core[0]]
-    embedded[...] = (dot(att[...], wq[3]) + src[...]).astype(BF)
-    grads = dot(pick_t, up[...]) + dot_nt(s_q, wq[0])
-    grads += dot_nt(s_kv[:, :DM], wq[1]) + dot_nt(s_kv[:, DM:], wq[2])
+
+
+def events_kernel(att, src, pick_t, s_qkv, up, w, embedded, d_slots):
+    embedded[...] = (dot(att[...], w[3]) + src[...].astype(F32)).astype(BF)
+    grads = dot(pick_t[...], up[...])
+    for i in range(3):
+        grads += dot_nt(s_qkv[:, i * DM : (i + 1) * DM], w[i])
     d_slots[...] = grads.astype(BF)
+
+
+def events(att, src, pick_t, s_qkv, up, weights):
+    whole = pl.BlockSpec(memory_space=pltpu.VMEM)
+    return pl.pallas_call(
+        events_kernel,
+        in_specs=[whole] * 6,
+        out_specs=[whole] * 2,
+        out_shape=[jax.ShapeDtypeStruct((E, DM), BF), jax.ShapeDtypeStruct((SLOTS, DM), BF)],
+        compiler_params=pltpu.CompilerParams(vmem_limit_bytes=16 << 20),
+        cost_estimate=pl.CostEstimate(flops=1 << 29, bytes_accessed=4 << 20, transcendentals=0),
+        name="events",
+    )(att, src, pick_t, s_qkv, up, weights)
 
 
 def attend(core, slots, chosen, chosen_t, time_kv, code_t, up, weights):
@@ -303,23 +324,22 @@
     return pl.pallas_call(
         attend_kernel,
         in_specs=[pl.BlockSpec(memory_space=pltpu.SMEM)] + [whole] * 7,
-        out_specs=[whole] * 4,
+        out_specs=[whole] * 6,
         out_shape=[
-            jax.ShapeDtypeStruct((E, DM), BF),
-            jax.ShapeDtypeStruct((SLOTS, DM), BF),
             jax.ShapeDtypeStruct((PLANE, PIECE, DM), BF),
             jax.ShapeDtypeStruct((PLANE, PIECE, DM), BF),
+            jax.ShapeDtypeStruct((E, DM), BF),
+            jax.ShapeDtypeStruct((E, DM), BF),
+            jax.ShapeDtypeStruct((SLOTS, E), BF),
+            jax.ShapeDtypeStruct((SLOTS, 3 * DM), BF),
         ],
         scratch_shapes=[
             pltpu.VMEM((SLOTS, 2 * DM), BF),
             pltpu.VMEM((E, DM), F32),
             pltpu.VMEM((E, DM), F32),
-            pltpu.VMEM((E, DM), F32),
             pltpu.VMEM((TILES, ROWS, 2 * DM), F32),
             pltpu.VMEM((TILES, ROWS, 2 * DM), BF),
             pltpu.VMEM((E, DM), BF),
-            pltpu.VMEM((E, DM), BF),
-            pltpu.VMEM((PLANE, CORES, PIECE, DM), BF),
         ],
         compiler_params=pltpu.CompilerParams(vmem_limit_bytes=40 << 20),
         cost_estimate=pl.CostEstimate(
@@ -471,35 +491,38 @@
 ):
     seg = lax.axis_index("y").reshape(1)
     core = lax.axis_index("core").reshape(1)
-    written, ids = gru(
-        touched, request_rows.reshape(1, SLOTS), memory_base, messages[0], gru_input, gru_state
-    )
+    swap = [(0, 1), (1, 0)]
+    ids = request_rows.reshape(1, SLOTS)
+    ids_far = lax.ppermute(ids, "core", swap)
+    written = gru(touched, memory_base, messages[0], gru_input, gru_state)
     r1 = lax.ppermute(written, "y", [(0, 1), (1, 2), (2, 3)])
     r2 = lax.ppermute(written, "y", [(0, 2), (1, 3)])
     r3 = lax.ppermute(written, "y", [(0, 3)])
     written, late, seg, core = lax.optimization_barrier((written, delays[0].T, seg, core))
     chosen_t = event_slots.transpose(2, 0, 1)
-    code_t, time_kv, chosen = time_parts(late, frequency.reshape(1, DM), attn_weights, chosen_t)
-    written, ids, code_t, time_kv, chosen = lax.optimization_barrier(
-        (written, ids, code_t, time_kv, chosen)
+    code_t, time_kv, chosen, wanted = time_parts(
+        core, ids, ids_far, late, frequency.reshape(1, DM), attn_weights, chosen_t
     )
-    asked = exchange(ids, NODE, OWNERS)
+    written, wanted, code_t, time_kv, chosen = lax.optimization_barrier(
+        (written, wanted, code_t, time_kv, chosen)
+    )
+    asked = plane(wanted).reshape(SLOTS, 128)
     memory, rows = start_rows(seg, memory_base, written, r1, r2, r3, asked)
     slots = exchange(rows, NODE, OWNERS)
     up = upstream[0]
-    embedded, d_slots, mine, other = attend(
+    mine, other, *kept = attend(
         core, slots, chosen, chosen_t, time_kv, code_t, up, attn_weights
     )
-    swap = [(0, 1), (1, 0)]
     partner = lax.ppermute(other, "core", swap)
+    embedded, d_slots = events(*kept, up, attn_weights)
     parts = plane(pair_sum(mine, partner, d_slots))
     part, keep, give = plane_sum(core, parts)
     got = lax.ppermute(give, "core", swap)
-    r2, r1, r3 = (
-        lax.ppermute(part, "y", [(i, (i + s) % SEG) for i in range(SEG)]) for s in (2, 1, 3)
-    )
+    turns = {s: [(i, (i + s) % SEG) for i in range(SEG)] for s in (1, 2, 3)}
+    r2 = lax.ppermute(part, "y", turns[2])
     memory_grad = owner_sum(core, asked, keep, got)
-    r2, memory_grad = lax.optimization_barrier((r2, memory_grad))
+    late, memory_grad = lax.optimization_barrier((part, memory_grad))
+    r1, r3 = (lax.ppermute(late, "y", turns[s]) for s in (1, 3))
     half = plane(seg_sum(seg, part, r1, r2, r3))
     far = lax.ppermute(half, "core", swap)
     weight_grad = whole_grad(core, far, whole_grad(core, half))

time: 116 us -> 117 us (level)
    all_to_all x2 -> x1, blocking collectives: 29.3 us -> 14.4 us  [exchange(): lax.all_to_all(blocks, axes, split_axis=0, concat_axis=0, tiled=True)]
    all_to_all x2 -> x3, blocking collectives: 39.8 us -> 54.2 us  [plane(): return lax.all_to_all(x, FLAT, split_axis=0, concat_axis=0, tiled=True)]
    pallas_call x2 -> x3, Pallas kernels: 8.62 us -> 9.52 us  [the longest x1 4.37 us: time_parts(): pl.pallas_call(time_kernel, in_specs=[pl.BlockSpec(memory_space=pltpu.SME...]
    ppermute x3 -> x4, starting transfers between devices: 2.13 us -> 2.97 us  [the longest x1 1.5 us: on_device(): ids_far = lax.ppermute(ids, 'core', swap)]
    ppermute x3 -> x4, waiting for transfers between devices: 3.2 us -> 4.03 us  [the longest x2 2.45 us: on_device(): r1, r3 = (lax.ppermute(late, 'y', turns[s]) for s in (1, 3))]
  transfers between devices with their start and end apart: 9 -> 10, of which waited for: 4 -> 6; matrix products, arithmetic and copies ran while one was open for 0% -> 0% of each run, Pallas kernels for 6% -> 10%
where the time goes in v7:
time: 117 us; the launch traced here: 116 us
  blocking collectives  68.6 us (59%)
  Pallas kernels  22.6 us (19%)
  starting transfers between devices  16.7 us (14%)
  waiting for transfers between devices  7.37 us (6%)
    all_to_all x3, blocking collectives, plane(): return lax.all_to_all(x, FLAT, split_axis=0, concat_axis=0, tiled=True)  54.2 us
    all_to_all x1, blocking collectives, exchange(): lax.all_to_all(blocks, axes, split_axis=0, concat_axis=0, tiled=True)  14.4 us
    pallas_call x1, Pallas kernels, attend(): pl.pallas_call(attend_kernel, in_specs=[pl.BlockSpec(memory_space=pltpu.S...  7.44 us
    ppermute x1, starting transfers between devices, on_device(): r3 = lax.ppermute(written, 'y', [(0, 3)])  4.74 us
    pallas_call x1, Pallas kernels, time_parts(): pl.pallas_call(time_kernel, in_specs=[pl.BlockSpec(memory_space=pltpu.SME...  4.37 us
    pallas_call x1, Pallas kernels, gru(): pl.pallas_call(gru_kernel, in_specs=[whole] + [far] * 4, out_specs=whole,...  4.14 us
    ppermute x1, starting transfers between devices, on_device(): far = lax.ppermute(half, 'core', swap)  3.07 us
    pallas_call x2, Pallas kernels, whole_grad(): pl.pallas_call(functools.partial(half_kernel, own), in_specs=[pl.BlockSpe...  2.76 us
  transfers between devices with their start and end apart: 10, of which 6 were waited for; matrix products, arithmetic and copies ran while one was open for 0% of the time, Pallas kernels for 10%

profile of v7, /device:TPU:1, one launch (start us, length us, event | category | flops | bytes accessed | tf_op | source)
XLA Modules:
  0.0 116.3 jit_solution(7814660943387257247)
XLA Ops:
  0.6 0.0 copy-start.7
  0.6 0.0 copy-start.5
  0.7 0.0 copy-start
  0.7 0.0 copy-start.4
  0.7 0.0 copy-start.6
  0.7 1.5 %collective-permute-start = (s32[1,256]{1,0:T(1,128)}, s32[1,256]{1,0:T(1,128)S(1)}, u32[]{:S(2)}, u32[]{:S(2)}) collective-permute-start(s32[1,256]{1,0:T(1,128)} %bitcast.28), channel_id=1, source_target_pairs={{0,1},{1,0},{2,3},{3,2},{4,5},{5,4},{6,7},{7,6},{8,9},{9,8},{10,11... | collective-permute-start | bytes 3080 | tf_op jit(solution)/shard_map/ppermute | solution.py:496
  2.2 4.1 %gru.1.written = bf16[256,512]{1,0:T(8,128)(2,1)} custom-call(s32[1,256]{1,0:T(1,128)} %touched.1, bf16[256,512]{1,0:T(8,128)(2,1)} %state.3, bf16[256,512]{1,0:T(8,128)(2,1)} %bitcast.32, bf16[512,1536]{1,0:T(8,128)(2,1)} %w_input.1, bf16[512,1536]{1,0:T(8,128)(2,1)} %w_state.1), custom_call_target="tpu_custom_call" | custom-call | flops 805306368 | bytes 4194304 | tf_op jit(solution)/shard_map/gru/pallas_call | solution.py:90
  6.3 4.7 %collective-permute-start.3 = (bf16[256,512]{1,0:T(8,128)(2,1)}, bf16[256,512]{1,0:T(8,128)(2,1)S(1)}, u32[]{:S(2)}, u32[]{:S(2)}) collective-permute-start(bf16[256,512]{1,0:T(8,128)(2,1)} %gru.1.written), channel_id=1, source_target_pairs={{0,96},{1,97},{2,98},{3,99},{4,100},{5,101},{6,102},{7,103},{8,104... | collective-permute-start | bytes 786440 | tf_op jit(solution)/shard_map/ppermute | solution.py:500
  11.1 1.3 %collective-permute-start.2 = (bf16[256,512]{1,0:T(8,128)(2,1)}, bf16[256,512]{1,0:T(8,128)(2,1)S(1)}, u32[]{:S(2)}, u32[]{:S(2)}) collective-permute-start(bf16[256,512]{1,0:T(8,128)(2,1)} %gru.1.written), channel_id=1, source_target_pairs={{0,64},{32,96},{1,65},{33,97},{2,66},{34,98},{3,67},{35,99},{4,68}... | collective-permute-start | bytes 786440 | tf_op jit(solution)/shard_map/ppermute | solution.py:499
  12.4 2.5 %collective-permute-start.1 = (bf16[256,512]{1,0:T(8,128)(2,1)}, bf16[256,512]{1,0:T(8,128)(2,1)S(1)}, u32[]{:S(2)}, u32[]{:S(2)}) collective-permute-start(bf16[256,512]{1,0:T(8,128)(2,1)} %gru.1.written), channel_id=1, source_target_pairs={{0,32},{32,64},{64,96},{1,33},{33,65},{65,97},{2,34},{34,66},{66,9... | collective-permute-start | bytes 786440 | tf_op jit(solution)/shard_map/ppermute | solution.py:498
  14.9 0.0 collective-permute-done.ids_far
  14.9 0.0 copy-done.7
  14.9 0.0 copy-done.5
  14.9 0.0 copy-done
  14.9 0.0 copy-done.4
  14.9 0.0 copy-start.1
  15.0 0.0 copy-start.2
  15.0 4.4 %time_parts.1 = (bf16[2,512,1024]{2,1,0:T(8,128)(2,1)S(1)}, bf16[2,1024,1024]{2,1,0:T(8,128)(2,1)S(1)}, s32[256,128]{1,0:T(8,128)S(1)}, s32[16,2,8,128]{3,2,1,0:T(8,128)S(1)}) custom-call(s32[1]{0:T(128)} %bitcast.4.core, s32[1,256]{1,0:T(1,128)S(1)} %bitcast.29, s32[1,256]{1,0:T(1,128)S(1)} %collective-permute-done.ids_far, s32[8,256]{1,0:T(8,128)S(1)} %bitcast.26, ...), custom_call_target="tpu_custom_call" | custom-call | flops 2147483648 | bytes 8388608 | tf_op jit(solution)/shard_map/time_parts/pallas_call | solution.py:142
  19.3 0.0 copy-start.3
  19.4 14.4 %all_to_all.20.asked = s32[16,2,8,128]{3,2,1,0:T(8,128)S(1)} all-to-all(s32[16,2,8,128]{3,2,1,0:T(8,128)S(1)} %get-tuple-element.41), channel_id=1, replica_groups=mesh['y'=4,'x'=4,'z'=4,'core'=2] {'x','z'}, dimensions={0} | all-to-all | bytes 262144 | tf_op jit(solution)/shard_map/all_to_all | solution.py:476
  33.7 0.0 collective-permute-done.3.r3
  33.7 0.0 collective-permute-done.2.r2
  33.7 0.0 collective-permute-done.1.r1
  33.7 1.1 start_rows.1
  34.8 14.4 %all_to_all.21 = bf16[32,8,512]{2,1,0:T(8,128)(2,1)S(1)} all-to-all(bf16[32,8,512]{2,1,0:T(8,128)(2,1)S(1)} %bitcast.21), channel_id=1, replica_groups=mesh['y'=4,'x'=4,'z'=4,'core'=2] {'x','z','core'}, dimensions={0} | all-to-all | bytes 524288 | tf_op jit(solution)/shard_map/all_to_all | solution.py:472
  49.3 0.0 copy-done.3
  49.3 7.4 %attend.1 = (bf16[16,64,512]{2,1,0:T(8,128)(2,1)S(1)}, bf16[16,64,512]{2,1,0:T(8,128)(2,1)S(1)}, bf16[256,512]{1,0:T(8,128)(2,1)S(1)}, bf16[256,512]{1,0:T(8,128...) custom-call(s32[1]{0:T(128)} %bitcast.4.core, bf16[256,512]{1,0:T(8,128)(2,1)S(1)} %bitcast.20, ...), custom_call_target="tpu_custom_call" | custom-call | flops 6442450944 | bytes 14680064 | tf_op jit(solution)/shard_map/attend/pallas_call | solution.py:324
  56.7 0.3 collective-permute-start.4
  57.0 1.0 events.1
  58.0 1.5 %collective-permute-done.4.b = bf16[16,64,512]{2,1,0:T(8,128)(2,1)S(1)} collective-permute-done((bf16[16,64,512]{2,1,0:T(8,128)(2,1)S(1)}, bf16[16,64,512]{2,1,0:T(8,128)(2,1)S(1)}, u32[]{:S(2)}, u32[]{:S(2)}) %collective-permute-start.4) | collective-permute-done | bytes 1048608 | tf_op jit(solution)/shard_map/ppermute | solution.py:516
  59.5 0.3 pair_sum.1
  59.8 21.7 %all_to_all.22.a = bf16[16,80,512]{2,1,0:T(8,128)(2,1)S(1)} all-to-all(bf16[16,80,512]{2,1,0:T(8,128)(2,1)S(1)} %pair_sum.1), channel_id=1, replica_groups=mesh['y'=4,'x'=4,'z'=4,'core'=2] {'x','z'}, dimensions={0} | all-to-all | bytes 2621440 | tf_op jit(solution)/shard_map/all_to_all | solution.py:476
  81.4 0.2 plane_sum.1
  81.6 1.9 %collective-permute-start.5 = (bf16[128,512]{1,0:T(8,128)(2,1)S(1)}, bf16[128,512]{1,0:T(8,128)(2,1)S(1)}, u32[]{:S(2)}, u32[]{:S(2)}) collective-permute-start(bf16[128,512]{1,0:T(8,128)(2,1)S(1)} %get-tuple-element.57), channel_id=1, source_target_pairs={{0,1},{1,0},{2,3},{3,2},{4,5},{5,4},{6,7},{7,6},{8,9},{9,8},{10,11... | collective-permute-start | bytes 393224 | tf_op jit(solution)/shard_map/ppermute | solution.py:520
  83.5 0.0 collective-permute-start.7
  83.5 1.0 collective-permute-done.5.got
  84.5 1.1 owner_sum.1
  85.6 1.2 %collective-permute-start.8 = (bf16[64,512]{1,0:T(8,128)(2,1)S(1)}, bf16[64,512]{1,0:T(8,128)(2,1)S(1)}, u32[]{:S(2)}, u32[]{:S(2)}) collective-permute-start(bf16[64,512]{1,0:T(8,128)(2,1)S(1)} %get-tuple-element.59.own), channel_id=1, source_target_pairs={{0,96},{32,0},{64,32},{96,64},{1,97},{33,1},{65,33},{97,65},{2,98}... | collective-permute-start | bytes 196616 | tf_op jit(solution)/shard_map/ppermute | solution.py:525
  86.8 0.3 collective-permute-start.6
  87.1 1.6 %collective-permute-done.7.r2 = bf16[64,512]{1,0:T(8,128)(2,1)S(1)} collective-permute-done((bf16[64,512]{1,0:T(8,128)(2,1)S(1)}, bf16[64,512]{1,0:T(8,128)(2,1)S(1)}, u32[]{:S(2)}, u32[]{:S(2)}) %collective-permute-start.7) | collective-permute-done | bytes 65568 | tf_op jit(solution)/shard_map/ppermute | solution.py:522
  88.7 0.4 collective-permute-done.8.r3
  89.0 2.1 %collective-permute-done.6.r1 = bf16[64,512]{1,0:T(8,128)(2,1)S(1)} collective-permute-done((bf16[64,512]{1,0:T(8,128)(2,1)S(1)}, bf16[64,512]{1,0:T(8,128)(2,1)S(1)}, u32[]{:S(2)}, u32[]{:S(2)}) %collective-permute-start.6) | collective-permute-done | bytes 65568 | tf_op jit(solution)/shard_map/ppermute | solution.py:525
  91.1 0.1 seg_sum.1
  91.3 18.1 %all_to_all.23.half = bf16[16,64,512]{2,1,0:T(8,128)(2,1)S(1)} all-to-all(bf16[16,64,512]{2,1,0:T(8,128)(2,1)S(1)} %seg_sum.1), channel_id=1, replica_groups=mesh['y'=4,'x'=4,'z'=4,'core'=2] {'x','z'}, dimensions={0} | all-to-all | bytes 2097152 | tf_op jit(solution)/shard_map/all_to_all | solution.py:476
  109.4 3.1 %collective-permute-start.9 = (bf16[16,64,512]{2,1,0:T(8,128)(2,1)S(1)}, bf16[16,64,512]{2,1,0:T(8,128)(2,1)S(1)}, u32[]{:S(2)}, u32[]{:S(2)}) collective-permute-start(bf16[16,64,512]{2,1,0:T(8,128)(2,1)S(1)} %all_to_all.23.half), channel_id=1, source_target_pairs={{0,1},{1,0},{2,3},{3,2},{4,5},{5,4},{6,7},{7,6},{8,9},{9,8},{10,11... | collective-permute-start | bytes 3145736 | tf_op jit(solution)/shard_map/ppermute | solution.py:527
  112.5 1.4 %own_half.1.rest_0_ = f32[16,2,64,512]{3,2,1,0:T(8,128)} custom-call(s32[1]{0:T(128)} %bitcast.4.core, bf16[16,64,512]{2,1,0:T(8,128)(2,1)S(1)} %all_to_all.23.half), custom_call_target="tpu_custom_call" | custom-call | flops 262144 | bytes 3145728 | tf_op jit(solution)/shard_map/own_half/pallas_call | solution.py:435
  113.9 0.9 collective-permute-done.9.half
  114.8 1.4 %far_half.1 = f32[16,2,64,512]{3,2,1,0:T(8,128)} custom-call(s32[1]{0:T(128)} %bitcast.4.core, bf16[16,64,512]{2,1,0:T(8,128)(2,1)S(1)} %collective-permute-done.9.half, f32[16,2,64,512]{3,2,1,0:T(8,128)} %own_half.1.rest_0_), custom_call_target="tpu_custom_call", output_to_operand_aliasing={{}: (2, {})} | custom-call | flops 262144 | bytes 3145728 | tf_op jit(solution)/shard_map/far_half/pallas_call | solution.py:435
  (3 shorter events, 0.0 us)
Async XLA Ops:
  0.6 14.3 %copy-start.7 = (s32[1,1,256]{2,1,0:T(1,128)S(1)}, s32[1,1,256]{2,1,0:T(1,128)}, u32[]{:S(2)}) copy-start(s32[1,1,256]{2,1,0:T(1,128)} %param.18) | copy-start | bytes 3076
  0.6 14.3 %copy-start.5 = (s32[1,256,8]{1,2,0:T(8,128)S(1)}, s32[1,256,8]{1,2,0:T(8,128)}, u32[]{:S(2)}) copy-start(s32[1,256,8]{1,2,0:T(8,128)} %param.20) | copy-start | bytes 24580
  0.7 14.3 %copy-start = (bf16[4,512,512]{2,1,0:T(8,128)(2,1)S(1)}, bf16[4,512,512]{2,1,0:T(8,128)(2,1)}, u32[]{:S(2)}) copy-start(bf16[4,512,512]{2,1,0:T(8,128)(2,1)} %w.3) | copy-start | bytes 6291460
  0.7 14.3 %copy-start.4 = (s32[1,256,9]{1,0,2:T(1,128)S(1)}, s32[1,256,9]{1,0,2:T(1,128)}, u32[]{:S(2)}) copy-start(s32[1,256,9]{1,0,2:T(1,128)} %param.19) | copy-start | bytes 27652
  0.7 14.3 %copy-start.6 = (f32[512]{0:T(512)S(1)}, f32[512]{0:T(512)}, u32[]{:S(2)}) copy-start(f32[512]{0:T(512)} %param.17) | copy-start | bytes 6148
  0.7 14.2 %collective-permute-start = (s32[1,256]{1,0:T(1,128)}, s32[1,256]{1,0:T(1,128)S(1)}, u32[]{:S(2)}, u32[]{:S(2)}) collective-permute-start(s32[1,256]{1,0:T(1,128)} %bitcast.28), channel_id=1, source_target_pairs={{0,1},{1,0},{2,3},{3,2},{4,5},{5,4},{6,7},{7,6},{8,9},{9,8},{10,11... | collective-permute-start | bytes 3080 | tf_op jit(solution)/shard_map/ppermute | solution.py:496
  6.3 27.4 %collective-permute-start.3 = (bf16[256,512]{1,0:T(8,128)(2,1)}, bf16[256,512]{1,0:T(8,128)(2,1)S(1)}, u32[]{:S(2)}, u32[]{:S(2)}) collective-permute-start(bf16[256,512]{1,0:T(8,128)(2,1)} %gru.1.written), channel_id=1, source_target_pairs={{0,96},{1,97},{2,98},{3,99},{4,100},{5,101},{6,102},{7,103},{8,104... | collective-permute-start | bytes 786440 | tf_op jit(solution)/shard_map/ppermute | solution.py:500
  11.1 22.6 %collective-permute-start.2 = (bf16[256,512]{1,0:T(8,128)(2,1)}, bf16[256,512]{1,0:T(8,128)(2,1)S(1)}, u32[]{:S(2)}, u32[]{:S(2)}) collective-permute-start(bf16[256,512]{1,0:T(8,128)(2,1)} %gru.1.written), channel_id=1, source_target_pairs={{0,64},{32,96},{1,65},{33,97},{2,66},{34,98},{3,67},{35,99},{4,68}... | collective-permute-start | bytes 786440 | tf_op jit(solution)/shard_map/ppermute | solution.py:499
  12.4 21.3 %collective-permute-start.1 = (bf16[256,512]{1,0:T(8,128)(2,1)}, bf16[256,512]{1,0:T(8,128)(2,1)S(1)}, u32[]{:S(2)}, u32[]{:S(2)}) collective-permute-start(bf16[256,512]{1,0:T(8,128)(2,1)} %gru.1.written), channel_id=1, source_target_pairs={{0,32},{32,64},{64,96},{1,33},{33,65},{65,97},{2,34},{34,66},{66,9... | collective-permute-start | bytes 786440 | tf_op jit(solution)/shard_map/ppermute | solution.py:498
  14.9 18.8 %copy-start.1 = (bf16[256,512]{1,0:T(8,128)(2,1)S(1)}, bf16[256,512]{1,0:T(8,128)(2,1)}, u32[]{:S(2)}) copy-start(bf16[256,512]{1,0:T(8,128)(2,1)} %state.3) | copy-start | bytes 786436
  15.0 18.8 %copy-start.2 = (bf16[256,512]{1,0:T(8,128)(2,1)S(1)}, bf16[256,512]{1,0:T(8,128)(2,1)}, u32[]{:S(2)}) copy-start(bf16[256,512]{1,0:T(8,128)(2,1)} %gru.1.written) | copy-start | bytes 786436
  19.3 29.9 %copy-start.3 = (bf16[1,256,512]{2,1,0:T(8,128)(2,1)S(1)}, bf16[1,256,512]{2,1,0:T(8,128)(2,1)}, u32[]{:S(2)}) copy-start(bf16[1,256,512]{2,1,0:T(8,128)(2,1)} %param.21) | copy-start | bytes 786436
  56.7 2.7 %collective-permute-start.4 = (bf16[16,64,512]{2,1,0:T(8,128)(2,1)S(1)}, bf16[16,64,512]{2,1,0:T(8,128)(2,1)S(1)}, u32[]{:S(2)}, u32[]{:S(2)}) collective-permute-start(bf16[16,64,512]{2,1,0:T(8,128)(2,1)S(1)} %get-tuple-element.53), channel_id=1, source_target_pairs={{0,1},{1,0},{2,3},{3,2},{4,5},{5,4},{6,7},{7,6},{8,9},{9,8},{10,11... | collective-permute-start | bytes 3145736 | tf_op jit(solution)/shard_map/ppermute | solution.py:516
  81.6 2.9 %collective-permute-start.5 = (bf16[128,512]{1,0:T(8,128)(2,1)S(1)}, bf16[128,512]{1,0:T(8,128)(2,1)S(1)}, u32[]{:S(2)}, u32[]{:S(2)}) collective-permute-start(bf16[128,512]{1,0:T(8,128)(2,1)S(1)} %get-tuple-element.57), channel_id=1, source_target_pairs={{0,1},{1,0},{2,3},{3,2},{4,5},{5,4},{6,7},{7,6},{8,9},{9,8},{10,11... | collective-permute-start | bytes 393224 | tf_op jit(solution)/shard_map/ppermute | solution.py:520
  83.5 5.2 %collective-permute-start.7 = (bf16[64,512]{1,0:T(8,128)(2,1)S(1)}, bf16[64,512]{1,0:T(8,128)(2,1)S(1)}, u32[]{:S(2)}, u32[]{:S(2)}) collective-permute-start(bf16[64,512]{1,0:T(8,128)(2,1)S(1)} %get-tuple-element.59.own), channel_id=1, source_target_pairs={{0,64},{32,96},{64,0},{96,32},{1,65},{33,97},{65,1},{97,33},{2,66}... | collective-permute-start | bytes 196616 | tf_op jit(solution)/shard_map/ppermute | solution.py:522
  85.6 3.4 %collective-permute-start.8 = (bf16[64,512]{1,0:T(8,128)(2,1)S(1)}, bf16[64,512]{1,0:T(8,128)(2,1)S(1)}, u32[]{:S(2)}, u32[]{:S(2)}) collective-permute-start(bf16[64,512]{1,0:T(8,128)(2,1)S(1)} %get-tuple-element.59.own), channel_id=1, source_target_pairs={{0,96},{32,0},{64,32},{96,64},{1,97},{33,1},{65,33},{97,65},{2,98}... | collective-permute-start | bytes 196616 | tf_op jit(solution)/shard_map/ppermute | solution.py:525
  86.8 4.3 %collective-permute-start.6 = (bf16[64,512]{1,0:T(8,128)(2,1)S(1)}, bf16[64,512]{1,0:T(8,128)(2,1)S(1)}, u32[]{:S(2)}, u32[]{:S(2)}) collective-permute-start(bf16[64,512]{1,0:T(8,128)(2,1)S(1)} %get-tuple-element.59.own), channel_id=1, source_target_pairs={{0,32},{32,64},{64,96},{96,0},{1,33},{33,65},{65,97},{97,1},{2,34}... | collective-permute-start | bytes 196616 | tf_op jit(solution)/shard_map/ppermute | solution.py:525
  109.4 5.4 %collective-permute-start.9 = (bf16[16,64,512]{2,1,0:T(8,128)(2,1)S(1)}, bf16[16,64,512]{2,1,0:T(8,128)(2,1)S(1)}, u32[]{:S(2)}, u32[]{:S(2)}) collective-permute-start(bf16[16,64,512]{2,1,0:T(8,128)(2,1)S(1)} %all_to_all.23.half), channel_id=1, source_target_pairs={{0,1},{1,0},{2,3},{3,2},{4,5},{5,4},{6,7},{7,6},{8,9},{9,8},{10,11... | collective-permute-start | bytes 3145736 | tf_op jit(solution)/shard_map/ppermute | solution.py:527

commit v8 on v7

--- a/solution.py
+++ b/solution.py
@@ -32,13 +32,12 @@
 F32 = jnp.float32
 
 COS = (
-    0.9999999698385398,
-    -19.739198571306687,
-    64.93882672218028,
-    -85.44499716023202,
-    60.126952745697146,
-    -25.820504473745327,
-    6.330480832160802,
+    0.9999992107823232,
+    -19.738980355764145,
+    64.92865742103731,
+    -85.27162153434116,
+    58.79049212030933,
+    -21.07110562791079,
 )
 
 
@@ -67,8 +66,8 @@
 def gru_kernel(touched, state, message, w_input, w_state, out, st, ms, wi, ws, sem):
     moves = ((state, st), (w_state, ws), (message, ms), (w_input, wi))
     copies = [pltpu.make_async_copy(a, b, sem.at[i]) for i, (a, b) in enumerate(moves)]
-    for copy in copies:
-        copy.start()
+    for i, copy in enumerate(copies):
+        copy.start(priority=i % 2)
     keep = column(touched[...]) > 0.5
     copies[0].wait()
     copies[1].wait()
@@ -119,13 +118,11 @@
         columns = jnp.where(lane == j, column(chosen[j]), columns)
     picked[...] = columns.astype(jnp.int32)
     turns = frequency[...] * (1.0 / (2.0 * math.pi))
-    high = jnp.round(turns * 16384.0) * (1.0 / 16384.0)
-    low = turns - high
     for tile in range(TILES):
         for k in range(K):
             delay = column(delays[k : k + 1, tile * TILE : (tile + 1) * TILE])
-            coarse = delay * high
-            part = (coarse - jnp.round(coarse)) + delay * low
+            angle = delay * turns
+            part = angle - jnp.round(angle)
             u = part * part
             wave = jnp.full_like(u, COS[-1])
             for c in COS[-2::-1]:
@@ -298,25 +295,30 @@
     store(3, dot_tn(att[...], up[...]))
 
 
-def events_kernel(att, src, pick_t, s_qkv, up, w, embedded, d_slots):
+def events_kernel(core, att, src, pick_t, s_qkv, up, w, embedded, keep, give):
     embedded[...] = (dot(att[...], w[3]) + src[...].astype(F32)).astype(BF)
     grads = dot(pick_t[...], up[...])
     for i in range(3):
         grads += dot_nt(s_qkv[:, i * DM : (i + 1) * DM], w[i])
-    d_slots[...] = grads.astype(BF)
-
-
-def events(att, src, pick_t, s_qkv, up, weights):
+    blocks = grads.reshape(PLANE, CORES, CAP, DM)
+    first = core[0] == 0
+    low, high = (blocks[:, i].reshape(SLOTS // 2, DM) for i in range(2))
+    keep[...] = jnp.where(first, low, high).astype(BF)
+    give[...] = jnp.where(first, high, low).astype(BF)
+
+
+def events(core, att, src, pick_t, s_qkv, up, weights):
     whole = pl.BlockSpec(memory_space=pltpu.VMEM)
     return pl.pallas_call(
         events_kernel,
-        in_specs=[whole] * 6,
-        out_specs=[whole] * 2,
-        out_shape=[jax.ShapeDtypeStruct((E, DM), BF), jax.ShapeDtypeStruct((SLOTS, DM), BF)],
+        in_specs=[pl.BlockSpec(memory_space=pltpu.SMEM)] + [whole] * 6,
+        out_specs=[whole] * 3,
+        out_shape=[jax.ShapeDtypeStruct((E, DM), BF)]
+        + [jax.ShapeDtypeStruct((SLOTS // 2, DM), BF)] * 2,
         compiler_params=pltpu.CompilerParams(vmem_limit_bytes=16 << 20),
         cost_estimate=pl.CostEstimate(flops=1 << 29, bytes_accessed=4 << 20, transcendentals=0),
         name="events",
-    )(att, src, pick_t, s_qkv, up, weights)
+    )(core, att, src, pick_t, s_qkv, up, weights)
 
 
 def attend(core, slots, chosen, chosen_t, time_kv, code_t, up, weights):
@@ -349,49 +351,49 @@
     )(core, slots, chosen, chosen_t, time_kv, code_t, up, weights)
 
 
-def pair_kernel(a, b, d_slots, out):
+def pair_kernel(a, b, keep, got, out):
     out[:, :PIECE] = (a[...].astype(F32) + b[...].astype(F32)).astype(BF)
-    out[:, PIECE:] = d_slots[...]
-
-
-def pair_sum(a, b, d_slots):
+    near, far = (x[...].astype(F32).reshape(4, CAP, DM) for x in (keep, got))
+    out[:, PIECE:] = jnp.concatenate([near, far], axis=1).astype(BF)
+
+
+def pair_sum(a, b, keep, got):
     spec = pl.BlockSpec((4, PIECE, DM), lambda i: (i, 0, 0))
+    rows = pl.BlockSpec((4 * CAP, DM), lambda i: (i, 0))
     return pl.pallas_call(
         pair_kernel,
         grid=(PLANE // 4,),
-        in_specs=[spec, spec, pl.BlockSpec((4, 2 * CAP, DM), lambda i: (i, 0, 0))],
+        in_specs=[spec, spec, rows, rows],
         out_specs=pl.BlockSpec((4, PIECE + 2 * CAP, DM), lambda i: (i, 0, 0)),
         out_shape=jax.ShapeDtypeStruct((PLANE, PIECE + 2 * CAP, DM), BF),
         compiler_params=pltpu.CompilerParams(vmem_limit_bytes=16 << 20),
         cost_estimate=pl.CostEstimate(flops=1 << 19, bytes_accessed=3 << 20, transcendentals=0),
         name="pair_sum",
-    )(a, b, d_slots.reshape(PLANE, 2 * CAP, DM))
-
-
-def plane_kernel(core, a, part, keep, give):
+    )(a, b, keep, got)
+
+
+def plane_kernel(a, part, near, far):
     total = a[0, :PIECE].astype(F32)
     for i in range(1, PLANE):
         total += a[i, :PIECE].astype(F32)
     part[...] = total.astype(BF)
     grads = a[:, PIECE:].astype(F32)
-    low, high = grads[:, :CAP].reshape(SLOTS // 2, DM), grads[:, CAP:].reshape(SLOTS // 2, DM)
-    first = core[0] == 0
-    keep[...] = jnp.where(first, low, high).astype(BF)
-    give[...] = jnp.where(first, high, low).astype(BF)
-
-
-def plane_sum(core, a):
+    near[...] = grads[:, :CAP].reshape(SLOTS // 2, DM).astype(BF)
+    far[...] = grads[:, CAP:].reshape(SLOTS // 2, DM).astype(BF)
+
+
+def plane_sum(a):
     whole = pl.BlockSpec(memory_space=pltpu.VMEM)
     half = jax.ShapeDtypeStruct((SLOTS // 2, DM), BF)
     return pl.pallas_call(
         plane_kernel,
-        in_specs=[pl.BlockSpec(memory_space=pltpu.SMEM), whole],
+        in_specs=[whole],
         out_specs=[whole] * 3,
         out_shape=[jax.ShapeDtypeStruct((PIECE, DM), BF), half, half],
         compiler_params=pltpu.CompilerParams(vmem_limit_bytes=16 << 20),
         cost_estimate=pl.CostEstimate(flops=1 << 19, bytes_accessed=2 << 20, transcendentals=0),
         name="plane_sum",
-    )(core, a)
+    )(a)
 
 
 def seg_kernel(seg, own, r1, r2, r3, out, parts):
@@ -424,7 +426,7 @@
         at = pl.ds(i * PLANE // 4, PLANE // 4)
         wide[at] = half[at].astype(F32)
         copies.append(pltpu.make_async_copy(wide.at[at], out.at[at, place], sem.at[i]))
-        copies[-1].start()
+        copies[-1].start(priority=i % 2)
     for copy in copies:
         copy.wait()
 
@@ -514,16 +516,14 @@
         core, slots, chosen, chosen_t, time_kv, code_t, up, attn_weights
     )
     partner = lax.ppermute(other, "core", swap)
-    embedded, d_slots = events(*kept, up, attn_weights)
-    parts = plane(pair_sum(mine, partner, d_slots))
-    part, keep, give = plane_sum(core, parts)
+    embedded, keep, give = events(core, *kept, up, attn_weights)
     got = lax.ppermute(give, "core", swap)
-    turns = {s: [(i, (i + s) % SEG) for i in range(SEG)] for s in (1, 2, 3)}
-    r2 = lax.ppermute(part, "y", turns[2])
-    memory_grad = owner_sum(core, asked, keep, got)
-    late, memory_grad = lax.optimization_barrier((part, memory_grad))
-    r1, r3 = (lax.ppermute(late, "y", turns[s]) for s in (1, 3))
+    part, near, far = plane_sum(plane(pair_sum(mine, partner, keep, got)))
+    r2, r3, r1 = (
+        lax.ppermute(part, "y", [(i, (i + s) % SEG) for i in range(SEG)]) for s in (2, 3, 1)
+    )
     half = plane(seg_sum(seg, part, r1, r2, r3))
+    memory_grad = owner_sum(core, asked, near, far)
     far = lax.ppermute(half, "core", swap)
     weight_grad = whole_grad(core, far, whole_grad(core, half))
     return embedded[None], memory[None], memory_grad[None], weight_grad.reshape(4, DM, DM)

time: 117 us -> 113 us (0.966)
  waiting for transfers between devices: 7.37 us -> 5.66 us
  blocking collectives: 68.6 us -> 67.1 us
    ppermute x1, starting transfers between devices: 3.07 us -> 4.83 us  [on_device(): far = lax.ppermute(half, 'core', swap)]
    ppermute x1, starting transfers between devices: 1.87 us -> 0.32 us  [on_device(): got = lax.ppermute(give, 'core', swap)]
    all_to_all x3, blocking collectives: 54.2 us -> 52.7 us  [plane(): return lax.all_to_all(x, FLAT, split_axis=0, concat_axis=0, tiled=True)]
    ppermute x1, waiting for transfers between devices: 1.45 us -> 0.01 us  [on_device(): partner = lax.ppermute(other, 'core', swap)]
  transfers between devices with their start and end apart: 10 -> 10, of which waited for: 6 -> 4; matrix products, arithmetic and copies ran while one was open for 0% -> 0% of each run, Pallas kernels for 10% -> 10%
where the time goes in v8:
time: 113 us
  blocking collectives  67.1 us (59%)
  Pallas kernels  22.1 us (20%)
  starting transfers between devices  17 us (15%)
  waiting for transfers between devices  5.66 us (5%)
    all_to_all x3, blocking collectives, plane(): return lax.all_to_all(x, FLAT, split_axis=0, concat_axis=0, tiled=True)  52.7 us
    all_to_all x1, blocking collectives, exchange(): lax.all_to_all(blocks, axes, split_axis=0, concat_axis=0, tiled=True)  14.4 us
    pallas_call x1, Pallas kernels, attend(): pl.pallas_call(attend_kernel, in_specs=[pl.BlockSpec(memory_space=pltpu.S...  7.44 us
    ppermute x1, starting transfers between devices, on_device(): far = lax.ppermute(half, 'core', swap)  4.83 us
    ppermute x1, starting transfers between devices, on_device(): r3 = lax.ppermute(written, 'y', [(0, 3)])  4.74 us
    ppermute x3, waiting for transfers between devices, on_device(): lax.ppermute(part, 'y', [(i, (i + s) % SEG) for i in range(SEG)])  4.32 us
    pallas_call x1, Pallas kernels, gru(): pl.pallas_call(gru_kernel, in_specs=[whole] + [far] * 4, out_specs=whole,...  4.2 us
    pallas_call x1, Pallas kernels, time_parts(): pl.pallas_call(time_kernel, in_specs=[pl.BlockSpec(memory_space=pltpu.SME...  3.91 us
  transfers between devices with their start and end apart: 10, of which 4 were waited for; matrix products, arithmetic and copies ran while one was open for 0% of the time, Pallas kernels for 10%

profile of v8, /device:TPU:1, one launch (start us, length us, event | category | flops | bytes accessed | tf_op | source)
XLA Modules:
  0.0 113.0 jit_solution(18269599868634469149)
XLA Ops:
  0.6 0.0 copy-start.7
  0.6 0.0 copy-start.5
  0.7 0.0 copy-start
  0.7 0.0 copy-start.4
  0.7 0.0 copy-start.6
  0.7 1.5 %collective-permute-start = (s32[1,256]{1,0:T(1,128)}, s32[1,256]{1,0:T(1,128)S(1)}, u32[]{:S(2)}, u32[]{:S(2)}) collective-permute-start(s32[1,256]{1,0:T(1,128)} %bitcast.26), channel_id=1, source_target_pairs={{0,1},{1,0},{2,3},{3,2},{4,5},{5,4},{6,7},{7,6},{8,9},{9,8},{10,11... | collective-permute-start | bytes 3080 | tf_op jit(solution)/shard_map/ppermute | solution.py:498
  2.2 4.2 %gru.1.written = bf16[256,512]{1,0:T(8,128)(2,1)} custom-call(s32[1,256]{1,0:T(1,128)} %touched.1, bf16[256,512]{1,0:T(8,128)(2,1)} %state.3, bf16[256,512]{1,0:T(8,128)(2,1)} %bitcast.30, bf16[512,1536]{1,0:T(8,128)(2,1)} %w_input.1, bf16[512,1536]{1,0:T(8,128)(2,1)} %w_state.1), custom_call_target="tpu_custom_call" | custom-call | flops 805306368 | bytes 4194304 | tf_op jit(solution)/shard_map/gru/pallas_call | solution.py:89
  6.4 4.7 %collective-permute-start.3 = (bf16[256,512]{1,0:T(8,128)(2,1)}, bf16[256,512]{1,0:T(8,128)(2,1)S(1)}, u32[]{:S(2)}, u32[]{:S(2)}) collective-permute-start(bf16[256,512]{1,0:T(8,128)(2,1)} %gru.1.written), channel_id=1, source_target_pairs={{0,96},{1,97},{2,98},{3,99},{4,100},{5,101},{6,102},{7,103},{8,104... | collective-permute-start | bytes 786440 | tf_op jit(solution)/shard_map/ppermute | solution.py:502
  11.1 1.3 %collective-permute-start.2 = (bf16[256,512]{1,0:T(8,128)(2,1)}, bf16[256,512]{1,0:T(8,128)(2,1)S(1)}, u32[]{:S(2)}, u32[]{:S(2)}) collective-permute-start(bf16[256,512]{1,0:T(8,128)(2,1)} %gru.1.written), channel_id=1, source_target_pairs={{0,64},{32,96},{1,65},{33,97},{2,66},{34,98},{3,67},{35,99},{4,68}... | collective-permute-start | bytes 786440 | tf_op jit(solution)/shard_map/ppermute | solution.py:501
  12.5 2.5 %collective-permute-start.1 = (bf16[256,512]{1,0:T(8,128)(2,1)}, bf16[256,512]{1,0:T(8,128)(2,1)S(1)}, u32[]{:S(2)}, u32[]{:S(2)}) collective-permute-start(bf16[256,512]{1,0:T(8,128)(2,1)} %gru.1.written), channel_id=1, source_target_pairs={{0,32},{32,64},{64,96},{1,33},{33,65},{65,97},{2,34},{34,66},{66,9... | collective-permute-start | bytes 786440 | tf_op jit(solution)/shard_map/ppermute | solution.py:500
  14.9 0.0 collective-permute-done.ids_far
  15.0 0.0 copy-done.7
  15.0 0.0 copy-done.5
  15.0 0.0 copy-done
  15.0 0.0 copy-done.4
  15.0 0.0 copy-done.6
  15.0 0.0 copy-start.1
  15.0 0.0 copy-start.2
  15.0 3.9 %time_parts.1 = (bf16[2,512,1024]{2,1,0:T(8,128)(2,1)S(1)}, bf16[2,1024,1024]{2,1,0:T(8,128)(2,1)S(1)}, s32[256,128]{1,0:T(8,128)S(1)}, s32[16,2,8,128]{3,2,1,0:T(8,128)S(1)}) custom-call(s32[1]{0:T(128)} %bitcast.4.core, s32[1,256]{1,0:T(1,128)S(1)} %bitcast.27, s32[1,256]{1,0:T(1,128)S(1)} %collective-permute-done.ids_far, s32[8,256]{1,0:T(8,128)S(1)} %bitcast.24, ...), custom_call_target="tpu_custom_call" | custom-call | flops 2147483648 | bytes 8388608 | tf_op jit(solution)/shard_map/time_parts/pallas_call | solution.py:139
  19.0 0.0 copy-start.3
  19.0 14.4 %all_to_all.20.asked = s32[16,2,8,128]{3,2,1,0:T(8,128)S(1)} all-to-all(s32[16,2,8,128]{3,2,1,0:T(8,128)S(1)} %get-tuple-element.40), channel_id=1, replica_groups=mesh['y'=4,'x'=4,'z'=4,'core'=2] {'x','z'}, dimensions={0} | all-to-all | bytes 262144 | tf_op jit(solution)/shard_map/all_to_all | solution.py:478
  33.3 0.0 collective-permute-done.3.r3
  33.3 0.0 collective-permute-done.2.r2
  33.3 0.0 collective-permute-done.1.r1
  33.4 1.1 start_rows.1
  34.5 14.4 %all_to_all.21 = bf16[32,8,512]{2,1,0:T(8,128)(2,1)S(1)} all-to-all(bf16[32,8,512]{2,1,0:T(8,128)(2,1)S(1)} %bitcast.21), channel_id=1, replica_groups=mesh['y'=4,'x'=4,'z'=4,'core'=2] {'x','z','core'}, dimensions={0} | all-to-all | bytes 524288 | tf_op jit(solution)/shard_map/all_to_all | solution.py:474
  48.9 7.4 %attend.1 = (bf16[16,64,512]{2,1,0:T(8,128)(2,1)S(1)}, bf16[16,64,512]{2,1,0:T(8,128)(2,1)S(1)}, bf16[256,512]{1,0:T(8,128)(2,1)S(1)}, bf16[256,512]{1,0:T(8,128...) custom-call(s32[1]{0:T(128)} %bitcast.4.core, bf16[256,512]{1,0:T(8,128)(2,1)S(1)} %bitcast.20, ...), custom_call_target="tpu_custom_call" | custom-call | flops 6442450944 | bytes 14680064 | tf_op jit(solution)/shard_map/attend/pallas_call | solution.py:326
  56.3 0.3 collective-permute-start.4
  56.6 1.0 events.1
  57.6 0.3 collective-permute-start.5
  57.9 1.3 %collective-permute-done.5.got = bf16[128,512]{1,0:T(8,128)(2,1)S(1)} collective-permute-done((bf16[128,512]{1,0:T(8,128)(2,1)S(1)}, bf16[128,512]{1,0:T(8,128)(2,1)S(1)}, u32[]{:S(2)}, u32[]{:S(2)}) %collective-permute-start.5) | collective-permute-done | bytes 131104 | tf_op jit(solution)/shard_map/ppermute | solution.py:520
  59.3 0.0 collective-permute-done.4.b
  59.3 0.3 pair_sum.1
  59.6 21.7 %all_to_all.22.a = bf16[16,80,512]{2,1,0:T(8,128)(2,1)S(1)} all-to-all(bf16[16,80,512]{2,1,0:T(8,128)(2,1)S(1)} %pair_sum.1), channel_id=1, replica_groups=mesh['y'=4,'x'=4,'z'=4,'core'=2] {'x','z'}, dimensions={0} | all-to-all | bytes 2621440 | tf_op jit(solution)/shard_map/all_to_all | solution.py:478
  81.2 0.1 plane_sum.1
  81.4 0.1 collective-permute-start.8
  81.5 1.5 %collective-permute-start.7 = (bf16[64,512]{1,0:T(8,128)(2,1)S(1)}, bf16[64,512]{1,0:T(8,128)(2,1)S(1)}, u32[]{:S(2)}, u32[]{:S(2)}) collective-permute-start(bf16[64,512]{1,0:T(8,128)(2,1)S(1)} %get-tuple-element.57.own), channel_id=1, source_target_pairs={{0,64},{32,96},{64,0},{96,32},{1,65},{33,97},{65,1},{97,33},{2,66}... | collective-permute-start | bytes 196616 | tf_op jit(solution)/shard_map/ppermute | solution.py:523
  83.0 0.0 collective-permute-start.6
  83.0 1.6 %collective-permute-done.8.r3 = bf16[64,512]{1,0:T(8,128)(2,1)S(1)} collective-permute-done((bf16[64,512]{1,0:T(8,128)(2,1)S(1)}, bf16[64,512]{1,0:T(8,128)(2,1)S(1)}, u32[]{:S(2)}, u32[]{:S(2)}) %collective-permute-start.8) | collective-permute-done | bytes 65568 | tf_op jit(solution)/shard_map/ppermute | solution.py:523
  84.6 1.6 %collective-permute-done.7.r2 = bf16[64,512]{1,0:T(8,128)(2,1)S(1)} collective-permute-done((bf16[64,512]{1,0:T(8,128)(2,1)S(1)}, bf16[64,512]{1,0:T(8,128)(2,1)S(1)}, u32[]{:S(2)}, u32[]{:S(2)}) %collective-permute-start.7) | collective-permute-done | bytes 65568 | tf_op jit(solution)/shard_map/ppermute | solution.py:523
  86.2 1.1 %collective-permute-done.6.r1 = bf16[64,512]{1,0:T(8,128)(2,1)S(1)} collective-permute-done((bf16[64,512]{1,0:T(8,128)(2,1)S(1)}, bf16[64,512]{1,0:T(8,128)(2,1)S(1)}, u32[]{:S(2)}, u32[]{:S(2)}) %collective-permute-start.6) | collective-permute-done | bytes 65568 | tf_op jit(solution)/shard_map/ppermute | solution.py:523
  87.3 0.1 seg_sum.1
  87.4 16.6 %all_to_all.23.half = bf16[16,64,512]{2,1,0:T(8,128)(2,1)S(1)} all-to-all(bf16[16,64,512]{2,1,0:T(8,128)(2,1)S(1)} %seg_sum.1), channel_id=1, replica_groups=mesh['y'=4,'x'=4,'z'=4,'core'=2] {'x','z'}, dimensions={0} | all-to-all | bytes 2097152 | tf_op jit(solution)/shard_map/all_to_all | solution.py:478
  104.1 4.8 %collective-permute-start.9 = (bf16[16,64,512]{2,1,0:T(8,128)(2,1)S(1)}, bf16[16,64,512]{2,1,0:T(8,128)(2,1)S(1)}, u32[]{:S(2)}, u32[]{:S(2)}) collective-permute-start(bf16[16,64,512]{2,1,0:T(8,128)(2,1)S(1)} %all_to_all.23.half), channel_id=1, source_target_pairs={{0,1},{1,0},{2,3},{3,2},{4,5},{5,4},{6,7},{7,6},{8,9},{9,8},{10,11... | collective-permute-start | bytes 3145736 | tf_op jit(solution)/shard_map/ppermute | solution.py:527
  108.9 1.1 owner_sum.1
  110.0 1.4 %own_half.1.rest_0_ = f32[16,2,64,512]{3,2,1,0:T(8,128)} custom-call(s32[1]{0:T(128)} %bitcast.4.core, bf16[16,64,512]{2,1,0:T(8,128)(2,1)S(1)} %all_to_all.23.half), custom_call_target="tpu_custom_call" | custom-call | flops 262144 | bytes 3145728 | tf_op jit(solution)/shard_map/own_half/pallas_call | solution.py:437
  111.4 0.0 collective-permute-done.9.half
  111.4 1.4 %far_half.1 = f32[16,2,64,512]{3,2,1,0:T(8,128)} custom-call(s32[1]{0:T(128)} %bitcast.4.core, bf16[16,64,512]{2,1,0:T(8,128)(2,1)S(1)} %collective-permute-done.9.half, f32[16,2,64,512]{3,2,1,0:T(8,128)} %own_half.1.rest_0_), custom_call_target="tpu_custom_call", output_to_operand_aliasing={{}: (2, {})} | custom-call | flops 262144 | bytes 3145728 | tf_op jit(solution)/shard_map/far_half/pallas_call | solution.py:437
  (3 shorter events, 0.0 us)
Async XLA Ops:
  0.6 14.3 %copy-start.7 = (s32[1,1,256]{2,1,0:T(1,128)S(1)}, s32[1,1,256]{2,1,0:T(1,128)}, u32[]{:S(2)}) copy-start(s32[1,1,256]{2,1,0:T(1,128)} %param.18) | copy-start | bytes 3076
  0.6 14.3 %copy-start.5 = (s32[1,256,8]{1,2,0:T(8,128)S(1)}, s32[1,256,8]{1,2,0:T(8,128)}, u32[]{:S(2)}) copy-start(s32[1,256,8]{1,2,0:T(8,128)} %param.20) | copy-start | bytes 24580
  0.7 14.3 %copy-start = (bf16[4,512,512]{2,1,0:T(8,128)(2,1)S(1)}, bf16[4,512,512]{2,1,0:T(8,128)(2,1)}, u32[]{:S(2)}) copy-start(bf16[4,512,512]{2,1,0:T(8,128)(2,1)} %w.3) | copy-start | bytes 6291460
  0.7 14.3 %copy-start.4 = (s32[1,256,9]{1,0,2:T(1,128)S(1)}, s32[1,256,9]{1,0,2:T(1,128)}, u32[]{:S(2)}) copy-start(s32[1,256,9]{1,0,2:T(1,128)} %param.19) | copy-start | bytes 27652
  0.7 14.3 %copy-start.6 = (f32[512]{0:T(512)S(1)}, f32[512]{0:T(512)}, u32[]{:S(2)}) copy-start(f32[512]{0:T(512)} %param.17) | copy-start | bytes 6148
  0.7 14.3 %collective-permute-start = (s32[1,256]{1,0:T(1,128)}, s32[1,256]{1,0:T(1,128)S(1)}, u32[]{:S(2)}, u32[]{:S(2)}) collective-permute-start(s32[1,256]{1,0:T(1,128)} %bitcast.26), channel_id=1, source_target_pairs={{0,1},{1,0},{2,3},{3,2},{4,5},{5,4},{6,7},{7,6},{8,9},{9,8},{10,11... | collective-permute-start | bytes 3080 | tf_op jit(solution)/shard_map/ppermute | solution.py:498
  6.4 26.9 %collective-permute-start.3 = (bf16[256,512]{1,0:T(8,128)(2,1)}, bf16[256,512]{1,0:T(8,128)(2,1)S(1)}, u32[]{:S(2)}, u32[]{:S(2)}) collective-permute-start(bf16[256,512]{1,0:T(8,128)(2,1)} %gru.1.written), channel_id=1, source_target_pairs={{0,96},{1,97},{2,98},{3,99},{4,100},{5,101},{6,102},{7,103},{8,104... | collective-permute-start | bytes 786440 | tf_op jit(solution)/shard_map/ppermute | solution.py:502
  11.1 22.2 %collective-permute-start.2 = (bf16[256,512]{1,0:T(8,128)(2,1)}, bf16[256,512]{1,0:T(8,128)(2,1)S(1)}, u32[]{:S(2)}, u32[]{:S(2)}) collective-permute-start(bf16[256,512]{1,0:T(8,128)(2,1)} %gru.1.written), channel_id=1, source_target_pairs={{0,64},{32,96},{1,65},{33,97},{2,66},{34,98},{3,67},{35,99},{4,68}... | collective-permute-start | bytes 786440 | tf_op jit(solution)/shard_map/ppermute | solution.py:501
  12.5 20.9 %collective-permute-start.1 = (bf16[256,512]{1,0:T(8,128)(2,1)}, bf16[256,512]{1,0:T(8,128)(2,1)S(1)}, u32[]{:S(2)}, u32[]{:S(2)}) collective-permute-start(bf16[256,512]{1,0:T(8,128)(2,1)} %gru.1.written), channel_id=1, source_target_pairs={{0,32},{32,64},{64,96},{1,33},{33,65},{65,97},{2,34},{34,66},{66,9... | collective-permute-start | bytes 786440 | tf_op jit(solution)/shard_map/ppermute | solution.py:500
  15.0 18.3 %copy-start.1 = (bf16[256,512]{1,0:T(8,128)(2,1)S(1)}, bf16[256,512]{1,0:T(8,128)(2,1)}, u32[]{:S(2)}) copy-start(bf16[256,512]{1,0:T(8,128)(2,1)} %state.3) | copy-start | bytes 786436
  15.0 18.3 %copy-start.2 = (bf16[256,512]{1,0:T(8,128)(2,1)S(1)}, bf16[256,512]{1,0:T(8,128)(2,1)}, u32[]{:S(2)}) copy-start(bf16[256,512]{1,0:T(8,128)(2,1)} %gru.1.written) | copy-start | bytes 786436
  19.0 29.9 %copy-start.3 = (bf16[1,256,512]{2,1,0:T(8,128)(2,1)S(1)}, bf16[1,256,512]{2,1,0:T(8,128)(2,1)}, u32[]{:S(2)}) copy-start(bf16[1,256,512]{2,1,0:T(8,128)(2,1)} %param.21) | copy-start | bytes 786436
  56.3 2.9 %collective-permute-start.4 = (bf16[16,64,512]{2,1,0:T(8,128)(2,1)S(1)}, bf16[16,64,512]{2,1,0:T(8,128)(2,1)S(1)}, u32[]{:S(2)}, u32[]{:S(2)}) collective-permute-start(bf16[16,64,512]{2,1,0:T(8,128)(2,1)S(1)} %get-tuple-element.52), channel_id=1, source_target_pairs={{0,1},{1,0},{2,3},{3,2},{4,5},{5,4},{6,7},{7,6},{8,9},{9,8},{10,11... | collective-permute-start | bytes 3145736 | tf_op jit(solution)/shard_map/ppermute | solution.py:518
  57.6 1.6 %collective-permute-start.5 = (bf16[128,512]{1,0:T(8,128)(2,1)S(1)}, bf16[128,512]{1,0:T(8,128)(2,1)S(1)}, u32[]{:S(2)}, u32[]{:S(2)}) collective-permute-start(bf16[128,512]{1,0:T(8,128)(2,1)S(1)} %get-tuple-element.54), channel_id=1, source_target_pairs={{0,1},{1,0},{2,3},{3,2},{4,5},{5,4},{6,7},{7,6},{8,9},{9,8},{10,11... | collective-permute-start | bytes 393224 | tf_op jit(solution)/shard_map/ppermute | solution.py:520
  81.4 3.2 %collective-permute-start.8 = (bf16[64,512]{1,0:T(8,128)(2,1)S(1)}, bf16[64,512]{1,0:T(8,128)(2,1)S(1)}, u32[]{:S(2)}, u32[]{:S(2)}) collective-permute-start(bf16[64,512]{1,0:T(8,128)(2,1)S(1)} %get-tuple-element.57.own), channel_id=1, source_target_pairs={{0,96},{32,0},{64,32},{96,64},{1,97},{33,1},{65,33},{97,65},{2,98}... | collective-permute-start | bytes 196616 | tf_op jit(solution)/shard_map/ppermute | solution.py:523
  81.5 4.7 %collective-permute-start.7 = (bf16[64,512]{1,0:T(8,128)(2,1)S(1)}, bf16[64,512]{1,0:T(8,128)(2,1)S(1)}, u32[]{:S(2)}, u32[]{:S(2)}) collective-permute-start(bf16[64,512]{1,0:T(8,128)(2,1)S(1)} %get-tuple-element.57.own), channel_id=1, source_target_pairs={{0,64},{32,96},{64,0},{96,32},{1,65},{33,97},{65,1},{97,33},{2,66}... | collective-permute-start | bytes 196616 | tf_op jit(solution)/shard_map/ppermute | solution.py:523
  83.0 4.3 %collective-permute-start.6 = (bf16[64,512]{1,0:T(8,128)(2,1)S(1)}, bf16[64,512]{1,0:T(8,128)(2,1)S(1)}, u32[]{:S(2)}, u32[]{:S(2)}) collective-permute-start(bf16[64,512]{1,0:T(8,128)(2,1)S(1)} %get-tuple-element.57.own), channel_id=1, source_target_pairs={{0,32},{32,64},{64,96},{96,0},{1,33},{33,65},{65,97},{97,1},{2,34}... | collective-permute-start | bytes 196616 | tf_op jit(solution)/shard_map/ppermute | solution.py:523
  104.1 7.3 %collective-permute-start.9 = (bf16[16,64,512]{2,1,0:T(8,128)(2,1)S(1)}, bf16[16,64,512]{2,1,0:T(8,128)(2,1)S(1)}, u32[]{:S(2)}, u32[]{:S(2)}) collective-permute-start(bf16[16,64,512]{2,1,0:T(8,128)(2,1)S(1)} %all_to_all.23.half), channel_id=1, source_target_pairs={{0,1},{1,0},{2,3},{3,2},{4,5},{5,4},{6,7},{7,6},{8,9},{9,8},{10,11... | collective-permute-start | bytes 3145736 | tf_op jit(solution)/shard_map/ppermute | solution.py:527

commit v9 on v8

--- a/solution.py
+++ b/solution.py
@@ -106,12 +106,8 @@
     )(touched, state, message, w_input, w_state)
 
 
-def time_kernel(core, ids, ids_far, delays, frequency, w, chosen, code_t, time_kv, picked, wanted):
-    first = core[0] == 0
-    for side, row in ((0, ids), (1, ids_far)):
-        blocks = jnp.broadcast_to(column(row[...]), (SLOTS, 128)).reshape(PLANE, CORES, CAP, 128)
-        mine = jnp.where(first, blocks[:, 0], blocks[:, 1]).astype(jnp.int32)
-        wanted[:, core[0] if side == 0 else 1 - core[0]] = mine
+def time_kernel(ids, delays, frequency, w, chosen, code_t, time_kv, picked, wanted):
+    wanted[...] = jnp.broadcast_to(column(ids[...]), (SLOTS, 128)).astype(jnp.int32)
     lane = iota((E, 128), 1)
     columns = jnp.zeros((E, 128), F32)
     for j in range(K + 1):
@@ -134,24 +130,24 @@
             time_kv[tile, at, DM:] = dot(wave, w[2]).astype(BF)
 
 
-def time_parts(core, ids, ids_far, delays, frequency, weights, chosen):
+def time_parts(ids, delays, frequency, weights, chosen):
     whole = pl.BlockSpec(memory_space=pltpu.VMEM)
     return pl.pallas_call(
         time_kernel,
-        in_specs=[pl.BlockSpec(memory_space=pltpu.SMEM)] + [whole] * 6,
+        in_specs=[whole] * 5,
         out_specs=[whole] * 4,
         out_shape=[
             jax.ShapeDtypeStruct((TILES, DM, ROWS), BF),
             jax.ShapeDtypeStruct((TILES, ROWS, 2 * DM), BF),
             jax.ShapeDtypeStruct((E, 128), jnp.int32),
-            jax.ShapeDtypeStruct((PLANE, CORES, CAP, 128), jnp.int32),
+            jax.ShapeDtypeStruct((SLOTS, 128), jnp.int32),
         ],
         compiler_params=pltpu.CompilerParams(vmem_limit_bytes=24 << 20),
         cost_estimate=pl.CostEstimate(
             flops=4 * K * E * DM * DM, bytes_accessed=8 << 20, transcendentals=K * E * DM
         ),
         name="time_parts",
-    )(core, ids, ids_far, delays, frequency, weights, chosen)
+    )(ids, delays, frequency, weights, chosen)
 
 
 def owner_pick(asked):
@@ -295,30 +291,25 @@
     store(3, dot_tn(att[...], up[...]))
 
 
-def events_kernel(core, att, src, pick_t, s_qkv, up, w, embedded, keep, give):
+def events_kernel(att, src, pick_t, s_qkv, up, w, embedded, d_slots):
     embedded[...] = (dot(att[...], w[3]) + src[...].astype(F32)).astype(BF)
     grads = dot(pick_t[...], up[...])
     for i in range(3):
         grads += dot_nt(s_qkv[:, i * DM : (i + 1) * DM], w[i])
-    blocks = grads.reshape(PLANE, CORES, CAP, DM)
-    first = core[0] == 0
-    low, high = (blocks[:, i].reshape(SLOTS // 2, DM) for i in range(2))
-    keep[...] = jnp.where(first, low, high).astype(BF)
-    give[...] = jnp.where(first, high, low).astype(BF)
-
-
-def events(core, att, src, pick_t, s_qkv, up, weights):
+    d_slots[...] = grads.astype(BF)
+
+
+def events(att, src, pick_t, s_qkv, up, weights):
     whole = pl.BlockSpec(memory_space=pltpu.VMEM)
     return pl.pallas_call(
         events_kernel,
-        in_specs=[pl.BlockSpec(memory_space=pltpu.SMEM)] + [whole] * 6,
-        out_specs=[whole] * 3,
-        out_shape=[jax.ShapeDtypeStruct((E, DM), BF)]
-        + [jax.ShapeDtypeStruct((SLOTS // 2, DM), BF)] * 2,
+        in_specs=[whole] * 6,
+        out_specs=[whole] * 2,
+        out_shape=[jax.ShapeDtypeStruct((E, DM), BF), jax.ShapeDtypeStruct((SLOTS, DM), BF)],
         compiler_params=pltpu.CompilerParams(vmem_limit_bytes=16 << 20),
         cost_estimate=pl.CostEstimate(flops=1 << 29, bytes_accessed=4 << 20, transcendentals=0),
         name="events",
-    )(core, att, src, pick_t, s_qkv, up, weights)
+    )(att, src, pick_t, s_qkv, up, weights)
 
 
 def attend(core, slots, chosen, chosen_t, time_kv, code_t, up, weights):
@@ -351,45 +342,37 @@
     )(core, slots, chosen, chosen_t, time_kv, code_t, up, weights)
 
 
-def pair_kernel(a, b, keep, got, out):
-    out[:, :PIECE] = (a[...].astype(F32) + b[...].astype(F32)).astype(BF)
-    near, far = (x[...].astype(F32).reshape(4, CAP, DM) for x in (keep, got))
-    out[:, PIECE:] = jnp.concatenate([near, far], axis=1).astype(BF)
-
-
-def pair_sum(a, b, keep, got):
-    spec = pl.BlockSpec((4, PIECE, DM), lambda i: (i, 0, 0))
-    rows = pl.BlockSpec((4 * CAP, DM), lambda i: (i, 0))
+def pair_kernel(a, b, out):
+    out[...] = (a[...].astype(F32) + b[...].astype(F32)).astype(BF)
+
+
+def pair_sum(a, b):
+    whole = pl.BlockSpec(memory_space=pltpu.VMEM)
     return pl.pallas_call(
         pair_kernel,
-        grid=(PLANE // 4,),
-        in_specs=[spec, spec, rows, rows],
-        out_specs=pl.BlockSpec((4, PIECE + 2 * CAP, DM), lambda i: (i, 0, 0)),
-        out_shape=jax.ShapeDtypeStruct((PLANE, PIECE + 2 * CAP, DM), BF),
+        in_specs=[whole] * 2,
+        out_specs=whole,
+        out_shape=jax.ShapeDtypeStruct((PLANE, PIECE, DM), BF),
         compiler_params=pltpu.CompilerParams(vmem_limit_bytes=16 << 20),
         cost_estimate=pl.CostEstimate(flops=1 << 19, bytes_accessed=3 << 20, transcendentals=0),
         name="pair_sum",
-    )(a, b, keep, got)
-
-
-def plane_kernel(a, part, near, far):
-    total = a[0, :PIECE].astype(F32)
+    )(a, b)
+
+
+def plane_kernel(a, part):
+    total = a[0].astype(F32)
     for i in range(1, PLANE):
-        total += a[i, :PIECE].astype(F32)
+        total += a[i].astype(F32)
     part[...] = total.astype(BF)
-    grads = a[:, PIECE:].astype(F32)
-    near[...] = grads[:, :CAP].reshape(SLOTS // 2, DM).astype(BF)
-    far[...] = grads[:, CAP:].reshape(SLOTS // 2, DM).astype(BF)
 
 
 def plane_sum(a):
     whole = pl.BlockSpec(memory_space=pltpu.VMEM)
-    half = jax.ShapeDtypeStruct((SLOTS // 2, DM), BF)
     return pl.pallas_call(
         plane_kernel,
         in_specs=[whole],
-        out_specs=[whole] * 3,
-        out_shape=[jax.ShapeDtypeStruct((PIECE, DM), BF), half, half],
+        out_specs=whole,
+        out_shape=jax.ShapeDtypeStruct((PIECE, DM), BF),
         compiler_params=pltpu.CompilerParams(vmem_limit_bytes=16 << 20),
         cost_estimate=pl.CostEstimate(flops=1 << 19, bytes_accessed=2 << 20, transcendentals=0),
         name="plane_sum",
@@ -448,17 +431,15 @@
     )(core, half, *([] if own else [before]))
 
 
-def owner_kernel(core, asked, keep, got, out):
-    near = asked[:, core[0]].reshape(SLOTS // 2, 128)
-    far = asked[:, 1 - core[0]].reshape(SLOTS // 2, 128)
-    out[...] = dot_tn(owner_pick(near), keep[...]) + dot_tn(owner_pick(far), got[...])
-
-
-def owner_sum(core, asked, keep, got):
+def owner_kernel(asked, grads, out):
+    out[...] = dot_tn(owner_pick(asked[...]), grads[...])
+
+
+def owner_sum(asked, grads):
     whole = pl.BlockSpec(memory_space=pltpu.VMEM)
     return pl.pallas_call(
         owner_kernel,
-        in_specs=[pl.BlockSpec(memory_space=pltpu.SMEM)] + [whole] * 3,
+        in_specs=[whole] * 2,
         out_specs=whole,
         out_shape=jax.ShapeDtypeStruct((N, DM), F32),
         compiler_params=pltpu.CompilerParams(vmem_limit_bytes=16 << 20),
@@ -466,7 +447,7 @@
             flops=2 * N * DM * SLOTS, bytes_accessed=1 << 20, transcendentals=0
         ),
         name="owner_sum",
-    )(core, asked.reshape(PLANE, CORES, CAP, 128), keep, got)
+    )(asked, grads)
 
 
 def exchange(rows, axes, count):
@@ -495,7 +476,6 @@
     core = lax.axis_index("core").reshape(1)
     swap = [(0, 1), (1, 0)]
     ids = request_rows.reshape(1, SLOTS)
-    ids_far = lax.ppermute(ids, "core", swap)
     written = gru(touched, memory_base, messages[0], gru_input, gru_state)
     r1 = lax.ppermute(written, "y", [(0, 1), (1, 2), (2, 3)])
     r2 = lax.ppermute(written, "y", [(0, 2), (1, 3)])
@@ -503,12 +483,12 @@
     written, late, seg, core = lax.optimization_barrier((written, delays[0].T, seg, core))
     chosen_t = event_slots.transpose(2, 0, 1)
     code_t, time_kv, chosen, wanted = time_parts(
-        core, ids, ids_far, late, frequency.reshape(1, DM), attn_weights, chosen_t
+        ids, late, frequency.reshape(1, DM), attn_weights, chosen_t
     )
     written, wanted, code_t, time_kv, chosen = lax.optimization_barrier(
         (written, wanted, code_t, time_kv, chosen)
     )
-    asked = plane(wanted).reshape(SLOTS, 128)
+    asked = exchange(wanted, NODE, OWNERS)
     memory, rows = start_rows(seg, memory_base, written, r1, r2, r3, asked)
     slots = exchange(rows, NODE, OWNERS)
     up = upstream[0]
@@ -516,14 +496,15 @@
         core, slots, chosen, chosen_t, time_kv, code_t, up, attn_weights
     )
     partner = lax.ppermute(other, "core", swap)
-    embedded, keep, give = events(core, *kept, up, attn_weights)
-    got = lax.ppermute(give, "core", swap)
-    part, near, far = plane_sum(plane(pair_sum(mine, partner, keep, got)))
+    embedded, d_slots = events(*kept, up, attn_weights)
+    pairs, d_slots = lax.optimization_barrier((pair_sum(mine, partner), d_slots))
+    parts, back = lax.optimization_barrier((plane(pairs), exchange(d_slots, NODE, OWNERS)))
+    part = plane_sum(parts)
     r2, r3, r1 = (
         lax.ppermute(part, "y", [(i, (i + s) % SEG) for i in range(SEG)]) for s in (2, 3, 1)
     )
     half = plane(seg_sum(seg, part, r1, r2, r3))
-    memory_grad = owner_sum(core, asked, near, far)
+    memory_grad = owner_sum(asked, back)
     far = lax.ppermute(half, "core", swap)
     weight_grad = whole_grad(core, far, whole_grad(core, half))
     return embedded[None], memory[None], memory_grad[None], weight_grad.reshape(4, DM, DM)

time: 113 us -> 123 us (1.088)
  blocking collectives: 67.1 us -> 77.2 us
    all_to_all x1 -> x3, blocking collectives: 14.4 us -> 41.8 us  [exchange(): lax.all_to_all(blocks, axes, split_axis=0, concat_axis=0, tiled=True)]
    all_to_all x3 -> x2, blocking collectives: 52.7 us -> 35.5 us  [plane(): return lax.all_to_all(x, FLAT, split_axis=0, concat_axis=0, tiled=True)]
    ppermute x2 -> x0, starting transfers between devices: 1.82 us -> none  [the longest x1 1.5 us: on_device(): ids_far = lax.ppermute(ids, 'core', swap)]
    ppermute x1, waiting for transfers between devices: 0.01 us -> 1.46 us  [on_device(): partner = lax.ppermute(other, 'core', swap)]
    ppermute x2 -> x0, waiting for transfers between devices: 1.33 us -> none  [the longest x1 1.32 us: on_device(): got = lax.ppermute(give, 'core', swap)]
  transfers between devices with their start and end apart: 10 -> 8, of which waited for: 4 -> 4; matrix products, arithmetic and copies ran while one was open for 0% -> 0% of each run, Pallas kernels for 10% -> 6%
where the time goes in v9:
time: 123 us; the launch traced here: 122 us
  blocking collectives  77.2 us (63%)
  Pallas kernels  22.1 us (18%)
  starting transfers between devices  15.9 us (13%)
  waiting for transfers between devices  5.79 us (5%)
    all_to_all x3, blocking collectives, exchange(): lax.all_to_all(blocks, axes, split_axis=0, concat_axis=0, tiled=True)  41.8 us
    all_to_all x2, blocking collectives, plane(): return lax.all_to_all(x, FLAT, split_axis=0, concat_axis=0, tiled=True)  35.5 us
    pallas_call x1, Pallas kernels, attend(): pl.pallas_call(attend_kernel, in_specs=[pl.BlockSpec(memory_space=pltpu.S...  7.44 us
    ppermute x1, starting transfers between devices, on_device(): r3 = lax.ppermute(written, 'y', [(0, 3)])  5.48 us
    ppermute x1, starting transfers between devices, on_device(): far = lax.ppermute(half, 'core', swap)  4.83 us
    pallas_call x1, Pallas kernels, gru(): pl.pallas_call(gru_kernel, in_specs=[whole] + [far] * 4, out_specs=whole,...  4.35 us
    ppermute x3, waiting for transfers between devices, on_device(): lax.ppermute(part, 'y', [(i, (i + s) % SEG) for i in range(SEG)])  4.32 us
    pallas_call x1, Pallas kernels, time_parts(): pl.pallas_call(time_kernel, in_specs=[whole] * 5, out_specs=[whole] * 4,...  3.89 us
  transfers between devices with their start and end apart: 8, of which 4 were waited for; matrix products, arithmetic and copies ran while one was open for 0% of the time, Pallas kernels for 6%

profile of v9, /device:TPU:1, one launch (start us, length us, event | category | flops | bytes accessed | tf_op | source)
XLA Modules:
  0.0 122.1 jit_solution(7911981898201210623)
XLA Ops:
  0.6 0.0 copy-start.5
  0.6 0.0 copy-start
  0.7 0.0 copy-start.4
  0.7 0.0 copy-start.7
  0.7 0.0 copy-start.6
  0.7 4.3 %gru.1.written = bf16[256,512]{1,0:T(8,128)(2,1)} custom-call(s32[1,256]{1,0:T(1,128)} %touched.1, bf16[256,512]{1,0:T(8,128)(2,1)} %state.3, bf16[256,512]{1,0:T(8,128)(2,1)} %bitcast.36, bf16[512,1536]{1,0:T(8,128)(2,1)} %w_input.1, bf16[512,1536]{1,0:T(8,128)(2,1)} %w_state.1), custom_call_target="tpu_custom_call" | custom-call | flops 805306368 | bytes 4194304 | tf_op jit(solution)/shard_map/gru/pallas_call | solution.py:89
  5.0 5.5 %collective-permute-start.2 = (bf16[256,512]{1,0:T(8,128)(2,1)}, bf16[256,512]{1,0:T(8,128)(2,1)S(1)}, u32[]{:S(2)}, u32[]{:S(2)}) collective-permute-start(bf16[256,512]{1,0:T(8,128)(2,1)} %gru.1.written), channel_id=1, source_target_pairs={{0,96},{1,97},{2,98},{3,99},{4,100},{5,101},{6,102},{7,103},{8,104... | collective-permute-start | bytes 786440 | tf_op jit(solution)/shard_map/ppermute | solution.py:482
  10.5 1.3 %collective-permute-start.1 = (bf16[256,512]{1,0:T(8,128)(2,1)}, bf16[256,512]{1,0:T(8,128)(2,1)S(1)}, u32[]{:S(2)}, u32[]{:S(2)}) collective-permute-start(bf16[256,512]{1,0:T(8,128)(2,1)} %gru.1.written), channel_id=1, source_target_pairs={{0,64},{32,96},{1,65},{33,97},{2,66},{34,98},{3,67},{35,99},{4,68}... | collective-permute-start | bytes 786440 | tf_op jit(solution)/shard_map/ppermute | solution.py:481
  11.8 2.5 %collective-permute-start = (bf16[256,512]{1,0:T(8,128)(2,1)}, bf16[256,512]{1,0:T(8,128)(2,1)S(1)}, u32[]{:S(2)}, u32[]{:S(2)}) collective-permute-start(bf16[256,512]{1,0:T(8,128)(2,1)} %gru.1.written), channel_id=1, source_target_pairs={{0,32},{32,64},{64,96},{1,33},{33,65},{65,97},{2,34},{34,66},{66,9... | collective-permute-start | bytes 786440 | tf_op jit(solution)/shard_map/ppermute | solution.py:480
  14.3 0.0 copy-done.5
  14.3 0.0 copy-done
  14.4 0.0 copy-done.4
  14.4 0.0 copy-done.7
  14.4 0.0 copy-done.6
  14.4 0.0 copy-start.1
  14.4 0.0 copy-start.2
  14.4 3.9 %time_parts.1 = (bf16[2,512,1024]{2,1,0:T(8,128)(2,1)S(1)}, bf16[2,1024,1024]{2,1,0:T(8,128)(2,1)S(1)}, s32[256,128]{1,0:T(8,128)S(1)}, s32[256,128]{1,0:T(8,128)S(1)}) custom-call(s32[1,256]{1,0:T(1,128)S(1)} %bitcast.33, s32[8,256]{1,0:T(8,128)S(1)} %bitcast.31, f32[1,512]{1,0:T(1,128)S(1)} %bitcast.32, bf16[4,512,512]{2,1,0:T(8,128)(2,1)S(1)} %copy-done, ...), custom_call_target="tpu_custom_call" | custom-call | flops 2147483648 | bytes 8388608 | tf_op jit(solution)/shard_map/time_parts/pallas_call | solution.py:135
  18.3 0.0 copy-start.3
  18.3 16.8 %all_to_all.25 = s32[32,8,128]{2,1,0:T(8,128)S(1)} all-to-all(s32[32,8,128]{2,1,0:T(8,128)S(1)} %bitcast.28), channel_id=1, replica_groups=mesh['y'=4,'x'=4,'z'=4,'core'=2] {'x','z','core'}, dimensions={0} | all-to-all | bytes 262144 | tf_op jit(solution)/shard_map/all_to_all | solution.py:455
  35.1 0.0 collective-permute-done.2.r3
  35.1 0.0 collective-permute-done.1.r2
  35.1 0.0 collective-permute-done.r1
  35.1 0.0 copy-done.1
  35.1 0.0 copy-done.2
  35.2 1.1 start_rows.1
  36.2 12.5 %all_to_all.26 = bf16[32,8,512]{2,1,0:T(8,128)(2,1)S(1)} all-to-all(bf16[32,8,512]{2,1,0:T(8,128)(2,1)S(1)} %bitcast.25), channel_id=1, replica_groups=mesh['y'=4,'x'=4,'z'=4,'core'=2] {'x','z','core'}, dimensions={0} | all-to-all | bytes 524288 | tf_op jit(solution)/shard_map/all_to_all | solution.py:455
  48.8 0.0 copy-done.3
  48.8 7.4 %attend.1 = (bf16[16,64,512]{2,1,0:T(8,128)(2,1)S(1)}, bf16[16,64,512]{2,1,0:T(8,128)(2,1)S(1)}, bf16[256,512]{1,0:T(8,128)(2,1)S(1)}, bf16[256,512]{1,0:T(8,128...) custom-call(s32[1]{0:T(128)} %bitcast.4.core, bf16[256,512]{1,0:T(8,128)(2,1)S(1)} %bitcast.24, ...), custom_call_target="tpu_custom_call" | custom-call | flops 6442450944 | bytes 14680064 | tf_op jit(solution)/shard_map/attend/pallas_call | solution.py:317
  56.2 0.3 collective-permute-start.3
  56.5 1.0 events.1
  57.5 1.5 %collective-permute-done.3.b = bf16[16,64,512]{2,1,0:T(8,128)(2,1)S(1)} collective-permute-done((bf16[16,64,512]{2,1,0:T(8,128)(2,1)S(1)}, bf16[16,64,512]{2,1,0:T(8,128)(2,1)S(1)}, u32[]{:S(2)}, u32[]{:S(2)}) %collective-permute-start.3) | collective-permute-done | bytes 1048608 | tf_op jit(solution)/shard_map/ppermute | solution.py:498
  59.0 0.2 pair_sum.1
  59.2 12.5 %all_to_all.27 = bf16[32,8,512]{2,1,0:T(8,128)(2,1)S(1)} all-to-all(bf16[32,8,512]{2,1,0:T(8,128)(2,1)S(1)} %bitcast.23), channel_id=1, replica_groups=mesh['y'=4,'x'=4,'z'=4,'core'=2] {'x','z','core'}, dimensions={0} | all-to-all | bytes 524288 | tf_op jit(solution)/shard_map/all_to_all | solution.py:455
  71.7 18.7 %all_to_all.28.a = bf16[16,64,512]{2,1,0:T(8,128)(2,1)S(1)} all-to-all(bf16[16,64,512]{2,1,0:T(8,128)(2,1)S(1)} %pair_sum.1), channel_id=1, replica_groups=mesh['y'=4,'x'=4,'z'=4,'core'=2] {'x','z'}, dimensions={0} | all-to-all | bytes 2097152 | tf_op jit(solution)/shard_map/all_to_all | solution.py:459
  90.4 0.1 plane_sum.1.own
  90.5 0.1 collective-permute-start.6
  90.6 1.5 %collective-permute-start.5 = (bf16[64,512]{1,0:T(8,128)(2,1)S(1)}, bf16[64,512]{1,0:T(8,128)(2,1)S(1)}, u32[]{:S(2)}, u32[]{:S(2)}) collective-permute-start(bf16[64,512]{1,0:T(8,128)(2,1)S(1)} %plane_sum.1.own), channel_id=1, source_target_pairs={{0,64},{32,96},{64,0},{96,32},{1,65},{33,97},{65,1},{97,33},{2,66}... | collective-permute-start | bytes 196616 | tf_op jit(solution)/shard_map/ppermute | solution.py:504
  92.1 0.0 collective-permute-start.4
  92.1 1.6 %collective-permute-done.6.r3 = bf16[64,512]{1,0:T(8,128)(2,1)S(1)} collective-permute-done((bf16[64,512]{1,0:T(8,128)(2,1)S(1)}, bf16[64,512]{1,0:T(8,128)(2,1)S(1)}, u32[]{:S(2)}, u32[]{:S(2)}) %collective-permute-start.6) | collective-permute-done | bytes 65568 | tf_op jit(solution)/shard_map/ppermute | solution.py:504
  93.7 1.6 %collective-permute-done.5.r2 = bf16[64,512]{1,0:T(8,128)(2,1)S(1)} collective-permute-done((bf16[64,512]{1,0:T(8,128)(2,1)S(1)}, bf16[64,512]{1,0:T(8,128)(2,1)S(1)}, u32[]{:S(2)}, u32[]{:S(2)}) %collective-permute-start.5) | collective-permute-done | bytes 65568 | tf_op jit(solution)/shard_map/ppermute | solution.py:504
  95.3 1.1 collective-permute-done.4.r1
  96.4 0.1 seg_sum.1
  96.6 16.8 %all_to_all.29.half = bf16[16,64,512]{2,1,0:T(8,128)(2,1)S(1)} all-to-all(bf16[16,64,512]{2,1,0:T(8,128)(2,1)S(1)} %seg_sum.1), channel_id=1, replica_groups=mesh['y'=4,'x'=4,'z'=4,'core'=2] {'x','z'}, dimensions={0} | all-to-all | bytes 2097152 | tf_op jit(solution)/shard_map/all_to_all | solution.py:459
  113.3 4.8 %collective-permute-start.7 = (bf16[16,64,512]{2,1,0:T(8,128)(2,1)S(1)}, bf16[16,64,512]{2,1,0:T(8,128)(2,1)S(1)}, u32[]{:S(2)}, u32[]{:S(2)}) collective-permute-start(bf16[16,64,512]{2,1,0:T(8,128)(2,1)S(1)} %all_to_all.29.half), channel_id=1, source_target_pairs={{0,1},{1,0},{2,3},{3,2},{4,5},{5,4},{6,7},{7,6},{8,9},{9,8},{10,11... | collective-permute-start | bytes 3145736 | tf_op jit(solution)/shard_map/ppermute | solution.py:508
  118.2 1.0 owner_sum.1
  119.2 1.4 %own_half.1.rest_0_ = f32[16,2,64,512]{3,2,1,0:T(8,128)} custom-call(s32[1]{0:T(128)} %bitcast.4.core, bf16[16,64,512]{2,1,0:T(8,128)(2,1)S(1)} %all_to_all.29.half), custom_call_target="tpu_custom_call" | custom-call | flops 262144 | bytes 3145728 | tf_op jit(solution)/shard_map/own_half/pallas_call | solution.py:420
  120.6 0.0 collective-permute-done.7.half
  120.6 1.4 %far_half.1 = f32[16,2,64,512]{3,2,1,0:T(8,128)} custom-call(s32[1]{0:T(128)} %bitcast.4.core, bf16[16,64,512]{2,1,0:T(8,128)(2,1)S(1)} %collective-permute-done.7.half, f32[16,2,64,512]{3,2,1,0:T(8,128)} %own_half.1.rest_0_), custom_call_target="tpu_custom_call", output_to_operand_aliasing={{}: (2, {})} | custom-call | flops 262144 | bytes 3145728 | tf_op jit(solution)/shard_map/far_half/pallas_call | solution.py:420
Async XLA Ops:
  0.6 13.7 %copy-start.5 = (s32[1,256,8]{1,2,0:T(8,128)S(1)}, s32[1,256,8]{1,2,0:T(8,128)}, u32[]{:S(2)}) copy-start(s32[1,256,8]{1,2,0:T(8,128)} %param.20) | copy-start | bytes 24580
  0.6 13.7 %copy-start = (bf16[4,512,512]{2,1,0:T(8,128)(2,1)S(1)}, bf16[4,512,512]{2,1,0:T(8,128)(2,1)}, u32[]{:S(2)}) copy-start(bf16[4,512,512]{2,1,0:T(8,128)(2,1)} %w.3) | copy-start | bytes 6291460
  0.7 13.7 %copy-start.4 = (s32[1,256,9]{1,0,2:T(1,128)S(1)}, s32[1,256,9]{1,0,2:T(1,128)}, u32[]{:S(2)}) copy-start(s32[1,256,9]{1,0,2:T(1,128)} %param.19) | copy-start | bytes 27652
  0.7 13.7 %copy-start.7 = (s32[1,1,256]{2,1,0:T(1,128)S(1)}, s32[1,1,256]{2,1,0:T(1,128)}, u32[]{:S(2)}) copy-start(s32[1,1,256]{2,1,0:T(1,128)} %param.18) | copy-start | bytes 3076
  0.7 13.7 %copy-start.6 = (f32[512]{0:T(512)S(1)}, f32[512]{0:T(512)}, u32[]{:S(2)}) copy-start(f32[512]{0:T(512)} %param.17) | copy-start | bytes 6148
  5.0 30.1 %collective-permute-start.2 = (bf16[256,512]{1,0:T(8,128)(2,1)}, bf16[256,512]{1,0:T(8,128)(2,1)S(1)}, u32[]{:S(2)}, u32[]{:S(2)}) collective-permute-start(bf16[256,512]{1,0:T(8,128)(2,1)} %gru.1.written), channel_id=1, source_target_pairs={{0,96},{1,97},{2,98},{3,99},{4,100},{5,101},{6,102},{7,103},{8,104... | collective-permute-start | bytes 786440 | tf_op jit(solution)/shard_map/ppermute | solution.py:482
  10.5 24.6 %collective-permute-start.1 = (bf16[256,512]{1,0:T(8,128)(2,1)}, bf16[256,512]{1,0:T(8,128)(2,1)S(1)}, u32[]{:S(2)}, u32[]{:S(2)}) collective-permute-start(bf16[256,512]{1,0:T(8,128)(2,1)} %gru.1.written), channel_id=1, source_target_pairs={{0,64},{32,96},{1,65},{33,97},{2,66},{34,98},{3,67},{35,99},{4,68}... | collective-permute-start | bytes 786440 | tf_op jit(solution)/shard_map/ppermute | solution.py:481
  11.8 23.3 %collective-permute-start = (bf16[256,512]{1,0:T(8,128)(2,1)}, bf16[256,512]{1,0:T(8,128)(2,1)S(1)}, u32[]{:S(2)}, u32[]{:S(2)}) collective-permute-start(bf16[256,512]{1,0:T(8,128)(2,1)} %gru.1.written), channel_id=1, source_target_pairs={{0,32},{32,64},{64,96},{1,33},{33,65},{65,97},{2,34},{34,66},{66,9... | collective-permute-start | bytes 786440 | tf_op jit(solution)/shard_map/ppermute | solution.py:480
  14.4 20.7 %copy-start.1 = (bf16[256,512]{1,0:T(8,128)(2,1)S(1)}, bf16[256,512]{1,0:T(8,128)(2,1)}, u32[]{:S(2)}) copy-start(bf16[256,512]{1,0:T(8,128)(2,1)} %state.3) | copy-start | bytes 786436
  14.4 20.7 %copy-start.2 = (bf16[256,512]{1,0:T(8,128)(2,1)S(1)}, bf16[256,512]{1,0:T(8,128)(2,1)}, u32[]{:S(2)}) copy-start(bf16[256,512]{1,0:T(8,128)(2,1)} %gru.1.written) | copy-start | bytes 786436
  18.3 30.5 %copy-start.3 = (bf16[1,256,512]{2,1,0:T(8,128)(2,1)S(1)}, bf16[1,256,512]{2,1,0:T(8,128)(2,1)}, u32[]{:S(2)}) copy-start(bf16[1,256,512]{2,1,0:T(8,128)(2,1)} %param.21) | copy-start | bytes 786436
  56.2 2.7 %collective-permute-start.3 = (bf16[16,64,512]{2,1,0:T(8,128)(2,1)S(1)}, bf16[16,64,512]{2,1,0:T(8,128)(2,1)S(1)}, u32[]{:S(2)}, u32[]{:S(2)}) collective-permute-start(bf16[16,64,512]{2,1,0:T(8,128)(2,1)S(1)} %get-tuple-element.52), channel_id=1, source_target_pairs={{0,1},{1,0},{2,3},{3,2},{4,5},{5,4},{6,7},{7,6},{8,9},{9,8},{10,11... | collective-permute-start | bytes 3145736 | tf_op jit(solution)/shard_map/ppermute | solution.py:498
  90.5 3.2 %collective-permute-start.6 = (bf16[64,512]{1,0:T(8,128)(2,1)S(1)}, bf16[64,512]{1,0:T(8,128)(2,1)S(1)}, u32[]{:S(2)}, u32[]{:S(2)}) collective-permute-start(bf16[64,512]{1,0:T(8,128)(2,1)S(1)} %plane_sum.1.own), channel_id=1, source_target_pairs={{0,96},{32,0},{64,32},{96,64},{1,97},{33,1},{65,33},{97,65},{2,98}... | collective-permute-start | bytes 196616 | tf_op jit(solution)/shard_map/ppermute | solution.py:504
  90.6 4.7 %collective-permute-start.5 = (bf16[64,512]{1,0:T(8,128)(2,1)S(1)}, bf16[64,512]{1,0:T(8,128)(2,1)S(1)}, u32[]{:S(2)}, u32[]{:S(2)}) collective-permute-start(bf16[64,512]{1,0:T(8,128)(2,1)S(1)} %plane_sum.1.own), channel_id=1, source_target_pairs={{0,64},{32,96},{64,0},{96,32},{1,65},{33,97},{65,1},{97,33},{2,66}... | collective-permute-start | bytes 196616 | tf_op jit(solution)/shard_map/ppermute | solution.py:504
  92.1 4.3 %collective-permute-start.4 = (bf16[64,512]{1,0:T(8,128)(2,1)S(1)}, bf16[64,512]{1,0:T(8,128)(2,1)S(1)}, u32[]{:S(2)}, u32[]{:S(2)}) collective-permute-start(bf16[64,512]{1,0:T(8,128)(2,1)S(1)} %plane_sum.1.own), channel_id=1, source_target_pairs={{0,32},{32,64},{64,96},{96,0},{1,33},{33,65},{65,97},{97,1},{2,34}... | collective-permute-start | bytes 196616 | tf_op jit(solution)/shard_map/ppermute | solution.py:504
  113.3 7.3 %collective-permute-start.7 = (bf16[16,64,512]{2,1,0:T(8,128)(2,1)S(1)}, bf16[16,64,512]{2,1,0:T(8,128)(2,1)S(1)}, u32[]{:S(2)}, u32[]{:S(2)}) collective-permute-start(bf16[16,64,512]{2,1,0:T(8,128)(2,1)S(1)} %all_to_all.29.half), channel_id=1, source_target_pairs={{0,1},{1,0},{2,3},{3,2},{4,5},{5,4},{6,7},{7,6},{8,9},{9,8},{10,11... | collective-permute-start | bytes 3145736 | tf_op jit(solution)/shard_map/ppermute | solution.py:508

commit v10 on v8

--- a/solution.py
+++ b/solution.py
@@ -106,12 +106,8 @@
     )(touched, state, message, w_input, w_state)
 
 
-def time_kernel(core, ids, ids_far, delays, frequency, w, chosen, code_t, time_kv, picked, wanted):
-    first = core[0] == 0
-    for side, row in ((0, ids), (1, ids_far)):
-        blocks = jnp.broadcast_to(column(row[...]), (SLOTS, 128)).reshape(PLANE, CORES, CAP, 128)
-        mine = jnp.where(first, blocks[:, 0], blocks[:, 1]).astype(jnp.int32)
-        wanted[:, core[0] if side == 0 else 1 - core[0]] = mine
+def time_kernel(ids, delays, frequency, w, chosen, code_t, time_kv, picked, wanted, code):
+    wanted[...] = jnp.broadcast_to(column(ids[...]), (SLOTS, 128)).astype(jnp.int32)
     lane = iota((E, 128), 1)
     columns = jnp.zeros((E, 128), F32)
     for j in range(K + 1):
@@ -129,29 +125,30 @@
                 wave = wave * u + c
             at = slice(k * TILE, (k + 1) * TILE)
             code_t[tile, :, at] = wave.T.astype(BF)
-            wave = wave.astype(BF)
-            time_kv[tile, at, :DM] = dot(wave, w[1]).astype(BF)
-            time_kv[tile, at, DM:] = dot(wave, w[2]).astype(BF)
-
-
-def time_parts(core, ids, ids_far, delays, frequency, weights, chosen):
+            code[tile, at] = wave.astype(BF)
+        for i in range(2):
+            time_kv[tile, :, i * DM : (i + 1) * DM] = dot(code[tile], w[1 + i]).astype(BF)
+
+
+def time_parts(ids, delays, frequency, weights, chosen):
     whole = pl.BlockSpec(memory_space=pltpu.VMEM)
     return pl.pallas_call(
         time_kernel,
-        in_specs=[pl.BlockSpec(memory_space=pltpu.SMEM)] + [whole] * 6,
+        in_specs=[whole] * 5,
         out_specs=[whole] * 4,
         out_shape=[
             jax.ShapeDtypeStruct((TILES, DM, ROWS), BF),
             jax.ShapeDtypeStruct((TILES, ROWS, 2 * DM), BF),
             jax.ShapeDtypeStruct((E, 128), jnp.int32),
-            jax.ShapeDtypeStruct((PLANE, CORES, CAP, 128), jnp.int32),
+            jax.ShapeDtypeStruct((SLOTS, 128), jnp.int32),
         ],
+        scratch_shapes=[pltpu.VMEM((TILES, ROWS, DM), BF)],
         compiler_params=pltpu.CompilerParams(vmem_limit_bytes=24 << 20),
         cost_estimate=pl.CostEstimate(
             flops=4 * K * E * DM * DM, bytes_accessed=8 << 20, transcendentals=K * E * DM
         ),
         name="time_parts",
-    )(core, ids, ids_far, delays, frequency, weights, chosen)
+    )(ids, delays, frequency, weights, chosen)
 
 
 def owner_pick(asked):
@@ -495,7 +492,6 @@
     core = lax.axis_index("core").reshape(1)
     swap = [(0, 1), (1, 0)]
     ids = request_rows.reshape(1, SLOTS)
-    ids_far = lax.ppermute(ids, "core", swap)
     written = gru(touched, memory_base, messages[0], gru_input, gru_state)
     r1 = lax.ppermute(written, "y", [(0, 1), (1, 2), (2, 3)])
     r2 = lax.ppermute(written, "y", [(0, 2), (1, 3)])
@@ -503,12 +499,12 @@
     written, late, seg, core = lax.optimization_barrier((written, delays[0].T, seg, core))
     chosen_t = event_slots.transpose(2, 0, 1)
     code_t, time_kv, chosen, wanted = time_parts(
-        core, ids, ids_far, late, frequency.reshape(1, DM), attn_weights, chosen_t
+        ids, late, frequency.reshape(1, DM), attn_weights, chosen_t
     )
     written, wanted, code_t, time_kv, chosen = lax.optimization_barrier(
         (written, wanted, code_t, time_kv, chosen)
     )
-    asked = plane(wanted).reshape(SLOTS, 128)
+    asked = exchange(wanted, NODE, OWNERS)
     memory, rows = start_rows(seg, memory_base, written, r1, r2, r3, asked)
     slots = exchange(rows, NODE, OWNERS)
     up = upstream[0]

time: 113 us -> 113 us (level)
    all_to_all x1 -> x2, blocking collectives: 14.4 us -> 29.3 us  [exchange(): lax.all_to_all(blocks, axes, split_axis=0, concat_axis=0, tiled=True)]
    all_to_all x3 -> x2, blocking collectives: 52.7 us -> 38.3 us  [plane(): return lax.all_to_all(x, FLAT, split_axis=0, concat_axis=0, tiled=True)]
    ppermute x1 -> x0, starting transfers between devices: 1.5 us -> none  [on_device(): ids_far = lax.ppermute(ids, 'core', swap)]
  transfers between devices with their start and end apart: 10 -> 9, of which waited for: 4 -> 4; matrix products, arithmetic and copies ran while one was open for 0% -> 0% of each run, Pallas kernels for 10% -> 7%
where the time goes in v10:
time: 113 us
  blocking collectives  67.7 us (60%)
  Pallas kernels  22.2 us (20%)
  starting transfers between devices  16.3 us (14%)
  waiting for transfers between devices  5.66 us (5%)
    all_to_all x2, blocking collectives, plane(): return lax.all_to_all(x, FLAT, split_axis=0, concat_axis=0, tiled=True)  38.3 us
    all_to_all x2, blocking collectives, exchange(): lax.all_to_all(blocks, axes, split_axis=0, concat_axis=0, tiled=True)  29.3 us
    pallas_call x1, Pallas kernels, attend(): pl.pallas_call(attend_kernel, in_specs=[pl.BlockSpec(memory_space=pltpu.S...  7.44 us
    ppermute x1, starting transfers between devices, on_device(): r3 = lax.ppermute(written, 'y', [(0, 3)])  5.48 us
    ppermute x1, starting transfers between devices, on_device(): far = lax.ppermute(half, 'core', swap)  4.83 us
    pallas_call x1, Pallas kernels, gru(): pl.pallas_call(gru_kernel, in_specs=[whole] + [far] * 4, out_specs=whole,...  4.35 us
    ppermute x3, waiting for transfers between devices, on_device(): lax.ppermute(part, 'y', [(i, (i + s) % SEG) for i in range(SEG)])  4.32 us
    pallas_call x1, Pallas kernels, time_parts(): pl.pallas_call(time_kernel, in_specs=[whole] * 5, out_specs=[whole] * 4,...  3.82 us
  transfers between devices with their start and end apart: 9, of which 4 were waited for; matrix products, arithmetic and copies ran while one was open for 0% of the time, Pallas kernels for 7%

profile of v10, /device:TPU:1, one launch (start us, length us, event | category | flops | bytes accessed | tf_op | source)
XLA Modules:
  0.0 112.8 jit_solution(18205183609351949276)
XLA Ops:
  0.6 0.0 copy-start.5
  0.6 0.0 copy-start
  0.7 0.0 copy-start.4
  0.7 0.0 copy-start.7
  0.7 0.0 copy-start.6
  0.7 4.3 %gru.1.written = bf16[256,512]{1,0:T(8,128)(2,1)} custom-call(s32[1,256]{1,0:T(1,128)} %touched.1, bf16[256,512]{1,0:T(8,128)(2,1)} %state.3, bf16[256,512]{1,0:T(8,128)(2,1)} %bitcast.33, bf16[512,1536]{1,0:T(8,128)(2,1)} %w_input.1, bf16[512,1536]{1,0:T(8,128)(2,1)} %w_state.1), custom_call_target="tpu_custom_call" | custom-call | flops 805306368 | bytes 4194304 | tf_op jit(solution)/shard_map/gru/pallas_call | solution.py:89
  5.0 5.5 %collective-permute-start.2 = (bf16[256,512]{1,0:T(8,128)(2,1)}, bf16[256,512]{1,0:T(8,128)(2,1)S(1)}, u32[]{:S(2)}, u32[]{:S(2)}) collective-permute-start(bf16[256,512]{1,0:T(8,128)(2,1)} %gru.1.written), channel_id=1, source_target_pairs={{0,96},{1,97},{2,98},{3,99},{4,100},{5,101},{6,102},{7,103},{8,104... | collective-permute-start | bytes 786440 | tf_op jit(solution)/shard_map/ppermute | solution.py:498
  10.5 1.3 %collective-permute-start.1 = (bf16[256,512]{1,0:T(8,128)(2,1)}, bf16[256,512]{1,0:T(8,128)(2,1)S(1)}, u32[]{:S(2)}, u32[]{:S(2)}) collective-permute-start(bf16[256,512]{1,0:T(8,128)(2,1)} %gru.1.written), channel_id=1, source_target_pairs={{0,64},{32,96},{1,65},{33,97},{2,66},{34,98},{3,67},{35,99},{4,68}... | collective-permute-start | bytes 786440 | tf_op jit(solution)/shard_map/ppermute | solution.py:497
  11.8 2.5 %collective-permute-start = (bf16[256,512]{1,0:T(8,128)(2,1)}, bf16[256,512]{1,0:T(8,128)(2,1)S(1)}, u32[]{:S(2)}, u32[]{:S(2)}) collective-permute-start(bf16[256,512]{1,0:T(8,128)(2,1)} %gru.1.written), channel_id=1, source_target_pairs={{0,32},{32,64},{64,96},{1,33},{33,65},{65,97},{2,34},{34,66},{66,9... | collective-permute-start | bytes 786440 | tf_op jit(solution)/shard_map/ppermute | solution.py:496
  14.3 0.0 copy-done.5
  14.3 0.0 copy-done
  14.4 0.0 copy-done.4
  14.4 0.0 copy-done.7
  14.4 0.0 copy-done.6
  14.4 0.0 copy-start.1
  14.4 0.0 copy-start.2
  14.4 3.8 %time_parts.1 = (bf16[2,512,1024]{2,1,0:T(8,128)(2,1)S(1)}, bf16[2,1024,1024]{2,1,0:T(8,128)(2,1)S(1)}, s32[256,128]{1,0:T(8,128)S(1)}, s32[256,128]{1,0:T(8,128)S(1)}) custom-call(s32[1,256]{1,0:T(1,128)S(1)} %bitcast.30, s32[8,256]{1,0:T(8,128)S(1)} %bitcast.28, f32[1,512]{1,0:T(1,128)S(1)} %bitcast.29, bf16[4,512,512]{2,1,0:T(8,128)(2,1)S(1)} %copy-done, ...), custom_call_target="tpu_custom_call" | custom-call | flops 2147483648 | bytes 8388608 | tf_op jit(solution)/shard_map/time_parts/pallas_call | solution.py:135
  18.2 0.0 copy-start.3
  18.3 16.8 %all_to_all.20 = s32[32,8,128]{2,1,0:T(8,128)S(1)} all-to-all(s32[32,8,128]{2,1,0:T(8,128)S(1)} %bitcast.25), channel_id=1, replica_groups=mesh['y'=4,'x'=4,'z'=4,'core'=2] {'x','z','core'}, dimensions={0} | all-to-all | bytes 262144 | tf_op jit(solution)/shard_map/all_to_all | solution.py:471
  35.1 0.0 collective-permute-done.2.r3
  35.1 0.0 collective-permute-done.1.r2
  35.1 0.0 collective-permute-done.r1
  35.1 0.0 copy-done.1
  35.1 0.0 copy-done.2
  35.1 1.1 start_rows.1
  36.2 12.5 %all_to_all.21 = bf16[32,8,512]{2,1,0:T(8,128)(2,1)S(1)} all-to-all(bf16[32,8,512]{2,1,0:T(8,128)(2,1)S(1)} %bitcast.24), channel_id=1, replica_groups=mesh['y'=4,'x'=4,'z'=4,'core'=2] {'x','z','core'}, dimensions={0} | all-to-all | bytes 524288 | tf_op jit(solution)/shard_map/all_to_all | solution.py:471
  48.7 7.4 %attend.1 = (bf16[16,64,512]{2,1,0:T(8,128)(2,1)S(1)}, bf16[16,64,512]{2,1,0:T(8,128)(2,1)S(1)}, bf16[256,512]{1,0:T(8,128)(2,1)S(1)}, bf16[256,512]{1,0:T(8,128...) custom-call(s32[1]{0:T(128)} %bitcast.4.core, bf16[256,512]{1,0:T(8,128)(2,1)S(1)} %bitcast.23, ...), custom_call_target="tpu_custom_call" | custom-call | flops 6442450944 | bytes 14680064 | tf_op jit(solution)/shard_map/attend/pallas_call | solution.py:323
  56.2 0.3 collective-permute-start.3
  56.5 1.0 events.1
  57.5 0.3 collective-permute-start.4
  57.8 1.3 %collective-permute-done.4.got = bf16[128,512]{1,0:T(8,128)(2,1)S(1)} collective-permute-done((bf16[128,512]{1,0:T(8,128)(2,1)S(1)}, bf16[128,512]{1,0:T(8,128)(2,1)S(1)}, u32[]{:S(2)}, u32[]{:S(2)}) %collective-permute-start.4) | collective-permute-done | bytes 131104 | tf_op jit(solution)/shard_map/ppermute | solution.py:516
  59.1 0.0 collective-permute-done.3.b
  59.1 0.3 pair_sum.1
  59.4 21.7 %all_to_all.22.a = bf16[16,80,512]{2,1,0:T(8,128)(2,1)S(1)} all-to-all(bf16[16,80,512]{2,1,0:T(8,128)(2,1)S(1)} %pair_sum.1), channel_id=1, replica_groups=mesh['y'=4,'x'=4,'z'=4,'core'=2] {'x','z'}, dimensions={0} | all-to-all | bytes 2621440 | tf_op jit(solution)/shard_map/all_to_all | solution.py:475
  81.1 0.1 plane_sum.1
  81.2 0.1 collective-permute-start.7
  81.3 1.5 %collective-permute-start.6 = (bf16[64,512]{1,0:T(8,128)(2,1)S(1)}, bf16[64,512]{1,0:T(8,128)(2,1)S(1)}, u32[]{:S(2)}, u32[]{:S(2)}) collective-permute-start(bf16[64,512]{1,0:T(8,128)(2,1)S(1)} %get-tuple-element.57.own), channel_id=1, source_target_pairs={{0,64},{32,96},{64,0},{96,32},{1,65},{33,97},{65,1},{97,33},{2,66}... | collective-permute-start | bytes 196616 | tf_op jit(solution)/shard_map/ppermute | solution.py:519
  82.8 0.0 collective-permute-start.5
  82.8 1.6 %collective-permute-done.7.r3 = bf16[64,512]{1,0:T(8,128)(2,1)S(1)} collective-permute-done((bf16[64,512]{1,0:T(8,128)(2,1)S(1)}, bf16[64,512]{1,0:T(8,128)(2,1)S(1)}, u32[]{:S(2)}, u32[]{:S(2)}) %collective-permute-start.7) | collective-permute-done | bytes 65568 | tf_op jit(solution)/shard_map/ppermute | solution.py:519
  84.4 1.6 %collective-permute-done.6.r2 = bf16[64,512]{1,0:T(8,128)(2,1)S(1)} collective-permute-done((bf16[64,512]{1,0:T(8,128)(2,1)S(1)}, bf16[64,512]{1,0:T(8,128)(2,1)S(1)}, u32[]{:S(2)}, u32[]{:S(2)}) %collective-permute-start.6) | collective-permute-done | bytes 65568 | tf_op jit(solution)/shard_map/ppermute | solution.py:519
  86.0 1.1 collective-permute-done.5.r1
  87.1 0.1 seg_sum.1
  87.3 16.6 %all_to_all.23.half = bf16[16,64,512]{2,1,0:T(8,128)(2,1)S(1)} all-to-all(bf16[16,64,512]{2,1,0:T(8,128)(2,1)S(1)} %seg_sum.1), channel_id=1, replica_groups=mesh['y'=4,'x'=4,'z'=4,'core'=2] {'x','z'}, dimensions={0} | all-to-all | bytes 2097152 | tf_op jit(solution)/shard_map/all_to_all | solution.py:475
  103.9 4.8 %collective-permute-start.8 = (bf16[16,64,512]{2,1,0:T(8,128)(2,1)S(1)}, bf16[16,64,512]{2,1,0:T(8,128)(2,1)S(1)}, u32[]{:S(2)}, u32[]{:S(2)}) collective-permute-start(bf16[16,64,512]{2,1,0:T(8,128)(2,1)S(1)} %all_to_all.23.half), channel_id=1, source_target_pairs={{0,1},{1,0},{2,3},{3,2},{4,5},{5,4},{6,7},{7,6},{8,9},{9,8},{10,11... | collective-permute-start | bytes 3145736 | tf_op jit(solution)/shard_map/ppermute | solution.py:523
  108.8 1.1 owner_sum.1
  109.9 1.4 %own_half.1.rest_0_ = f32[16,2,64,512]{3,2,1,0:T(8,128)} custom-call(s32[1]{0:T(128)} %bitcast.4.core, bf16[16,64,512]{2,1,0:T(8,128)(2,1)S(1)} %all_to_all.23.half), custom_call_target="tpu_custom_call" | custom-call | flops 262144 | bytes 3145728 | tf_op jit(solution)/shard_map/own_half/pallas_call | solution.py:434
  111.3 0.0 collective-permute-done.8.half
  111.3 1.4 %far_half.1 = f32[16,2,64,512]{3,2,1,0:T(8,128)} custom-call(s32[1]{0:T(128)} %bitcast.4.core, bf16[16,64,512]{2,1,0:T(8,128)(2,1)S(1)} %collective-permute-done.8.half, f32[16,2,64,512]{3,2,1,0:T(8,128)} %own_half.1.rest_0_), custom_call_target="tpu_custom_call", output_to_operand_aliasing={{}: (2, {})} | custom-call | flops 262144 | bytes 3145728 | tf_op jit(solution)/shard_map/far_half/pallas_call | solution.py:434
  (1 shorter events, 0.0 us)
Async XLA Ops:
  0.6 13.7 %copy-start.5 = (s32[1,256,8]{1,2,0:T(8,128)S(1)}, s32[1,256,8]{1,2,0:T(8,128)}, u32[]{:S(2)}) copy-start(s32[1,256,8]{1,2,0:T(8,128)} %param.20) | copy-start | bytes 24580
  0.6 13.7 %copy-start = (bf16[4,512,512]{2,1,0:T(8,128)(2,1)S(1)}, bf16[4,512,512]{2,1,0:T(8,128)(2,1)}, u32[]{:S(2)}) copy-start(bf16[4,512,512]{2,1,0:T(8,128)(2,1)} %w.3) | copy-start | bytes 6291460
  0.7 13.7 %copy-start.4 = (s32[1,256,9]{1,0,2:T(1,128)S(1)}, s32[1,256,9]{1,0,2:T(1,128)}, u32[]{:S(2)}) copy-start(s32[1,256,9]{1,0,2:T(1,128)} %param.19) | copy-start | bytes 27652
  0.7 13.7 %copy-start.7 = (s32[1,1,256]{2,1,0:T(1,128)S(1)}, s32[1,1,256]{2,1,0:T(1,128)}, u32[]{:S(2)}) copy-start(s32[1,1,256]{2,1,0:T(1,128)} %param.18) | copy-start | bytes 3076
  0.7 13.7 %copy-start.6 = (f32[512]{0:T(512)S(1)}, f32[512]{0:T(512)}, u32[]{:S(2)}) copy-start(f32[512]{0:T(512)} %param.17) | copy-start | bytes 6148
  5.0 30.0 %collective-permute-start.2 = (bf16[256,512]{1,0:T(8,128)(2,1)}, bf16[256,512]{1,0:T(8,128)(2,1)S(1)}, u32[]{:S(2)}, u32[]{:S(2)}) collective-permute-start(bf16[256,512]{1,0:T(8,128)(2,1)} %gru.1.written), channel_id=1, source_target_pairs={{0,96},{1,97},{2,98},{3,99},{4,100},{5,101},{6,102},{7,103},{8,104... | collective-permute-start | bytes 786440 | tf_op jit(solution)/shard_map/ppermute | solution.py:498
  10.5 24.5 %collective-permute-start.1 = (bf16[256,512]{1,0:T(8,128)(2,1)}, bf16[256,512]{1,0:T(8,128)(2,1)S(1)}, u32[]{:S(2)}, u32[]{:S(2)}) collective-permute-start(bf16[256,512]{1,0:T(8,128)(2,1)} %gru.1.written), channel_id=1, source_target_pairs={{0,64},{32,96},{1,65},{33,97},{2,66},{34,98},{3,67},{35,99},{4,68}... | collective-permute-start | bytes 786440 | tf_op jit(solution)/shard_map/ppermute | solution.py:497
  11.8 23.2 %collective-permute-start = (bf16[256,512]{1,0:T(8,128)(2,1)}, bf16[256,512]{1,0:T(8,128)(2,1)S(1)}, u32[]{:S(2)}, u32[]{:S(2)}) collective-permute-start(bf16[256,512]{1,0:T(8,128)(2,1)} %gru.1.written), channel_id=1, source_target_pairs={{0,32},{32,64},{64,96},{1,33},{33,65},{65,97},{2,34},{34,66},{66,9... | collective-permute-start | bytes 786440 | tf_op jit(solution)/shard_map/ppermute | solution.py:496
  14.4 20.7 %copy-start.1 = (bf16[256,512]{1,0:T(8,128)(2,1)S(1)}, bf16[256,512]{1,0:T(8,128)(2,1)}, u32[]{:S(2)}) copy-start(bf16[256,512]{1,0:T(8,128)(2,1)} %state.3) | copy-start | bytes 786436
  14.4 20.7 %copy-start.2 = (bf16[256,512]{1,0:T(8,128)(2,1)S(1)}, bf16[256,512]{1,0:T(8,128)(2,1)}, u32[]{:S(2)}) copy-start(bf16[256,512]{1,0:T(8,128)(2,1)} %gru.1.written) | copy-start | bytes 786436
  18.2 30.5 %copy-start.3 = (bf16[1,256,512]{2,1,0:T(8,128)(2,1)S(1)}, bf16[1,256,512]{2,1,0:T(8,128)(2,1)}, u32[]{:S(2)}) copy-start(bf16[1,256,512]{2,1,0:T(8,128)(2,1)} %param.21) | copy-start | bytes 786436
  56.2 2.9 %collective-permute-start.3 = (bf16[16,64,512]{2,1,0:T(8,128)(2,1)S(1)}, bf16[16,64,512]{2,1,0:T(8,128)(2,1)S(1)}, u32[]{:S(2)}, u32[]{:S(2)}) collective-permute-start(bf16[16,64,512]{2,1,0:T(8,128)(2,1)S(1)} %get-tuple-element.52), channel_id=1, source_target_pairs={{0,1},{1,0},{2,3},{3,2},{4,5},{5,4},{6,7},{7,6},{8,9},{9,8},{10,11... | collective-permute-start | bytes 3145736 | tf_op jit(solution)/shard_map/ppermute | solution.py:514
  57.5 1.6 %collective-permute-start.4 = (bf16[128,512]{1,0:T(8,128)(2,1)S(1)}, bf16[128,512]{1,0:T(8,128)(2,1)S(1)}, u32[]{:S(2)}, u32[]{:S(2)}) collective-permute-start(bf16[128,512]{1,0:T(8,128)(2,1)S(1)} %get-tuple-element.54), channel_id=1, source_target_pairs={{0,1},{1,0},{2,3},{3,2},{4,5},{5,4},{6,7},{7,6},{8,9},{9,8},{10,11... | collective-permute-start | bytes 393224 | tf_op jit(solution)/shard_map/ppermute | solution.py:516
  81.2 3.2 %collective-permute-start.7 = (bf16[64,512]{1,0:T(8,128)(2,1)S(1)}, bf16[64,512]{1,0:T(8,128)(2,1)S(1)}, u32[]{:S(2)}, u32[]{:S(2)}) collective-permute-start(bf16[64,512]{1,0:T(8,128)(2,1)S(1)} %get-tuple-element.57.own), channel_id=1, source_target_pairs={{0,96},{32,0},{64,32},{96,64},{1,97},{33,1},{65,33},{97,65},{2,98}... | collective-permute-start | bytes 196616 | tf_op jit(solution)/shard_map/ppermute | solution.py:519
  81.3 4.7 %collective-permute-start.6 = (bf16[64,512]{1,0:T(8,128)(2,1)S(1)}, bf16[64,512]{1,0:T(8,128)(2,1)S(1)}, u32[]{:S(2)}, u32[]{:S(2)}) collective-permute-start(bf16[64,512]{1,0:T(8,128)(2,1)S(1)} %get-tuple-element.57.own), channel_id=1, source_target_pairs={{0,64},{32,96},{64,0},{96,32},{1,65},{33,97},{65,1},{97,33},{2,66}... | collective-permute-start | bytes 196616 | tf_op jit(solution)/shard_map/ppermute | solution.py:519
  82.8 4.3 %collective-permute-start.5 = (bf16[64,512]{1,0:T(8,128)(2,1)S(1)}, bf16[64,512]{1,0:T(8,128)(2,1)S(1)}, u32[]{:S(2)}, u32[]{:S(2)}) collective-permute-start(bf16[64,512]{1,0:T(8,128)(2,1)S(1)} %get-tuple-element.57.own), channel_id=1, source_target_pairs={{0,32},{32,64},{64,96},{96,0},{1,33},{33,65},{65,97},{97,1},{2,34}... | collective-permute-start | bytes 196616 | tf_op jit(solution)/shard_map/ppermute | solution.py:519
  103.9 7.3 %collective-permute-start.8 = (bf16[16,64,512]{2,1,0:T(8,128)(2,1)S(1)}, bf16[16,64,512]{2,1,0:T(8,128)(2,1)S(1)}, u32[]{:S(2)}, u32[]{:S(2)}) collective-permute-start(bf16[16,64,512]{2,1,0:T(8,128)(2,1)S(1)} %all_to_all.23.half), channel_id=1, source_target_pairs={{0,1},{1,0},{2,3},{3,2},{4,5},{5,4},{6,7},{7,6},{8,9},{9,8},{10,11... | collective-permute-start | bytes 3145736 | tf_op jit(solution)/shard_map/ppermute | solution.py:523

commit v11 on v10

--- a/solution.py
+++ b/solution.py
@@ -124,8 +124,9 @@
             for c in COS[-2::-1]:
                 wave = wave * u + c
             at = slice(k * TILE, (k + 1) * TILE)
-            code_t[tile, :, at] = wave.T.astype(BF)
-            code[tile, at] = wave.astype(BF)
+            wave = wave.astype(BF)
+            code_t[tile, :, at] = wave.T
+            code[tile, at] = wave
         for i in range(2):
             time_kv[tile, :, i * DM : (i + 1) * DM] = dot(code[tile], w[1 + i]).astype(BF)
 
@@ -515,11 +516,12 @@
     embedded, keep, give = events(core, *kept, up, attn_weights)
     got = lax.ppermute(give, "core", swap)
     part, near, far = plane_sum(plane(pair_sum(mine, partner, keep, got)))
-    r2, r3, r1 = (
-        lax.ppermute(part, "y", [(i, (i + s) % SEG) for i in range(SEG)]) for s in (2, 3, 1)
-    )
+    turns = {s: [(i, (i + s) % SEG) for i in range(SEG)] for s in (1, 2, 3)}
+    r2 = lax.ppermute(part, "y", turns[2])
+    memory_grad = owner_sum(core, asked, near, far)
+    late, memory_grad = lax.optimization_barrier((part, memory_grad))
+    r1, r3 = (lax.ppermute(late, "y", turns[s]) for s in (1, 3))
     half = plane(seg_sum(seg, part, r1, r2, r3))
-    memory_grad = owner_sum(core, asked, near, far)
     far = lax.ppermute(half, "core", swap)
     weight_grad = whole_grad(core, far, whole_grad(core, half))
     return embedded[None], memory[None], memory_grad[None], weight_grad.reshape(4, DM, DM)

time: 113 us -> 115 us (1.018)
  transfers between devices with their start and end apart: 9 -> 9, of which waited for: 4 -> 4; matrix products, arithmetic and copies ran while one was open for 0% -> 0% of each run, Pallas kernels for 7% -> 6%
where the time goes in v11:
time: 115 us; the launch traced here: 114 us
  blocking collectives  67.5 us (59%)
  Pallas kernels  22.2 us (19%)
  starting transfers between devices  16.9 us (15%)
  waiting for transfers between devices  6.74 us (6%)
    all_to_all x2, blocking collectives, plane(): return lax.all_to_all(x, FLAT, split_axis=0, concat_axis=0, tiled=True)  38.1 us
    all_to_all x2, blocking collectives, exchange(): lax.all_to_all(blocks, axes, split_axis=0, concat_axis=0, tiled=True)  29.3 us
    pallas_call x1, Pallas kernels, attend(): pl.pallas_call(attend_kernel, in_specs=[pl.BlockSpec(memory_space=pltpu.S...  7.44 us
    ppermute x1, starting transfers between devices, on_device(): r3 = lax.ppermute(written, 'y', [(0, 3)])  5.48 us
    ppermute x1, starting transfers between devices, on_device(): far = lax.ppermute(half, 'core', swap)  4.84 us
    pallas_call x1, Pallas kernels, gru(): pl.pallas_call(gru_kernel, in_specs=[whole] + [far] * 4, out_specs=whole,...  4.35 us
    pallas_call x1, Pallas kernels, time_parts(): pl.pallas_call(time_kernel, in_specs=[whole] * 5, out_specs=[whole] * 4,...  3.84 us
    ppermute x2, waiting for transfers between devices, on_device(): r1, r3 = (lax.ppermute(late, 'y', turns[s]) for s in (1, 3))  3.13 us
  transfers between devices with their start and end apart: 9, of which 4 were waited for; matrix products, arithmetic and copies ran while one was open for 0% of the time, Pallas kernels for 6%

profile of v11, /device:TPU:1, one launch (start us, length us, event | category | flops | bytes accessed | tf_op | source)
XLA Modules:
  0.0 114.3 jit_solution(2286083745622631061)
XLA Ops:
  0.6 0.0 copy-start.5
  0.6 0.0 copy-start
  0.7 0.0 copy-start.4
  0.7 0.0 copy-start.7
  0.7 0.0 copy-start.6
  0.7 4.3 %gru.1.written = bf16[256,512]{1,0:T(8,128)(2,1)} custom-call(s32[1,256]{1,0:T(1,128)} %touched.1, bf16[256,512]{1,0:T(8,128)(2,1)} %state.3, bf16[256,512]{1,0:T(8,128)(2,1)} %bitcast.33, bf16[512,1536]{1,0:T(8,128)(2,1)} %w_input.1, bf16[512,1536]{1,0:T(8,128)(2,1)} %w_state.1), custom_call_target="tpu_custom_call" | custom-call | flops 805306368 | bytes 4194304 | tf_op jit(solution)/shard_map/gru/pallas_call | solution.py:89
  5.0 5.5 %collective-permute-start.2 = (bf16[256,512]{1,0:T(8,128)(2,1)}, bf16[256,512]{1,0:T(8,128)(2,1)S(1)}, u32[]{:S(2)}, u32[]{:S(2)}) collective-permute-start(bf16[256,512]{1,0:T(8,128)(2,1)} %gru.1.written), channel_id=1, source_target_pairs={{0,96},{1,97},{2,98},{3,99},{4,100},{5,101},{6,102},{7,103},{8,104... | collective-permute-start | bytes 786440 | tf_op jit(solution)/shard_map/ppermute | solution.py:499
  10.5 1.3 %collective-permute-start.1 = (bf16[256,512]{1,0:T(8,128)(2,1)}, bf16[256,512]{1,0:T(8,128)(2,1)S(1)}, u32[]{:S(2)}, u32[]{:S(2)}) collective-permute-start(bf16[256,512]{1,0:T(8,128)(2,1)} %gru.1.written), channel_id=1, source_target_pairs={{0,64},{32,96},{1,65},{33,97},{2,66},{34,98},{3,67},{35,99},{4,68}... | collective-permute-start | bytes 786440 | tf_op jit(solution)/shard_map/ppermute | solution.py:498
  11.8 2.5 %collective-permute-start = (bf16[256,512]{1,0:T(8,128)(2,1)}, bf16[256,512]{1,0:T(8,128)(2,1)S(1)}, u32[]{:S(2)}, u32[]{:S(2)}) collective-permute-start(bf16[256,512]{1,0:T(8,128)(2,1)} %gru.1.written), channel_id=1, source_target_pairs={{0,32},{32,64},{64,96},{1,33},{33,65},{65,97},{2,34},{34,66},{66,9... | collective-permute-start | bytes 786440 | tf_op jit(solution)/shard_map/ppermute | solution.py:497
  14.3 0.0 copy-done.5
  14.3 0.0 copy-done
  14.4 0.0 copy-done.4
  14.4 0.0 copy-done.7
  14.4 0.0 copy-done.6
  14.4 0.0 copy-start.1
  14.4 0.0 copy-start.2
  14.4 3.8 %time_parts.1 = (bf16[2,512,1024]{2,1,0:T(8,128)(2,1)S(1)}, bf16[2,1024,1024]{2,1,0:T(8,128)(2,1)S(1)}, s32[256,128]{1,0:T(8,128)S(1)}, s32[256,128]{1,0:T(8,128)S(1)}) custom-call(s32[1,256]{1,0:T(1,128)S(1)} %bitcast.30, s32[8,256]{1,0:T(8,128)S(1)} %bitcast.28, f32[1,512]{1,0:T(1,128)S(1)} %bitcast.29, bf16[4,512,512]{2,1,0:T(8,128)(2,1)S(1)} %copy-done, ...), custom_call_target="tpu_custom_call" | custom-call | flops 2147483648 | bytes 8388608 | tf_op jit(solution)/shard_map/time_parts/pallas_call | solution.py:136
  18.3 0.0 copy-start.3
  18.3 16.8 %all_to_all.20 = s32[32,8,128]{2,1,0:T(8,128)S(1)} all-to-all(s32[32,8,128]{2,1,0:T(8,128)S(1)} %bitcast.25), channel_id=1, replica_groups=mesh['y'=4,'x'=4,'z'=4,'core'=2] {'x','z','core'}, dimensions={0} | all-to-all | bytes 262144 | tf_op jit(solution)/shard_map/all_to_all | solution.py:472
  35.1 0.0 collective-permute-done.2.r3
  35.1 0.0 collective-permute-done.1.r2
  35.1 0.0 collective-permute-done.r1
  35.1 0.0 copy-done.1
  35.1 1.1 start_rows.1
  36.2 12.5 %all_to_all.21 = bf16[32,8,512]{2,1,0:T(8,128)(2,1)S(1)} all-to-all(bf16[32,8,512]{2,1,0:T(8,128)(2,1)S(1)} %bitcast.24), channel_id=1, replica_groups=mesh['y'=4,'x'=4,'z'=4,'core'=2] {'x','z','core'}, dimensions={0} | all-to-all | bytes 524288 | tf_op jit(solution)/shard_map/all_to_all | solution.py:472
  48.7 0.0 copy-done.3
  48.7 7.4 %attend.1 = (bf16[16,64,512]{2,1,0:T(8,128)(2,1)S(1)}, bf16[16,64,512]{2,1,0:T(8,128)(2,1)S(1)}, bf16[256,512]{1,0:T(8,128)(2,1)S(1)}, bf16[256,512]{1,0:T(8,128...) custom-call(s32[1]{0:T(128)} %bitcast.4.core, bf16[256,512]{1,0:T(8,128)(2,1)S(1)} %bitcast.23, ...), custom_call_target="tpu_custom_call" | custom-call | flops 6442450944 | bytes 14680064 | tf_op jit(solution)/shard_map/attend/pallas_call | solution.py:324
  56.2 0.3 collective-permute-start.3
  56.5 1.0 events.1
  57.5 0.3 collective-permute-start.4
  57.8 1.3 %collective-permute-done.4.got = bf16[128,512]{1,0:T(8,128)(2,1)S(1)} collective-permute-done((bf16[128,512]{1,0:T(8,128)(2,1)S(1)}, bf16[128,512]{1,0:T(8,128)(2,1)S(1)}, u32[]{:S(2)}, u32[]{:S(2)}) %collective-permute-start.4) | collective-permute-done | bytes 131104 | tf_op jit(solution)/shard_map/ppermute | solution.py:517
  59.1 0.0 collective-permute-done.3.b
  59.1 0.3 pair_sum.1
  59.4 21.7 %all_to_all.22.a = bf16[16,80,512]{2,1,0:T(8,128)(2,1)S(1)} all-to-all(bf16[16,80,512]{2,1,0:T(8,128)(2,1)S(1)} %pair_sum.1), channel_id=1, replica_groups=mesh['y'=4,'x'=4,'z'=4,'core'=2] {'x','z'}, dimensions={0} | all-to-all | bytes 2621440 | tf_op jit(solution)/shard_map/all_to_all | solution.py:476
  81.1 0.1 plane_sum.1
  81.3 0.1 collective-permute-start.6
  81.3 1.1 owner_sum.1
  82.5 2.1 %collective-permute-start.7 = (bf16[64,512]{1,0:T(8,128)(2,1)S(1)}, bf16[64,512]{1,0:T(8,128)(2,1)S(1)}, u32[]{:S(2)}, u32[]{:S(2)}) collective-permute-start(bf16[64,512]{1,0:T(8,128)(2,1)S(1)} %get-tuple-element.61.own), channel_id=1, source_target_pairs={{0,96},{32,0},{64,32},{96,64},{1,97},{33,1},{65,33},{97,65},{2,98}... | collective-permute-start | bytes 196616 | tf_op jit(solution)/shard_map/ppermute | solution.py:523
  84.6 0.0 collective-permute-start.5
  84.6 1.4 %collective-permute-done.6.r2 = bf16[64,512]{1,0:T(8,128)(2,1)S(1)} collective-permute-done((bf16[64,512]{1,0:T(8,128)(2,1)S(1)}, bf16[64,512]{1,0:T(8,128)(2,1)S(1)}, u32[]{:S(2)}, u32[]{:S(2)}) %collective-permute-start.6) | collective-permute-done | bytes 65568 | tf_op jit(solution)/shard_map/ppermute | solution.py:520
  86.0 0.0 collective-permute-done.7.r3
  86.0 3.1 %collective-permute-done.5.r1 = bf16[64,512]{1,0:T(8,128)(2,1)S(1)} collective-permute-done((bf16[64,512]{1,0:T(8,128)(2,1)S(1)}, bf16[64,512]{1,0:T(8,128)(2,1)S(1)}, u32[]{:S(2)}, u32[]{:S(2)}) %collective-permute-start.5) | collective-permute-done | bytes 65568 | tf_op jit(solution)/shard_map/ppermute | solution.py:523
  89.1 0.1 seg_sum.1
  89.2 16.4 %all_to_all.23.half = bf16[16,64,512]{2,1,0:T(8,128)(2,1)S(1)} all-to-all(bf16[16,64,512]{2,1,0:T(8,128)(2,1)S(1)} %seg_sum.1), channel_id=1, replica_groups=mesh['y'=4,'x'=4,'z'=4,'core'=2] {'x','z'}, dimensions={0} | all-to-all | bytes 2097152 | tf_op jit(solution)/shard_map/all_to_all | solution.py:476
  105.7 4.8 %collective-permute-start.8 = (bf16[16,64,512]{2,1,0:T(8,128)(2,1)S(1)}, bf16[16,64,512]{2,1,0:T(8,128)(2,1)S(1)}, u32[]{:S(2)}, u32[]{:S(2)}) collective-permute-start(bf16[16,64,512]{2,1,0:T(8,128)(2,1)S(1)} %all_to_all.23.half), channel_id=1, source_target_pairs={{0,1},{1,0},{2,3},{3,2},{4,5},{5,4},{6,7},{7,6},{8,9},{9,8},{10,11... | collective-permute-start | bytes 3145736 | tf_op jit(solution)/shard_map/ppermute | solution.py:525
  110.5 1.4 %own_half.1.rest_0_ = f32[16,2,64,512]{3,2,1,0:T(8,128)} custom-call(s32[1]{0:T(128)} %bitcast.4.core, bf16[16,64,512]{2,1,0:T(8,128)(2,1)S(1)} %all_to_all.23.half), custom_call_target="tpu_custom_call" | custom-call | flops 262144 | bytes 3145728 | tf_op jit(solution)/shard_map/own_half/pallas_call | solution.py:435
  111.9 0.9 collective-permute-done.8.half
  112.8 1.4 %far_half.1 = f32[16,2,64,512]{3,2,1,0:T(8,128)} custom-call(s32[1]{0:T(128)} %bitcast.4.core, bf16[16,64,512]{2,1,0:T(8,128)(2,1)S(1)} %collective-permute-done.8.half, f32[16,2,64,512]{3,2,1,0:T(8,128)} %own_half.1.rest_0_), custom_call_target="tpu_custom_call", output_to_operand_aliasing={{}: (2, {})} | custom-call | flops 262144 | bytes 3145728 | tf_op jit(solution)/shard_map/far_half/pallas_call | solution.py:435
  (1 shorter events, 0.0 us)
Async XLA Ops:
  0.6 13.7 %copy-start.5 = (s32[1,256,8]{1,2,0:T(8,128)S(1)}, s32[1,256,8]{1,2,0:T(8,128)}, u32[]{:S(2)}) copy-start(s32[1,256,8]{1,2,0:T(8,128)} %param.20) | copy-start | bytes 24580
  0.6 13.7 %copy-start = (bf16[4,512,512]{2,1,0:T(8,128)(2,1)S(1)}, bf16[4,512,512]{2,1,0:T(8,128)(2,1)}, u32[]{:S(2)}) copy-start(bf16[4,512,512]{2,1,0:T(8,128)(2,1)} %w.3) | copy-start | bytes 6291460
  0.7 13.7 %copy-start.4 = (s32[1,256,9]{1,0,2:T(1,128)S(1)}, s32[1,256,9]{1,0,2:T(1,128)}, u32[]{:S(2)}) copy-start(s32[1,256,9]{1,0,2:T(1,128)} %param.19) | copy-start | bytes 27652
  0.7 13.7 %copy-start.7 = (s32[1,1,256]{2,1,0:T(1,128)S(1)}, s32[1,1,256]{2,1,0:T(1,128)}, u32[]{:S(2)}) copy-start(s32[1,1,256]{2,1,0:T(1,128)} %param.18) | copy-start | bytes 3076
  0.7 13.7 %copy-start.6 = (f32[512]{0:T(512)S(1)}, f32[512]{0:T(512)}, u32[]{:S(2)}) copy-start(f32[512]{0:T(512)} %param.17) | copy-start | bytes 6148
  5.0 30.0 %collective-permute-start.2 = (bf16[256,512]{1,0:T(8,128)(2,1)}, bf16[256,512]{1,0:T(8,128)(2,1)S(1)}, u32[]{:S(2)}, u32[]{:S(2)}) collective-permute-start(bf16[256,512]{1,0:T(8,128)(2,1)} %gru.1.written), channel_id=1, source_target_pairs={{0,96},{1,97},{2,98},{3,99},{4,100},{5,101},{6,102},{7,103},{8,104... | collective-permute-start | bytes 786440 | tf_op jit(solution)/shard_map/ppermute | solution.py:499
  10.5 24.5 %collective-permute-start.1 = (bf16[256,512]{1,0:T(8,128)(2,1)}, bf16[256,512]{1,0:T(8,128)(2,1)S(1)}, u32[]{:S(2)}, u32[]{:S(2)}) collective-permute-start(bf16[256,512]{1,0:T(8,128)(2,1)} %gru.1.written), channel_id=1, source_target_pairs={{0,64},{32,96},{1,65},{33,97},{2,66},{34,98},{3,67},{35,99},{4,68}... | collective-permute-start | bytes 786440 | tf_op jit(solution)/shard_map/ppermute | solution.py:498
  11.8 23.2 %collective-permute-start = (bf16[256,512]{1,0:T(8,128)(2,1)}, bf16[256,512]{1,0:T(8,128)(2,1)S(1)}, u32[]{:S(2)}, u32[]{:S(2)}) collective-permute-start(bf16[256,512]{1,0:T(8,128)(2,1)} %gru.1.written), channel_id=1, source_target_pairs={{0,32},{32,64},{64,96},{1,33},{33,65},{65,97},{2,34},{34,66},{66,9... | collective-permute-start | bytes 786440 | tf_op jit(solution)/shard_map/ppermute | solution.py:497
  14.4 20.7 %copy-start.1 = (bf16[256,512]{1,0:T(8,128)(2,1)S(1)}, bf16[256,512]{1,0:T(8,128)(2,1)}, u32[]{:S(2)}) copy-start(bf16[256,512]{1,0:T(8,128)(2,1)} %state.3) | copy-start | bytes 786436
  14.4 20.7 %copy-start.2 = (bf16[256,512]{1,0:T(8,128)(2,1)S(1)}, bf16[256,512]{1,0:T(8,128)(2,1)}, u32[]{:S(2)}) copy-start(bf16[256,512]{1,0:T(8,128)(2,1)} %gru.1.written) | copy-start | bytes 786436
  18.3 30.5 %copy-start.3 = (bf16[1,256,512]{2,1,0:T(8,128)(2,1)S(1)}, bf16[1,256,512]{2,1,0:T(8,128)(2,1)}, u32[]{:S(2)}) copy-start(bf16[1,256,512]{2,1,0:T(8,128)(2,1)} %param.21) | copy-start | bytes 786436
  56.2 2.9 %collective-permute-start.3 = (bf16[16,64,512]{2,1,0:T(8,128)(2,1)S(1)}, bf16[16,64,512]{2,1,0:T(8,128)(2,1)S(1)}, u32[]{:S(2)}, u32[]{:S(2)}) collective-permute-start(bf16[16,64,512]{2,1,0:T(8,128)(2,1)S(1)} %get-tuple-element.54), channel_id=1, source_target_pairs={{0,1},{1,0},{2,3},{3,2},{4,5},{5,4},{6,7},{7,6},{8,9},{9,8},{10,11... | collective-permute-start | bytes 3145736 | tf_op jit(solution)/shard_map/ppermute | solution.py:515
  57.5 1.6 %collective-permute-start.4 = (bf16[128,512]{1,0:T(8,128)(2,1)S(1)}, bf16[128,512]{1,0:T(8,128)(2,1)S(1)}, u32[]{:S(2)}, u32[]{:S(2)}) collective-permute-start(bf16[128,512]{1,0:T(8,128)(2,1)S(1)} %get-tuple-element.56), channel_id=1, source_target_pairs={{0,1},{1,0},{2,3},{3,2},{4,5},{5,4},{6,7},{7,6},{8,9},{9,8},{10,11... | collective-permute-start | bytes 393224 | tf_op jit(solution)/shard_map/ppermute | solution.py:517
  81.3 4.7 %collective-permute-start.6 = (bf16[64,512]{1,0:T(8,128)(2,1)S(1)}, bf16[64,512]{1,0:T(8,128)(2,1)S(1)}, u32[]{:S(2)}, u32[]{:S(2)}) collective-permute-start(bf16[64,512]{1,0:T(8,128)(2,1)S(1)} %get-tuple-element.61.own), channel_id=1, source_target_pairs={{0,64},{32,96},{64,0},{96,32},{1,65},{33,97},{65,1},{97,33},{2,66}... | collective-permute-start | bytes 196616 | tf_op jit(solution)/shard_map/ppermute | solution.py:520
  82.5 3.5 %collective-permute-start.7 = (bf16[64,512]{1,0:T(8,128)(2,1)S(1)}, bf16[64,512]{1,0:T(8,128)(2,1)S(1)}, u32[]{:S(2)}, u32[]{:S(2)}) collective-permute-start(bf16[64,512]{1,0:T(8,128)(2,1)S(1)} %get-tuple-element.61.own), channel_id=1, source_target_pairs={{0,96},{32,0},{64,32},{96,64},{1,97},{33,1},{65,33},{97,65},{2,98}... | collective-permute-start | bytes 196616 | tf_op jit(solution)/shard_map/ppermute | solution.py:523
  84.6 4.5 %collective-permute-start.5 = (bf16[64,512]{1,0:T(8,128)(2,1)S(1)}, bf16[64,512]{1,0:T(8,128)(2,1)S(1)}, u32[]{:S(2)}, u32[]{:S(2)}) collective-permute-start(bf16[64,512]{1,0:T(8,128)(2,1)S(1)} %get-tuple-element.61.own), channel_id=1, source_target_pairs={{0,32},{32,64},{64,96},{96,0},{1,33},{33,65},{65,97},{97,1},{2,34}... | collective-permute-start | bytes 196616 | tf_op jit(solution)/shard_map/ppermute | solution.py:523
  105.7 7.1 %collective-permute-start.8 = (bf16[16,64,512]{2,1,0:T(8,128)(2,1)S(1)}, bf16[16,64,512]{2,1,0:T(8,128)(2,1)S(1)}, u32[]{:S(2)}, u32[]{:S(2)}) collective-permute-start(bf16[16,64,512]{2,1,0:T(8,128)(2,1)S(1)} %all_to_all.23.half), channel_id=1, source_target_pairs={{0,1},{1,0},{2,3},{3,2},{4,5},{5,4},{6,7},{7,6},{8,9},{9,8},{10,11... | collective-permute-start | bytes 3145736 | tf_op jit(solution)/shard_map/ppermute | solution.py:525

commit v12 on v10

--- a/solution.py
+++ b/solution.py
@@ -124,8 +124,9 @@
             for c in COS[-2::-1]:
                 wave = wave * u + c
             at = slice(k * TILE, (k + 1) * TILE)
-            code_t[tile, :, at] = wave.T.astype(BF)
-            code[tile, at] = wave.astype(BF)
+            wave = wave.astype(BF)
+            code_t[tile, :, at] = wave.T
+            code[tile, at] = wave
         for i in range(2):
             time_kv[tile, :, i * DM : (i + 1) * DM] = dot(code[tile], w[1 + i]).astype(BF)
 
@@ -269,7 +270,8 @@
             ],
             axis=1,
         ).astype(BF)
-        one, two = dot(spread, dkv[i]), dot(tt[i], dkv[i])
+        sums = dot(jnp.concatenate([tt[i], spread], axis=0), dkv[i])
+        one, two = sums[DM:], sums[:DM]
         s_kv = one if i == 0 else s_kv + one
         dot_t = two if i == 0 else dot_t + two
     s_kv = s_kv.astype(BF)

time: 113 us -> 113 us (level)
  no operation moved by 1% of the time
where the time goes in v12:
time: 113 us
  blocking collectives  67.7 us (60%)
  Pallas kernels  22 us (19%)
  starting transfers between devices  16.3 us (14%)
  waiting for transfers between devices  5.66 us (5%)
    all_to_all x2, blocking collectives, plane(): return lax.all_to_all(x, FLAT, split_axis=0, concat_axis=0, tiled=True)  38.3 us
    all_to_all x2, blocking collectives, exchange(): lax.all_to_all(blocks, axes, split_axis=0, concat_axis=0, tiled=True)  29.3 us
    pallas_call x1, Pallas kernels, attend(): pl.pallas_call(attend_kernel, in_specs=[pl.BlockSpec(memory_space=pltpu.S...  7.24 us
    ppermute x1, starting transfers between devices, on_device(): r3 = lax.ppermute(written, 'y', [(0, 3)])  5.48 us
    ppermute x1, starting transfers between devices, on_device(): far = lax.ppermute(half, 'core', swap)  4.83 us
    pallas_call x1, Pallas kernels, gru(): pl.pallas_call(gru_kernel, in_specs=[whole] + [far] * 4, out_specs=whole,...  4.35 us
    ppermute x3, waiting for transfers between devices, on_device(): lax.ppermute(part, 'y', [(i, (i + s) % SEG) for i in range(SEG)])  4.32 us
    pallas_call x1, Pallas kernels, time_parts(): pl.pallas_call(time_kernel, in_specs=[whole] * 5, out_specs=[whole] * 4,...  3.84 us
  transfers between devices with their start and end apart: 9, of which 4 were waited for; matrix products, arithmetic and copies ran while one was open for 0% of the time, Pallas kernels for 7%

profile of v12, /device:TPU:1, one launch (start us, length us, event | category | flops | bytes accessed | tf_op | source)
XLA Modules:
  0.0 112.6 jit_solution(13235303746616491134)
XLA Ops:
  0.6 0.0 copy-start.5
  0.6 0.0 copy-start
  0.7 0.0 copy-start.4
  0.7 0.0 copy-start.7
  0.7 0.0 copy-start.6
  0.7 4.3 %gru.1.written = bf16[256,512]{1,0:T(8,128)(2,1)} custom-call(s32[1,256]{1,0:T(1,128)} %touched.1, bf16[256,512]{1,0:T(8,128)(2,1)} %state.3, bf16[256,512]{1,0:T(8,128)(2,1)} %bitcast.33, bf16[512,1536]{1,0:T(8,128)(2,1)} %w_input.1, bf16[512,1536]{1,0:T(8,128)(2,1)} %w_state.1), custom_call_target="tpu_custom_call" | custom-call | flops 805306368 | bytes 4194304 | tf_op jit(solution)/shard_map/gru/pallas_call | solution.py:89
  5.0 5.5 %collective-permute-start.2 = (bf16[256,512]{1,0:T(8,128)(2,1)}, bf16[256,512]{1,0:T(8,128)(2,1)S(1)}, u32[]{:S(2)}, u32[]{:S(2)}) collective-permute-start(bf16[256,512]{1,0:T(8,128)(2,1)} %gru.1.written), channel_id=1, source_target_pairs={{0,96},{1,97},{2,98},{3,99},{4,100},{5,101},{6,102},{7,103},{8,104... | collective-permute-start | bytes 786440 | tf_op jit(solution)/shard_map/ppermute | solution.py:500
  10.5 1.3 %collective-permute-start.1 = (bf16[256,512]{1,0:T(8,128)(2,1)}, bf16[256,512]{1,0:T(8,128)(2,1)S(1)}, u32[]{:S(2)}, u32[]{:S(2)}) collective-permute-start(bf16[256,512]{1,0:T(8,128)(2,1)} %gru.1.written), channel_id=1, source_target_pairs={{0,64},{32,96},{1,65},{33,97},{2,66},{34,98},{3,67},{35,99},{4,68}... | collective-permute-start | bytes 786440 | tf_op jit(solution)/shard_map/ppermute | solution.py:499
  11.8 2.5 %collective-permute-start = (bf16[256,512]{1,0:T(8,128)(2,1)}, bf16[256,512]{1,0:T(8,128)(2,1)S(1)}, u32[]{:S(2)}, u32[]{:S(2)}) collective-permute-start(bf16[256,512]{1,0:T(8,128)(2,1)} %gru.1.written), channel_id=1, source_target_pairs={{0,32},{32,64},{64,96},{1,33},{33,65},{65,97},{2,34},{34,66},{66,9... | collective-permute-start | bytes 786440 | tf_op jit(solution)/shard_map/ppermute | solution.py:498
  14.3 0.0 copy-done.5
  14.3 0.0 copy-done
  14.4 0.0 copy-done.4
  14.4 0.0 copy-done.7
  14.4 0.0 copy-done.6
  14.4 0.0 copy-start.1
  14.4 0.0 copy-start.2
  14.4 3.8 %time_parts.1 = (bf16[2,512,1024]{2,1,0:T(8,128)(2,1)S(1)}, bf16[2,1024,1024]{2,1,0:T(8,128)(2,1)S(1)}, s32[256,128]{1,0:T(8,128)S(1)}, s32[256,128]{1,0:T(8,128)S(1)}) custom-call(s32[1,256]{1,0:T(1,128)S(1)} %bitcast.30, s32[8,256]{1,0:T(8,128)S(1)} %bitcast.28, f32[1,512]{1,0:T(1,128)S(1)} %bitcast.29, bf16[4,512,512]{2,1,0:T(8,128)(2,1)S(1)} %copy-done, ...), custom_call_target="tpu_custom_call" | custom-call | flops 2147483648 | bytes 8388608 | tf_op jit(solution)/shard_map/time_parts/pallas_call | solution.py:136
  18.3 0.0 copy-start.3
  18.3 16.8 %all_to_all.20 = s32[32,8,128]{2,1,0:T(8,128)S(1)} all-to-all(s32[32,8,128]{2,1,0:T(8,128)S(1)} %bitcast.25), channel_id=1, replica_groups=mesh['y'=4,'x'=4,'z'=4,'core'=2] {'x','z','core'}, dimensions={0} | all-to-all | bytes 262144 | tf_op jit(solution)/shard_map/all_to_all | solution.py:473
  35.1 0.0 collective-permute-done.2.r3
  35.1 0.0 collective-permute-done.1.r2
  35.1 0.0 collective-permute-done.r1
  35.1 0.0 copy-done.1
  35.1 0.0 copy-done.2
  35.1 1.1 start_rows.1
  36.2 12.5 %all_to_all.21 = bf16[32,8,512]{2,1,0:T(8,128)(2,1)S(1)} all-to-all(bf16[32,8,512]{2,1,0:T(8,128)(2,1)S(1)} %bitcast.24), channel_id=1, replica_groups=mesh['y'=4,'x'=4,'z'=4,'core'=2] {'x','z','core'}, dimensions={0} | all-to-all | bytes 524288 | tf_op jit(solution)/shard_map/all_to_all | solution.py:473
  48.7 7.2 %attend.1 = (bf16[16,64,512]{2,1,0:T(8,128)(2,1)S(1)}, bf16[16,64,512]{2,1,0:T(8,128)(2,1)S(1)}, bf16[256,512]{1,0:T(8,128)(2,1)S(1)}, bf16[256,512]{1,0:T(8,128...) custom-call(s32[1]{0:T(128)} %bitcast.4.core, bf16[256,512]{1,0:T(8,128)(2,1)S(1)} %bitcast.23, ...), custom_call_target="tpu_custom_call" | custom-call | flops 6442450944 | bytes 14680064 | tf_op jit(solution)/shard_map/attend/pallas_call | solution.py:325
  56.0 0.3 collective-permute-start.3
  56.3 1.0 events.1
  57.3 0.3 collective-permute-start.4
  57.6 1.3 %collective-permute-done.4.got = bf16[128,512]{1,0:T(8,128)(2,1)S(1)} collective-permute-done((bf16[128,512]{1,0:T(8,128)(2,1)S(1)}, bf16[128,512]{1,0:T(8,128)(2,1)S(1)}, u32[]{:S(2)}, u32[]{:S(2)}) %collective-permute-start.4) | collective-permute-done | bytes 131104 | tf_op jit(solution)/shard_map/ppermute | solution.py:518
  58.9 0.0 collective-permute-done.3.b
  58.9 0.3 pair_sum.1
  59.2 21.7 %all_to_all.22.a = bf16[16,80,512]{2,1,0:T(8,128)(2,1)S(1)} all-to-all(bf16[16,80,512]{2,1,0:T(8,128)(2,1)S(1)} %pair_sum.1), channel_id=1, replica_groups=mesh['y'=4,'x'=4,'z'=4,'core'=2] {'x','z'}, dimensions={0} | all-to-all | bytes 2621440 | tf_op jit(solution)/shard_map/all_to_all | solution.py:477
  80.9 0.1 plane_sum.1
  81.0 0.1 collective-permute-start.7
  81.1 1.5 %collective-permute-start.6 = (bf16[64,512]{1,0:T(8,128)(2,1)S(1)}, bf16[64,512]{1,0:T(8,128)(2,1)S(1)}, u32[]{:S(2)}, u32[]{:S(2)}) collective-permute-start(bf16[64,512]{1,0:T(8,128)(2,1)S(1)} %get-tuple-element.57.own), channel_id=1, source_target_pairs={{0,64},{32,96},{64,0},{96,32},{1,65},{33,97},{65,1},{97,33},{2,66}... | collective-permute-start | bytes 196616 | tf_op jit(solution)/shard_map/ppermute | solution.py:521
  82.6 0.0 collective-permute-start.5
  82.6 1.6 %collective-permute-done.7.r3 = bf16[64,512]{1,0:T(8,128)(2,1)S(1)} collective-permute-done((bf16[64,512]{1,0:T(8,128)(2,1)S(1)}, bf16[64,512]{1,0:T(8,128)(2,1)S(1)}, u32[]{:S(2)}, u32[]{:S(2)}) %collective-permute-start.7) | collective-permute-done | bytes 65568 | tf_op jit(solution)/shard_map/ppermute | solution.py:521
  84.2 1.6 %collective-permute-done.6.r2 = bf16[64,512]{1,0:T(8,128)(2,1)S(1)} collective-permute-done((bf16[64,512]{1,0:T(8,128)(2,1)S(1)}, bf16[64,512]{1,0:T(8,128)(2,1)S(1)}, u32[]{:S(2)}, u32[]{:S(2)}) %collective-permute-start.6) | collective-permute-done | bytes 65568 | tf_op jit(solution)/shard_map/ppermute | solution.py:521
  85.8 1.1 %collective-permute-done.5.r1 = bf16[64,512]{1,0:T(8,128)(2,1)S(1)} collective-permute-done((bf16[64,512]{1,0:T(8,128)(2,1)S(1)}, bf16[64,512]{1,0:T(8,128)(2,1)S(1)}, u32[]{:S(2)}, u32[]{:S(2)}) %collective-permute-start.5) | collective-permute-done | bytes 65568 | tf_op jit(solution)/shard_map/ppermute | solution.py:521
  87.0 0.1 seg_sum.1
  87.1 16.6 %all_to_all.23.half = bf16[16,64,512]{2,1,0:T(8,128)(2,1)S(1)} all-to-all(bf16[16,64,512]{2,1,0:T(8,128)(2,1)S(1)} %seg_sum.1), channel_id=1, replica_groups=mesh['y'=4,'x'=4,'z'=4,'core'=2] {'x','z'}, dimensions={0} | all-to-all | bytes 2097152 | tf_op jit(solution)/shard_map/all_to_all | solution.py:477
  103.7 4.8 %collective-permute-start.8 = (bf16[16,64,512]{2,1,0:T(8,128)(2,1)S(1)}, bf16[16,64,512]{2,1,0:T(8,128)(2,1)S(1)}, u32[]{:S(2)}, u32[]{:S(2)}) collective-permute-start(bf16[16,64,512]{2,1,0:T(8,128)(2,1)S(1)} %all_to_all.23.half), channel_id=1, source_target_pairs={{0,1},{1,0},{2,3},{3,2},{4,5},{5,4},{6,7},{7,6},{8,9},{9,8},{10,11... | collective-permute-start | bytes 3145736 | tf_op jit(solution)/shard_map/ppermute | solution.py:525
  108.6 1.1 owner_sum.1
  109.7 1.4 %own_half.1.rest_0_ = f32[16,2,64,512]{3,2,1,0:T(8,128)} custom-call(s32[1]{0:T(128)} %bitcast.4.core, bf16[16,64,512]{2,1,0:T(8,128)(2,1)S(1)} %all_to_all.23.half), custom_call_target="tpu_custom_call" | custom-call | flops 262144 | bytes 3145728 | tf_op jit(solution)/shard_map/own_half/pallas_call | solution.py:436
  111.1 0.0 collective-permute-done.8.half
  111.1 1.4 %far_half.1 = f32[16,2,64,512]{3,2,1,0:T(8,128)} custom-call(s32[1]{0:T(128)} %bitcast.4.core, bf16[16,64,512]{2,1,0:T(8,128)(2,1)S(1)} %collective-permute-done.8.half, f32[16,2,64,512]{3,2,1,0:T(8,128)} %own_half.1.rest_0_), custom_call_target="tpu_custom_call", output_to_operand_aliasing={{}: (2, {})} | custom-call | flops 262144 | bytes 3145728 | tf_op jit(solution)/shard_map/far_half/pallas_call | solution.py:436
  (1 shorter events, 0.0 us)
Async XLA Ops:
  0.6 13.7 %copy-start.5 = (s32[1,256,8]{1,2,0:T(8,128)S(1)}, s32[1,256,8]{1,2,0:T(8,128)}, u32[]{:S(2)}) copy-start(s32[1,256,8]{1,2,0:T(8,128)} %param.20) | copy-start | bytes 24580
  0.6 13.7 %copy-start = (bf16[4,512,512]{2,1,0:T(8,128)(2,1)S(1)}, bf16[4,512,512]{2,1,0:T(8,128)(2,1)}, u32[]{:S(2)}) copy-start(bf16[4,512,512]{2,1,0:T(8,128)(2,1)} %w.3) | copy-start | bytes 6291460
  0.7 13.7 %copy-start.4 = (s32[1,256,9]{1,0,2:T(1,128)S(1)}, s32[1,256,9]{1,0,2:T(1,128)}, u32[]{:S(2)}) copy-start(s32[1,256,9]{1,0,2:T(1,128)} %param.19) | copy-start | bytes 27652
  0.7 13.7 %copy-start.7 = (s32[1,1,256]{2,1,0:T(1,128)S(1)}, s32[1,1,256]{2,1,0:T(1,128)}, u32[]{:S(2)}) copy-start(s32[1,1,256]{2,1,0:T(1,128)} %param.18) | copy-start | bytes 3076
  0.7 13.7 %copy-start.6 = (f32[512]{0:T(512)S(1)}, f32[512]{0:T(512)}, u32[]{:S(2)}) copy-start(f32[512]{0:T(512)} %param.17) | copy-start | bytes 6148
  5.0 30.0 %collective-permute-start.2 = (bf16[256,512]{1,0:T(8,128)(2,1)}, bf16[256,512]{1,0:T(8,128)(2,1)S(1)}, u32[]{:S(2)}, u32[]{:S(2)}) collective-permute-start(bf16[256,512]{1,0:T(8,128)(2,1)} %gru.1.written), channel_id=1, source_target_pairs={{0,96},{1,97},{2,98},{3,99},{4,100},{5,101},{6,102},{7,103},{8,104... | collective-permute-start | bytes 786440 | tf_op jit(solution)/shard_map/ppermute | solution.py:500
  10.5 24.5 %collective-permute-start.1 = (bf16[256,512]{1,0:T(8,128)(2,1)}, bf16[256,512]{1,0:T(8,128)(2,1)S(1)}, u32[]{:S(2)}, u32[]{:S(2)}) collective-permute-start(bf16[256,512]{1,0:T(8,128)(2,1)} %gru.1.written), channel_id=1, source_target_pairs={{0,64},{32,96},{1,65},{33,97},{2,66},{34,98},{3,67},{35,99},{4,68}... | collective-permute-start | bytes 786440 | tf_op jit(solution)/shard_map/ppermute | solution.py:499
  11.8 23.2 %collective-permute-start = (bf16[256,512]{1,0:T(8,128)(2,1)}, bf16[256,512]{1,0:T(8,128)(2,1)S(1)}, u32[]{:S(2)}, u32[]{:S(2)}) collective-permute-start(bf16[256,512]{1,0:T(8,128)(2,1)} %gru.1.written), channel_id=1, source_target_pairs={{0,32},{32,64},{64,96},{1,33},{33,65},{65,97},{2,34},{34,66},{66,9... | collective-permute-start | bytes 786440 | tf_op jit(solution)/shard_map/ppermute | solution.py:498
  14.4 20.7 %copy-start.1 = (bf16[256,512]{1,0:T(8,128)(2,1)S(1)}, bf16[256,512]{1,0:T(8,128)(2,1)}, u32[]{:S(2)}) copy-start(bf16[256,512]{1,0:T(8,128)(2,1)} %state.3) | copy-start | bytes 786436
  14.4 20.7 %copy-start.2 = (bf16[256,512]{1,0:T(8,128)(2,1)S(1)}, bf16[256,512]{1,0:T(8,128)(2,1)}, u32[]{:S(2)}) copy-start(bf16[256,512]{1,0:T(8,128)(2,1)} %gru.1.written) | copy-start | bytes 786436
  18.3 30.5 %copy-start.3 = (bf16[1,256,512]{2,1,0:T(8,128)(2,1)S(1)}, bf16[1,256,512]{2,1,0:T(8,128)(2,1)}, u32[]{:S(2)}) copy-start(bf16[1,256,512]{2,1,0:T(8,128)(2,1)} %param.21) | copy-start | bytes 786436
  56.0 2.9 %collective-permute-start.3 = (bf16[16,64,512]{2,1,0:T(8,128)(2,1)S(1)}, bf16[16,64,512]{2,1,0:T(8,128)(2,1)S(1)}, u32[]{:S(2)}, u32[]{:S(2)}) collective-permute-start(bf16[16,64,512]{2,1,0:T(8,128)(2,1)S(1)} %get-tuple-element.52), channel_id=1, source_target_pairs={{0,1},{1,0},{2,3},{3,2},{4,5},{5,4},{6,7},{7,6},{8,9},{9,8},{10,11... | collective-permute-start | bytes 3145736 | tf_op jit(solution)/shard_map/ppermute | solution.py:516
  57.3 1.6 %collective-permute-start.4 = (bf16[128,512]{1,0:T(8,128)(2,1)S(1)}, bf16[128,512]{1,0:T(8,128)(2,1)S(1)}, u32[]{:S(2)}, u32[]{:S(2)}) collective-permute-start(bf16[128,512]{1,0:T(8,128)(2,1)S(1)} %get-tuple-element.54), channel_id=1, source_target_pairs={{0,1},{1,0},{2,3},{3,2},{4,5},{5,4},{6,7},{7,6},{8,9},{9,8},{10,11... | collective-permute-start | bytes 393224 | tf_op jit(solution)/shard_map/ppermute | solution.py:518
  81.0 3.2 %collective-permute-start.7 = (bf16[64,512]{1,0:T(8,128)(2,1)S(1)}, bf16[64,512]{1,0:T(8,128)(2,1)S(1)}, u32[]{:S(2)}, u32[]{:S(2)}) collective-permute-start(bf16[64,512]{1,0:T(8,128)(2,1)S(1)} %get-tuple-element.57.own), channel_id=1, source_target_pairs={{0,96},{32,0},{64,32},{96,64},{1,97},{33,1},{65,33},{97,65},{2,98}... | collective-permute-start | bytes 196616 | tf_op jit(solution)/shard_map/ppermute | solution.py:521
  81.1 4.7 %collective-permute-start.6 = (bf16[64,512]{1,0:T(8,128)(2,1)S(1)}, bf16[64,512]{1,0:T(8,128)(2,1)S(1)}, u32[]{:S(2)}, u32[]{:S(2)}) collective-permute-start(bf16[64,512]{1,0:T(8,128)(2,1)S(1)} %get-tuple-element.57.own), channel_id=1, source_target_pairs={{0,64},{32,96},{64,0},{96,32},{1,65},{33,97},{65,1},{97,33},{2,66}... | collective-permute-start | bytes 196616 | tf_op jit(solution)/shard_map/ppermute | solution.py:521
  82.6 4.3 %collective-permute-start.5 = (bf16[64,512]{1,0:T(8,128)(2,1)S(1)}, bf16[64,512]{1,0:T(8,128)(2,1)S(1)}, u32[]{:S(2)}, u32[]{:S(2)}) collective-permute-start(bf16[64,512]{1,0:T(8,128)(2,1)S(1)} %get-tuple-element.57.own), channel_id=1, source_target_pairs={{0,32},{32,64},{64,96},{96,0},{1,33},{33,65},{65,97},{97,1},{2,34}... | collective-permute-start | bytes 196616 | tf_op jit(solution)/shard_map/ppermute | solution.py:521
  103.7 7.3 %collective-permute-start.8 = (bf16[16,64,512]{2,1,0:T(8,128)(2,1)S(1)}, bf16[16,64,512]{2,1,0:T(8,128)(2,1)S(1)}, u32[]{:S(2)}, u32[]{:S(2)}) collective-permute-start(bf16[16,64,512]{2,1,0:T(8,128)(2,1)S(1)} %all_to_all.23.half), channel_id=1, source_target_pairs={{0,1},{1,0},{2,3},{3,2},{4,5},{5,4},{6,7},{7,6},{8,9},{9,8},{10,11... | collective-permute-start | bytes 3145736 | tf_op jit(solution)/shard_map/ppermute | solution.py:525
